TPU v7x, 512 devices: a whole 4x4x16 slice. The times are simulated.
512 devices in a mesh: dp: 32 (over x, y, core), tensor: 4 (over z_lo), replica: 4 (over z_hi).
Axes of the slice: x: 4, y: 4, z: 16 (z_hi: 4, z_lo: 4; z = z_hi * 4 + z_lo), core: 2. Of those that a mesh axis runs over, the one named last changes fastest.
Arguments:
- hidden_state: bfloat16 [128, 2, 128, 3584], P(('dp', 'replica'), None, None, 'tensor'), may hold values from -6 to 6
- attn_out: bfloat16 [128, 2, 128, 3584], P(('dp', 'replica'), None, None, 'tensor'), may hold values from -6 to 6
- o_weight: bfloat16 [3584, 3584], P('tensor', 'replica'), may hold values from -0.09375 to 0.09375
- norm_gain: float32 [3584], P('tensor'), may hold values from 0.1 to 1.9
- lengths: int32 [128, 2], P(('dp', 'replica')), may hold values from 32 to 128
- positive: int32 [128], P(('dp', 'replica')), may hold values from 0 to 31
Outputs:
- grad_hidden: bfloat16 [128, 2, 128, 3584], P(('dp', 'replica'), None, None, 'tensor')
- grad_attn: bfloat16 [128, 2, 128, 3584], P(('dp', 'replica'), None, None, 'tensor')
- grad_weight: bfloat16 [3584, 3584], P('tensor', 'replica')
- grad_gain: float32 [3584], P('tensor')
- loss: float32 [], replicated
All inputs are finite; a program needn't handle non-finite values.
Results may differ from a plain program's by a relative error of at most 0.002.
Values may be sent and summed in bfloat16 or wider, within the bound.
No kernel may reach another device: no remote copies, remote signals or barrier semaphores. Data moves between devices by JAX's collectives and lax.ppermute only.
A program may use at most 128 MiB of HBM per device.

v0:
```python
import jax
import jax.numpy as jnp
from jax import lax
from jax.sharding import PartitionSpec as P

logit_scale = 20.0
grad_scale = 256.0
epsilon = 1e-06


def body(hidden_state, attn_out, o_weight, norm_gain, lengths, positive):
    highest = lax.Precision.HIGHEST
    pairs_here, sides, seq_len, feat_here = hidden_state.shape
    full_width = feat_here * lax.axis_size("tensor")
    group_size = pairs_here * lax.axis_size("dp")
    states = hidden_state.astype(jnp.float32)
    square_part = jnp.sum(states * states, -1)
    mean_square = lax.psum(square_part, "tensor") / full_width
    inv_rms = lax.rsqrt(mean_square + epsilon)[..., None]
    positions = jnp.arange(seq_len, dtype=jnp.int32)
    valid_mask = (positions[None, None, :] < lengths[:, :, None]).astype(jnp.float32)
    token_count = lengths.astype(jnp.float32)
    embeds = (
        jnp.einsum("nst,nstd->nsd", valid_mask, states * inv_rms * norm_gain, precision=highest)
        / token_count[..., None]
    )
    embed_sq = lax.psum(jnp.sum(embeds * embeds, -1), "tensor")
    inv_norm = lax.rsqrt(embed_sq + epsilon)[..., None]
    unit_emb = embeds * inv_norm
    query_unit = unit_emb[:, 0]
    passage_unit = unit_emb[:, 1]
    contract_first = (((0,), (0,)), ((), ()))
    contract_last = (((1,), (1,)), ((), ()))
    passage_all = lax.all_gather(passage_unit, "dp", axis=0, tiled=True)
    partial_value = logit_scale * lax.dot_general(
        query_unit, passage_all, contract_last, precision=highest
    )
    logits = lax.psum(partial_value, "tensor")
    log_total = jnp.log(jnp.sum(jnp.exp(logits), -1))
    one_hot = (jnp.arange(group_size, dtype=jnp.int32)[None, :] == positive[:, None]).astype(
        jnp.float32
    )
    chosen = jnp.sum(logits * one_hot, -1)
    loss_part = jnp.sum(log_total - chosen)
    score_grad = grad_scale * (jnp.exp(logits - log_total[:, None]) - one_hot)
    query_grad = logit_scale * jnp.dot(score_grad, passage_all, precision=highest)
    passage_terms = logit_scale * lax.dot_general(
        score_grad, query_unit, contract_first, precision=highest
    )
    passage_grad = lax.psum_scatter(passage_terms, "dp", scatter_dimension=0, tiled=True)
    embed_grad = jnp.stack([query_grad, passage_grad], 1)
    along = lax.psum(jnp.sum(unit_emb * embed_grad, -1), "tensor")
    pooled_grad = (embed_grad - unit_emb * along[..., None]) * inv_norm
    normed_grad = valid_mask[..., None] * (pooled_grad / token_count[..., None])[:, :, None, :]
    scaled_grad = norm_gain * normed_grad
    norm_part = jnp.sum(scaled_grad * states, -1)
    norm_term = (lax.psum(norm_part, "tensor") / full_width)[..., None]
    state_grad = inv_rms * scaled_grad - states * (inv_rms * inv_rms * inv_rms) * norm_term
    grad_rounded = state_grad.astype(jnp.bfloat16)
    gain_part = jnp.sum(normed_grad * states * inv_rms, (0, 1, 2))
    loss_total, gain_total = lax.psum((loss_part, gain_part), ("dp", "replica"))
    token_rows = pairs_here * sides * seq_len
    flat_grad = state_grad.reshape(token_rows, feat_here)
    flat_attn = attn_out.reshape(token_rows, feat_here)
    grad_full = lax.all_gather(flat_grad, "tensor", axis=1, tiled=True)
    grad_columns = lax.all_to_all(grad_full, "replica", split_axis=1, concat_axis=0, tiled=True)
    attn_all = lax.all_gather(flat_attn, "replica", axis=0, tiled=True)
    weight_part = lax.dot_general(
        attn_all.astype(jnp.float32), grad_columns, contract_first, precision=highest
    )
    weight_out = lax.psum(weight_part, "dp").astype(jnp.bfloat16)
    attn_grad = lax.dot_general(
        grad_full,
        lax.all_gather(o_weight, "replica", axis=1, tiled=True).astype(jnp.float32),
        contract_last,
        precision=highest,
    )
    grad_attn = attn_grad.astype(jnp.bfloat16).reshape(pairs_here, sides, seq_len, feat_here)
    return (grad_rounded, grad_attn, weight_out, gain_total, loss_total)


def solution(mesh):
    placed = (
        P(("dp", "replica"), None, None, "tensor"),
        P(("dp", "replica"), None, None, "tensor"),
        P("tensor", "replica"),
        P("tensor"),
        P(("dp", "replica"), None),
        P(("dp", "replica")),
    )
    return jax.shard_map(
        body,
        mesh=mesh,
        in_specs=placed,
        out_specs=(
            P(("dp", "replica"), None, None, "tensor"),
            P(("dp", "replica"), None, None, "tensor"),
            P("tensor", "replica"),
            P("tensor"),
            P(),
        ),
        check_vma=False,
    )
```

profile of v0, /device:TPU:1, one launch (start us, length us, event | category | flops | bytes accessed | tf_op | source)
XLA Modules:
  0.0 1286.1 jit_solution(4832671633806279504)
XLA Ops:
  7.2 0.0 all-reduce.5.cloned.1.call-start
  7.2 0.7 convert_bitcast_fusion
  7.9 1.2 fusion.4
  9.1 11.8 psum.56
  20.9 0.7 fusion.23
  21.6 1.6 fusion.7
  23.2 0.2 multiply_reduce_fusion.1
  23.4 6.6 psum.57
  30.0 0.1 multiply_bitcast_fusion
  30.8 29.1 %all-gather = f32[32,1,896]{2,1,0:T(1,128)S(1)} all-gather(f32[1,1,896]{2,1,0:T(1,128)S(1)} %get-tuple-element.35), channel_id=2, replica_groups=mesh['dp'=32,'tensor'=4,'replica'=4] {'dp'}, dimensions={0}, use_global_device_ids=true | all-gather | bytes 118272 | tf_op jit(solution)/shard_map/all_gather | solution.py:34
  59.9 0.2 fusion.2
  60.1 8.4 psum.58
  68.5 0.6 fusion.26
  69.8 0.7 multiply_multiply_fusion.1
  70.5 0.0 all-reduce.5.cloned.1.call-update
  70.5 0.0 all-gather.5.cloned.1.call-start
  70.6 0.2 convolution_reduce_fusion
  70.8 1.3 dynamic-slice
  72.1 129.3 %all-reduce.5.cloned.1.call-done = f32[32,896]{1,0:T(8,128)} async-done(((f32[32,896]{1,0:T(8,128)}), f32[32,896]{1,0:T(8,128)}) %all-reduce.5.cloned.1.call-update) | async-done | bytes 114704
  201.4 1.4 constant_dynamic-slice_fusion
  202.8 0.2 multiply_reduce_fusion
  203.0 9.9 psum.59
  212.9 0.1 multiply_divide_fusion
  212.9 1.5 fusion.12
  214.5 6.6 psum.60
  221.1 2.1 fusion.3
  223.2 1.2 copy.21
  224.4 0.0 all-gather.5.cloned.1.call-update
  224.5 0.0 all-gather.7.cloned.1.call-start
  224.5 0.7 all-gather.7.cloned.1.call-update
  225.2 80.5 %all-gather.5.cloned.1.call-done = f32[256,3584]{0,1:T(8,128)} async-done(((f32[256,896]{0,1:T(8,128)}), f32[256,3584]{0,1:T(8,128)}) %all-gather.5.cloned.1.call-update) | async-done | bytes 3670032 | tf_op jit(solution)/shard_map/all_gather | solution.py:65
  305.7 10.9 all-to-all-start
  316.6 0.0 all-gather.9.cloned.1.call-start
  316.6 0.6 all-gather.9.cloned.1.call-update
  317.8 780.8 %all-reduce.1 = (f32[896]{0:T(1024)}, f32[]{:T(128)}) all-reduce(f32[896]{0:T(1024)S(1)} %get-tuple-element.25, f32[]{:T(128)S(6)} %sub.27), channel_id=1, replica_groups=mesh['dp'=32,'tensor'=4,'replica'=4] {'dp','replica'}, use_global_device_ids=true, to_apply=%region_13.0 | all-reduce | flops 897 | bytes 7176 | tf_op jit(solution)/shard_map/psum | solution.py:61
  1098.6 0.0 all-gather.7.cloned.1.call-done
  1098.6 15.0 %convolution_convert_fusion = bf16[256,896]{1,0:T(8,128)(2,1)} fusion(f32[256,3584]{0,1:T(8,128)} %all-gather.5.cloned.1.call-done, bf16[896,3584]{1,0:T(8,128)(2,1)} %all-gather.7.cloned.1.call-done), kind=kOutput, calls=%fused_computation.7 | convolution fusion | flops 9865232384 | bytes 10551296 | tf_op jit(solution)/shard_map/dot_general | solution.py:72
  1113.6 0.0 all-to-all-done
  1113.6 4.7 copy.17
  1118.2 0.0 all-gather.9.cloned.1.call-done
  1118.2 9.6 convolution_bitcast_fusion
  1127.9 149.4 %all-reduce.6 = bf16[896,896]{0,1:T(8,128)(2,1)S(1)} all-reduce(f32[896,896]{0,1:T(8,128)} %convolution_bitcast_fusion), channel_id=1, replica_groups=mesh['dp'=32,'tensor'=4,'replica'=4] {'dp'}, use_global_device_ids=true, to_apply=%region_11.0 | all-reduce | flops 802816 | bytes 4816896 | tf_op jit(solution)/shard_map/psum | solution.py:71
  1277.2 2.3 copy.18
  (8 shorter events, 0.1 us)
Async XLA Ops:
  7.2 194.2 %all-reduce.5.cloned.1.call-start = ((), (), s32[]{:S(2)}) async-start(), calls=%async_computation.4 | async-start | bytes 229376
  70.5 235.1 %all-gather.5.cloned.1.call-start = ((), (), s32[]{:S(2)}) async-start(), calls=%async_computation.1 | async-start | bytes 4587520 | tf_op jit(solution)/shard_map/all_gather | solution.py:65
  224.5 874.1 %all-gather.7.cloned.1.call-start = ((), (), s32[]{:S(2)}) async-start(), calls=%async_computation.2 | async-start | bytes 8028160 | tf_op jit(solution)/shard_map/all_gather | solution.py:74
  305.7 807.9 %all-to-all-start = ((f32[256,4,896]{0,2,1:T(8,128)}), f32[256,4,896]{0,2,1:T(8,128)}, u32[]{:S(2)}, u32[]{:S(2)}) async-start(f32[256,4,896]{0,2,1:T(8,128)} %bitcast.62), calls=%async_computation | async-start | bytes 7340032 | tf_op jit(solution)/shard_map/all_to_all | solution.py:66
  316.6 801.6 %all-gather.9.cloned.1.call-start = ((), (), s32[]{:S(2)}) async-start(), calls=%async_computation.3 | async-start | bytes 2293760 | tf_op jit(solution)/shard_map/all_gather | solution.py:67
Sparse Core Ops, SparseCore 0:
  70.7 130.6 all-reduce.4
  224.6 81.0 all-gather.4
  308.0 386.9 all-gather.6
  697.2 81.5 all-gather.8
where the time goes:
time: 1290 us
  blocking collectives  1000 us (78%)
  waiting for transfers between devices  211 us (16%)
  matrix products  26.6 us (2%)
  between operations  15.8 us (1%)
    psum x1, blocking collectives, body(): loss_total, gain_total = lax.psum((loss_part, gain_part), ('dp', 'replica'))  781 us
    psum x1, blocking collectives, body(): weight_out = lax.psum(weight_part, 'dp').astype(jnp.bfloat16)  149 us
    unnamed x5, waiting for transfers between devices  131 us
    all_gather x1, waiting for transfers between devices, body(): grad_full = lax.all_gather(flat_grad, 'tensor', axis=1, tiled=True)  80.5 us
    all_gather x1, blocking collectives, body(): passage_all = lax.all_gather(passage_unit, 'dp', axis=0, tiled=True)  29.1 us
  transfers between devices with their start and end apart: 5, of which 2 were waited for; matrix products, arithmetic and copies ran while one was open for 2% of the time, Pallas kernels for 0%

commit v1 on v0

v1 whole, which is shorter than its diff:
```python
import jax
import jax.numpy as jnp
from jax import lax
from jax.sharding import Mesh, PartitionSpec as P

logit_scale = 20.0
grad_scale = 256.0
epsilon = 1e-06

f32 = jnp.float32
bf16 = jnp.bfloat16

NX, NY, NC, NT, NR = 4, 4, 2, 4, 4
PLANE = ("x", "y")
DP = ("x", "y", "c")

D = 3584
FEAT = D // NT
COLS = D // NR
SEQ = 128
TOK = 2 * SEQ
HALF = FEAT // NC
SLICE = HALF // (NX * NY)
W_ROWS = FEAT // (NY * NC)

AT_RMS = D
AT_U = D + SEQ
AT_LEN = AT_U + SLICE
AT_POS = AT_LEN + 1
WIDTH = D + 2 * SEQ


def swap_core(value):
    return lax.ppermute(value, "c", [(0, 1), (1, 0)])


def split3(value):
    high = lax.reduce_precision(value, 8, 7)
    rest = value - high
    mid = lax.reduce_precision(rest, 8, 7)
    low = rest - mid
    return high.astype(bf16), mid.astype(bf16), low.astype(bf16)


def body(hidden_state, attn_out, o_weight, norm_gain, lengths, positive):
    highest = lax.Precision.HIGHEST
    ix, iy, ic = lax.axis_index("x"), lax.axis_index("y"), lax.axis_index("c")
    it, ir = lax.axis_index("t"), lax.axis_index("r")
    dp_index = (ix * NY + iy) * NC + ic

    state = hidden_state.reshape(TOK, FEAT)
    attn = attn_out.reshape(TOK, FEAT)
    state_all = lax.all_gather(state, "t")
    w_start = (iy * NC + ic) * W_ROWS
    w_mine = lax.dynamic_slice(o_weight, (w_start, 0), (W_ROWS, COLS))
    w_moved = lax.ppermute(
        w_mine,
        ("x", "r"),
        [(i * NR + (j + i) % NR, i * NR + j) for i in range(NX) for j in range(NR)],
    )
    w_all = lax.all_gather(w_moved, DP).reshape(NX, FEAT, COLS)
    attn_keep = jnp.where(ic == 0, attn[:, :HALF], attn[:, HALF:])
    attn_give = jnp.where(ic == 0, attn[:, HALF:], attn[:, :HALF])
    attn_other = swap_core(attn_give)

    states = state.astype(f32).reshape(2, SEQ, FEAT)
    square = lax.psum(jnp.sum(states * states, -1), "t") / D
    inv_rms = lax.rsqrt(square + epsilon)
    token_count = lengths.reshape(2).astype(f32)
    valid = (jnp.arange(SEQ, dtype=jnp.int32)[None, :] < lengths.reshape(2)[:, None]).astype(f32)
    pool_weight = valid * inv_rms / token_count[:, None]
    pooled = jnp.sum(pool_weight[..., None] * states, 1)
    attn_pool = jnp.sum(pool_weight[..., None] * attn.astype(f32).reshape(2, SEQ, FEAT), 1)

    near = jnp.concatenate([pooled, norm_gain[None]], 0)
    near = lax.all_to_all(jnp.broadcast_to(near[None], (NT, 3, FEAT)), "t", 0, 0)
    pooled_row = near[:, :2].transpose(1, 0, 2).reshape(2, D)
    gain = near[:, 2].reshape(D)

    u_parts = attn_pool.reshape(2, NC, NX * NY, SLICE).transpose(2, 1, 0, 3)
    u_parts = u_parts.reshape(NX * NY * NC, 2, SLICE)
    extra = jnp.stack(
        [token_count, jnp.broadcast_to(positive.astype(f32), (2,))], -1
    )
    row = jnp.concatenate([pooled_row, inv_rms], -1)
    group = NX * NY * NC
    send = jnp.concatenate(
        [
            jnp.broadcast_to(row[None], (group, 2, D + SEQ)),
            u_parts,
            jnp.broadcast_to(extra[None], (group, 2, 2)),
            jnp.zeros((group, 2, WIDTH - AT_POS - 1), f32),
        ],
        -1,
    )
    got = lax.all_to_all(send, DP, 0, 0)

    raw = got[..., :D]
    embeds = raw * gain
    inv_norm = lax.rsqrt(jnp.sum(embeds * embeds, -1, keepdims=True) + epsilon)
    unit = embeds * inv_norm
    query, passage = unit[:, 0], unit[:, 1]
    target = got[:, 0, AT_POS].astype(jnp.int32)
    contract_last = (((1,), (1,)), ((), ()))
    contract_first = (((0,), (0,)), ((), ()))
    logits = logit_scale * lax.dot_general(query, passage, contract_last, precision=highest)
    log_total = jnp.log(jnp.sum(jnp.exp(logits), -1))
    one_hot = (jnp.arange(group, dtype=jnp.int32)[None, :] == target[:, None]).astype(f32)
    loss_part = jnp.sum(log_total - jnp.sum(logits * one_hot, -1))
    score_grad = grad_scale * (jnp.exp(logits - log_total[:, None]) - one_hot)
    query_grad = logit_scale * jnp.dot(score_grad, passage, precision=highest)
    passage_grad = logit_scale * lax.dot_general(
        score_grad, query, contract_first, precision=highest
    )
    embed_grad = jnp.stack([query_grad, passage_grad], 1)
    along = jnp.sum(unit * embed_grad, -1, keepdims=True)
    pooled_grad = (embed_grad - unit * along) * inv_norm
    gain_part = jnp.sum(pooled_grad * raw, (0, 1))
    scaled = pooled_grad * gain
    gain_mine = lax.dynamic_slice(gain_part, (it * FEAT,), (FEAT,))
    totals = lax.psum(jnp.concatenate([gain_mine, loss_part[None]]), "r")

    other_index = dp_index + 1 - 2 * ic
    state_other = swap_core(state_all)
    rows = jnp.stack([scaled[dp_index], scaled[other_index]])
    counts = jnp.stack([got[dp_index, :, AT_LEN], got[other_index, :, AT_LEN]])
    rms = jnp.stack([got[dp_index, :, AT_RMS:AT_U], got[other_index, :, AT_RMS:AT_U]])
    place = jnp.arange(SEQ, dtype=jnp.int32).astype(f32)
    first_coef = jnp.where(place < counts[..., None], rms / counts[..., None], 0.0)
    both = jnp.stack([state_all, state_other]).reshape(2, NT, 2, SEQ, FEAT)
    inner = jnp.einsum(
        "ptskf,pstf->psk",
        both.astype(f32),
        rows.reshape(2, 2, NT, FEAT),
        precision=highest,
    )
    coef = first_coef * rms * rms * inner / D

    attn_pair = jnp.stack([attn_keep, attn_other]).astype(f32)
    attn_scaled = (attn_pair * coef.reshape(2, TOK, 1)).astype(bf16).reshape(2 * TOK, HALF)
    flat_states = both.reshape(2, NT, TOK, FEAT)
    parts = []
    for block in range(NR):
        block_states = flat_states[:, block].reshape(2 * TOK, FEAT)
        part = lax.dot_general(
            attn_scaled, block_states, contract_first, preferred_element_type=f32
        )
        parts.append(part.astype(bf16).reshape(NX * NY, 1, SLICE, COLS))
    partial = jnp.concatenate(parts, 1).reshape(NX * NY, NR * SLICE, COLS)
    spread = lax.all_to_all(partial, PLANE, 0, 0)
    second = jnp.sum(spread.astype(f32), 0).reshape(NR, SLICE, COLS)

    u_all = got[..., AT_U:AT_LEN].reshape(2 * group, SLICE)
    first = lax.dot_general(
        u_all, scaled.reshape(2 * group, D), contract_first, precision=highest
    )
    mine = first.reshape(SLICE, NR, COLS).transpose(1, 0, 2) - second
    total = lax.dynamic_index_in_dim(mine, ir, 0, keepdims=False)
    for step in range(1, NR):
        outgoing = lax.dynamic_index_in_dim(mine, (ir + step) % NR, 0, keepdims=False)
        total = total + lax.ppermute(
            outgoing, "r", [(j, (j + step) % NR) for j in range(NR)]
        )
    done = jnp.broadcast_to(total.astype(bf16)[None], (NX * NY, SLICE, COLS))
    half = lax.all_to_all(done, PLANE, 0, 0).reshape(HALF, COLS)
    half_other = swap_core(half)
    grad_weight = jnp.where(
        ic == 0,
        jnp.concatenate([half, half_other], 0),
        jnp.concatenate([half_other, half], 0),
    )

    own_first = first_coef[0]
    own_coef = coef[0]
    own_rows = rows[0].reshape(2, NT, FEAT)
    row_here = lax.dynamic_index_in_dim(own_rows, it, 1, keepdims=False)
    state_grad = own_first[..., None] * row_here[:, None, :] - states * own_coef[..., None]
    grad_hidden = state_grad.astype(bf16).reshape(1, 2, SEQ, FEAT)

    pieces = jnp.stack(split3(own_rows)).reshape(6, NT, FEAT)
    token_part = jnp.zeros((TOK, FEAT), f32)
    row_part = jnp.zeros((6, FEAT), f32)
    for block in range(NX):
        which = (ir + block) % NR
        token_part = token_part + lax.dot_general(
            lax.dynamic_index_in_dim(state_all, which, 0, keepdims=False),
            w_all[block],
            contract_last,
            preferred_element_type=f32,
        )
        row_part = row_part + lax.dot_general(
            lax.dynamic_index_in_dim(pieces, which, 1, keepdims=False),
            w_all[block],
            contract_last,
            preferred_element_type=f32,
        )
    row_sum = jnp.sum(row_part.reshape(3, 2, FEAT)[::-1], 0)
    attn_grad = (
        own_first[..., None] * row_sum[:, None, :]
        - token_part.reshape(2, SEQ, FEAT) * own_coef[..., None]
    )
    grad_attn = attn_grad.astype(bf16).reshape(1, 2, SEQ, FEAT)
    return (grad_hidden, grad_attn, grad_weight, totals[:FEAT], totals[FEAT])


def solution(mesh):
    fine = Mesh(mesh.devices.reshape(NX, NY, NC, NT, NR), ("x", "y", "c", "t", "r"))
    pairs = ("x", "y", "c", "r")
    placed = (
        P(pairs, None, None, "t"),
        P(pairs, None, None, "t"),
        P("t", "r"),
        P("t"),
        P(pairs, None),
        P(pairs),
    )
    return jax.shard_map(
        body,
        mesh=fine,
        in_specs=placed,
        out_specs=(
            P(pairs, None, None, "t"),
            P(pairs, None, None, "t"),
            P("t", "r"),
            P("t"),
            P(),
        ),
        check_vma=False,
    )
```

time: 1290 us -> 300 us (0.23)
  blocking collectives: 1000 us -> 23.9 us
  waiting for transfers between devices: 211 us -> 90.3 us
  starting transfers between devices: 11 us -> 83.8 us
  local copies, waits for them, and re-layouts: 10.9 us -> 25.8 us
  other arithmetic: 8.12 us -> 22 us
    psum x7 -> x2, blocking collectives: 973 us -> 23.9 us  [the longest x1 12.1 us: body(): totals = lax.psum(jnp.concatenate([gain_mine, loss_part[None]]), 'r')]
    unnamed x5 -> x2, waiting for transfers between devices: 131 us -> 1.37 us
    all_gather x3 -> x2, waiting for transfers between devices: 80.5 us -> 0.02 us  [the longest x1 0.02 us: body(): state_all = lax.all_gather(state, 't')]
    all_to_all x1 -> x4, waiting for transfers between devices: 0.01 us -> 79.5 us  [the longest x1 55 us: body(): spread = lax.all_to_all(partial, PLANE, 0, 0)]
    all_to_all x1 -> x4, starting transfers between devices: 10.9 us -> 51.4 us  [the longest x1 19.4 us: body(): got = lax.all_to_all(send, DP, 0, 0)]
    ppermute x0 -> x7, starting transfers between devices: none -> 32.3 us  [the longest x3 19.7 us: body(): lax.ppermute(outgoing, 'r', [(j, (j + step) % NR) for j in range(NR)])]
    all_gather x1 -> x0, blocking collectives: 29.1 us -> none  [body(): passage_all = lax.all_gather(passage_unit, 'dp', axis=0, tiled=True)]
    dot_general x5 -> x17, matrix products: 26.6 us -> 34.1 us  [the longest x4 9.99 us: body(): lax.dot_general(attn_scaled, block_states, contract_first, preferred_elem...]
  transfers between devices with their start and end apart: 5 -> 13, of which waited for: 2 -> 4; matrix products, arithmetic and copies ran while one was open for 2% -> 20% of each run, Pallas kernels for 0% -> 0%
where the time goes in v1:
time: 300 us; the launch traced here: 295 us
  waiting for transfers between devices  90.3 us (30%)
  starting transfers between devices  83.8 us (28%)
  matrix products  34.1 us (11%)
  local copies, waits for them, and re-layouts  25.8 us (9%)
  blocking collectives  23.9 us (8%)
  other arithmetic  22 us (7%)
  between operations  15.4 us (5%)
    all_to_all x1, waiting for transfers between devices, body(): spread = lax.all_to_all(partial, PLANE, 0, 0)  55 us
    ppermute x3, starting transfers between devices, body(): lax.ppermute(outgoing, 'r', [(j, (j + step) % NR) for j in range(NR)])  19.7 us
    all_to_all x1, starting transfers between devices, body(): got = lax.all_to_all(send, DP, 0, 0)  19.4 us
    all_to_all x1, starting transfers between devices, body(): spread = lax.all_to_all(partial, PLANE, 0, 0)  17.4 us
    all_to_all x1, waiting for transfers between devices, body(): half = lax.all_to_all(done, PLANE, 0, 0).reshape(HALF, COLS)  14.1 us
    psum x1, blocking collectives, body(): totals = lax.psum(jnp.concatenate([gain_mine, loss_part[None]]), 'r')  12.1 us
    psum x1, blocking collectives, body(): square = lax.psum(jnp.sum(states * states, -1), 't') / D  11.8 us
    all_to_all x1, starting transfers between devices, body(): half = lax.all_to_all(done, PLANE, 0, 0).reshape(HALF, COLS)  11.3 us
  transfers between devices with their start and end apart: 13, of which 4 were waited for; matrix products, arithmetic and copies ran while one was open for 20% of the time, Pallas kernels for 0%

profile of v1, /device:TPU:1, one launch (start us, length us, event | category | flops | bytes accessed | tf_op | source)
XLA Modules:
  0.0 295.2 jit_solution(8845490270377161173)
XLA Ops:
  8.6 1.2 fusion.45
  9.8 11.8 %psum.14 = f32[2,128]{1,0:T(2,128)S(1)} all-reduce(f32[2,128]{1,0:T(2,128)S(1)} %fusion.45), channel_id=1, replica_groups=mesh['x'=4,'y'=4,'c'=2,'t'=4,'r'=4] {'t'}, use_global_device_ids=true, to_apply=%region_1.2 | all-reduce | flops 256 | bytes 2048 | tf_op jit(solution)/shard_map/psum | solution.py:67
  23.1 1.4 fusion.54
  25.1 3.3 %all-to-all-start = ((f32[4,3,896]{2,1,0:T(4,128)}), f32[4,3,896]{2,1,0:T(4,128)S(1)}, u32[]{:S(2)}, u32[]{:S(2)}) async-start(f32[4,3,896]{2,1,0:T(4,128)} %broadcast_in_dim.18), calls=%async_computation | async-start | bytes 114688 | tf_op jit(solution)/shard_map/all_to_all | solution.py:76
  29.2 3.4 %collective-permute-start.1 = (bf16[112,896]{1,0:T(8,128)(2,1)}, bf16[112,896]{1,0:T(8,128)(2,1)}, u32[]{:S(2)}, u32[]{:S(2)}) collective-permute-start(bf16[112,896]{1,0:T(8,128)(2,1)} %constant_dynamic-slice_fusion.3), channel_id=1, source_target_pairs={{0,0},{1,1},{2,2},{3,3},{129,128},{130,129},{131,130},{128,131},{2... | collective-permute-start | bytes 602120 | tf_op jit(solution)/shard_map/ppermute | solution.py:56
  34.4 2.2 concatenate.24
  36.6 19.4 %all-to-all-start.1 = ((f32[32,2,3840]{2,1,0:T(2,128)}), f32[32,2,3840]{2,1,0:T(2,128)S(1)}, u32[]{:S(2)}, u32[]{:S(2)}) async-start(f32[32,2,3840]{2,1,0:T(2,128)} %concatenate.24), calls=%async_computation.1 | async-start | bytes 1966080 | tf_op jit(solution)/shard_map/all_to_all | solution.py:96
  56.8 2.0 select_bitcast_fusion
  58.8 2.1 collective-permute-start.2
  61.8 10.4 %all-to-all-done.1 = f32[32,2,3840]{2,1,0:T(2,128)S(1)} async-done(((f32[32,2,3840]{2,1,0:T(2,128)}), f32[32,2,3840]{2,1,0:T(2,128)S(1)}, u32[]{:S(2)}, u32[]{:S(2)}) %all-to-all-start.1) | async-done | bytes 983072 | tf_op jit(solution)/shard_map/all_to_all | solution.py:96
  73.4 2.2 collective-permute-start
  75.6 1.5 fusion.70
  82.8 5.1 %fusion.6 = f32[2,2,1,128,1]{3,2,4,1,0:T(1,128)S(1)} fusion(f32[2,2,4,896,1]{3,2,0,1,4:T(4,128)S(1)} %reshape.341, bf16[1,4,2,128,896]{4,3,2,1,0:T(8,128)(2,1)} %bitcast.16, bf16[1,4,2,128,896]{4,3,2,1,0:T(8,128)(2,1)} %bitcast.141), kind=kOutput, calls=%fused_computation.17 | convolution fusion | flops 23855104 | bytes 3729408 | tf_op jit(solution)/shard_map/ptskf,pstf->psk/dot_general | solution.py:131
  88.6 2.8 fusion.50
  91.4 1.1 multiply_convert_fusion
  93.4 1.6 convolution_convert_fusion.2
  95.0 1.2 reshape.324
  96.2 2.6 convolution_convert_fusion.3
  98.8 1.2 reshape.323
  100.0 2.9 convolution_convert_fusion.1
  102.9 2.1 reshape.325
  105.0 2.9 convolution_convert_fusion
  108.0 2.1 reshape.326
  110.0 1.9 pad_maximum_fusion.1
  111.9 1.1 copy.43
  113.0 2.3 copy.44
  115.4 17.4 %all-to-all-start.2 = ((bf16[16,112,896]{2,1,0:T(8,128)(2,1)}), bf16[16,112,896]{2,1,0:T(8,128)(2,1)}, u32[]{:S(2)}, u32[]{:S(2)}) async-start(bf16[16,112,896]{2,1,0:T(8,128)(2,1)} %copy.44), calls=%async_computation.2 | async-start | bytes 6422528 | tf_op jit(solution)/shard_map/all_to_all | solution.py:150
  134.2 55.0 %all-to-all-done.2 = bf16[16,112,896]{2,1,0:T(8,128)(2,1)} async-done(((bf16[16,112,896]{2,1,0:T(8,128)(2,1)}), bf16[16,112,896]{2,1,0:T(8,128)(2,1)}, u32[]{:S(2)}, u32[]{:S(2)}) %all-to-all-start.2) | async-done | bytes 3211296 | tf_op jit(solution)/shard_map/all_to_all | solution.py:150
  189.3 2.4 convert_reduce_fusion
  192.4 8.1 %collective-permute-start.3 = (f32[28,896]{1,0:T(8,128)S(1)}, f32[28,896]{1,0:T(8,128)S(1)}, u32[]{:S(2)}, u32[]{:S(2)}) collective-permute-start(f32[28,896]{1,0:T(8,128)S(1)} %get-tuple-element.24), channel_id=1, source_target_pairs={{0,1},{1,2},{2,3},{3,0},{4,5},{5,6},{6,7},{7,4},{8,9},{9,10},{10,1... | collective-permute-start | bytes 301064 | tf_op jit(solution)/shard_map/ppermute | solution.py:161
  200.5 2.4 collective-permute-start.5
  202.9 9.2 %collective-permute-start.4 = (f32[28,896]{1,0:T(8,128)S(1)}, f32[28,896]{1,0:T(8,128)S(1)}, u32[]{:S(2)}, u32[]{:S(2)}) collective-permute-start(f32[28,896]{1,0:T(8,128)S(1)} %get-tuple-element.26), channel_id=1, source_target_pairs={{0,2},{1,3},{2,0},{3,1},{4,6},{5,7},{6,4},{7,5},{8,10},{9,11},{10,... | collective-permute-start | bytes 301064 | tf_op jit(solution)/shard_map/ppermute | solution.py:161
  212.1 9.4 %collective-permute-done.4 = f32[28,896]{1,0:T(8,128)S(1)} collective-permute-done((f32[28,896]{1,0:T(8,128)S(1)}, f32[28,896]{1,0:T(8,128)S(1)}, u32[]{:S(2)}, u32[]{:S(2)}) %collective-permute-start.4) | collective-permute-done | bytes 100384 | tf_op jit(solution)/shard_map/ppermute | solution.py:161
  222.6 11.3 %all-to-all-start.3 = ((bf16[16,28,896]{2,1,0:T(8,128)(2,1)}), bf16[16,28,896]{2,1,0:T(8,128)(2,1)S(1)}, u32[]{:S(2)}, u32[]{:S(2)}) async-start(bf16[16,28,896]{2,1,0:T(8,128)(2,1)} %broadcast_in_dim.23), calls=%async_computation.3 | async-start | bytes 1835008 | tf_op jit(solution)/shard_map/all_to_all | solution.py:165
  234.0 14.1 %all-to-all-done.3 = bf16[16,28,896]{2,1,0:T(8,128)(2,1)S(1)} async-done(((bf16[16,28,896]{2,1,0:T(8,128)(2,1)}), bf16[16,28,896]{2,1,0:T(8,128)(2,1)S(1)}, u32[]{:S(2)}, u32[]{:S(2)}) %all-to-all-start.3) | async-done | bytes 802848 | tf_op jit(solution)/shard_map/all_to_all | solution.py:165
  248.2 4.8 %collective-permute-start.6 = (bf16[448,896]{1,0:T(8,128)(2,1)S(1)}, bf16[448,896]{1,0:T(8,128)(2,1)S(1)}, u32[]{:S(2)}, u32[]{:S(2)}) collective-permute-start(bf16[448,896]{1,0:T(8,128)(2,1)S(1)} %reshape.329), channel_id=1, source_target_pairs={{0,16},{16,0},{1,17},{17,1},{2,18},{18,2},{3,19},{19,3},{4,20},{20... | collective-permute-start | bytes 2408456 | tf_op jit(solution)/shard_map/ppermute | solution.py:34
  253.7 12.1 %psum.15 = f32[897]{0:T(1024)S(1)} all-reduce(f32[897]{0:T(1024)S(1)} %pad_maximum_fusion.9), channel_id=1, replica_groups=mesh['x'=4,'y'=4,'c'=2,'t'=4,'r'=4] {'r'}, use_global_device_ids=true, to_apply=%region_12.13 | all-reduce | flops 897 | bytes 7176 | tf_op jit(solution)/shard_map/psum | solution.py:121
  267.2 1.2 slice_bitcast_fusion.6
  268.4 1.8 maximum_select_fusion
  270.2 2.1 fusion.8
  272.3 2.0 fusion.12
  274.3 2.0 fusion.16
  276.2 2.0 fusion.42
  278.3 2.2 fusion.14
  280.5 2.2 fusion.18
  282.6 2.2 fusion.10
  284.8 2.3 fusion.30
  287.1 1.2 subtract_convert_fusion
  (97 shorter events, 20.5 us)
Async XLA Ops:
  7.2 21.3 %copy-start = (bf16[896,896]{1,0:T(8,128)(2,1)S(1)}, bf16[896,896]{1,0:T(8,128)(2,1)}, u32[]{:S(2)}) copy-start(bf16[896,896]{1,0:T(8,128)(2,1)} %param.8) | copy-start | bytes 4816900
  7.2 66.2 %all-gather.4.cloned.1.call-start = ((), (), s32[]{:S(2)}) async-start(), calls=%async_computation.4 | async-start | bytes 2293760 | tf_op jit(solution)/shard_map/all_gather | solution.py:53
  25.1 8.4 %all-to-all-start = ((f32[4,3,896]{2,1,0:T(4,128)}), f32[4,3,896]{2,1,0:T(4,128)S(1)}, u32[]{:S(2)}, u32[]{:S(2)}) async-start(f32[4,3,896]{2,1,0:T(4,128)} %broadcast_in_dim.18), calls=%async_computation | async-start | bytes 114688 | tf_op jit(solution)/shard_map/all_to_all | solution.py:76
  29.2 26.9 %collective-permute-start.1 = (bf16[112,896]{1,0:T(8,128)(2,1)}, bf16[112,896]{1,0:T(8,128)(2,1)}, u32[]{:S(2)}, u32[]{:S(2)}) collective-permute-start(bf16[112,896]{1,0:T(8,128)(2,1)} %constant_dynamic-slice_fusion.3), channel_id=1, source_target_pairs={{0,0},{1,1},{2,2},{3,3},{129,128},{130,129},{131,130},{128,131},{2... | collective-permute-start | bytes 602120 | tf_op jit(solution)/shard_map/ppermute | solution.py:56
  33.5 0.6 copy-start.9
  36.6 35.6 %all-to-all-start.1 = ((f32[32,2,3840]{2,1,0:T(2,128)}), f32[32,2,3840]{2,1,0:T(2,128)S(1)}, u32[]{:S(2)}, u32[]{:S(2)}) async-start(f32[32,2,3840]{2,1,0:T(2,128)} %concatenate.24), calls=%async_computation.1 | async-start | bytes 1966080 | tf_op jit(solution)/shard_map/all_to_all | solution.py:96
  56.0 214.2 %all-gather.6.cloned.1.call-start = ((), (), s32[]{:S(2)}) async-start(), calls=%async_computation.5 | async-start | bytes 6623232 | tf_op jit(solution)/shard_map/all_gather | solution.py:61
  58.8 32.7 %collective-permute-start.2 = (bf16[256,448]{1,0:T(8,128)(2,1)}, bf16[256,448]{1,0:T(8,128)(2,1)}, u32[]{:S(2)}, u32[]{:S(2)}) collective-permute-start(bf16[256,448]{1,0:T(8,128)(2,1)} %get-tuple-element.28), channel_id=1, source_target_pairs={{0,16},{16,0},{1,17},{17,1},{2,18},{18,2},{3,19},{19,3},{4,20},{20... | collective-permute-start | bytes 688136 | tf_op jit(solution)/shard_map/ppermute | solution.py:34
  72.2 0.9 copy-start.2
  73.4 9.4 %collective-permute-start = (bf16[4,256,896]{2,1,0:T(8,128)(2,1)}, bf16[4,256,896]{2,1,0:T(8,128)(2,1)}, u32[]{:S(2)}, u32[]{:S(2)}) collective-permute-start(bf16[4,256,896]{2,1,0:T(8,128)(2,1)} %all-gather.4.cloned.1.call-done), channel_id=1, source_target_pairs={{0,16},{16,0},{1,17},{17,1},{2,18},{18,2},{3,19},{19,3},{4,20},{20... | collective-permute-start | bytes 5505032 | tf_op jit(solution)/shard_map/ppermute | solution.py:34
  80.0 0.9 copy-start.6
  82.8 5.8 %copy-start.3 = (bf16[4,256,896]{2,1,0:T(8,128)(2,1)S(1)}, bf16[4,256,896]{2,1,0:T(8,128)(2,1)}, u32[]{:S(2)}) copy-start(bf16[4,256,896]{2,1,0:T(8,128)(2,1)} %all-gather.4.cloned.1.call-done) | copy-start | bytes 5505028
  88.6 2.8 copy-start.5
  92.6 0.8 copy-start.8
  115.4 17.5 %copy-start.7 = (f32[32,2,3584]{2,0,1:T(8,128)S(1)}, f32[32,2,3584]{2,0,1:T(8,128)}, u32[]{:S(2)}) copy-start(f32[32,2,3584]{2,0,1:T(8,128)} %copy-done.6) | copy-start | bytes 2752516
  115.4 73.9 %all-to-all-start.2 = ((bf16[16,112,896]{2,1,0:T(8,128)(2,1)}), bf16[16,112,896]{2,1,0:T(8,128)(2,1)}, u32[]{:S(2)}, u32[]{:S(2)}) async-start(bf16[16,112,896]{2,1,0:T(8,128)(2,1)} %copy.44), calls=%async_computation.2 | async-start | bytes 6422528 | tf_op jit(solution)/shard_map/all_to_all | solution.py:150
  133.6 58.2 %slice-start = ((f32[32,2,3840]{2,1,0:T(2,128)}), f32[32,2,28]{2,1,0:T(2,128)S(1)}, s32[]{:S(2)}) async-start(f32[32,2,3840]{2,1,0:T(2,128)} %copy-done.2), calls=%async_computation.6 | async-start | bytes 65536 | tf_op jit(solution)/shard_map/slice | solution.py:153
  192.4 19.8 %collective-permute-start.3 = (f32[28,896]{1,0:T(8,128)S(1)}, f32[28,896]{1,0:T(8,128)S(1)}, u32[]{:S(2)}, u32[]{:S(2)}) collective-permute-start(f32[28,896]{1,0:T(8,128)S(1)} %get-tuple-element.24), channel_id=1, source_target_pairs={{0,1},{1,2},{2,3},{3,0},{4,5},{5,6},{6,7},{7,4},{8,9},{9,10},{10,1... | collective-permute-start | bytes 301064 | tf_op jit(solution)/shard_map/ppermute | solution.py:161
  200.5 11.7 %collective-permute-start.5 = (f32[28,896]{1,0:T(8,128)S(1)}, f32[28,896]{1,0:T(8,128)S(1)}, u32[]{:S(2)}, u32[]{:S(2)}) collective-permute-start(f32[28,896]{1,0:T(8,128)S(1)} %get-tuple-element.25), channel_id=1, source_target_pairs={{0,3},{1,0},{2,1},{3,2},{4,7},{5,4},{6,5},{7,6},{8,11},{9,8},{10,9... | collective-permute-start | bytes 301064 | tf_op jit(solution)/shard_map/ppermute | solution.py:161
  202.9 18.7 %collective-permute-start.4 = (f32[28,896]{1,0:T(8,128)S(1)}, f32[28,896]{1,0:T(8,128)S(1)}, u32[]{:S(2)}, u32[]{:S(2)}) collective-permute-start(f32[28,896]{1,0:T(8,128)S(1)} %get-tuple-element.26), channel_id=1, source_target_pairs={{0,2},{1,3},{2,0},{3,1},{4,6},{5,7},{6,4},{7,5},{8,10},{9,11},{10,... | collective-permute-start | bytes 301064 | tf_op jit(solution)/shard_map/ppermute | solution.py:161
  222.6 25.5 %all-to-all-start.3 = ((bf16[16,28,896]{2,1,0:T(8,128)(2,1)}), bf16[16,28,896]{2,1,0:T(8,128)(2,1)S(1)}, u32[]{:S(2)}, u32[]{:S(2)}) async-start(bf16[16,28,896]{2,1,0:T(8,128)(2,1)} %broadcast_in_dim.23), calls=%async_computation.3 | async-start | bytes 1835008 | tf_op jit(solution)/shard_map/all_to_all | solution.py:165
  248.2 20.3 %collective-permute-start.6 = (bf16[448,896]{1,0:T(8,128)(2,1)S(1)}, bf16[448,896]{1,0:T(8,128)(2,1)S(1)}, u32[]{:S(2)}, u32[]{:S(2)}) collective-permute-start(bf16[448,896]{1,0:T(8,128)(2,1)S(1)} %reshape.329), channel_id=1, source_target_pairs={{0,16},{16,0},{1,17},{17,1},{2,18},{18,2},{3,19},{19,3},{4,20},{20... | collective-permute-start | bytes 2408456 | tf_op jit(solution)/shard_map/ppermute | solution.py:34
  265.9 0.6 copy-start.12
  270.2 8.1 %copy-start.4 = (bf16[4,256,896]{2,1,0:T(8,128)(2,1)S(1)}, bf16[4,256,896]{2,1,0:T(8,128)(2,1)}, u32[]{:S(2)}) copy-start(bf16[4,256,896]{2,1,0:T(8,128)(2,1)} %all-gather.4.cloned.1.call-done) | copy-start | bytes 5505028
  284.8 2.3 copy-start.1
  284.8 2.3 copy-start.10
  284.8 2.3 copy-start.11
Sparse Core Ops, SparseCore 0:
  10.1 55.9 all-gather.3
  69.3 121.7 all-gather.5

commit v2 on v1

--- a/solution.py
+++ b/solution.py
@@ -1,6 +1,8 @@
 import jax
 import jax.numpy as jnp
 from jax import lax
+from jax.experimental import pallas as pl
+from jax.experimental.pallas import tpu as pltpu
 from jax.sharding import Mesh, PartitionSpec as P
 
 logit_scale = 20.0
@@ -21,7 +23,8 @@
 TOK = 2 * SEQ
 HALF = FEAT // NC
 SLICE = HALF // (NX * NY)
-W_ROWS = FEAT // (NY * NC)
+W_ROWS = HALF // NY
+PIECES = 16
 
 AT_RMS = D
 AT_U = D + SEQ
@@ -42,6 +45,100 @@
     return high.astype(bf16), mid.astype(bf16), low.astype(bf16)
 
 
+contract_last = (((1,), (1,)), ((), ()))
+contract_first = (((0,), (0,)), ((), ()))
+
+
+def dot_last(left, right):
+    return lax.dot_general(left, right, contract_last, preferred_element_type=f32)
+
+
+def weight_kernel(
+    own_ref, other_ref, keep_ref, given_ref, pieces_ref, scale_ref, out_ref, coef_ref, acc_ref
+):
+    token = lax.broadcasted_iota(jnp.int32, (TOK, PIECES), 0)
+    part = lax.broadcasted_iota(jnp.int32, (TOK, PIECES), 1)
+    part = part - jnp.where(token < SEQ, 0, 3)
+    mask = (part >= 0) & (part < 3)
+    scaled = []
+    for pair, (state_ref, attn_ref) in enumerate(
+        ((own_ref, keep_ref), (other_ref, given_ref))
+    ):
+        inner = jnp.zeros((TOK, PIECES), f32)
+        for block in range(NT):
+            inner = inner + dot_last(state_ref[block], pieces_ref[pair, block])
+        inner = jnp.sum(jnp.where(mask, inner, 0.0), -1, keepdims=True)
+        coef = scale_ref[pair] * inner
+        coef_ref[pair] = coef
+        scaled.append((attn_ref[...].astype(f32) * coef).astype(bf16))
+    for block in range(NT):
+        acc_ref[block] = lax.dot_general(
+            scaled[0], own_ref[block], contract_first, preferred_element_type=f32
+        ) + lax.dot_general(
+            scaled[1], other_ref[block], contract_first, preferred_element_type=f32
+        )
+    for place in range(NX * NY):
+        rows = [
+            acc_ref[block, place * SLICE : (place + 1) * SLICE, :] for block in range(NR)
+        ]
+        out_ref[place] = jnp.concatenate(rows, 0).astype(bf16)
+
+
+def weight_partials(own, other, keep, given, pieces, scale):
+    spec = pl.BlockSpec(memory_space=pltpu.VMEM)
+    return pl.pallas_call(
+        weight_kernel,
+        out_shape=(
+            jax.ShapeDtypeStruct((NX * NY, NR * SLICE, COLS), bf16),
+            jax.ShapeDtypeStruct((NC, TOK, 1), f32),
+        ),
+        in_specs=[spec] * 6,
+        out_specs=(spec, spec),
+        scratch_shapes=[pltpu.VMEM((NR, HALF, COLS), f32)],
+        compiler_params=pltpu.CompilerParams(vmem_limit_bytes=48 * 1024 * 1024),
+        cost_estimate=pl.CostEstimate(
+            flops=4 * TOK * HALF * D, bytes_accessed=8 * 1024 * 1024, transcendentals=0
+        ),
+        name="weight_partials",
+    )(own, other, keep, given, pieces, scale)
+
+
+def attn_kernel(
+    shift_ref, own_ref, other_ref, pieces_ref, w_ref, coef_ref, first_ref, keep_ref, give_ref
+):
+    shift = shift_ref[0]
+    for pair, (state_ref, out_ref) in enumerate(((own_ref, keep_ref), (other_ref, give_ref))):
+        tokens = jnp.zeros((TOK, HALF), f32)
+        rows = jnp.zeros((PIECES, HALF), f32)
+        for block in range(NX):
+            which = lax.rem(shift + block, NR)
+            tokens = tokens + dot_last(state_ref[which], w_ref[block])
+            rows = rows + dot_last(pieces_ref[pair, which], w_ref[block])
+        for side in range(2):
+            row = rows[3 * side + 2 : 3 * side + 3] + rows[3 * side + 1 : 3 * side + 2]
+            row = row + rows[3 * side : 3 * side + 1]
+            here = slice(side * SEQ, (side + 1) * SEQ)
+            out_ref[here, :] = (
+                first_ref[pair, here, :] * row - coef_ref[pair, here, :] * tokens[here]
+            ).astype(bf16)
+
+
+def attn_grads(shift, own, other, pieces, w_all, coef, first):
+    spec = pl.BlockSpec(memory_space=pltpu.VMEM)
+    out = jax.ShapeDtypeStruct((TOK, HALF), bf16)
+    return pl.pallas_call(
+        attn_kernel,
+        out_shape=(out, out),
+        in_specs=[pl.BlockSpec(memory_space=pltpu.SMEM)] + [spec] * 6,
+        out_specs=(spec, spec),
+        compiler_params=pltpu.CompilerParams(vmem_limit_bytes=48 * 1024 * 1024),
+        cost_estimate=pl.CostEstimate(
+            flops=4 * TOK * HALF * D, bytes_accessed=8 * 1024 * 1024, transcendentals=0
+        ),
+        name="attn_grads",
+    )(shift, own, other, pieces, w_all, coef, first)
+
+
 def body(hidden_state, attn_out, o_weight, norm_gain, lengths, positive):
     highest = lax.Precision.HIGHEST
     ix, iy, ic = lax.axis_index("x"), lax.axis_index("y"), lax.axis_index("c")
@@ -50,15 +147,15 @@
 
     state = hidden_state.reshape(TOK, FEAT)
     attn = attn_out.reshape(TOK, FEAT)
-    state_all = lax.all_gather(state, "t")
-    w_start = (iy * NC + ic) * W_ROWS
+    state_all = lax.all_to_all(jnp.broadcast_to(state[None], (NT, TOK, FEAT)), "t", 0, 0)
+    w_start = (ic * NY + iy) * W_ROWS
     w_mine = lax.dynamic_slice(o_weight, (w_start, 0), (W_ROWS, COLS))
     w_moved = lax.ppermute(
         w_mine,
         ("x", "r"),
         [(i * NR + (j + i) % NR, i * NR + j) for i in range(NX) for j in range(NR)],
     )
-    w_all = lax.all_gather(w_moved, DP).reshape(NX, FEAT, COLS)
+    w_all = lax.all_gather(w_moved, PLANE).reshape(NX, HALF, COLS)
     attn_keep = jnp.where(ic == 0, attn[:, :HALF], attn[:, HALF:])
     attn_give = jnp.where(ic == 0, attn[:, HALF:], attn[:, :HALF])
     attn_other = swap_core(attn_give)
@@ -101,8 +198,6 @@
     unit = embeds * inv_norm
     query, passage = unit[:, 0], unit[:, 1]
     target = got[:, 0, AT_POS].astype(jnp.int32)
-    contract_last = (((1,), (1,)), ((), ()))
-    contract_first = (((0,), (0,)), ((), ()))
     logits = logit_scale * lax.dot_general(query, passage, contract_last, precision=highest)
     log_total = jnp.log(jnp.sum(jnp.exp(logits), -1))
     one_hot = (jnp.arange(group, dtype=jnp.int32)[None, :] == target[:, None]).astype(f32)
@@ -118,7 +213,6 @@
     gain_part = jnp.sum(pooled_grad * raw, (0, 1))
     scaled = pooled_grad * gain
     gain_mine = lax.dynamic_slice(gain_part, (it * FEAT,), (FEAT,))
-    totals = lax.psum(jnp.concatenate([gain_mine, loss_part[None]]), "r")
 
     other_index = dp_index + 1 - 2 * ic
     state_other = swap_core(state_all)
@@ -127,26 +221,14 @@
     rms = jnp.stack([got[dp_index, :, AT_RMS:AT_U], got[other_index, :, AT_RMS:AT_U]])
     place = jnp.arange(SEQ, dtype=jnp.int32).astype(f32)
     first_coef = jnp.where(place < counts[..., None], rms / counts[..., None], 0.0)
-    both = jnp.stack([state_all, state_other]).reshape(2, NT, 2, SEQ, FEAT)
-    inner = jnp.einsum(
-        "ptskf,pstf->psk",
-        both.astype(f32),
-        rows.reshape(2, 2, NT, FEAT),
-        precision=highest,
-    )
-    coef = first_coef * rms * rms * inner / D
-
-    attn_pair = jnp.stack([attn_keep, attn_other]).astype(f32)
-    attn_scaled = (attn_pair * coef.reshape(2, TOK, 1)).astype(bf16).reshape(2 * TOK, HALF)
-    flat_states = both.reshape(2, NT, TOK, FEAT)
-    parts = []
-    for block in range(NR):
-        block_states = flat_states[:, block].reshape(2 * TOK, FEAT)
-        part = lax.dot_general(
-            attn_scaled, block_states, contract_first, preferred_element_type=f32
-        )
-        parts.append(part.astype(bf16).reshape(NX * NY, 1, SLICE, COLS))
-    partial = jnp.concatenate(parts, 1).reshape(NX * NY, NR * SLICE, COLS)
+    scale = (first_coef * rms * rms / D).reshape(NC, TOK, 1)
+    first_col = first_coef.reshape(NC, TOK, 1)
+    pieces = jnp.stack(split3(rows), 2).reshape(NC, 6, NT, FEAT).transpose(0, 2, 1, 3)
+    pieces = jnp.pad(pieces, ((0, 0), (0, 0), (0, PIECES - 6), (0, 0)))
+
+    partial, coef = weight_partials(
+        state_all, state_other, attn_keep, attn_other, pieces, scale
+    )
     spread = lax.all_to_all(partial, PLANE, 0, 0)
     second = jnp.sum(spread.astype(f32), 0).reshape(NR, SLICE, COLS)
 
@@ -154,13 +236,34 @@
     first = lax.dot_general(
         u_all, scaled.reshape(2 * group, D), contract_first, precision=highest
     )
-    mine = first.reshape(SLICE, NR, COLS).transpose(1, 0, 2) - second
-    total = lax.dynamic_index_in_dim(mine, ir, 0, keepdims=False)
+    first = first.reshape(SLICE, NR, COLS).transpose(1, 0, 2)
+    tail = jnp.stack([gain_mine, jnp.broadcast_to(loss_part, (FEAT,))])
+    tails = [tail]
+    first_sum = lax.dynamic_index_in_dim(first, ir, 0, keepdims=False)
     for step in range(1, NR):
-        outgoing = lax.dynamic_index_in_dim(mine, (ir + step) % NR, 0, keepdims=False)
-        total = total + lax.ppermute(
+        outgoing = lax.dynamic_index_in_dim(first, (ir + step) % NR, 0, keepdims=False)
+        arrived = lax.ppermute(
+            jnp.concatenate([outgoing, tail], 0),
+            "r",
+            [(j, (j + step) % NR) for j in range(NR)],
+        )
+        first_sum = first_sum + arrived[:SLICE]
+        tails.append(arrived[SLICE:])
+    tails = jnp.stack(tails)
+    totals = jnp.zeros((2, FEAT), f32)
+    for source in range(NR):
+        totals = totals + lax.dynamic_index_in_dim(
+            tails, (ir - source) % NR, 0, keepdims=False
+        )
+
+    second_sum = lax.dynamic_index_in_dim(second, ir, 0, keepdims=False)
+    second_cut = second.astype(bf16)
+    for step in range(1, NR):
+        outgoing = lax.dynamic_index_in_dim(second_cut, (ir + step) % NR, 0, keepdims=False)
+        second_sum = second_sum + lax.ppermute(
             outgoing, "r", [(j, (j + step) % NR) for j in range(NR)]
-        )
+        ).astype(f32)
+    total = first_sum - second_sum
     done = jnp.broadcast_to(total.astype(bf16)[None], (NX * NY, SLICE, COLS))
     half = lax.all_to_all(done, PLANE, 0, 0).reshape(HALF, COLS)
     half_other = swap_core(half)
@@ -170,37 +273,22 @@
         jnp.concatenate([half_other, half], 0),
     )
 
-    own_first = first_coef[0]
-    own_coef = coef[0]
-    own_rows = rows[0].reshape(2, NT, FEAT)
-    row_here = lax.dynamic_index_in_dim(own_rows, it, 1, keepdims=False)
-    state_grad = own_first[..., None] * row_here[:, None, :] - states * own_coef[..., None]
+    row_here = lax.dynamic_index_in_dim(
+        rows[0].reshape(2, NT, FEAT), it, 1, keepdims=False
+    )
+    state_grad = first_coef[0][..., None] * row_here[:, None, :] - states * coef[0].reshape(
+        2, SEQ, 1
+    )
     grad_hidden = state_grad.astype(bf16).reshape(1, 2, SEQ, FEAT)
 
-    pieces = jnp.stack(split3(own_rows)).reshape(6, NT, FEAT)
-    token_part = jnp.zeros((TOK, FEAT), f32)
-    row_part = jnp.zeros((6, FEAT), f32)
-    for block in range(NX):
-        which = (ir + block) % NR
-        token_part = token_part + lax.dot_general(
-            lax.dynamic_index_in_dim(state_all, which, 0, keepdims=False),
-            w_all[block],
-            contract_last,
-            preferred_element_type=f32,
-        )
-        row_part = row_part + lax.dot_general(
-            lax.dynamic_index_in_dim(pieces, which, 1, keepdims=False),
-            w_all[block],
-            contract_last,
-            preferred_element_type=f32,
-        )
-    row_sum = jnp.sum(row_part.reshape(3, 2, FEAT)[::-1], 0)
-    attn_grad = (
-        own_first[..., None] * row_sum[:, None, :]
-        - token_part.reshape(2, SEQ, FEAT) * own_coef[..., None]
-    )
-    grad_attn = attn_grad.astype(bf16).reshape(1, 2, SEQ, FEAT)
-    return (grad_hidden, grad_attn, grad_weight, totals[:FEAT], totals[FEAT])
+    keep, give = attn_grads(
+        ir.reshape(1), state_all, state_other, pieces, w_all, coef, first_col
+    )
+    arrived = swap_core(give)
+    grad_attn = jnp.where(
+        ic == 0, jnp.concatenate([keep, arrived], 1), jnp.concatenate([arrived, keep], 1)
+    ).reshape(1, 2, SEQ, FEAT)
+    return (grad_hidden, grad_attn, grad_weight, totals[0], totals[1, 0])
 
 
 def solution(mesh):

time: 300 us -> 311 us (1.037)
  the two profiles are of different devices: /device:TPU:1 before, /device:TPU:33 now
where the time goes in v2:
time: 311 us; the launch traced here: 308 us
  starting transfers between devices  98 us (32%)
  waiting for transfers between devices  70.1 us (23%)
  local copies, waits for them, and re-layouts  47.2 us (15%)
  blocking collectives  34.5 us (11%)
  other arithmetic  24.6 us (8%)
  between operations  15.3 us (5%)
  Pallas kernels  13.3 us (4%)
  matrix products  5.44 us (2%)
    all_to_all x1, starting transfers between devices, body(): spread = lax.all_to_all(partial, PLANE, 0, 0)  33.3 us
    all_to_all x1, blocking collectives, body(): got = lax.all_to_all(send, DP, 0, 0)  27 us
    all_to_all x1, waiting for transfers between devices, body(): spread = lax.all_to_all(partial, PLANE, 0, 0)  26.3 us
    all_to_all x1, waiting for transfers between devices, body(): lax.all_to_all(jnp.broadcast_to(state[None], (NT, TOK, FEAT)), 't', 0, 0)  25.8 us
    ppermute x3, starting transfers between devices, body(): lax.ppermute(jnp.concatenate([outgoing, tail], 0), 'r', [(j, (j + step) %...  15.3 us
    ppermute x4, starting transfers between devices, swap_core(): return lax.ppermute(value, 'c', [(0, 1), (1, 0)])  14.5 us
    ppermute x3, starting transfers between devices, body(): lax.ppermute(outgoing, 'r', [(j, (j + step) % NR) for j in range(NR)])  12.1 us
    all_to_all x1, waiting for transfers between devices, body(): half = lax.all_to_all(done, PLANE, 0, 0).reshape(HALF, COLS)  9.18 us
  transfers between devices with their start and end apart: 16, of which 7 were waited for; matrix products, arithmetic and copies ran while one was open for 18% of the time, Pallas kernels for 4%

profile of v2, /device:TPU:33, one launch (start us, length us, event | category | flops | bytes accessed | tf_op | source)
XLA Modules:
  0.0 308.5 jit_solution(4729323407378377541)
XLA Ops:
  8.0 1.2 fusion.8
  9.2 7.5 %psum.7 = f32[2,128]{1,0:T(2,128)S(1)} all-reduce(f32[2,128]{1,0:T(2,128)S(1)} %fusion.8), channel_id=1, replica_groups=mesh['x'=4,'y'=4,'c'=2,'t'=4,'r'=4] {'t'}, use_global_device_ids=true, to_apply=%region_1.2 | all-reduce | flops 256 | bytes 2048 | tf_op jit(solution)/shard_map/psum | solution.py:164
  18.1 1.4 fusion.15
  20.2 6.5 %all-to-all-start = ((f32[4,3,896]{2,1,0:T(4,128)}), f32[4,3,896]{2,1,0:T(4,128)S(1)}, u32[]{:S(2)}, u32[]{:S(2)}) async-start(f32[4,3,896]{2,1,0:T(4,128)} %broadcast_in_dim.22), calls=%async_computation | async-start | bytes 114688 | tf_op jit(solution)/shard_map/all_to_all | solution.py:173
  27.6 2.8 all-to-all-done
  31.7 2.8 concatenate.100
  34.5 27.0 %all_to_all.25 = f32[32,2,3840]{2,1,0:T(2,128)} all-to-all(f32[32,2,3840]{2,1,0:T(2,128)S(1)} %concatenate.100), channel_id=1, replica_groups=mesh['x'=4,'y'=4,'c'=2,'t'=4,'r'=4] {'x','y','c'}, dimensions={0} | all-to-all | bytes 1966080 | tf_op jit(solution)/shard_map/all_to_all | solution.py:193
  61.5 1.4 broadcast_in_dim.28
  63.0 4.4 %all-to-all-start.2 = ((bf16[4,256,896]{2,1,0:T(8,128)(2,1)}), bf16[4,256,896]{2,1,0:T(8,128)(2,1)S(1)}, u32[]{:S(2)}, u32[]{:S(2)}) async-start(bf16[4,256,896]{2,1,0:T(8,128)(2,1)} %broadcast_in_dim.28), calls=%async_computation.2 | async-start | bytes 3670016 | tf_op jit(solution)/shard_map/all_to_all | solution.py:150
  67.4 2.0 broadcast_select_fusion
  69.4 2.3 collective-permute-start.1
  72.4 3.4 %collective-permute-start.2 = (bf16[112,896]{1,0:T(8,128)(2,1)}, bf16[112,896]{1,0:T(8,128)(2,1)}, u32[]{:S(2)}, u32[]{:S(2)}) collective-permute-start(bf16[112,896]{1,0:T(8,128)(2,1)} %constant_dynamic-slice_fusion), channel_id=1, source_target_pairs={{0,0},{1,1},{2,2},{3,3},{129,128},{130,129},{131,130},{128,131},{2... | collective-permute-start | bytes 602120 | tf_op jit(solution)/shard_map/ppermute | solution.py:153
  77.0 1.3 slice.81
  81.2 25.8 %all-to-all-done.2.own_ref = bf16[4,256,896]{2,1,0:T(8,128)(2,1)S(1)} async-done(((bf16[4,256,896]{2,1,0:T(8,128)(2,1)}), bf16[4,256,896]{2,1,0:T(8,128)(2,1)S(1)}, u32[]{:S(2)}, u32[]{:S(2)}) %all-to-all-start.2) | async-done | bytes 1835040 | tf_op jit(solution)/shard_map/all_to_all | solution.py:150
  107.0 3.0 collective-permute-start
  110.0 1.6 fusion.4
  111.6 1.5 fusion.5
  119.9 1.6 lt.168
  121.5 1.3 constant_dynamic-slice_fusion.3
  122.8 1.4 copy.62
  124.3 1.5 copy.63
  125.8 2.0 fusion.18
  128.7 6.7 %weight_partials.1 = (bf16[16,112,896]{2,1,0:T(8,128)(2,1)}, f32[2,256,1]{2,1,0:T(8,128)S(1)}) custom-call(bf16[4,256,896]{2,1,0:T(8,128)(2,1)S(1)} %all-to-all-done.2.own_ref, bf16[4,256,896]{2,1,0:T(8,128)(2,1)} %collective-permute-done.other_ref, bf16[256,448]{1,0:T(8,128)(2,1)S(1)} %copy-done.6, bf16[256,448]{1,0:T(8,128)(2,1)} %collective-permute-done.1.given_ref, ...), custom_call_target="tpu_custom_call" | custom-call | flops 1644167168 | bytes 8388608 | tf_op jit(solution)/shard_map/weight_partials/pallas_call | solution.py:89
  136.1 33.3 %all-to-all-start.3 = ((bf16[16,112,896]{2,1,0:T(8,128)(2,1)}), bf16[16,112,896]{2,1,0:T(8,128)(2,1)}, u32[]{:S(2)}, u32[]{:S(2)}) async-start(bf16[16,112,896]{2,1,0:T(8,128)(2,1)} %get-tuple-element.12), calls=%async_computation.3 | async-start | bytes 6422528 | tf_op jit(solution)/shard_map/all_to_all | solution.py:232
  169.6 2.9 copy.65
  173.0 2.7 reshape.457
  177.2 1.8 fusion.12
  180.6 5.4 %collective-permute-start.6 = (f32[30,896]{1,0:T(8,128)}, f32[30,896]{1,0:T(8,128)S(1)}, u32[]{:S(2)}, u32[]{:S(2)}) collective-permute-start(f32[30,896]{1,0:T(8,128)} %get-tuple-element.41), channel_id=1, source_target_pairs={{0,3},{1,0},{2,1},{3,2},{4,7},{5,4},{6,5},{7,6},{8,11},{9,8},{10,9... | collective-permute-start | bytes 322568 | tf_op jit(solution)/shard_map/ppermute | solution.py:245
  186.0 2.6 collective-permute-start.5
  188.6 7.3 %collective-permute-start.4 = (f32[30,896]{1,0:T(8,128)}, f32[30,896]{1,0:T(8,128)}, u32[]{:S(2)}, u32[]{:S(2)}) collective-permute-start(f32[30,896]{1,0:T(8,128)} %get-tuple-element.39), channel_id=1, source_target_pairs={{0,1},{1,2},{2,3},{3,0},{4,5},{5,6},{6,7},{7,4},{8,9},{9,10},{10,1... | collective-permute-start | bytes 322568 | tf_op jit(solution)/shard_map/ppermute | solution.py:245
  195.9 1.4 reshape_squeeze_stack_squeeze.3
  197.3 1.9 pad_bitcast_fusion
  199.2 1.3 fusion.35
  200.6 26.3 %all-to-all-done.3 = bf16[16,112,896]{2,1,0:T(8,128)(2,1)} async-done(((bf16[16,112,896]{2,1,0:T(8,128)(2,1)}), bf16[16,112,896]{2,1,0:T(8,128)(2,1)}, u32[]{:S(2)}, u32[]{:S(2)}) %all-to-all-start.3) | async-done | bytes 3211296 | tf_op jit(solution)/shard_map/all_to_all | solution.py:232
  226.9 3.2 %convert_reduce_fusion = f32[112,896]{1,0:T(8,128)} fusion(bf16[16,112,896]{2,1,0:T(8,128)(2,1)} %all-to-all-done.3), kind=kLoop, calls=%fused_computation.1 | loop fusion | flops 3110912 | bytes 3612672 | tf_op jit(solution)/shard_map/reduce_sum | solution.py:233
  230.0 1.8 reshape.458
  232.9 1.9 collective-permute-start.7
  234.8 8.3 %collective-permute-start.8 = (bf16[28,896]{1,0:T(8,128)(2,1)S(1)}, bf16[28,896]{1,0:T(8,128)(2,1)S(1)}, u32[]{:S(2)}, u32[]{:S(2)}) collective-permute-start(bf16[28,896]{1,0:T(8,128)(2,1)S(1)} %get-tuple-element.35), channel_id=1, source_target_pairs={{0,2},{1,3},{2,0},{3,1},{4,6},{5,7},{6,4},{7,5},{8,10},{9,11},{10,... | collective-permute-start | bytes 150536 | tf_op jit(solution)/shard_map/ppermute | solution.py:263
  243.1 1.9 collective-permute-start.9
  246.4 2.3 collective-permute-done.8
  248.7 3.5 %collective-permute-done.9 = bf16[28,896]{1,0:T(8,128)(2,1)S(1)} collective-permute-done((bf16[28,896]{1,0:T(8,128)(2,1)S(1)}, bf16[28,896]{1,0:T(8,128)(2,1)S(1)}, u32[]{:S(2)}, u32[]{:S(2)}) %collective-permute-start.9) | collective-permute-done | bytes 50208 | tf_op jit(solution)/shard_map/ppermute | solution.py:263
  254.3 8.4 %all-to-all-start.4 = ((bf16[16,28,896]{2,1,0:T(8,128)(2,1)}), bf16[16,28,896]{2,1,0:T(8,128)(2,1)}, u32[]{:S(2)}, u32[]{:S(2)}) async-start(bf16[16,28,896]{2,1,0:T(8,128)(2,1)} %broadcast_in_dim.31), calls=%async_computation.4 | async-start | bytes 1835008 | tf_op jit(solution)/shard_map/all_to_all | solution.py:268
  264.9 9.2 %all-to-all-done.4 = bf16[16,28,896]{2,1,0:T(8,128)(2,1)} async-done(((bf16[16,28,896]{2,1,0:T(8,128)(2,1)}), bf16[16,28,896]{2,1,0:T(8,128)(2,1)}, u32[]{:S(2)}, u32[]{:S(2)}) %all-to-all-start.4) | async-done | bytes 802848 | tf_op jit(solution)/shard_map/all_to_all | solution.py:268
  274.1 2.0 reshape.459
  276.1 7.2 %collective-permute-start.10 = (bf16[448,896]{1,0:T(8,128)(2,1)}, bf16[448,896]{1,0:T(8,128)(2,1)}, u32[]{:S(2)}, u32[]{:S(2)}) collective-permute-start(bf16[448,896]{1,0:T(8,128)(2,1)} %reshape.459), channel_id=1, source_target_pairs={{0,16},{16,0},{1,17},{17,1},{2,18},{18,2},{3,19},{19,3},{4,20},{20... | collective-permute-start | bytes 2408456 | tf_op jit(solution)/shard_map/ppermute | solution.py:37
  287.3 6.6 %attn_grads.1 = (bf16[256,448]{1,0:T(8,128)(2,1)S(1)}, bf16[256,448]{1,0:T(8,128)(2,1)S(1)}) custom-call(s32[1]{0:T(128)} %bitcast.22.shift_ref, bf16[4,256,896]{2,1,0:T(8,128)(2,1)S(1)} %all-to-all-done.2.own_ref, bf16[4,256,896]{2,1,0:T(8,128)(2,1)} %collective-permute-done.other_ref, bf16[2,4,16,896]{3,2,1,0:T(8,128)(2,1)S(1)} %copy-done.3, ...), custom_call_target="tpu_custom_call" | custom-call | flops 1644167168 | bytes 8388608 | tf_op jit(solution)/shard_map/attn_grads/pallas_call | solution.py:129
  294.0 2.1 collective-permute-start.3
  298.6 3.0 maximum_select_fusion
  (117 shorter events, 34.5 us)
Async XLA Ops:
  7.2 64.5 %copy-start = (bf16[896,896]{1,0:T(8,128)(2,1)S(1)}, bf16[896,896]{1,0:T(8,128)(2,1)}, u32[]{:S(2)}) copy-start(bf16[896,896]{1,0:T(8,128)(2,1)} %param.8) | copy-start | bytes 4816900
  20.2 10.2 %all-to-all-start = ((f32[4,3,896]{2,1,0:T(4,128)}), f32[4,3,896]{2,1,0:T(4,128)S(1)}, u32[]{:S(2)}, u32[]{:S(2)}) async-start(f32[4,3,896]{2,1,0:T(4,128)} %broadcast_in_dim.22), calls=%async_computation | async-start | bytes 114688 | tf_op jit(solution)/shard_map/all_to_all | solution.py:173
  31.7 29.9 %copy-start.10 = (bf16[1,2,128,896]{3,2,1,0:T(8,128)(2,1)S(1)}, bf16[1,2,128,896]{3,2,1,0:T(8,128)(2,1)}, u32[]{:S(2)}) copy-start(bf16[1,2,128,896]{3,2,1,0:T(8,128)(2,1)} %param.6) | copy-start | bytes 1376260
  63.0 44.0 %all-to-all-start.2 = ((bf16[4,256,896]{2,1,0:T(8,128)(2,1)}), bf16[4,256,896]{2,1,0:T(8,128)(2,1)S(1)}, u32[]{:S(2)}, u32[]{:S(2)}) async-start(bf16[4,256,896]{2,1,0:T(8,128)(2,1)} %broadcast_in_dim.28), calls=%async_computation.2 | async-start | bytes 3670016 | tf_op jit(solution)/shard_map/all_to_all | solution.py:150
  67.4 217.1 %all-gather.3.cloned.1.call-start = ((), (), s32[]{:S(2)}) async-start(), calls=%async_computation.5 | async-start | bytes 3411968 | tf_op jit(solution)/shard_map/all_gather | solution.py:158
  69.4 58.4 %collective-permute-start.1 = (bf16[256,448]{1,0:T(8,128)(2,1)}, bf16[256,448]{1,0:T(8,128)(2,1)}, u32[]{:S(2)}, u32[]{:S(2)}) collective-permute-start(bf16[256,448]{1,0:T(8,128)(2,1)} %get-tuple-element.31), channel_id=1, source_target_pairs={{0,16},{16,0},{1,17},{17,1},{2,18},{18,2},{3,19},{19,3},{4,20},{20... | collective-permute-start | bytes 688136 | tf_op jit(solution)/shard_map/ppermute | solution.py:37
  72.4 4.6 %collective-permute-start.2 = (bf16[112,896]{1,0:T(8,128)(2,1)}, bf16[112,896]{1,0:T(8,128)(2,1)}, u32[]{:S(2)}, u32[]{:S(2)}) collective-permute-start(bf16[112,896]{1,0:T(8,128)(2,1)} %constant_dynamic-slice_fusion), channel_id=1, source_target_pairs={{0,0},{1,1},{2,2},{3,3},{129,128},{130,129},{131,130},{128,131},{2... | collective-permute-start | bytes 602120 | tf_op jit(solution)/shard_map/ppermute | solution.py:153
  75.8 0.5 copy-start.21
  77.0 1.5 copy-start.12
  78.5 1.7 copy-start.7
  79.7 1.0 copy-start.9
  107.0 6.2 %copy-start.8 = (f32[32,2,3584]{2,1,0:T(2,128)S(1)}, f32[32,2,3584]{2,1,0:T(2,128)}, u32[]{:S(2)}) copy-start(f32[32,2,3584]{2,1,0:T(2,128)} %copy-done.7) | copy-start | bytes 2752516
  107.0 20.8 %collective-permute-start = (bf16[4,256,896]{2,1,0:T(8,128)(2,1)S(1)}, bf16[4,256,896]{2,1,0:T(8,128)(2,1)}, u32[]{:S(2)}, u32[]{:S(2)}) collective-permute-start(bf16[4,256,896]{2,1,0:T(8,128)(2,1)S(1)} %all-to-all-done.2.own_ref), channel_id=1, source_target_pairs={{0,16},{16,0},{1,17},{17,1},{2,18},{18,2},{3,19},{19,3},{4,20},{20... | collective-permute-start | bytes 5505032 | tf_op jit(solution)/shard_map/ppermute | solution.py:37
  114.3 0.9 copy-start.15
  118.7 0.6 copy-start.18
  125.8 9.6 %copy-start.2 = (bf16[2,4,16,896]{3,2,1,0:T(8,128)(2,1)}, bf16[2,4,16,896]{3,2,1,0:T(8,128)(2,1)S(1)}, u32[]{:S(2)}) copy-start(bf16[2,4,16,896]{3,2,1,0:T(8,128)(2,1)S(1)} %pad.6.pieces_ref) | copy-start | bytes 688132
  127.8 1.0 copy-start.6
  135.4 0.7 copy-start.4
  136.1 90.8 %all-to-all-start.3 = ((bf16[16,112,896]{2,1,0:T(8,128)(2,1)}), bf16[16,112,896]{2,1,0:T(8,128)(2,1)}, u32[]{:S(2)}, u32[]{:S(2)}) async-start(bf16[16,112,896]{2,1,0:T(8,128)(2,1)} %get-tuple-element.12), calls=%async_computation.3 | async-start | bytes 6422528 | tf_op jit(solution)/shard_map/all_to_all | solution.py:232
  169.4 3.0 copy-start.19
  169.5 7.6 %slice-start = ((f32[32,2,3840]{2,1,0:T(2,128)}), f32[32,2,28]{2,1,0:T(2,128)S(1)}, s32[]{:S(2)}) async-start(f32[32,2,3840]{2,1,0:T(2,128)} %all_to_all.25), calls=%async_computation.6 | async-start | bytes 65536 | tf_op jit(solution)/shard_map/slice | solution.py:235
  176.5 4.1 %copy-start.16 = (f32[1,896]{1,0:T(1,128)}, f32[1,896]{1,0:T(1,128)S(1)}, u32[]{:S(2)}) copy-start(f32[1,896]{1,0:T(1,128)S(1)} %stack.72) | copy-start | bytes 10756
  178.9 0.8 copy-start.14
  180.6 62.5 %collective-permute-start.6 = (f32[30,896]{1,0:T(8,128)}, f32[30,896]{1,0:T(8,128)S(1)}, u32[]{:S(2)}, u32[]{:S(2)}) collective-permute-start(f32[30,896]{1,0:T(8,128)} %get-tuple-element.41), channel_id=1, source_target_pairs={{0,3},{1,0},{2,1},{3,2},{4,7},{5,4},{6,5},{7,6},{8,11},{9,8},{10,9... | collective-permute-start | bytes 322568 | tf_op jit(solution)/shard_map/ppermute | solution.py:245
  186.0 60.4 %collective-permute-start.5 = (f32[30,896]{1,0:T(8,128)}, f32[30,896]{1,0:T(8,128)}, u32[]{:S(2)}, u32[]{:S(2)}) collective-permute-start(f32[30,896]{1,0:T(8,128)} %get-tuple-element.40), channel_id=1, source_target_pairs={{0,2},{1,3},{2,0},{3,1},{4,6},{5,7},{6,4},{7,5},{8,10},{9,11},{10,... | collective-permute-start | bytes 322568 | tf_op jit(solution)/shard_map/ppermute | solution.py:245
  188.6 57.8 %collective-permute-start.4 = (f32[30,896]{1,0:T(8,128)}, f32[30,896]{1,0:T(8,128)}, u32[]{:S(2)}, u32[]{:S(2)}) collective-permute-start(f32[30,896]{1,0:T(8,128)} %get-tuple-element.39), channel_id=1, source_target_pairs={{0,1},{1,2},{2,3},{3,0},{4,5},{5,6},{6,7},{7,4},{8,9},{9,10},{10,1... | collective-permute-start | bytes 322568 | tf_op jit(solution)/shard_map/ppermute | solution.py:245
  232.9 13.5 %collective-permute-start.7 = (bf16[28,896]{1,0:T(8,128)(2,1)S(1)}, bf16[28,896]{1,0:T(8,128)(2,1)S(1)}, u32[]{:S(2)}, u32[]{:S(2)}) collective-permute-start(bf16[28,896]{1,0:T(8,128)(2,1)S(1)} %get-tuple-element.33), channel_id=1, source_target_pairs={{0,1},{1,2},{2,3},{3,0},{4,5},{5,6},{6,7},{7,4},{8,9},{9,10},{10,1... | collective-permute-start | bytes 150536 | tf_op jit(solution)/shard_map/ppermute | solution.py:263
  234.8 13.9 %collective-permute-start.8 = (bf16[28,896]{1,0:T(8,128)(2,1)S(1)}, bf16[28,896]{1,0:T(8,128)(2,1)S(1)}, u32[]{:S(2)}, u32[]{:S(2)}) collective-permute-start(bf16[28,896]{1,0:T(8,128)(2,1)S(1)} %get-tuple-element.35), channel_id=1, source_target_pairs={{0,2},{1,3},{2,0},{3,1},{4,6},{5,7},{6,4},{7,5},{8,10},{9,11},{10,... | collective-permute-start | bytes 150536 | tf_op jit(solution)/shard_map/ppermute | solution.py:263
  243.1 9.0 %collective-permute-start.9 = (bf16[28,896]{1,0:T(8,128)(2,1)S(1)}, bf16[28,896]{1,0:T(8,128)(2,1)S(1)}, u32[]{:S(2)}, u32[]{:S(2)}) collective-permute-start(bf16[28,896]{1,0:T(8,128)(2,1)S(1)} %get-tuple-element.34), channel_id=1, source_target_pairs={{0,3},{1,0},{2,1},{3,2},{4,7},{5,4},{6,5},{7,6},{8,11},{9,8},{10,9... | collective-permute-start | bytes 150536 | tf_op jit(solution)/shard_map/ppermute | solution.py:263
  254.3 19.8 %all-to-all-start.4 = ((bf16[16,28,896]{2,1,0:T(8,128)(2,1)}), bf16[16,28,896]{2,1,0:T(8,128)(2,1)}, u32[]{:S(2)}, u32[]{:S(2)}) async-start(bf16[16,28,896]{2,1,0:T(8,128)(2,1)} %broadcast_in_dim.31), calls=%async_computation.4 | async-start | bytes 1835008 | tf_op jit(solution)/shard_map/all_to_all | solution.py:268
  276.1 22.4 %collective-permute-start.10 = (bf16[448,896]{1,0:T(8,128)(2,1)}, bf16[448,896]{1,0:T(8,128)(2,1)}, u32[]{:S(2)}, u32[]{:S(2)}) collective-permute-start(bf16[448,896]{1,0:T(8,128)(2,1)} %reshape.459), channel_id=1, source_target_pairs={{0,16},{16,0},{1,17},{17,1},{2,18},{18,2},{3,19},{19,3},{4,20},{20... | collective-permute-start | bytes 2408456 | tf_op jit(solution)/shard_map/ppermute | solution.py:37
  284.5 1.0 copy-start.1
  285.4 0.9 copy-start.3
  286.4 0.9 copy-start.5
  287.3 8.8 %copy-start.11 = (bf16[1,2,128,896]{3,2,1,0:T(8,128)(2,1)S(1)}, bf16[1,2,128,896]{3,2,1,0:T(8,128)(2,1)}, u32[]{:S(2)}) copy-start(bf16[1,2,128,896]{3,2,1,0:T(8,128)(2,1)} %param.6) | copy-start | bytes 1376260
  287.3 8.8 %copy-start.17 = (f32[2,1,896]{2,0,1:T(2,128)S(1)}, f32[2,1,896]{2,0,1:T(2,128)}, u32[]{:S(2)}) copy-start(f32[2,1,896]{2,0,1:T(2,128)} %copy.93) | copy-start | bytes 21508
  287.3 8.8 %copy-start.20 = (f32[2,128]{1,0:T(2,128)S(1)}, f32[2,128]{1,0:T(2,128)}, u32[]{:S(2)}) copy-start(f32[2,128]{1,0:T(2,128)} %fusion.35) | copy-start | bytes 3076
  294.0 4.6 %copy-start.13 = (bf16[448,896]{1,0:T(8,128)(2,1)S(1)}, bf16[448,896]{1,0:T(8,128)(2,1)}, u32[]{:S(2)}) copy-start(bf16[448,896]{1,0:T(8,128)(2,1)} %reshape.459) | copy-start | bytes 2408452
  294.0 3.6 %collective-permute-start.3 = (bf16[256,448]{1,0:T(8,128)(2,1)S(1)}, bf16[256,448]{1,0:T(8,128)(2,1)S(1)}, u32[]{:S(2)}, u32[]{:S(2)}) collective-permute-start(bf16[256,448]{1,0:T(8,128)(2,1)S(1)} %get-tuple-element.11), channel_id=1, source_target_pairs={{0,16},{16,0},{1,17},{17,1},{2,18},{18,2},{3,19},{19,3},{4,20},{20... | collective-permute-start | bytes 688136 | tf_op jit(solution)/shard_map/ppermute | solution.py:37
Sparse Core Ops, SparseCore 0:
  77.1 150.3 all-gather.2

commit v3 on v2

--- a/solution.py
+++ b/solution.py
@@ -25,6 +25,7 @@
 SLICE = HALF // (NX * NY)
 W_ROWS = HALF // NY
 PIECES = 16
+GROUP = NX * NY * NC
 
 AT_RMS = D
 AT_U = D + SEQ
@@ -37,20 +38,108 @@
     return lax.ppermute(value, "c", [(0, 1), (1, 0)])
 
 
-def split3(value):
-    high = lax.reduce_precision(value, 8, 7)
-    rest = value - high
-    mid = lax.reduce_precision(rest, 8, 7)
-    low = rest - mid
-    return high.astype(bf16), mid.astype(bf16), low.astype(bf16)
-
-
 contract_last = (((1,), (1,)), ((), ()))
 contract_first = (((0,), (0,)), ((), ()))
 
 
 def dot_last(left, right):
     return lax.dot_general(left, right, contract_last, preferred_element_type=f32)
+
+
+def dot_exact(left, right, dims):
+    return lax.dot_general(
+        left, right, dims, precision=lax.Precision.HIGHEST, preferred_element_type=f32
+    )
+
+
+def group_kernel(
+    index_ref, got_ref, gain_ref,
+    scaled_ref, first_ref, gain_out_ref, loss_ref, pieces_ref, scale_ref, column_ref,
+):
+    gain = gain_ref[...]
+    raw, unit, inv_norm = [], [], []
+    for side in range(2):
+        raw.append(got_ref[side, :, :D])
+        embeds = raw[side] * gain
+        square = jnp.sum(embeds * embeds, -1, keepdims=True)
+        inv_norm.append(lax.rsqrt(square + epsilon))
+        unit.append(embeds * inv_norm[side])
+    logits = logit_scale * dot_exact(unit[0], unit[1], contract_last)
+    log_total = jnp.log(jnp.sum(jnp.exp(logits), -1, keepdims=True))
+    target = got_ref[0, :, AT_POS : AT_POS + 1]
+    passage = lax.broadcasted_iota(jnp.int32, (GROUP, GROUP), 1).astype(f32)
+    one_hot = jnp.where(passage == target, 1.0, 0.0)
+    chosen = jnp.sum(logits * one_hot, -1, keepdims=True)
+    loss = jnp.sum(log_total - chosen, 0, keepdims=True)
+    loss_ref[...] = jnp.broadcast_to(loss, (8, 128))
+    score_grad = grad_scale * (jnp.exp(logits - log_total) - one_hot)
+    grads = (
+        dot_exact(score_grad, unit[1], (((1,), (0,)), ((), ()))),
+        dot_exact(score_grad, unit[0], contract_first),
+    )
+    gain_sum = jnp.zeros((1, D), f32)
+    first = jnp.zeros((SLICE, D), f32)
+    for side in range(2):
+        grad = logit_scale * grads[side]
+        along = jnp.sum(unit[side] * grad, -1, keepdims=True)
+        pooled_grad = (grad - unit[side] * along) * inv_norm[side]
+        gain_sum = gain_sum + jnp.sum(pooled_grad * raw[side], 0, keepdims=True)
+        scaled = pooled_grad * gain
+        scaled_ref[side] = scaled
+        first = first + dot_exact(got_ref[side, :, AT_U:AT_LEN], scaled, contract_first)
+    for block in range(NR):
+        columns = slice(block * COLS, (block + 1) * COLS)
+        first_ref[block] = first[:, columns]
+        gain_out_ref[block] = gain_sum[:, columns]
+
+    token = lax.broadcasted_iota(jnp.int32, (SEQ, SEQ), 0)
+    lane = lax.broadcasted_iota(jnp.int32, (SEQ, SEQ), 1)
+    position = lax.broadcasted_iota(jnp.int32, (SEQ, 1), 0).astype(f32)
+    for pair in range(NC):
+        index = index_ref[pair]
+        chosen_row = lax.broadcasted_iota(jnp.int32, (GROUP, 1), 0) == index
+        parts = []
+        for side in range(2):
+            row = jnp.sum(jnp.where(chosen_row, scaled_ref[side], 0.0), 0, keepdims=True)
+            high = row.astype(bf16).astype(f32)
+            mid = (row - high).astype(bf16).astype(f32)
+            parts += [high, mid, row - high - mid]
+            rest = jnp.where(chosen_row, got_ref[side, :, AT_RMS:WIDTH], 0.0)
+            rest = jnp.sum(rest, 0, keepdims=True)
+            rms_row = rest[:, :SEQ]
+            count = rest[:, AT_LEN - AT_RMS : AT_LEN - AT_RMS + 1]
+            rms = jnp.sum(jnp.where(token == lane, rms_row, 0.0), -1, keepdims=True)
+            column = jnp.where(position < count, rms / count, 0.0)
+            here = slice(side * SEQ, (side + 1) * SEQ)
+            column_ref[pair, here, :] = column
+            scale_ref[pair, here, :] = column * rms * rms * (1.0 / D)
+        parts.append(jnp.zeros((PIECES - 6, D), f32))
+        piece = jnp.concatenate(parts, 0).astype(bf16)
+        for block in range(NR):
+            pieces_ref[pair, block] = piece[:, block * COLS : (block + 1) * COLS]
+
+
+def group_math(index, got, gain):
+    spec = pl.BlockSpec(memory_space=pltpu.VMEM)
+    return pl.pallas_call(
+        group_kernel,
+        out_shape=(
+            jax.ShapeDtypeStruct((2, GROUP, D), f32),
+            jax.ShapeDtypeStruct((NR, SLICE, COLS), f32),
+            jax.ShapeDtypeStruct((NR, 1, COLS), f32),
+            jax.ShapeDtypeStruct((8, 128), f32),
+            jax.ShapeDtypeStruct((NC, NR, PIECES, COLS), bf16),
+            jax.ShapeDtypeStruct((NC, TOK, 1), f32),
+            jax.ShapeDtypeStruct((NC, TOK, 1), f32),
+        ),
+        in_specs=[pl.BlockSpec(memory_space=pltpu.SMEM), spec, spec],
+        out_specs=(spec,) * 7,
+        compiler_params=pltpu.CompilerParams(vmem_limit_bytes=32 * 1024 * 1024),
+        cost_estimate=pl.CostEstimate(
+            flops=50 * GROUP * GROUP * D, bytes_accessed=3 * 1024 * 1024, transcendentals=4096
+        ),
+        name="group_math",
+    )(index, got, gain)
 
 
 def weight_kernel(
@@ -140,14 +229,13 @@
 
 
 def body(hidden_state, attn_out, o_weight, norm_gain, lengths, positive):
-    highest = lax.Precision.HIGHEST
     ix, iy, ic = lax.axis_index("x"), lax.axis_index("y"), lax.axis_index("c")
     it, ir = lax.axis_index("t"), lax.axis_index("r")
     dp_index = (ix * NY + iy) * NC + ic
 
     state = hidden_state.reshape(TOK, FEAT)
     attn = attn_out.reshape(TOK, FEAT)
-    state_all = lax.all_to_all(jnp.broadcast_to(state[None], (NT, TOK, FEAT)), "t", 0, 0)
+    state_all = lax.all_gather(state, "t")
     w_start = (ic * NY + iy) * W_ROWS
     w_mine = lax.dynamic_slice(o_weight, (w_start, 0), (W_ROWS, COLS))
     w_moved = lax.ppermute(
@@ -155,7 +243,6 @@
         ("x", "r"),
         [(i * NR + (j + i) % NR, i * NR + j) for i in range(NX) for j in range(NR)],
     )
-    w_all = lax.all_gather(w_moved, PLANE).reshape(NX, HALF, COLS)
     attn_keep = jnp.where(ic == 0, attn[:, :HALF], attn[:, HALF:])
     attn_give = jnp.where(ic == 0, attn[:, HALF:], attn[:, :HALF])
     attn_other = swap_core(attn_give)
@@ -172,72 +259,41 @@
     near = jnp.concatenate([pooled, norm_gain[None]], 0)
     near = lax.all_to_all(jnp.broadcast_to(near[None], (NT, 3, FEAT)), "t", 0, 0)
     pooled_row = near[:, :2].transpose(1, 0, 2).reshape(2, D)
-    gain = near[:, 2].reshape(D)
+    gain = near[:, 2].reshape(1, D)
 
     u_parts = attn_pool.reshape(2, NC, NX * NY, SLICE).transpose(2, 1, 0, 3)
-    u_parts = u_parts.reshape(NX * NY * NC, 2, SLICE)
+    u_parts = u_parts.reshape(GROUP, 2, SLICE)
     extra = jnp.stack(
         [token_count, jnp.broadcast_to(positive.astype(f32), (2,))], -1
     )
     row = jnp.concatenate([pooled_row, inv_rms], -1)
-    group = NX * NY * NC
     send = jnp.concatenate(
         [
-            jnp.broadcast_to(row[None], (group, 2, D + SEQ)),
+            jnp.broadcast_to(row[None], (GROUP, 2, D + SEQ)),
             u_parts,
-            jnp.broadcast_to(extra[None], (group, 2, 2)),
-            jnp.zeros((group, 2, WIDTH - AT_POS - 1), f32),
+            jnp.broadcast_to(extra[None], (GROUP, 2, 2)),
+            jnp.zeros((GROUP, 2, WIDTH - AT_POS - 1), f32),
         ],
         -1,
     )
     got = lax.all_to_all(send, DP, 0, 0)
-
-    raw = got[..., :D]
-    embeds = raw * gain
-    inv_norm = lax.rsqrt(jnp.sum(embeds * embeds, -1, keepdims=True) + epsilon)
-    unit = embeds * inv_norm
-    query, passage = unit[:, 0], unit[:, 1]
-    target = got[:, 0, AT_POS].astype(jnp.int32)
-    logits = logit_scale * lax.dot_general(query, passage, contract_last, precision=highest)
-    log_total = jnp.log(jnp.sum(jnp.exp(logits), -1))
-    one_hot = (jnp.arange(group, dtype=jnp.int32)[None, :] == target[:, None]).astype(f32)
-    loss_part = jnp.sum(log_total - jnp.sum(logits * one_hot, -1))
-    score_grad = grad_scale * (jnp.exp(logits - log_total[:, None]) - one_hot)
-    query_grad = logit_scale * jnp.dot(score_grad, passage, precision=highest)
-    passage_grad = logit_scale * lax.dot_general(
-        score_grad, query, contract_first, precision=highest
-    )
-    embed_grad = jnp.stack([query_grad, passage_grad], 1)
-    along = jnp.sum(unit * embed_grad, -1, keepdims=True)
-    pooled_grad = (embed_grad - unit * along) * inv_norm
-    gain_part = jnp.sum(pooled_grad * raw, (0, 1))
-    scaled = pooled_grad * gain
-    gain_mine = lax.dynamic_slice(gain_part, (it * FEAT,), (FEAT,))
+    got, state_all, w_moved = lax.optimization_barrier((got, state_all, w_moved))
+    w_all = lax.all_gather(w_moved, PLANE).reshape(NX, HALF, COLS)
 
     other_index = dp_index + 1 - 2 * ic
     state_other = swap_core(state_all)
-    rows = jnp.stack([scaled[dp_index], scaled[other_index]])
-    counts = jnp.stack([got[dp_index, :, AT_LEN], got[other_index, :, AT_LEN]])
-    rms = jnp.stack([got[dp_index, :, AT_RMS:AT_U], got[other_index, :, AT_RMS:AT_U]])
-    place = jnp.arange(SEQ, dtype=jnp.int32).astype(f32)
-    first_coef = jnp.where(place < counts[..., None], rms / counts[..., None], 0.0)
-    scale = (first_coef * rms * rms / D).reshape(NC, TOK, 1)
-    first_col = first_coef.reshape(NC, TOK, 1)
-    pieces = jnp.stack(split3(rows), 2).reshape(NC, 6, NT, FEAT).transpose(0, 2, 1, 3)
-    pieces = jnp.pad(pieces, ((0, 0), (0, 0), (0, PIECES - 6), (0, 0)))
+    scaled, first, gain_part, loss_part, pieces, scale, first_col = group_math(
+        jnp.stack([dp_index, other_index]), got.transpose(1, 0, 2), gain
+    )
 
     partial, coef = weight_partials(
         state_all, state_other, attn_keep, attn_other, pieces, scale
     )
+    partial, first = lax.optimization_barrier((partial, first))
     spread = lax.all_to_all(partial, PLANE, 0, 0)
-    second = jnp.sum(spread.astype(f32), 0).reshape(NR, SLICE, COLS)
-
-    u_all = got[..., AT_U:AT_LEN].reshape(2 * group, SLICE)
-    first = lax.dot_general(
-        u_all, scaled.reshape(2 * group, D), contract_first, precision=highest
-    )
-    first = first.reshape(SLICE, NR, COLS).transpose(1, 0, 2)
-    tail = jnp.stack([gain_mine, jnp.broadcast_to(loss_part, (FEAT,))])
+
+    gain_mine = lax.dynamic_index_in_dim(gain_part, it, 0, keepdims=False)
+    tail = jnp.concatenate([gain_mine, jnp.broadcast_to(loss_part[:1, :1], (1, FEAT))], 0)
     tails = [tail]
     first_sum = lax.dynamic_index_in_dim(first, ir, 0, keepdims=False)
     for step in range(1, NR):
@@ -256,16 +312,21 @@
             tails, (ir - source) % NR, 0, keepdims=False
         )
 
-    second_sum = lax.dynamic_index_in_dim(second, ir, 0, keepdims=False)
-    second_cut = second.astype(bf16)
-    for step in range(1, NR):
-        outgoing = lax.dynamic_index_in_dim(second_cut, (ir + step) % NR, 0, keepdims=False)
-        second_sum = second_sum + lax.ppermute(
-            outgoing, "r", [(j, (j + step) % NR) for j in range(NR)]
-        ).astype(f32)
+    spread, first_sum, totals = lax.optimization_barrier((spread, first_sum, totals))
+    second = jnp.sum(spread.astype(f32), 0).reshape(NR, SLICE, COLS)
+    second_sum = jnp.sum(
+        lax.all_to_all(second.astype(bf16), "r", 0, 0).astype(f32), 0
+    )
     total = first_sum - second_sum
     done = jnp.broadcast_to(total.astype(bf16)[None], (NX * NY, SLICE, COLS))
     half = lax.all_to_all(done, PLANE, 0, 0).reshape(HALF, COLS)
+    row_here = lax.dynamic_slice(scaled, (0, dp_index, it * FEAT), (2, 1, FEAT))
+    state_grad = first_col[0].reshape(2, SEQ, 1) * row_here - states * coef[0].reshape(2, SEQ, 1)
+    grad_hidden = state_grad.astype(bf16).reshape(1, 2, SEQ, FEAT)
+    keep, give = attn_grads(
+        ir.reshape(1), state_all, state_other, pieces, w_all, coef, first_col
+    )
+    half, keep, give = lax.optimization_barrier((half, keep, give))
     half_other = swap_core(half)
     grad_weight = jnp.where(
         ic == 0,
@@ -273,17 +334,6 @@
         jnp.concatenate([half_other, half], 0),
     )
 
-    row_here = lax.dynamic_index_in_dim(
-        rows[0].reshape(2, NT, FEAT), it, 1, keepdims=False
-    )
-    state_grad = first_coef[0][..., None] * row_here[:, None, :] - states * coef[0].reshape(
-        2, SEQ, 1
-    )
-    grad_hidden = state_grad.astype(bf16).reshape(1, 2, SEQ, FEAT)
-
-    keep, give = attn_grads(
-        ir.reshape(1), state_all, state_other, pieces, w_all, coef, first_col
-    )
     arrived = swap_core(give)
     grad_attn = jnp.where(
         ic == 0, jnp.concatenate([keep, arrived], 1), jnp.concatenate([arrived, keep], 1)

time: 311 us -> 240 us (0.77)
  the two profiles are of different devices: /device:TPU:33 before, /device:TPU:1 now
where the time goes in v3:
time: 240 us; the launch traced here: 239 us
  starting transfers between devices  92.1 us (38%)
  waiting for transfers between devices  41.3 us (17%)
  blocking collectives  35 us (15%)
  local copies, waits for them, and re-layouts  22.7 us (9%)
  Pallas kernels  17.5 us (7%)
  between operations  15.3 us (6%)
  other arithmetic  14.9 us (6%)
    all_to_all x1, blocking collectives, body(): lax.all_to_all(second.astype(bf16), 'r', 0, 0).astype(f32)  23.2 us
    ppermute x3, starting transfers between devices, body(): lax.ppermute(jnp.concatenate([outgoing, tail], 0), 'r', [(j, (j + step) %...  22.1 us
    all_to_all x1, starting transfers between devices, body(): spread = lax.all_to_all(partial, PLANE, 0, 0)  21.3 us
    ppermute x4, starting transfers between devices, swap_core(): return lax.ppermute(value, 'c', [(0, 1), (1, 0)])  19.5 us
    all_to_all x1, waiting for transfers between devices, body(): got = lax.all_to_all(send, DP, 0, 0)  15.4 us
    all_to_all x1, starting transfers between devices, body(): half = lax.all_to_all(done, PLANE, 0, 0).reshape(HALF, COLS)  14.2 us
    all_to_all x1, waiting for transfers between devices, body(): spread = lax.all_to_all(partial, PLANE, 0, 0)  12.9 us
    psum x1, blocking collectives, body(): square = lax.psum(jnp.sum(states * states, -1), 't') / D  11.8 us
  transfers between devices with their start and end apart: 14, of which 7 were waited for; matrix products, arithmetic and copies ran while one was open for 11% of the time, Pallas kernels for 7%

profile of v3, /device:TPU:1, one launch (start us, length us, event | category | flops | bytes accessed | tf_op | source)
XLA Modules:
  0.0 238.8 jit_solution(12956213652254757388)
XLA Ops:
  8.6 1.2 fusion.2
  9.8 11.8 %psum.7 = f32[2,128]{1,0:T(2,128)S(1)} all-reduce(f32[2,128]{1,0:T(2,128)S(1)} %fusion.2), channel_id=1, replica_groups=mesh['x'=4,'y'=4,'c'=2,'t'=4,'r'=4] {'t'}, use_global_device_ids=true, to_apply=%region_1.2 | all-reduce | flops 256 | bytes 2048 | tf_op jit(solution)/shard_map/psum | solution.py:251
  21.6 0.7 convert_bitcast_fusion.1
  22.3 0.7 fusion.10
  23.1 1.4 fusion.6
  25.1 3.3 %all-to-all-start = ((f32[4,3,896]{2,1,0:T(4,128)}), f32[4,3,896]{2,1,0:T(4,128)S(1)}, u32[]{:S(2)}, u32[]{:S(2)}) async-start(f32[4,3,896]{2,1,0:T(4,128)} %broadcast_in_dim.17), calls=%async_computation | async-start | bytes 114688 | tf_op jit(solution)/shard_map/all_to_all | solution.py:260
  29.4 3.6 %all-to-all-done = f32[4,3,896]{2,1,0:T(4,128)S(1)} async-done(((f32[4,3,896]{2,1,0:T(4,128)}), f32[4,3,896]{2,1,0:T(4,128)S(1)}, u32[]{:S(2)}, u32[]{:S(2)}) %all-to-all-start) | async-done | bytes 43040 | tf_op jit(solution)/shard_map/all_to_all | solution.py:260
  33.3 2.2 concatenate.56
  35.5 11.0 %all-to-all-start.1 = ((f32[32,2,3840]{2,1,0:T(2,128)}), f32[32,2,3840]{2,1,0:T(2,128)S(1)}, u32[]{:S(2)}, u32[]{:S(2)}) async-start(f32[32,2,3840]{2,1,0:T(2,128)} %concatenate.56), calls=%async_computation.1 | async-start | bytes 1966080 | tf_op jit(solution)/shard_map/all_to_all | solution.py:279
  47.4 15.4 %all-to-all-done.1 = f32[32,2,3840]{2,1,0:T(2,128)S(1)} async-done(((f32[32,2,3840]{2,1,0:T(2,128)}), f32[32,2,3840]{2,1,0:T(2,128)S(1)}, u32[]{:S(2)}, u32[]{:S(2)}) %all-to-all-start.1) | async-done | bytes 983072 | tf_op jit(solution)/shard_map/all_to_all | solution.py:279
  62.8 3.3 %all-gather.4.cloned.1.call-done.own_ref = bf16[4,256,896]{2,1,0:T(8,128)(2,1)} async-done(((bf16[1,256,896]{2,1,0:T(8,128)(2,1)}), bf16[4,256,896]{2,1,0:T(8,128)(2,1)}) %all-gather.4.cloned.1.call-update) | async-done | bytes 1835024 | tf_op jit(solution)/shard_map/all_gather | solution.py:238
  66.1 2.8 %collective-permute-start.1 = (bf16[4,256,896]{2,1,0:T(8,128)(2,1)}, bf16[4,256,896]{2,1,0:T(8,128)(2,1)}, u32[]{:S(2)}, u32[]{:S(2)}) collective-permute-start(bf16[4,256,896]{2,1,0:T(8,128)(2,1)} %all-gather.4.cloned.1.call-done.own_ref), channel_id=1, source_target_pairs={{0,16},{16,0},{1,17},{17,1},{2,18},{18,2},{3,19},{19,3},{4,20},{20... | collective-permute-start | bytes 5505032 | tf_op jit(solution)/shard_map/ppermute | solution.py:38
  69.0 2.1 broadcast_select_fusion
  71.1 1.9 collective-permute-start.2
  73.2 1.3 copy.24
  74.4 4.2 %group_math.1 = (f32[2,32,3584]{2,1,0:T(8,128)S(1)}, f32[4,28,896]{2,1,0:T(8,128)S(1)}, f32[4,1,896]{2,1,0:T(1,128)S(1)}, f32[8,128]{1,0:T(8,128)S(1)}, bf16[2,4...) custom-call(s32[2]{0:T(128)S(1)} %pad_add_fusion.index_ref, ...), custom_call_target="tpu_custom_call" | custom-call | flops 183500800 | bytes 3145728 | tf_op jit(solution)/shard_map/group_math/pallas_call | solution.py:124
  79.3 0.8 copy-done.8
  80.1 0.9 copy-done.14
  81.0 6.8 %weight_partials.1 = (bf16[16,112,896]{2,1,0:T(8,128)(2,1)}, f32[2,256,1]{2,1,0:T(8,128)S(1)}) custom-call(bf16[4,256,896]{2,1,0:T(8,128)(2,1)S(1)} %copy-done.1, bf16[4,256,896]{2,1,0:T(8,128)(2,1)} %collective-permute-done.1.other_ref, bf16[256,448]{1,0:T(8,128)(2,1)S(1)} %copy-done.11, bf16[256,448]{1,0:T(8,128)(2,1)} %collective-permute-done.2.given_ref, ...), custom_call_target="tpu_custom_call" | custom-call | flops 1644167168 | bytes 8388608 | tf_op jit(solution)/shard_map/weight_partials/pallas_call | solution.py:178
  87.8 0.7 copy-done.5
  88.5 21.3 %all-to-all-start.2 = ((bf16[16,112,896]{2,1,0:T(8,128)(2,1)}), bf16[16,112,896]{2,1,0:T(8,128)(2,1)}, u32[]{:S(2)}, u32[]{:S(2)}) async-start(bf16[16,112,896]{2,1,0:T(8,128)(2,1)} %get-tuple-element.36), calls=%async_computation.2 | async-start | bytes 6422528 | tf_op jit(solution)/shard_map/all_to_all | solution.py:293
  110.5 0.7 pad.22.clone
  111.2 1.0 dynamic-slice_bitcast_fusion.2
  112.3 9.4 %collective-permute-start.5 = (f32[30,896]{1,0:T(8,128)S(1)}, f32[30,896]{1,0:T(8,128)S(1)}, u32[]{:S(2)}, u32[]{:S(2)}) collective-permute-start(f32[30,896]{1,0:T(8,128)S(1)} %get-tuple-element.58), channel_id=1, source_target_pairs={{0,3},{1,0},{2,1},{3,2},{4,7},{5,4},{6,5},{7,6},{8,11},{9,8},{10,9... | collective-permute-start | bytes 322568 | tf_op jit(solution)/shard_map/ppermute | solution.py:301
  122.3 6.7 %collective-permute-start.4 = (f32[30,896]{1,0:T(8,128)S(1)}, f32[30,896]{1,0:T(8,128)S(1)}, u32[]{:S(2)}, u32[]{:S(2)}) collective-permute-start(f32[30,896]{1,0:T(8,128)S(1)} %get-tuple-element.57), channel_id=1, source_target_pairs={{0,2},{1,3},{2,0},{3,1},{4,6},{5,7},{6,4},{7,5},{8,10},{9,11},{10,... | collective-permute-start | bytes 322568 | tf_op jit(solution)/shard_map/ppermute | solution.py:301
  129.1 6.0 %collective-permute-start.3 = (f32[30,896]{1,0:T(8,128)S(1)}, f32[30,896]{1,0:T(8,128)S(1)}, u32[]{:S(2)}, u32[]{:S(2)}) collective-permute-start(f32[30,896]{1,0:T(8,128)S(1)} %get-tuple-element.56), channel_id=1, source_target_pairs={{0,1},{1,2},{2,3},{3,0},{4,5},{5,6},{6,7},{7,4},{8,9},{9,10},{10,1... | collective-permute-start | bytes 322568 | tf_op jit(solution)/shard_map/ppermute | solution.py:301
  135.1 1.6 collective-permute-done.4
  136.7 3.5 %collective-permute-done.3 = f32[30,896]{1,0:T(8,128)S(1)} collective-permute-done((f32[30,896]{1,0:T(8,128)S(1)}, f32[30,896]{1,0:T(8,128)S(1)}, u32[]{:S(2)}, u32[]{:S(2)}) %collective-permute-start.3) | collective-permute-done | bytes 107552 | tf_op jit(solution)/shard_map/ppermute | solution.py:301
  140.8 0.9 slice_add_fusion
  141.7 12.9 %all-to-all-done.2 = bf16[16,112,896]{2,1,0:T(8,128)(2,1)} async-done(((bf16[16,112,896]{2,1,0:T(8,128)(2,1)}), bf16[16,112,896]{2,1,0:T(8,128)(2,1)}, u32[]{:S(2)}, u32[]{:S(2)}) %all-to-all-start.2) | async-done | bytes 3211296 | tf_op jit(solution)/shard_map/all_to_all | solution.py:293
  154.6 3.1 %reduce_sum.51 = bf16[112,896]{1,0:T(8,128)(2,1)} reduce(bf16[16,112,896]{2,1,0:T(8,128)(2,1)} %all-to-all-done.2, bf16[]{:T(256)} %constant.112.clone.1), dimensions={0}, to_apply=%region_4.5 | reduce | flops 1505280 | bytes 3411970 | tf_op jit(solution)/shard_map/reduce_sum | solution.py:316
  157.7 1.7 convert_element_type.65
  159.4 23.2 %all_to_all.25 = bf16[4,28,896]{2,1,0:T(8,128)(2,1)S(1)} all-to-all(bf16[4,28,896]{2,1,0:T(8,128)(2,1)} %convert_element_type.65), channel_id=1, replica_groups=mesh['x'=4,'y'=4,'c'=2,'t'=4,'r'=4] {'r'}, dimensions={0} | all-to-all | bytes 401408 | tf_op jit(solution)/shard_map/all_to_all | solution.py:318
  182.6 1.0 broadcast_in_dim.23
  183.6 14.2 %all-to-all-start.4 = ((bf16[16,28,896]{2,1,0:T(8,128)(2,1)}), bf16[16,28,896]{2,1,0:T(8,128)(2,1)}, u32[]{:S(2)}, u32[]{:S(2)}) async-start(bf16[16,28,896]{2,1,0:T(8,128)(2,1)} %broadcast_in_dim.23), calls=%async_computation.4 | async-start | bytes 1835008 | tf_op jit(solution)/shard_map/all_to_all | solution.py:322
  197.8 0.9 copy-done.3
  198.8 0.9 copy-done.6
  199.7 0.9 copy-done.13
  200.7 6.6 %attn_grads.1 = (bf16[256,448]{1,0:T(8,128)(2,1)S(1)}, bf16[256,448]{1,0:T(8,128)(2,1)S(1)}) custom-call(s32[1]{0:T(128)} %bitcast.26.shift_ref, bf16[4,256,896]{2,1,0:T(8,128)(2,1)S(1)} %copy-done.1, bf16[4,256,896]{2,1,0:T(8,128)(2,1)} %collective-permute-done.1.other_ref, bf16[2,4,16,896]{3,2,1,0:T(8,128)(2,1)S(1)} %copy-done.13, ...), custom_call_target="tpu_custom_call" | custom-call | flops 1644167168 | bytes 8388608 | tf_op jit(solution)/shard_map/attn_grads/pallas_call | solution.py:218
  207.3 0.7 copy-done.9
  208.0 0.7 copy-done.15
  208.9 2.1 reshape.135
  211.1 12.8 %collective-permute-start.7 = (bf16[448,896]{1,0:T(8,128)(2,1)}, bf16[448,896]{1,0:T(8,128)(2,1)S(1)}, u32[]{:S(2)}, u32[]{:S(2)}) collective-permute-start(bf16[448,896]{1,0:T(8,128)(2,1)} %reshape.135), channel_id=1, source_target_pairs={{0,16},{16,0},{1,17},{17,1},{2,18},{18,2},{3,19},{19,3},{4,20},{20... | collective-permute-start | bytes 2408456 | tf_op jit(solution)/shard_map/ppermute | solution.py:38
  223.9 0.9 constant_dynamic-slice_fusion
  225.0 1.9 collective-permute-start.6
  227.0 1.0 fusion.5
  229.1 1.1 maximum_select_fusion.1
  230.1 1.8 maximum_select_fusion
  (81 shorter events, 7.8 us)
Async XLA Ops:
  7.2 39.5 %copy-start = (bf16[896,896]{1,0:T(8,128)(2,1)S(1)}, bf16[896,896]{1,0:T(8,128)(2,1)}, u32[]{:S(2)}) copy-start(bf16[896,896]{1,0:T(8,128)(2,1)} %param.8) | copy-start | bytes 4816900
  7.2 58.9 %all-gather.4.cloned.1.call-start = ((), (), s32[]{:S(2)}) async-start(), calls=%async_computation.5 | async-start | bytes 2293760 | tf_op jit(solution)/shard_map/all_gather | solution.py:238
  25.1 7.8 %all-to-all-start = ((f32[4,3,896]{2,1,0:T(4,128)}), f32[4,3,896]{2,1,0:T(4,128)S(1)}, u32[]{:S(2)}, u32[]{:S(2)}) async-start(f32[4,3,896]{2,1,0:T(4,128)} %broadcast_in_dim.17), calls=%async_computation | async-start | bytes 114688 | tf_op jit(solution)/shard_map/all_to_all | solution.py:260
  35.5 27.2 %all-to-all-start.1 = ((f32[32,2,3840]{2,1,0:T(2,128)}), f32[32,2,3840]{2,1,0:T(2,128)S(1)}, u32[]{:S(2)}, u32[]{:S(2)}) async-start(f32[32,2,3840]{2,1,0:T(2,128)} %concatenate.56), calls=%async_computation.1 | async-start | bytes 1966080 | tf_op jit(solution)/shard_map/all_to_all | solution.py:279
  46.6 151.3 %all-gather.6.cloned.1.call-start = ((), (), s32[]{:S(2)}) async-start(), calls=%async_computation.6 | async-start | bytes 3411968 | tf_op jit(solution)/shard_map/all_gather | solution.py:281
  46.7 0.7 collective-permute-start
  47.4 21.6 %copy-start.20 = (bf16[112,896]{1,0:T(8,128)(2,1)}, bf16[112,896]{1,0:T(8,128)(2,1)S(1)}, u32[]{:S(2)}) copy-start(bf16[112,896]{1,0:T(8,128)(2,1)S(1)} %collective-permute-done) | copy-start | bytes 602116
  62.8 6.2 %copy-start.18 = (f32[32,2,3840]{2,1,0:T(2,128)}, f32[32,2,3840]{2,1,0:T(2,128)S(1)}, u32[]{:S(2)}) copy-start(f32[32,2,3840]{2,1,0:T(2,128)S(1)} %all-to-all-done.1) | copy-start | bytes 2949124
  66.1 14.9 %collective-permute-start.1 = (bf16[4,256,896]{2,1,0:T(8,128)(2,1)}, bf16[4,256,896]{2,1,0:T(8,128)(2,1)}, u32[]{:S(2)}, u32[]{:S(2)}) collective-permute-start(bf16[4,256,896]{2,1,0:T(8,128)(2,1)} %all-gather.4.cloned.1.call-done.own_ref), channel_id=1, source_target_pairs={{0,16},{16,0},{1,17},{17,1},{2,18},{18,2},{3,19},{19,3},{4,20},{20... | collective-permute-start | bytes 5505032 | tf_op jit(solution)/shard_map/ppermute | solution.py:38
  69.0 12.0 %copy-start.1 = (bf16[4,256,896]{2,1,0:T(8,128)(2,1)S(1)}, bf16[4,256,896]{2,1,0:T(8,128)(2,1)}, u32[]{:S(2)}) copy-start(bf16[4,256,896]{2,1,0:T(8,128)(2,1)} %all-gather.4.cloned.1.call-done.own_ref) | copy-start | bytes 5505028
  71.1 9.9 %collective-permute-start.2 = (bf16[256,448]{1,0:T(8,128)(2,1)}, bf16[256,448]{1,0:T(8,128)(2,1)}, u32[]{:S(2)}, u32[]{:S(2)}) collective-permute-start(bf16[256,448]{1,0:T(8,128)(2,1)} %get-tuple-element.54), channel_id=1, source_target_pairs={{0,16},{16,0},{1,17},{17,1},{2,18},{18,2},{3,19},{19,3},{4,20},{20... | collective-permute-start | bytes 688136 | tf_op jit(solution)/shard_map/ppermute | solution.py:38
  73.0 8.0 %copy-start.11 = (bf16[256,448]{1,0:T(8,128)(2,1)S(1)}, bf16[256,448]{1,0:T(8,128)(2,1)}, u32[]{:S(2)}) copy-start(bf16[256,448]{1,0:T(8,128)(2,1)} %get-tuple-element.55.keep_ref) | copy-start | bytes 688132
  78.6 0.7 copy-start.2
  79.3 0.8 copy-start.8
  80.1 0.9 copy-start.14
  81.0 6.8 %copy-start.12 = (bf16[2,4,16,896]{3,2,1,0:T(8,128)(2,1)}, bf16[2,4,16,896]{3,2,1,0:T(8,128)(2,1)S(1)}, u32[]{:S(2)}) copy-start(bf16[2,4,16,896]{3,2,1,0:T(8,128)(2,1)S(1)} %get-tuple-element.31.pieces_ref) | copy-start | bytes 688132
  87.8 0.7 copy-start.5
  88.5 66.1 %all-to-all-start.2 = ((bf16[16,112,896]{2,1,0:T(8,128)(2,1)}), bf16[16,112,896]{2,1,0:T(8,128)(2,1)}, u32[]{:S(2)}, u32[]{:S(2)}) async-start(bf16[16,112,896]{2,1,0:T(8,128)(2,1)} %get-tuple-element.36), calls=%async_computation.2 | async-start | bytes 6422528 | tf_op jit(solution)/shard_map/all_to_all | solution.py:293
  112.3 22.7 %collective-permute-start.5 = (f32[30,896]{1,0:T(8,128)S(1)}, f32[30,896]{1,0:T(8,128)S(1)}, u32[]{:S(2)}, u32[]{:S(2)}) collective-permute-start(f32[30,896]{1,0:T(8,128)S(1)} %get-tuple-element.58), channel_id=1, source_target_pairs={{0,3},{1,0},{2,1},{3,2},{4,7},{5,4},{6,5},{7,6},{8,11},{9,8},{10,9... | collective-permute-start | bytes 322568 | tf_op jit(solution)/shard_map/ppermute | solution.py:301
  122.3 14.4 %collective-permute-start.4 = (f32[30,896]{1,0:T(8,128)S(1)}, f32[30,896]{1,0:T(8,128)S(1)}, u32[]{:S(2)}, u32[]{:S(2)}) collective-permute-start(f32[30,896]{1,0:T(8,128)S(1)} %get-tuple-element.57), channel_id=1, source_target_pairs={{0,2},{1,3},{2,0},{3,1},{4,6},{5,7},{6,4},{7,5},{8,10},{9,11},{10,... | collective-permute-start | bytes 322568 | tf_op jit(solution)/shard_map/ppermute | solution.py:301
  129.1 11.1 %collective-permute-start.3 = (f32[30,896]{1,0:T(8,128)S(1)}, f32[30,896]{1,0:T(8,128)S(1)}, u32[]{:S(2)}, u32[]{:S(2)}) collective-permute-start(f32[30,896]{1,0:T(8,128)S(1)} %get-tuple-element.56), channel_id=1, source_target_pairs={{0,1},{1,2},{2,3},{3,0},{4,5},{5,6},{6,7},{7,4},{8,9},{9,10},{10,1... | collective-permute-start | bytes 322568 | tf_op jit(solution)/shard_map/ppermute | solution.py:301
  183.6 25.3 %all-to-all-start.4 = ((bf16[16,28,896]{2,1,0:T(8,128)(2,1)}), bf16[16,28,896]{2,1,0:T(8,128)(2,1)}, u32[]{:S(2)}, u32[]{:S(2)}) async-start(bf16[16,28,896]{2,1,0:T(8,128)(2,1)} %broadcast_in_dim.23), calls=%async_computation.4 | async-start | bytes 1835008 | tf_op jit(solution)/shard_map/all_to_all | solution.py:322
  197.8 1.0 copy-start.3
  198.8 0.9 copy-start.6
  199.7 0.9 copy-start.13
  207.3 0.7 copy-start.9
  208.0 0.7 copy-start.15
  208.7 16.1 %copy-start.4 = (f32[2,256,1]{2,1,0:T(8,128)S(1)}, f32[2,256,1]{2,1,0:T(8,128)}, u32[]{:S(2)}) copy-start(f32[2,256,1]{2,1,0:T(8,128)} %copy-done.2) | copy-start | bytes 6148
  208.7 16.2 %copy-start.7 = (f32[2,256,1]{2,1,0:T(8,128)S(1)}, f32[2,256,1]{2,1,0:T(8,128)}, u32[]{:S(2)}) copy-start(f32[2,256,1]{2,1,0:T(8,128)} %copy-done.5) | copy-start | bytes 6148
  208.7 18.3 %copy-start.17 = (bf16[1,2,128,896]{3,2,1,0:T(8,128)(2,1)S(1)}, bf16[1,2,128,896]{3,2,1,0:T(8,128)(2,1)}, u32[]{:S(2)}) copy-start(bf16[1,2,128,896]{3,2,1,0:T(8,128)(2,1)} %param.6) | copy-start | bytes 1376260
  208.7 19.3 %copy-start.21 = (f32[2,896]{1,0:T(2,128)S(1)}, f32[2,896]{1,0:T(2,128)}, u32[]{:S(2)}) copy-start(f32[2,896]{1,0:T(2,128)} %add_bitcast_fusion) | copy-start | bytes 21508
  208.9 16.1 %copy-start.16 = (bf16[256,448]{1,0:T(8,128)(2,1)S(1)}, bf16[256,448]{1,0:T(8,128)(2,1)}, u32[]{:S(2)}) copy-start(bf16[256,448]{1,0:T(8,128)(2,1)} %copy-done.15) | copy-start | bytes 688132
  208.9 20.2 %copy-start.10 = (bf16[256,448]{1,0:T(8,128)(2,1)S(1)}, bf16[256,448]{1,0:T(8,128)(2,1)}, u32[]{:S(2)}) copy-start(bf16[256,448]{1,0:T(8,128)(2,1)} %copy-done.9) | copy-start | bytes 688132
  211.1 19.1 %copy-start.19 = (bf16[448,896]{1,0:T(8,128)(2,1)S(1)}, bf16[448,896]{1,0:T(8,128)(2,1)}, u32[]{:S(2)}) copy-start(bf16[448,896]{1,0:T(8,128)(2,1)} %reshape.135) | copy-start | bytes 2408452
  211.1 19.1 %collective-permute-start.7 = (bf16[448,896]{1,0:T(8,128)(2,1)}, bf16[448,896]{1,0:T(8,128)(2,1)S(1)}, u32[]{:S(2)}, u32[]{:S(2)}) collective-permute-start(bf16[448,896]{1,0:T(8,128)(2,1)} %reshape.135), channel_id=1, source_target_pairs={{0,16},{16,0},{1,17},{17,1},{2,18},{18,2},{3,19},{19,3},{4,20},{20... | collective-permute-start | bytes 2408456 | tf_op jit(solution)/shard_map/ppermute | solution.py:38
  225.0 4.0 %collective-permute-start.6 = (bf16[256,448]{1,0:T(8,128)(2,1)S(1)}, bf16[256,448]{1,0:T(8,128)(2,1)S(1)}, u32[]{:S(2)}, u32[]{:S(2)}) collective-permute-start(bf16[256,448]{1,0:T(8,128)(2,1)S(1)} %copy-done.16), channel_id=1, source_target_pairs={{0,16},{16,0},{1,17},{17,1},{2,18},{18,2},{3,19},{19,3},{4,20},{20... | collective-permute-start | bytes 688136 | tf_op jit(solution)/shard_map/ppermute | solution.py:38
Sparse Core Ops, SparseCore 0:
  10.1 55.9 all-gather.3
  69.2 102.1 all-gather.5

commit v4 on v3

--- a/solution.py
+++ b/solution.py
@@ -134,7 +134,7 @@
         ),
         in_specs=[pl.BlockSpec(memory_space=pltpu.SMEM), spec, spec],
         out_specs=(spec,) * 7,
-        compiler_params=pltpu.CompilerParams(vmem_limit_bytes=32 * 1024 * 1024),
+        compiler_params=pltpu.CompilerParams(vmem_limit_bytes=16 * 1024 * 1024),
         cost_estimate=pl.CostEstimate(
             flops=50 * GROUP * GROUP * D, bytes_accessed=3 * 1024 * 1024, transcendentals=4096
         ),
@@ -184,7 +184,7 @@
         in_specs=[spec] * 6,
         out_specs=(spec, spec),
         scratch_shapes=[pltpu.VMEM((NR, HALF, COLS), f32)],
-        compiler_params=pltpu.CompilerParams(vmem_limit_bytes=48 * 1024 * 1024),
+        compiler_params=pltpu.CompilerParams(vmem_limit_bytes=24 * 1024 * 1024),
         cost_estimate=pl.CostEstimate(
             flops=4 * TOK * HALF * D, bytes_accessed=8 * 1024 * 1024, transcendentals=0
         ),
@@ -220,7 +220,7 @@
         out_shape=(out, out),
         in_specs=[pl.BlockSpec(memory_space=pltpu.SMEM)] + [spec] * 6,
         out_specs=(spec, spec),
-        compiler_params=pltpu.CompilerParams(vmem_limit_bytes=48 * 1024 * 1024),
+        compiler_params=pltpu.CompilerParams(vmem_limit_bytes=24 * 1024 * 1024),
         cost_estimate=pl.CostEstimate(
             flops=4 * TOK * HALF * D, bytes_accessed=8 * 1024 * 1024, transcendentals=0
         ),
@@ -257,6 +257,7 @@
     attn_pool = jnp.sum(pool_weight[..., None] * attn.astype(f32).reshape(2, SEQ, FEAT), 1)
 
     near = jnp.concatenate([pooled, norm_gain[None]], 0)
+    near, w_moved = lax.optimization_barrier((near, w_moved))
     near = lax.all_to_all(jnp.broadcast_to(near[None], (NT, 3, FEAT)), "t", 0, 0)
     pooled_row = near[:, :2].transpose(1, 0, 2).reshape(2, D)
     gain = near[:, 2].reshape(1, D)
@@ -277,7 +278,9 @@
         -1,
     )
     got = lax.all_to_all(send, DP, 0, 0)
-    got, state_all, w_moved = lax.optimization_barrier((got, state_all, w_moved))
+    got, state_all, w_moved, attn_other = lax.optimization_barrier(
+        (got, state_all, w_moved, attn_other)
+    )
     w_all = lax.all_gather(w_moved, PLANE).reshape(NX, HALF, COLS)
 
     other_index = dp_index + 1 - 2 * ic
@@ -314,19 +317,27 @@
 
     spread, first_sum, totals = lax.optimization_barrier((spread, first_sum, totals))
     second = jnp.sum(spread.astype(f32), 0).reshape(NR, SLICE, COLS)
-    second_sum = jnp.sum(
-        lax.all_to_all(second.astype(bf16), "r", 0, 0).astype(f32), 0
-    )
-    total = first_sum - second_sum
-    done = jnp.broadcast_to(total.astype(bf16)[None], (NX * NY, SLICE, COLS))
-    half = lax.all_to_all(done, PLANE, 0, 0).reshape(HALF, COLS)
+    second = lax.all_to_all(second.astype(bf16), "r", 0, 0)
+
     row_here = lax.dynamic_slice(scaled, (0, dp_index, it * FEAT), (2, 1, FEAT))
     state_grad = first_col[0].reshape(2, SEQ, 1) * row_here - states * coef[0].reshape(2, SEQ, 1)
     grad_hidden = state_grad.astype(bf16).reshape(1, 2, SEQ, FEAT)
     keep, give = attn_grads(
         ir.reshape(1), state_all, state_other, pieces, w_all, coef, first_col
     )
-    half, keep, give = lax.optimization_barrier((half, keep, give))
+
+    second, keep, give = lax.optimization_barrier((second, keep, give))
+    second_sum = jnp.sum(second.astype(f32), 0)
+    total = first_sum - second_sum
+    done = jnp.broadcast_to(total.astype(bf16)[None], (NX * NY, SLICE, COLS))
+    half = lax.all_to_all(done, PLANE, 0, 0).reshape(HALF, COLS)
+    arrived = swap_core(give)
+    grad_attn = jnp.where(
+        ic == 0, jnp.concatenate([keep, arrived], 1), jnp.concatenate([arrived, keep], 1)
+    ).reshape(1, 2, SEQ, FEAT)
+    half, grad_attn, grad_hidden, totals = lax.optimization_barrier(
+        (half, grad_attn, grad_hidden, totals)
+    )
     half_other = swap_core(half)
     grad_weight = jnp.where(
         ic == 0,
@@ -334,10 +345,6 @@
         jnp.concatenate([half_other, half], 0),
     )
 
-    arrived = swap_core(give)
-    grad_attn = jnp.where(
-        ic == 0, jnp.concatenate([keep, arrived], 1), jnp.concatenate([arrived, keep], 1)
-    ).reshape(1, 2, SEQ, FEAT)
     return (grad_hidden, grad_attn, grad_weight, totals[0], totals[1, 0])
 
 

time: 240 us -> 238 us (level)
  blocking collectives: 35 us -> 11.8 us
  starting transfers between devices: 92.1 us -> 103 us
  waiting for transfers between devices: 41.3 us -> 48.9 us
  local copies, waits for them, and re-layouts: 22.7 us -> 27.9 us
  Pallas kernels: 17.5 us -> 14.8 us
    all_to_all x1, starting transfers between devices: 11 us -> 42.3 us  [body(): got = lax.all_to_all(send, DP, 0, 0)]
    all_to_all x1 -> x0, blocking collectives: 23.2 us -> none  [body(): lax.all_to_all(second.astype(bf16), 'r', 0, 0).astype(f32)]
    all_to_all x1, starting transfers between devices: 21.3 us -> 4.49 us  [body(): spread = lax.all_to_all(partial, PLANE, 0, 0)]
    ppermute x3, waiting for transfers between devices: 5.12 us -> 21 us  [body(): lax.ppermute(jnp.concatenate([outgoing, tail], 0), 'r', [(j, (j + step) %...]
    all_to_all x0 -> x1, starting transfers between devices: none -> 10.9 us  [body(): second = lax.all_to_all(second.astype(bf16), 'r', 0, 0)]
    ppermute x3, starting transfers between devices: 22.1 us -> 13.8 us  [body(): lax.ppermute(jnp.concatenate([outgoing, tail], 0), 'r', [(j, (j + step) %...]
    all_to_all x1, waiting for transfers between devices: 12.9 us -> 6.8 us  [body(): spread = lax.all_to_all(partial, PLANE, 0, 0)]
    unnamed x46 -> x54, local copies, waits for them, and re-layouts: 7.46 us -> 13.4 us
  transfers between devices with their start and end apart: 14 -> 15, of which waited for: 7 -> 11; matrix products, arithmetic and copies ran while one was open for 11% -> 10% of each run, Pallas kernels for 7% -> 6%
where the time goes in v4:
time: 238 us; the launch traced here: 236 us
  starting transfers between devices  103 us (43%)
  waiting for transfers between devices  48.9 us (21%)
  local copies, waits for them, and re-layouts  27.9 us (12%)
  between operations  15.3 us (6%)
  Pallas kernels  14.8 us (6%)
  other arithmetic  14.7 us (6%)
  blocking collectives  11.8 us (5%)
    all_to_all x1, starting transfers between devices, body(): got = lax.all_to_all(send, DP, 0, 0)  42.3 us
    ppermute x3, waiting for transfers between devices, body(): lax.ppermute(jnp.concatenate([outgoing, tail], 0), 'r', [(j, (j + step) %...  21 us
    ppermute x4, starting transfers between devices, swap_core(): return lax.ppermute(value, 'c', [(0, 1), (1, 0)])  17.5 us
    ppermute x3, starting transfers between devices, body(): lax.ppermute(jnp.concatenate([outgoing, tail], 0), 'r', [(j, (j + step) %...  13.8 us
    unnamed x54, local copies, waits for them, and re-layouts  13.4 us
    psum x1, blocking collectives, body(): square = lax.psum(jnp.sum(states * states, -1), 't') / D  11.8 us
    all_to_all x1, waiting for transfers between devices, body(): got = lax.all_to_all(send, DP, 0, 0)  11.1 us
    all_to_all x1, starting transfers between devices, body(): second = lax.all_to_all(second.astype(bf16), 'r', 0, 0)  10.9 us
  transfers between devices with their start and end apart: 15, of which 11 were waited for; matrix products, arithmetic and copies ran while one was open for 10% of the time, Pallas kernels for 6%

profile of v4, /device:TPU:1, one launch (start us, length us, event | category | flops | bytes accessed | tf_op | source)
XLA Modules:
  0.0 236.3 jit_solution(5079477909352186134)
XLA Ops:
  10.0 1.2 fusion.2
  11.2 11.8 %psum.7 = f32[2,128]{1,0:T(2,128)S(1)} all-reduce(f32[2,128]{1,0:T(2,128)S(1)} %fusion.2), channel_id=1, replica_groups=mesh['x'=4,'y'=4,'c'=2,'t'=4,'r'=4] {'t'}, use_global_device_ids=true, to_apply=%region_1.2 | all-reduce | flops 256 | bytes 2048 | tf_op jit(solution)/shard_map/psum | solution.py:251
  24.4 1.4 fusion.6
  26.6 3.3 %all-to-all-start = ((f32[4,3,896]{2,1,0:T(4,128)}), f32[4,3,896]{2,1,0:T(4,128)S(1)}, u32[]{:S(2)}, u32[]{:S(2)}) async-start(f32[4,3,896]{2,1,0:T(4,128)} %broadcast_in_dim.17), calls=%async_computation | async-start | bytes 114688 | tf_op jit(solution)/shard_map/all_to_all | solution.py:261
  30.8 3.6 %all-to-all-done = f32[4,3,896]{2,1,0:T(4,128)S(1)} async-done(((f32[4,3,896]{2,1,0:T(4,128)}), f32[4,3,896]{2,1,0:T(4,128)S(1)}, u32[]{:S(2)}, u32[]{:S(2)}) %all-to-all-start) | async-done | bytes 43040 | tf_op jit(solution)/shard_map/all_to_all | solution.py:261
  34.8 2.2 concatenate.56
  37.0 42.3 %all-to-all-start.1 = ((f32[32,2,3840]{2,1,0:T(2,128)}), f32[32,2,3840]{2,1,0:T(2,128)S(1)}, u32[]{:S(2)}, u32[]{:S(2)}) async-start(f32[32,2,3840]{2,1,0:T(2,128)} %concatenate.56), calls=%async_computation.1 | async-start | bytes 1966080 | tf_op jit(solution)/shard_map/all_to_all | solution.py:280
  79.4 0.8 broadcast_select_fusion
  80.2 2.1 collective-permute-start.1
  82.4 1.3 collective-permute-done.1.given_ref
  84.4 11.1 %all-to-all-done.1 = f32[32,2,3840]{2,1,0:T(2,128)S(1)} async-done(((f32[32,2,3840]{2,1,0:T(2,128)}), f32[32,2,3840]{2,1,0:T(2,128)S(1)}, u32[]{:S(2)}, u32[]{:S(2)}) %all-to-all-start.1) | async-done | bytes 983072 | tf_op jit(solution)/shard_map/all_to_all | solution.py:280
  95.5 0.9 copy-done.22
  96.5 2.2 collective-permute-start.2
  98.8 1.3 copy.24
  100.1 4.2 %group_math.1 = (f32[2,32,3584]{2,1,0:T(8,128)S(1)}, f32[4,28,896]{2,1,0:T(8,128)S(1)}, f32[4,1,896]{2,1,0:T(1,128)S(1)}, f32[8,128]{1,0:T(8,128)S(1)}, bf16[2,4...) custom-call(s32[2]{0:T(128)S(1)} %pad_add_fusion.index_ref, ...), custom_call_target="tpu_custom_call" | custom-call | flops 183500800 | bytes 3145728 | tf_op jit(solution)/shard_map/group_math/pallas_call | solution.py:124
  105.8 0.9 copy-done.16
  106.7 5.0 %weight_partials.1 = (bf16[16,112,896]{2,1,0:T(8,128)(2,1)S(1)}, f32[2,256,1]{2,1,0:T(8,128)S(1)}) custom-call(bf16[4,256,896]{2,1,0:T(8,128)(2,1)S(1)} %copy-done.3, bf16[4,256,896]{2,1,0:T(8,128)(2,1)} %collective-permute-done.2.other_ref, bf16[256,448]{1,0:T(8,128)(2,1)S(1)} %copy-done.13, bf16[256,448]{1,0:T(8,128)(2,1)S(1)} %copy-done.18, ...), custom_call_target="tpu_custom_call" | custom-call | flops 1644167168 | bytes 8388608 | tf_op jit(solution)/shard_map/weight_partials/pallas_call | solution.py:178
  111.8 1.7 copy-done.1
  114.2 4.5 %all-to-all-start.2 = ((bf16[16,112,896]{2,1,0:T(8,128)(2,1)}), bf16[16,112,896]{2,1,0:T(8,128)(2,1)}, u32[]{:S(2)}, u32[]{:S(2)}) async-start(bf16[16,112,896]{2,1,0:T(8,128)(2,1)} %copy-done.1), calls=%async_computation.2 | async-start | bytes 6422528 | tf_op jit(solution)/shard_map/all_to_all | solution.py:296
  120.0 1.0 dynamic-slice_bitcast_fusion.2
  121.2 1.9 collective-permute-start.3
  123.7 4.6 %collective-permute-start.4 = (f32[30,896]{1,0:T(8,128)S(1)}, f32[30,896]{1,0:T(8,128)S(1)}, u32[]{:S(2)}, u32[]{:S(2)}) collective-permute-start(f32[30,896]{1,0:T(8,128)S(1)} %get-tuple-element.71), channel_id=1, source_target_pairs={{0,2},{1,3},{2,0},{3,1},{4,6},{5,7},{6,4},{7,5},{8,10},{9,11},{10,... | collective-permute-start | bytes 322568 | tf_op jit(solution)/shard_map/ppermute | solution.py:304
  128.4 7.3 %collective-permute-start.5 = (f32[30,896]{1,0:T(8,128)S(1)}, f32[30,896]{1,0:T(8,128)S(1)}, u32[]{:S(2)}, u32[]{:S(2)}) collective-permute-start(f32[30,896]{1,0:T(8,128)S(1)} %get-tuple-element.72), channel_id=1, source_target_pairs={{0,3},{1,0},{2,1},{3,2},{4,7},{5,4},{6,5},{7,6},{8,11},{9,8},{10,9... | collective-permute-start | bytes 322568 | tf_op jit(solution)/shard_map/ppermute | solution.py:304
  135.6 4.7 %collective-permute-done.3 = f32[30,896]{1,0:T(8,128)S(1)} collective-permute-done((f32[30,896]{1,0:T(8,128)S(1)}, f32[30,896]{1,0:T(8,128)S(1)}, u32[]{:S(2)}, u32[]{:S(2)}) %collective-permute-start.3) | collective-permute-done | bytes 107552 | tf_op jit(solution)/shard_map/ppermute | solution.py:304
  140.4 7.9 %collective-permute-done.4 = f32[30,896]{1,0:T(8,128)S(1)} collective-permute-done((f32[30,896]{1,0:T(8,128)S(1)}, f32[30,896]{1,0:T(8,128)S(1)}, u32[]{:S(2)}, u32[]{:S(2)}) %collective-permute-start.4) | collective-permute-done | bytes 107552 | tf_op jit(solution)/shard_map/ppermute | solution.py:304
  148.3 8.4 %collective-permute-done.5 = f32[30,896]{1,0:T(8,128)S(1)} collective-permute-done((f32[30,896]{1,0:T(8,128)S(1)}, f32[30,896]{1,0:T(8,128)S(1)}, u32[]{:S(2)}, u32[]{:S(2)}) %collective-permute-start.5) | collective-permute-done | bytes 107552 | tf_op jit(solution)/shard_map/ppermute | solution.py:304
  157.3 0.9 slice_add_fusion
  158.2 6.8 %all-to-all-done.2 = bf16[16,112,896]{2,1,0:T(8,128)(2,1)} async-done(((bf16[16,112,896]{2,1,0:T(8,128)(2,1)}), bf16[16,112,896]{2,1,0:T(8,128)(2,1)}, u32[]{:S(2)}, u32[]{:S(2)}) %all-to-all-start.2) | async-done | bytes 3211296 | tf_op jit(solution)/shard_map/all_to_all | solution.py:296
  165.0 3.2 %reduce_sum.51 = bf16[112,896]{1,0:T(8,128)(2,1)} reduce(bf16[16,112,896]{2,1,0:T(8,128)(2,1)} %all-to-all-done.2, bf16[]{:T(256)} %constant.110.clone.1), dimensions={0}, to_apply=%region_4.5 | reduce | flops 1505280 | bytes 3411970 | tf_op jit(solution)/shard_map/reduce_sum | solution.py:319
  168.2 1.7 convert_element_type.63
  169.9 10.9 %all-to-all-start.3 = ((bf16[4,28,896]{2,1,0:T(8,128)(2,1)}), bf16[4,28,896]{2,1,0:T(8,128)(2,1)}, u32[]{:S(2)}, u32[]{:S(2)}) async-start(bf16[4,28,896]{2,1,0:T(8,128)(2,1)} %convert_element_type.63), calls=%async_computation.3 | async-start | bytes 458752 | tf_op jit(solution)/shard_map/all_to_all | solution.py:320
  180.8 1.9 copy-done.2
  182.7 0.9 copy-done.5
  183.6 0.9 copy-done.8
  184.6 0.9 copy-done.15
  185.5 5.6 %attn_grads.1 = (bf16[256,448]{1,0:T(8,128)(2,1)S(1)}, bf16[256,448]{1,0:T(8,128)(2,1)S(1)}) custom-call(s32[1]{0:T(128)} %bitcast.26.shift_ref, bf16[4,256,896]{2,1,0:T(8,128)(2,1)S(1)} %copy-done.3, bf16[4,256,896]{2,1,0:T(8,128)(2,1)} %collective-permute-done.2.other_ref, bf16[2,4,16,896]{3,2,1,0:T(8,128)(2,1)S(1)} %copy-done.15, ...), custom_call_target="tpu_custom_call" | custom-call | flops 1644167168 | bytes 8388608 | tf_op jit(solution)/shard_map/attn_grads/pallas_call | solution.py:218
  192.6 1.4 all-to-all-done.3
  194.0 1.1 convert_reduce_fusion
  195.1 1.0 broadcast_in_dim.23
  196.1 9.7 %all-to-all-start.4 = ((bf16[16,28,896]{2,1,0:T(8,128)(2,1)}), bf16[16,28,896]{2,1,0:T(8,128)(2,1)}, u32[]{:S(2)}, u32[]{:S(2)}) async-start(bf16[16,28,896]{2,1,0:T(8,128)(2,1)} %broadcast_in_dim.23), calls=%async_computation.4 | async-start | bytes 1835008 | tf_op jit(solution)/shard_map/all_to_all | solution.py:333
  205.8 0.9 constant_dynamic-slice_fusion
  207.0 5.8 %collective-permute-start.6 = (bf16[256,448]{1,0:T(8,128)(2,1)S(1)}, bf16[256,448]{1,0:T(8,128)(2,1)S(1)}, u32[]{:S(2)}, u32[]{:S(2)}) collective-permute-start(bf16[256,448]{1,0:T(8,128)(2,1)S(1)} %copy-done.20), channel_id=1, source_target_pairs={{0,16},{16,0},{1,17},{17,1},{2,18},{18,2},{3,19},{19,3},{4,20},{20... | collective-permute-start | bytes 688136 | tf_op jit(solution)/shard_map/ppermute | solution.py:38
  212.8 1.0 fusion.5
  213.9 1.1 maximum_select_fusion.1
  215.0 2.1 all-to-all-done.4
  217.1 1.3 reshape.137
  218.3 7.4 %collective-permute-start.7 = (bf16[448,896]{1,0:T(8,128)(2,1)S(1)}, bf16[448,896]{1,0:T(8,128)(2,1)S(1)}, u32[]{:S(2)}, u32[]{:S(2)}) collective-permute-start(bf16[448,896]{1,0:T(8,128)(2,1)S(1)} %reshape.137), channel_id=1, source_target_pairs={{0,16},{16,0},{1,17},{17,1},{2,18},{18,2},{3,19},{19,3},{4,20},{20... | collective-permute-start | bytes 2408456 | tf_op jit(solution)/shard_map/ppermute | solution.py:38
  227.6 1.8 maximum_select_fusion
  (90 shorter events, 14.9 us)
Async XLA Ops:
  7.2 1.4 copy-start
  7.2 89.3 %all-gather.4.cloned.1.call-start = ((), (), s32[]{:S(2)}) async-start(), calls=%async_computation.5 | async-start | bytes 2293760 | tf_op jit(solution)/shard_map/all_gather | solution.py:238
  8.6 17.3 %collective-permute-start = (bf16[112,896]{1,0:T(8,128)(2,1)S(1)}, bf16[112,896]{1,0:T(8,128)(2,1)S(1)}, u32[]{:S(2)}, u32[]{:S(2)}) collective-permute-start(bf16[112,896]{1,0:T(8,128)(2,1)S(1)} %constant_dynamic-slice_fusion.1), channel_id=1, source_target_pairs={{0,0},{1,1},{2,2},{3,3},{129,128},{130,129},{131,130},{128,131},{2... | collective-permute-start | bytes 602120 | tf_op jit(solution)/shard_map/ppermute | solution.py:241
  25.9 8.6 %copy-start.24 = (bf16[112,896]{1,0:T(8,128)(2,1)}, bf16[112,896]{1,0:T(8,128)(2,1)S(1)}, u32[]{:S(2)}) copy-start(bf16[112,896]{1,0:T(8,128)(2,1)S(1)} %collective-permute-done) | copy-start | bytes 602116
  26.6 7.8 %all-to-all-start = ((f32[4,3,896]{2,1,0:T(4,128)}), f32[4,3,896]{2,1,0:T(4,128)S(1)}, u32[]{:S(2)}, u32[]{:S(2)}) async-start(f32[4,3,896]{2,1,0:T(4,128)} %broadcast_in_dim.17), calls=%async_computation | async-start | bytes 114688 | tf_op jit(solution)/shard_map/all_to_all | solution.py:261
  34.8 44.6 %copy-start.23 = (bf16[1,2,128,896]{3,2,1,0:T(8,128)(2,1)S(1)}, bf16[1,2,128,896]{3,2,1,0:T(8,128)(2,1)}, u32[]{:S(2)}) copy-start(bf16[1,2,128,896]{3,2,1,0:T(8,128)(2,1)} %param.7) | copy-start | bytes 1376260
  37.0 58.5 %all-to-all-start.1 = ((f32[32,2,3840]{2,1,0:T(2,128)}), f32[32,2,3840]{2,1,0:T(2,128)S(1)}, u32[]{:S(2)}, u32[]{:S(2)}) async-start(f32[32,2,3840]{2,1,0:T(2,128)} %concatenate.56), calls=%async_computation.1 | async-start | bytes 1966080 | tf_op jit(solution)/shard_map/all_to_all | solution.py:280
  79.3 101.4 %all-gather.6.cloned.1.call-start = ((), (), s32[]{:S(2)}) async-start(), calls=%async_computation.6 | async-start | bytes 3411968 | tf_op jit(solution)/shard_map/all_gather | solution.py:284
  80.2 3.4 %collective-permute-start.1 = (bf16[256,448]{1,0:T(8,128)(2,1)S(1)}, bf16[256,448]{1,0:T(8,128)(2,1)S(1)}, u32[]{:S(2)}, u32[]{:S(2)}) collective-permute-start(bf16[256,448]{1,0:T(8,128)(2,1)S(1)} %get-tuple-element.69), channel_id=1, source_target_pairs={{0,16},{16,0},{1,17},{17,1},{2,18},{18,2},{3,19},{19,3},{4,20},{20... | collective-permute-start | bytes 688136 | tf_op jit(solution)/shard_map/ppermute | solution.py:38
  83.7 0.7 copy-start.17
  95.5 0.9 copy-start.22
  96.5 10.2 %copy-start.3 = (bf16[4,256,896]{2,1,0:T(8,128)(2,1)S(1)}, bf16[4,256,896]{2,1,0:T(8,128)(2,1)}, u32[]{:S(2)}) copy-start(bf16[4,256,896]{2,1,0:T(8,128)(2,1)} %all-gather.4.cloned.1.call-done.own_ref) | copy-start | bytes 5505028
  96.5 10.2 %collective-permute-start.2 = (bf16[4,256,896]{2,1,0:T(8,128)(2,1)}, bf16[4,256,896]{2,1,0:T(8,128)(2,1)}, u32[]{:S(2)}, u32[]{:S(2)}) collective-permute-start(bf16[4,256,896]{2,1,0:T(8,128)(2,1)} %all-gather.4.cloned.1.call-done.own_ref), channel_id=1, source_target_pairs={{0,16},{16,0},{1,17},{17,1},{2,18},{18,2},{3,19},{19,3},{4,20},{20... | collective-permute-start | bytes 5505032 | tf_op jit(solution)/shard_map/ppermute | solution.py:38
  98.7 8.0 %copy-start.13 = (bf16[256,448]{1,0:T(8,128)(2,1)S(1)}, bf16[256,448]{1,0:T(8,128)(2,1)}, u32[]{:S(2)}) copy-start(bf16[256,448]{1,0:T(8,128)(2,1)} %get-tuple-element.68.keep_ref) | copy-start | bytes 688132
  98.7 8.0 %copy-start.18 = (bf16[256,448]{1,0:T(8,128)(2,1)S(1)}, bf16[256,448]{1,0:T(8,128)(2,1)}, u32[]{:S(2)}) copy-start(bf16[256,448]{1,0:T(8,128)(2,1)} %copy-done.17) | copy-start | bytes 688132
  104.3 0.7 copy-start.4
  105.0 0.8 copy-start.10
  105.8 0.9 copy-start.16
  106.7 5.1 %copy-start.14 = (bf16[2,4,16,896]{3,2,1,0:T(8,128)(2,1)}, bf16[2,4,16,896]{3,2,1,0:T(8,128)(2,1)S(1)}, u32[]{:S(2)}) copy-start(bf16[2,4,16,896]{3,2,1,0:T(8,128)(2,1)S(1)} %get-tuple-element.39.pieces_ref) | copy-start | bytes 688132
  111.8 1.7 copy-start.1
  113.5 0.7 copy-start.7
  114.2 50.8 %all-to-all-start.2 = ((bf16[16,112,896]{2,1,0:T(8,128)(2,1)}), bf16[16,112,896]{2,1,0:T(8,128)(2,1)}, u32[]{:S(2)}, u32[]{:S(2)}) async-start(bf16[16,112,896]{2,1,0:T(8,128)(2,1)} %copy-done.1), calls=%async_computation.2 | async-start | bytes 6422528 | tf_op jit(solution)/shard_map/all_to_all | solution.py:296
  121.2 19.2 %collective-permute-start.3 = (f32[30,896]{1,0:T(8,128)S(1)}, f32[30,896]{1,0:T(8,128)S(1)}, u32[]{:S(2)}, u32[]{:S(2)}) collective-permute-start(f32[30,896]{1,0:T(8,128)S(1)} %get-tuple-element.70), channel_id=1, source_target_pairs={{0,1},{1,2},{2,3},{3,0},{4,5},{5,6},{6,7},{7,4},{8,9},{9,10},{10,1... | collective-permute-start | bytes 322568 | tf_op jit(solution)/shard_map/ppermute | solution.py:304
  123.7 24.5 %collective-permute-start.4 = (f32[30,896]{1,0:T(8,128)S(1)}, f32[30,896]{1,0:T(8,128)S(1)}, u32[]{:S(2)}, u32[]{:S(2)}) collective-permute-start(f32[30,896]{1,0:T(8,128)S(1)} %get-tuple-element.71), channel_id=1, source_target_pairs={{0,2},{1,3},{2,0},{3,1},{4,6},{5,7},{6,4},{7,5},{8,10},{9,11},{10,... | collective-permute-start | bytes 322568 | tf_op jit(solution)/shard_map/ppermute | solution.py:304
  128.4 28.3 %collective-permute-start.5 = (f32[30,896]{1,0:T(8,128)S(1)}, f32[30,896]{1,0:T(8,128)S(1)}, u32[]{:S(2)}, u32[]{:S(2)}) collective-permute-start(f32[30,896]{1,0:T(8,128)S(1)} %get-tuple-element.72), channel_id=1, source_target_pairs={{0,3},{1,0},{2,1},{3,2},{4,7},{5,4},{6,5},{7,6},{8,11},{9,8},{10,9... | collective-permute-start | bytes 322568 | tf_op jit(solution)/shard_map/ppermute | solution.py:304
  169.9 24.1 %all-to-all-start.3 = ((bf16[4,28,896]{2,1,0:T(8,128)(2,1)}), bf16[4,28,896]{2,1,0:T(8,128)(2,1)}, u32[]{:S(2)}, u32[]{:S(2)}) async-start(bf16[4,28,896]{2,1,0:T(8,128)(2,1)} %convert_element_type.63), calls=%async_computation.3 | async-start | bytes 458752 | tf_op jit(solution)/shard_map/all_to_all | solution.py:320
  180.8 1.9 copy-start.2
  182.7 0.9 copy-start.5
  183.6 0.9 copy-start.8
  184.6 0.9 copy-start.15
  191.1 0.7 copy-start.11
  191.9 0.7 copy-start.19
  192.6 14.2 %copy-start.6 = (f32[2,256,1]{2,1,0:T(8,128)S(1)}, f32[2,256,1]{2,1,0:T(8,128)}, u32[]{:S(2)}) copy-start(f32[2,256,1]{2,1,0:T(8,128)} %copy-done.4) | copy-start | bytes 6148
  192.6 14.3 %copy-start.9 = (f32[2,256,1]{2,1,0:T(8,128)S(1)}, f32[2,256,1]{2,1,0:T(8,128)}, u32[]{:S(2)}) copy-start(f32[2,256,1]{2,1,0:T(8,128)} %copy-done.7) | copy-start | bytes 6148
  194.0 13.0 %copy-start.20 = (bf16[256,448]{1,0:T(8,128)(2,1)S(1)}, bf16[256,448]{1,0:T(8,128)(2,1)}, u32[]{:S(2)}) copy-start(bf16[256,448]{1,0:T(8,128)(2,1)} %copy-done.19) | copy-start | bytes 688132
  194.0 18.8 %copy-start.21 = (bf16[1,2,128,896]{3,2,1,0:T(8,128)(2,1)S(1)}, bf16[1,2,128,896]{3,2,1,0:T(8,128)(2,1)}, u32[]{:S(2)}) copy-start(bf16[1,2,128,896]{3,2,1,0:T(8,128)(2,1)} %param.6) | copy-start | bytes 1376260
  195.0 18.9 %copy-start.12 = (bf16[256,448]{1,0:T(8,128)(2,1)S(1)}, bf16[256,448]{1,0:T(8,128)(2,1)}, u32[]{:S(2)}) copy-start(bf16[256,448]{1,0:T(8,128)(2,1)} %copy-done.11) | copy-start | bytes 688132
  196.1 21.0 %all-to-all-start.4 = ((bf16[16,28,896]{2,1,0:T(8,128)(2,1)}), bf16[16,28,896]{2,1,0:T(8,128)(2,1)}, u32[]{:S(2)}, u32[]{:S(2)}) async-start(bf16[16,28,896]{2,1,0:T(8,128)(2,1)} %broadcast_in_dim.23), calls=%async_computation.4 | async-start | bytes 1835008 | tf_op jit(solution)/shard_map/all_to_all | solution.py:333
  207.0 18.7 %copy-start.25 = (f32[2,896]{1,0:T(2,128)S(1)}, f32[2,896]{1,0:T(2,128)}, u32[]{:S(2)}) copy-start(f32[2,896]{1,0:T(2,128)} %add_bitcast_fusion) | copy-start | bytes 21508
  207.0 6.9 %collective-permute-start.6 = (bf16[256,448]{1,0:T(8,128)(2,1)S(1)}, bf16[256,448]{1,0:T(8,128)(2,1)S(1)}, u32[]{:S(2)}, u32[]{:S(2)}) collective-permute-start(bf16[256,448]{1,0:T(8,128)(2,1)S(1)} %copy-done.20), channel_id=1, source_target_pairs={{0,16},{16,0},{1,17},{17,1},{2,18},{18,2},{3,19},{19,3},{4,20},{20... | collective-permute-start | bytes 688136 | tf_op jit(solution)/shard_map/ppermute | solution.py:38
  218.3 9.3 %collective-permute-start.7 = (bf16[448,896]{1,0:T(8,128)(2,1)S(1)}, bf16[448,896]{1,0:T(8,128)(2,1)S(1)}, u32[]{:S(2)}, u32[]{:S(2)}) collective-permute-start(bf16[448,896]{1,0:T(8,128)(2,1)S(1)} %reshape.137), channel_id=1, source_target_pairs={{0,16},{16,0},{1,17},{17,1},{2,18},{18,2},{3,19},{19,3},{4,20},{20... | collective-permute-start | bytes 2408456 | tf_op jit(solution)/shard_map/ppermute | solution.py:38
Sparse Core Ops, SparseCore 0:
  10.1 56.4 all-gather.3
  96.6 79.1 all-gather.5

commit v5 on v4

--- a/solution.py
+++ b/solution.py
@@ -27,11 +27,13 @@
 PIECES = 16
 GROUP = NX * NY * NC
 
-AT_RMS = D
-AT_U = D + SEQ
+LANES = 1024
+ROWS = 8
+LAST = D - 3 * LANES
+AT_RMS = LAST
+AT_U = AT_RMS + SEQ
 AT_LEN = AT_U + SLICE
 AT_POS = AT_LEN + 1
-WIDTH = D + 2 * SEQ
 
 
 def swap_core(value):
@@ -50,6 +52,74 @@
     return lax.dot_general(
         left, right, dims, precision=lax.Precision.HIGHEST, preferred_element_type=f32
     )
+
+
+def front_kernel(length_ref, target_ref, state_ref, attn_ref, send_ref, base_ref):
+    square = jnp.zeros((TOK, FEAT), f32)
+    for block in range(NT):
+        part = state_ref[block].astype(f32)
+        square = square + part * part
+    square = jnp.sum(square, -1, keepdims=True)
+    inv_rms = lax.rsqrt(square * (1.0 / D) + epsilon)
+    token = lax.broadcasted_iota(jnp.int32, (SEQ, SEQ), 0)
+    lane = lax.broadcasted_iota(jnp.int32, (SEQ, SEQ), 1)
+    position = lax.broadcasted_iota(jnp.int32, (SEQ, 1), 0)
+    pools = []
+    for side in range(2):
+        here = slice(side * SEQ, (side + 1) * SEQ)
+        length = length_ref[side]
+        count = jnp.full((1, 1), length, jnp.int32).astype(f32)
+        rms = inv_rms[here]
+        weight = jnp.where(position < length, rms, 0.0) / count
+        pooled = [
+            jnp.sum(weight * state_ref[block, here, :].astype(f32), 0, keepdims=True)
+            for block in range(NT)
+        ]
+        rms_row = jnp.sum(jnp.where(token == lane, rms, 0.0), 0, keepdims=True)
+        row = jnp.concatenate(
+            pooled + [rms_row, jnp.zeros((1, LANES - AT_U), f32)], 1
+        )
+        for part in range(4):
+            base_ref[4 * side + part : 4 * side + part + 1, :] = row[
+                :, part * LANES : (part + 1) * LANES
+            ]
+        pools.append(
+            jnp.sum(weight * attn_ref[here, :].astype(f32), 0, keepdims=True)
+        )
+    base = base_ref[...]
+    fixed = base[:, AT_U : AT_U + 128]
+    row_index = lax.broadcasted_iota(jnp.int32, (ROWS, 128), 0)
+    lane_index = lax.broadcasted_iota(jnp.int32, (ROWS, 128), 1)
+    both = jnp.concatenate([pools[0]] * 4 + [pools[1]] * 4, 0)
+    first_side = row_index < 4
+    count = jnp.where(first_side, length_ref[0], length_ref[1]).astype(f32)
+    target = jnp.full((ROWS, 128), target_ref[0], jnp.int32).astype(f32)
+    last_row = (row_index == 3) | (row_index == 7)
+    for device in range(GROUP):
+        at = (device % NC) * HALF + (device // NC) * SLICE
+        moved = both if at == 0 else pltpu.roll(both, FEAT - at, 1)
+        extra = jnp.where(lane_index < SLICE, moved[:, :128], 0.0)
+        extra = jnp.where(lane_index == SLICE, count, extra)
+        extra = jnp.where(lane_index == SLICE + 1, target, extra)
+        send_ref[device] = base
+        send_ref[device, :, AT_U : AT_U + 128] = jnp.where(last_row, extra, fixed)
+
+
+def front(lengths, target, state_all, attn):
+    spec = pl.BlockSpec(memory_space=pltpu.VMEM)
+    scalars = pl.BlockSpec(memory_space=pltpu.SMEM)
+    return pl.pallas_call(
+        front_kernel,
+        out_shape=jax.ShapeDtypeStruct((GROUP, ROWS, LANES), f32),
+        in_specs=[scalars, scalars, spec, spec],
+        out_specs=spec,
+        scratch_shapes=[pltpu.VMEM((ROWS, LANES), f32)],
+        compiler_params=pltpu.CompilerParams(vmem_limit_bytes=16 * 1024 * 1024),
+        cost_estimate=pl.CostEstimate(
+            flops=8 * TOK * D, bytes_accessed=4 * 1024 * 1024, transcendentals=TOK
+        ),
+        name="front",
+    )(lengths, target, state_all, attn)
 
 
 def group_kernel(
@@ -59,14 +129,15 @@
     gain = gain_ref[...]
     raw, unit, inv_norm = [], [], []
     for side in range(2):
-        raw.append(got_ref[side, :, :D])
+        parts = [got_ref[4 * side + part] for part in range(4)]
+        raw.append(jnp.concatenate(parts, 1)[:, :D])
         embeds = raw[side] * gain
         square = jnp.sum(embeds * embeds, -1, keepdims=True)
         inv_norm.append(lax.rsqrt(square + epsilon))
         unit.append(embeds * inv_norm[side])
     logits = logit_scale * dot_exact(unit[0], unit[1], contract_last)
     log_total = jnp.log(jnp.sum(jnp.exp(logits), -1, keepdims=True))
-    target = got_ref[0, :, AT_POS : AT_POS + 1]
+    target = got_ref[3, :, AT_POS : AT_POS + 1]
     passage = lax.broadcasted_iota(jnp.int32, (GROUP, GROUP), 1).astype(f32)
     one_hot = jnp.where(passage == target, 1.0, 0.0)
     chosen = jnp.sum(logits * one_hot, -1, keepdims=True)
@@ -86,7 +157,7 @@
         gain_sum = gain_sum + jnp.sum(pooled_grad * raw[side], 0, keepdims=True)
         scaled = pooled_grad * gain
         scaled_ref[side] = scaled
-        first = first + dot_exact(got_ref[side, :, AT_U:AT_LEN], scaled, contract_first)
+        first = first + dot_exact(got_ref[4 * side + 3, :, AT_U:AT_LEN], scaled, contract_first)
     for block in range(NR):
         columns = slice(block * COLS, (block + 1) * COLS)
         first_ref[block] = first[:, columns]
@@ -104,7 +175,7 @@
             high = row.astype(bf16).astype(f32)
             mid = (row - high).astype(bf16).astype(f32)
             parts += [high, mid, row - high - mid]
-            rest = jnp.where(chosen_row, got_ref[side, :, AT_RMS:WIDTH], 0.0)
+            rest = jnp.where(chosen_row, got_ref[4 * side + 3, :, AT_RMS:], 0.0)
             rest = jnp.sum(rest, 0, keepdims=True)
             rms_row = rest[:, :SEQ]
             count = rest[:, AT_LEN - AT_RMS : AT_LEN - AT_RMS + 1]
@@ -234,8 +305,9 @@
     dp_index = (ix * NY + iy) * NC + ic
 
     state = hidden_state.reshape(TOK, FEAT)
+    states = state.astype(f32).reshape(2, SEQ, FEAT)
     attn = attn_out.reshape(TOK, FEAT)
-    state_all = lax.all_gather(state, "t")
+    state_all = lax.all_to_all(jnp.broadcast_to(state[None], (NT, TOK, FEAT)), "t", 0, 0)
     w_start = (ic * NY + iy) * W_ROWS
     w_mine = lax.dynamic_slice(o_weight, (w_start, 0), (W_ROWS, COLS))
     w_moved = lax.ppermute(
@@ -246,42 +318,25 @@
     attn_keep = jnp.where(ic == 0, attn[:, :HALF], attn[:, HALF:])
     attn_give = jnp.where(ic == 0, attn[:, HALF:], attn[:, :HALF])
     attn_other = swap_core(attn_give)
-
-    states = state.astype(f32).reshape(2, SEQ, FEAT)
-    square = lax.psum(jnp.sum(states * states, -1), "t") / D
-    inv_rms = lax.rsqrt(square + epsilon)
-    token_count = lengths.reshape(2).astype(f32)
-    valid = (jnp.arange(SEQ, dtype=jnp.int32)[None, :] < lengths.reshape(2)[:, None]).astype(f32)
-    pool_weight = valid * inv_rms / token_count[:, None]
-    pooled = jnp.sum(pool_weight[..., None] * states, 1)
-    attn_pool = jnp.sum(pool_weight[..., None] * attn.astype(f32).reshape(2, SEQ, FEAT), 1)
-
-    near = jnp.concatenate([pooled, norm_gain[None]], 0)
-    near, w_moved = lax.optimization_barrier((near, w_moved))
-    near = lax.all_to_all(jnp.broadcast_to(near[None], (NT, 3, FEAT)), "t", 0, 0)
-    pooled_row = near[:, :2].transpose(1, 0, 2).reshape(2, D)
-    gain = near[:, 2].reshape(1, D)
-
-    u_parts = attn_pool.reshape(2, NC, NX * NY, SLICE).transpose(2, 1, 0, 3)
-    u_parts = u_parts.reshape(GROUP, 2, SLICE)
-    extra = jnp.stack(
-        [token_count, jnp.broadcast_to(positive.astype(f32), (2,))], -1
-    )
-    row = jnp.concatenate([pooled_row, inv_rms], -1)
-    send = jnp.concatenate(
+    gains = [norm_gain.reshape(1, FEAT)]
+    for step in range(1, NT):
+        gains.append(
+            lax.ppermute(gains[0], "t", [(j, (j + step) % NT) for j in range(NT)])
+        )
+    gains = jnp.stack(gains)
+    gain = jnp.concatenate(
         [
-            jnp.broadcast_to(row[None], (GROUP, 2, D + SEQ)),
-            u_parts,
-            jnp.broadcast_to(extra[None], (GROUP, 2, 2)),
-            jnp.zeros((GROUP, 2, WIDTH - AT_POS - 1), f32),
+            lax.dynamic_index_in_dim(gains, (it - source) % NT, 0, keepdims=False)
+            for source in range(NT)
         ],
-        -1,
-    )
+        1,
+    )
+    state_all, attn_other, gain = lax.optimization_barrier((state_all, attn_other, gain))
+
+    send = front(lengths.reshape(2), positive, state_all, attn)
+    send, w_moved = lax.optimization_barrier((send, w_moved))
+    w_all = lax.all_gather(w_moved, PLANE).reshape(NX, HALF, COLS)
     got = lax.all_to_all(send, DP, 0, 0)
-    got, state_all, w_moved, attn_other = lax.optimization_barrier(
-        (got, state_all, w_moved, attn_other)
-    )
-    w_all = lax.all_gather(w_moved, PLANE).reshape(NX, HALF, COLS)
 
     other_index = dp_index + 1 - 2 * ic
     state_other = swap_core(state_all)
@@ -315,10 +370,6 @@
             tails, (ir - source) % NR, 0, keepdims=False
         )
 
-    spread, first_sum, totals = lax.optimization_barrier((spread, first_sum, totals))
-    second = jnp.sum(spread.astype(f32), 0).reshape(NR, SLICE, COLS)
-    second = lax.all_to_all(second.astype(bf16), "r", 0, 0)
-
     row_here = lax.dynamic_slice(scaled, (0, dp_index, it * FEAT), (2, 1, FEAT))
     state_grad = first_col[0].reshape(2, SEQ, 1) * row_here - states * coef[0].reshape(2, SEQ, 1)
     grad_hidden = state_grad.astype(bf16).reshape(1, 2, SEQ, FEAT)
@@ -326,18 +377,20 @@
         ir.reshape(1), state_all, state_other, pieces, w_all, coef, first_col
     )
 
-    second, keep, give = lax.optimization_barrier((second, keep, give))
+    arrived = swap_core(give)
+    grad_attn = jnp.where(
+        ic == 0, jnp.concatenate([keep, arrived], 1), jnp.concatenate([arrived, keep], 1)
+    ).reshape(1, 2, SEQ, FEAT)
+    spread, first_sum, totals, grad_attn, grad_hidden = lax.optimization_barrier(
+        (spread, first_sum, totals, grad_attn, grad_hidden)
+    )
+    second = jnp.sum(spread.astype(f32), 0).reshape(NR, SLICE, COLS)
+    second = lax.all_to_all(second.astype(bf16), "r", 0, 0)
+
     second_sum = jnp.sum(second.astype(f32), 0)
     total = first_sum - second_sum
     done = jnp.broadcast_to(total.astype(bf16)[None], (NX * NY, SLICE, COLS))
     half = lax.all_to_all(done, PLANE, 0, 0).reshape(HALF, COLS)
-    arrived = swap_core(give)
-    grad_attn = jnp.where(
-        ic == 0, jnp.concatenate([keep, arrived], 1), jnp.concatenate([arrived, keep], 1)
-    ).reshape(1, 2, SEQ, FEAT)
-    half, grad_attn, grad_hidden, totals = lax.optimization_barrier(
-        (half, grad_attn, grad_hidden, totals)
-    )
     half_other = swap_core(half)
     grad_weight = jnp.where(
         ic == 0,

time: 238 us -> 268 us (1.13)
  blocking collectives: 11.8 us -> 44 us
  waiting for transfers between devices: 48.9 us -> 61.8 us
  starting transfers between devices: 103 us -> 92.4 us
  other arithmetic: 14.7 us -> 9.99 us
    all_to_all x0 -> x2, blocking collectives: none -> 44 us  [the longest x1 28.9 us: body(): second = lax.all_to_all(second.astype(bf16), 'r', 0, 0)]
    ppermute x0 -> x3, waiting for transfers between devices: none -> 18.9 us  [body(): lax.ppermute(gains[0], 't', [(j, (j + step) % NT) for j in range(NT)])]
    all_to_all x1, starting transfers between devices: 42.3 us -> 24.5 us  [body(): got = lax.all_to_all(send, DP, 0, 0)]
    all_to_all x3 -> x1, starting transfers between devices: 23.9 us -> 6.57 us  [body(): lax.all_to_all(jnp.broadcast_to(state[None], (NT, TOK, FEAT)), 't', 0, 0)]
    psum x1 -> x0, blocking collectives: 11.8 us -> none  [body(): square = lax.psum(jnp.sum(states * states, -1), 't') / D]
    all_gather x1, waiting for transfers between devices: 0.01 us -> 11.6 us  [body(): w_all = lax.all_gather(w_moved, PLANE).reshape(NX, HALF, COLS)]
    ppermute x3, starting transfers between devices: 13.8 us -> 23.5 us  [body(): lax.ppermute(jnp.concatenate([outgoing, tail], 0), 'r', [(j, (j + step) %...]
    ppermute x0 -> x3, starting transfers between devices: none -> 9.55 us  [body(): lax.ppermute(gains[0], 't', [(j, (j + step) % NT) for j in range(NT)])]
  transfers between devices with their start and end apart: 15 -> 15, of which waited for: 11 -> 8; matrix products, arithmetic and copies ran while one was open for 10% -> 6% of each run, Pallas kernels for 6% -> 6%
where the time goes in v5:
time: 268 us; the launch traced here: 265 us
  starting transfers between devices  92.4 us (34%)
  waiting for transfers between devices  61.8 us (23%)
  blocking collectives  44 us (16%)
  local copies, waits for them, and re-layouts  25.3 us (9%)
  Pallas kernels  16.6 us (6%)
  between operations  15.3 us (6%)
  other arithmetic  9.99 us (4%)
    all_to_all x1, blocking collectives, body(): second = lax.all_to_all(second.astype(bf16), 'r', 0, 0)  28.9 us
    all_to_all x1, starting transfers between devices, body(): got = lax.all_to_all(send, DP, 0, 0)  24.5 us
    ppermute x3, starting transfers between devices, body(): lax.ppermute(jnp.concatenate([outgoing, tail], 0), 'r', [(j, (j + step) %...  23.5 us
    ppermute x4, starting transfers between devices, swap_core(): return lax.ppermute(value, 'c', [(0, 1), (1, 0)])  20.4 us
    ppermute x3, waiting for transfers between devices, body(): lax.ppermute(gains[0], 't', [(j, (j + step) % NT) for j in range(NT)])  18.9 us
    all_to_all x1, waiting for transfers between devices, body(): got = lax.all_to_all(send, DP, 0, 0)  16.9 us
    all_to_all x1, blocking collectives, body(): half = lax.all_to_all(done, PLANE, 0, 0).reshape(HALF, COLS)  15.1 us
    ppermute x3, waiting for transfers between devices, body(): lax.ppermute(jnp.concatenate([outgoing, tail], 0), 'r', [(j, (j + step) %...  13.3 us
  transfers between devices with their start and end apart: 15, of which 8 were waited for; matrix products, arithmetic and copies ran while one was open for 6% of the time, Pallas kernels for 6%

profile of v5, /device:TPU:1, one launch (start us, length us, event | category | flops | bytes accessed | tf_op | source)
XLA Modules:
  0.0 265.3 jit_solution(16103470376492681488)
XLA Ops:
  7.2 2.5 broadcast_in_dim.21
  9.7 6.6 %all-to-all-start = ((bf16[4,256,896]{2,1,0:T(8,128)(2,1)}), bf16[4,256,896]{2,1,0:T(8,128)(2,1)S(1)}, u32[]{:S(2)}, u32[]{:S(2)}) async-start(bf16[4,256,896]{2,1,0:T(8,128)(2,1)} %broadcast_in_dim.21), calls=%async_computation | async-start | bytes 3670016 | tf_op jit(solution)/shard_map/all_to_all | solution.py:310
  16.3 5.2 %collective-permute-start.3 = (f32[1,896]{1,0:T(1,128)S(1)}, f32[1,896]{1,0:T(1,128)S(1)}, u32[]{:S(2)}, u32[]{:S(2)}) collective-permute-start(f32[1,896]{1,0:T(1,128)S(1)} %reshape.103), channel_id=1, source_target_pairs={{0,12},{4,0},{8,4},{12,8},{1,13},{5,1},{9,5},{13,9},{2,14},{6,2},{... | collective-permute-start | bytes 10760 | tf_op jit(solution)/shard_map/ppermute | solution.py:324
  21.5 1.9 collective-permute-start.2
  23.4 2.5 collective-permute-start.1
  26.6 3.4 %collective-permute-start.5 = (bf16[112,896]{1,0:T(8,128)(2,1)}, bf16[112,896]{1,0:T(8,128)(2,1)}, u32[]{:S(2)}, u32[]{:S(2)}) collective-permute-start(bf16[112,896]{1,0:T(8,128)(2,1)} %constant_dynamic-slice_fusion.2), channel_id=1, source_target_pairs={{0,0},{1,1},{2,2},{3,3},{129,128},{130,129},{131,130},{128,131},{2... | collective-permute-start | bytes 602120 | tf_op jit(solution)/shard_map/ppermute | solution.py:313
  30.0 2.0 broadcast_select_fusion
  32.0 7.0 %collective-permute-start = (bf16[256,448]{1,0:T(8,128)(2,1)}, bf16[256,448]{1,0:T(8,128)(2,1)}, u32[]{:S(2)}, u32[]{:S(2)}) collective-permute-start(bf16[256,448]{1,0:T(8,128)(2,1)} %get-tuple-element.55), channel_id=1, source_target_pairs={{0,16},{16,0},{1,17},{17,1},{2,18},{18,2},{3,19},{19,3},{4,20},{20... | collective-permute-start | bytes 688136 | tf_op jit(solution)/shard_map/ppermute | solution.py:40
  39.7 2.7 %collective-permute-done.3 = f32[1,896]{1,0:T(1,128)S(1)} collective-permute-done((f32[1,896]{1,0:T(1,128)S(1)}, f32[1,896]{1,0:T(1,128)S(1)}, u32[]{:S(2)}, u32[]{:S(2)}) %collective-permute-start.3) | collective-permute-done | bytes 3616 | tf_op jit(solution)/shard_map/ppermute | solution.py:324
  42.4 16.3 %collective-permute-done.2 = f32[1,896]{1,0:T(1,128)S(1)} collective-permute-done((f32[1,896]{1,0:T(1,128)S(1)}, f32[1,896]{1,0:T(1,128)S(1)}, u32[]{:S(2)}, u32[]{:S(2)}) %collective-permute-start.2) | collective-permute-done | bytes 3616 | tf_op jit(solution)/shard_map/ppermute | solution.py:324
  58.8 1.0 copy-done.4
  59.8 1.7 front.1
  61.5 1.0 copy-done.1
  62.5 3.4 %collective-permute-start.4 = (bf16[4,256,896]{2,1,0:T(8,128)(2,1)S(1)}, bf16[4,256,896]{2,1,0:T(8,128)(2,1)}, u32[]{:S(2)}, u32[]{:S(2)}) collective-permute-start(bf16[4,256,896]{2,1,0:T(8,128)(2,1)S(1)} %all-to-all-done.state_ref.own_ref), channel_id=1, source_target_pairs={{0,16},{16,0},{1,17},{17,1},{2,18},{18,2},{3,19},{19,3},{4,20},{20... | collective-permute-start | bytes 5505032 | tf_op jit(solution)/shard_map/ppermute | solution.py:40
  65.9 24.5 %all-to-all-start.1 = ((f32[32,8,1024]{2,1,0:T(8,128)}), f32[32,8,1024]{2,1,0:T(8,128)}, u32[]{:S(2)}, u32[]{:S(2)}) async-start(f32[32,8,1024]{2,1,0:T(8,128)} %copy-done.1), calls=%async_computation.1 | async-start | bytes 2097152 | tf_op jit(solution)/shard_map/all_to_all | solution.py:339
  90.5 16.9 %all-to-all-done.1 = f32[32,8,1024]{2,1,0:T(8,128)} async-done(((f32[32,8,1024]{2,1,0:T(8,128)}), f32[32,8,1024]{2,1,0:T(8,128)}, u32[]{:S(2)}, u32[]{:S(2)}) %all-to-all-start.1) | async-done | bytes 1048608 | tf_op jit(solution)/shard_map/all_to_all | solution.py:339
  107.4 1.9 copy.17
  109.3 4.2 %group_math.1 = (f32[2,32,3584]{2,1,0:T(8,128)S(1)}, f32[4,28,896]{2,1,0:T(8,128)S(1)}, f32[4,1,896]{2,1,0:T(1,128)S(1)}, f32[8,128]{1,0:T(8,128)S(1)}, bf16[2,4...) custom-call(s32[2]{0:T(128)S(1)} %pad_add_fusion.index_ref, ...), custom_call_target="tpu_custom_call" | custom-call | flops 183500800 | bytes 3145728 | tf_op jit(solution)/shard_map/group_math/pallas_call | solution.py:195
  114.2 0.8 copy-done.9
  114.9 0.9 copy-done.14
  115.9 5.0 %weight_partials.1 = (bf16[16,112,896]{2,1,0:T(8,128)(2,1)S(1)}, f32[2,256,1]{2,1,0:T(8,128)S(1)}) custom-call(bf16[4,256,896]{2,1,0:T(8,128)(2,1)S(1)} %all-to-all-done.state_ref.own_ref, bf16[4,256,896]{2,1,0:T(8,128)(2,1)} %collective-permute-done.4.other_ref, bf16[256,448]{1,0:T(8,128)(2,1)S(1)} %copy-done.10, ...), custom_call_target="tpu_custom_call" | custom-call | flops 1644167168 | bytes 8388608 | tf_op jit(solution)/shard_map/weight_partials/pallas_call | solution.py:249
  120.9 1.7 copy-done.2
  123.3 4.5 %all-to-all-start.2 = ((bf16[16,112,896]{2,1,0:T(8,128)(2,1)}), bf16[16,112,896]{2,1,0:T(8,128)(2,1)}, u32[]{:S(2)}, u32[]{:S(2)}) async-start(bf16[16,112,896]{2,1,0:T(8,128)(2,1)} %copy-done.2), calls=%async_computation.2 | async-start | bytes 6422528 | tf_op jit(solution)/shard_map/all_to_all | solution.py:351
  128.5 0.9 constant_dynamic-slice_fusion
  130.8 1.0 slice_reduce_fusion.1
  131.8 1.0 dynamic-slice_bitcast_fusion.2
  132.9 9.5 %collective-permute-start.6 = (f32[30,896]{1,0:T(8,128)S(1)}, f32[30,896]{1,0:T(8,128)S(1)}, u32[]{:S(2)}, u32[]{:S(2)}) collective-permute-start(f32[30,896]{1,0:T(8,128)S(1)} %get-tuple-element.60), channel_id=1, source_target_pairs={{0,1},{1,2},{2,3},{3,0},{4,5},{5,6},{6,7},{7,4},{8,9},{9,10},{10,1... | collective-permute-start | bytes 322568 | tf_op jit(solution)/shard_map/ppermute | solution.py:359
  142.5 8.8 %collective-permute-start.7 = (f32[30,896]{1,0:T(8,128)S(1)}, f32[30,896]{1,0:T(8,128)S(1)}, u32[]{:S(2)}, u32[]{:S(2)}) collective-permute-start(f32[30,896]{1,0:T(8,128)S(1)} %get-tuple-element.61), channel_id=1, source_target_pairs={{0,2},{1,3},{2,0},{3,1},{4,6},{5,7},{6,4},{7,5},{8,10},{9,11},{10,... | collective-permute-start | bytes 322568 | tf_op jit(solution)/shard_map/ppermute | solution.py:359
  151.3 5.1 %collective-permute-start.8 = (f32[30,896]{1,0:T(8,128)S(1)}, f32[30,896]{1,0:T(8,128)S(1)}, u32[]{:S(2)}, u32[]{:S(2)}) collective-permute-start(f32[30,896]{1,0:T(8,128)S(1)} %get-tuple-element.62), channel_id=1, source_target_pairs={{0,3},{1,0},{2,1},{3,2},{4,7},{5,4},{6,5},{7,6},{8,11},{9,8},{10,9... | collective-permute-start | bytes 322568 | tf_op jit(solution)/shard_map/ppermute | solution.py:359
  156.4 1.0 slice_reduce_fusion
  157.5 1.0 subtract_convert_fusion
  158.4 10.8 %collective-permute-done.7 = f32[30,896]{1,0:T(8,128)S(1)} collective-permute-done((f32[30,896]{1,0:T(8,128)S(1)}, f32[30,896]{1,0:T(8,128)S(1)}, u32[]{:S(2)}, u32[]{:S(2)}) %collective-permute-start.7) | collective-permute-done | bytes 107552 | tf_op jit(solution)/shard_map/ppermute | solution.py:359
  169.9 2.5 collective-permute-done.8
  173.7 11.6 %all-gather.3.cloned.1.call-done = bf16[1792,896]{1,0:T(8,128)(2,1)} async-done(((bf16[112,896]{1,0:T(8,128)(2,1)}), bf16[1792,896]{1,0:T(8,128)(2,1)}) %all-gather.3.cloned.1.call-update) | async-done | bytes 3211280 | tf_op jit(solution)/shard_map/all_gather | solution.py:338
  185.3 1.9 copy-done.3
  187.2 0.9 copy-done.6
  188.2 0.9 copy-done.8
  189.1 0.9 copy-done.12
  190.1 5.7 %attn_grads.1 = (bf16[256,448]{1,0:T(8,128)(2,1)S(1)}, bf16[256,448]{1,0:T(8,128)(2,1)S(1)}) custom-call(s32[1]{0:T(128)} %bitcast.24.shift_ref, bf16[4,256,896]{2,1,0:T(8,128)(2,1)S(1)} %all-to-all-done.state_ref.own_ref, bf16[4,256,896]{2,1,0:T(8,128)(2,1)} %collective-permute-done.4.other_ref, bf16[2,4,16,896]{3,2,1,0:T(8,128)(2,1)S(1)} %copy-done.12, ...), custom_call_target="tpu_custom_call" | custom-call | flops 1644167168 | bytes 8388608 | tf_op jit(solution)/shard_map/attn_grads/pallas_call | solution.py:289
  195.7 2.6 collective-permute-start.9
  198.3 0.9 slice_add_fusion
  199.4 1.1 maximum_select_fusion.1
  200.5 2.4 reduce_sum.21
  203.0 28.9 %all_to_all.25 = bf16[4,28,896]{2,1,0:T(8,128)(2,1)S(1)} all-to-all(bf16[4,28,896]{2,1,0:T(8,128)(2,1)S(1)} %convert_element_type.22), channel_id=1, replica_groups=mesh['x'=4,'y'=4,'c'=2,'t'=4,'r'=4] {'r'}, dimensions={0} | all-to-all | bytes 401408 | tf_op jit(solution)/shard_map/all_to_all | solution.py:388
  232.0 15.1 %all_to_all.26 = bf16[16,28,896]{2,1,0:T(8,128)(2,1)S(1)} all-to-all(bf16[16,28,896]{2,1,0:T(8,128)(2,1)S(1)} %broadcast_in_dim.24), channel_id=1, replica_groups=mesh['x'=4,'y'=4,'c'=2,'t'=4,'r'=4] {'x','y'}, dimensions={0} | all-to-all | bytes 1605632 | tf_op jit(solution)/shard_map/all_to_all | solution.py:393
  247.3 7.5 %collective-permute-start.10 = (bf16[448,896]{1,0:T(8,128)(2,1)S(1)}, bf16[448,896]{1,0:T(8,128)(2,1)S(1)}, u32[]{:S(2)}, u32[]{:S(2)}) collective-permute-start(bf16[448,896]{1,0:T(8,128)(2,1)S(1)} %reshape.107), channel_id=1, source_target_pairs={{0,16},{16,0},{1,17},{17,1},{2,18},{18,2},{3,19},{19,3},{4,20},{20... | collective-permute-start | bytes 2408456 | tf_op jit(solution)/shard_map/ppermute | solution.py:40
  255.9 0.8 collective-permute-done.10
  256.7 1.8 maximum_select_fusion
  (70 shorter events, 7.9 us)
Async XLA Ops:
  7.2 18.7 %copy-start = (bf16[896,896]{1,0:T(8,128)(2,1)S(1)}, bf16[896,896]{1,0:T(8,128)(2,1)}, u32[]{:S(2)}) copy-start(bf16[896,896]{1,0:T(8,128)(2,1)} %param.8) | copy-start | bytes 4816900
  9.7 6.6 %copy-start.20 = (f32[896]{0:T(1024)S(1)}, f32[896]{0:T(1024)}, u32[]{:S(2)}) copy-start(f32[896]{0:T(1024)} %param.9) | copy-start | bytes 10756
  9.7 49.1 %copy-start.13 = (s32[1,2]{1,0:T(1,128)S(1)}, s32[1,2]{1,0:T(1,128)}, u32[]{:S(2)}) copy-start(s32[1,2]{1,0:T(1,128)} %param.10) | copy-start | bytes 28
  9.7 49.0 %all-to-all-start = ((bf16[4,256,896]{2,1,0:T(8,128)(2,1)}), bf16[4,256,896]{2,1,0:T(8,128)(2,1)S(1)}, u32[]{:S(2)}, u32[]{:S(2)}) async-start(bf16[4,256,896]{2,1,0:T(8,128)(2,1)} %broadcast_in_dim.21), calls=%async_computation | async-start | bytes 3670016 | tf_op jit(solution)/shard_map/all_to_all | solution.py:310
  16.3 169.0 %all-gather.3.cloned.1.call-start = ((), (), s32[]{:S(2)}) async-start(), calls=%async_computation.5 | async-start | bytes 3411968 | tf_op jit(solution)/shard_map/all_gather | solution.py:338
  16.3 26.1 %collective-permute-start.3 = (f32[1,896]{1,0:T(1,128)S(1)}, f32[1,896]{1,0:T(1,128)S(1)}, u32[]{:S(2)}, u32[]{:S(2)}) collective-permute-start(f32[1,896]{1,0:T(1,128)S(1)} %reshape.103), channel_id=1, source_target_pairs={{0,12},{4,0},{8,4},{12,8},{1,13},{5,1},{9,5},{13,9},{2,14},{6,2},{... | collective-permute-start | bytes 10760 | tf_op jit(solution)/shard_map/ppermute | solution.py:324
  21.5 37.2 %collective-permute-start.2 = (f32[1,896]{1,0:T(1,128)S(1)}, f32[1,896]{1,0:T(1,128)S(1)}, u32[]{:S(2)}, u32[]{:S(2)}) collective-permute-start(f32[1,896]{1,0:T(1,128)S(1)} %reshape.103), channel_id=1, source_target_pairs={{0,8},{4,12},{8,0},{12,4},{1,9},{5,13},{9,1},{13,5},{2,10},{6,14},... | collective-permute-start | bytes 10760 | tf_op jit(solution)/shard_map/ppermute | solution.py:324
  23.4 35.3 %collective-permute-start.1 = (f32[1,896]{1,0:T(1,128)S(1)}, f32[1,896]{1,0:T(1,128)S(1)}, u32[]{:S(2)}, u32[]{:S(2)}) collective-permute-start(f32[1,896]{1,0:T(1,128)S(1)} %reshape.103), channel_id=1, source_target_pairs={{0,4},{4,8},{8,12},{12,0},{1,5},{5,9},{9,13},{13,1},{2,6},{6,10},{... | collective-permute-start | bytes 10760 | tf_op jit(solution)/shard_map/ppermute | solution.py:324
  26.6 35.9 %collective-permute-start.5 = (bf16[112,896]{1,0:T(8,128)(2,1)}, bf16[112,896]{1,0:T(8,128)(2,1)}, u32[]{:S(2)}, u32[]{:S(2)}) collective-permute-start(bf16[112,896]{1,0:T(8,128)(2,1)} %constant_dynamic-slice_fusion.2), channel_id=1, source_target_pairs={{0,0},{1,1},{2,2},{3,3},{129,128},{130,129},{131,130},{128,131},{2... | collective-permute-start | bytes 602120 | tf_op jit(solution)/shard_map/ppermute | solution.py:313
  32.0 26.8 %collective-permute-start = (bf16[256,448]{1,0:T(8,128)(2,1)}, bf16[256,448]{1,0:T(8,128)(2,1)}, u32[]{:S(2)}, u32[]{:S(2)}) collective-permute-start(bf16[256,448]{1,0:T(8,128)(2,1)} %get-tuple-element.55), channel_id=1, source_target_pairs={{0,16},{16,0},{1,17},{17,1},{2,18},{18,2},{3,19},{19,3},{4,20},{20... | collective-permute-start | bytes 688136 | tf_op jit(solution)/shard_map/ppermute | solution.py:40
  58.8 1.0 copy-start.4
  61.5 1.0 copy-start.1
  62.5 53.3 %collective-permute-start.4 = (bf16[4,256,896]{2,1,0:T(8,128)(2,1)S(1)}, bf16[4,256,896]{2,1,0:T(8,128)(2,1)}, u32[]{:S(2)}, u32[]{:S(2)}) collective-permute-start(bf16[4,256,896]{2,1,0:T(8,128)(2,1)S(1)} %all-to-all-done.state_ref.own_ref), channel_id=1, source_target_pairs={{0,16},{16,0},{1,17},{17,1},{2,18},{18,2},{3,19},{19,3},{4,20},{20... | collective-permute-start | bytes 5505032 | tf_op jit(solution)/shard_map/ppermute | solution.py:40
  65.9 41.5 %all-to-all-start.1 = ((f32[32,8,1024]{2,1,0:T(8,128)}), f32[32,8,1024]{2,1,0:T(8,128)}, u32[]{:S(2)}, u32[]{:S(2)}) async-start(f32[32,8,1024]{2,1,0:T(8,128)} %copy-done.1), calls=%async_computation.1 | async-start | bytes 2097152 | tf_op jit(solution)/shard_map/all_to_all | solution.py:339
  107.4 8.5 %copy-start.10 = (bf16[256,448]{1,0:T(8,128)(2,1)S(1)}, bf16[256,448]{1,0:T(8,128)(2,1)}, u32[]{:S(2)}) copy-start(bf16[256,448]{1,0:T(8,128)(2,1)} %get-tuple-element.54.keep_ref) | copy-start | bytes 688132
  113.5 0.7 copy-start.5
  114.2 0.8 copy-start.9
  114.9 0.9 copy-start.14
  115.9 5.1 %copy-start.11 = (bf16[2,4,16,896]{3,2,1,0:T(8,128)(2,1)}, bf16[2,4,16,896]{3,2,1,0:T(8,128)(2,1)S(1)}, u32[]{:S(2)}) copy-start(bf16[2,4,16,896]{3,2,1,0:T(8,128)(2,1)S(1)} %get-tuple-element.32.pieces_ref) | copy-start | bytes 688132
  120.9 1.7 copy-start.2
  122.6 0.7 copy-start.7
  123.3 77.2 %all-to-all-start.2 = ((bf16[16,112,896]{2,1,0:T(8,128)(2,1)}), bf16[16,112,896]{2,1,0:T(8,128)(2,1)}, u32[]{:S(2)}, u32[]{:S(2)}) async-start(bf16[16,112,896]{2,1,0:T(8,128)(2,1)} %copy-done.2), calls=%async_computation.2 | async-start | bytes 6422528 | tf_op jit(solution)/shard_map/all_to_all | solution.py:351
  128.0 29.5 %copy-start.15 = (bf16[1,2,128,896]{3,2,1,0:T(8,128)(2,1)S(1)}, bf16[1,2,128,896]{3,2,1,0:T(8,128)(2,1)}, u32[]{:S(2)}) copy-start(bf16[1,2,128,896]{3,2,1,0:T(8,128)(2,1)} %param.6) | copy-start | bytes 1376260
  132.9 25.5 %collective-permute-start.6 = (f32[30,896]{1,0:T(8,128)S(1)}, f32[30,896]{1,0:T(8,128)S(1)}, u32[]{:S(2)}, u32[]{:S(2)}) collective-permute-start(f32[30,896]{1,0:T(8,128)S(1)} %get-tuple-element.60), channel_id=1, source_target_pairs={{0,1},{1,2},{2,3},{3,0},{4,5},{5,6},{6,7},{7,4},{8,9},{9,10},{10,1... | collective-permute-start | bytes 322568 | tf_op jit(solution)/shard_map/ppermute | solution.py:359
  142.5 26.7 %collective-permute-start.7 = (f32[30,896]{1,0:T(8,128)S(1)}, f32[30,896]{1,0:T(8,128)S(1)}, u32[]{:S(2)}, u32[]{:S(2)}) collective-permute-start(f32[30,896]{1,0:T(8,128)S(1)} %get-tuple-element.61), channel_id=1, source_target_pairs={{0,2},{1,3},{2,0},{3,1},{4,6},{5,7},{6,4},{7,5},{8,10},{9,11},{10,... | collective-permute-start | bytes 322568 | tf_op jit(solution)/shard_map/ppermute | solution.py:359
  151.3 21.0 %collective-permute-start.8 = (f32[30,896]{1,0:T(8,128)S(1)}, f32[30,896]{1,0:T(8,128)S(1)}, u32[]{:S(2)}, u32[]{:S(2)}) collective-permute-start(f32[30,896]{1,0:T(8,128)S(1)} %get-tuple-element.62), channel_id=1, source_target_pairs={{0,3},{1,0},{2,1},{3,2},{4,7},{5,4},{6,5},{7,6},{8,11},{9,8},{10,9... | collective-permute-start | bytes 322568 | tf_op jit(solution)/shard_map/ppermute | solution.py:359
  169.2 0.7 copy-start.16
  172.4 0.6 copy-start.18
  185.3 1.9 copy-start.3
  187.2 0.9 copy-start.6
  188.2 0.9 copy-start.8
  189.1 0.9 copy-start.12
  190.1 8.2 %copy-start.17 = (f32[30,896]{1,0:T(8,128)S(1)}, f32[30,896]{1,0:T(8,128)}, u32[]{:S(2)}) copy-start(f32[30,896]{1,0:T(8,128)} %copy-done.16) | copy-start | bytes 322564
  190.1 8.3 %copy-start.19 = (f32[30,896]{1,0:T(8,128)S(1)}, f32[30,896]{1,0:T(8,128)}, u32[]{:S(2)}) copy-start(f32[30,896]{1,0:T(8,128)} %copy-done.18) | copy-start | bytes 322564
  195.7 3.7 %collective-permute-start.9 = (bf16[256,448]{1,0:T(8,128)(2,1)S(1)}, bf16[256,448]{1,0:T(8,128)(2,1)S(1)}, u32[]{:S(2)}, u32[]{:S(2)}) collective-permute-start(bf16[256,448]{1,0:T(8,128)(2,1)S(1)} %get-tuple-element.44), channel_id=1, source_target_pairs={{0,16},{16,0},{1,17},{17,1},{2,18},{18,2},{3,19},{19,3},{4,20},{20... | collective-permute-start | bytes 688136 | tf_op jit(solution)/shard_map/ppermute | solution.py:40
  232.0 22.8 %copy-start.21 = (f32[2,896]{1,0:T(2,128)S(1)}, f32[2,896]{1,0:T(2,128)}, u32[]{:S(2)}) copy-start(f32[2,896]{1,0:T(2,128)} %add_bitcast_fusion) | copy-start | bytes 21508
  247.3 9.4 %collective-permute-start.10 = (bf16[448,896]{1,0:T(8,128)(2,1)S(1)}, bf16[448,896]{1,0:T(8,128)(2,1)S(1)}, u32[]{:S(2)}, u32[]{:S(2)}) collective-permute-start(bf16[448,896]{1,0:T(8,128)(2,1)S(1)} %reshape.107), channel_id=1, source_target_pairs={{0,16},{16,0},{1,17},{17,1},{2,18},{18,2},{3,19},{19,3},{4,20},{20... | collective-permute-start | bytes 2408456 | tf_op jit(solution)/shard_map/ppermute | solution.py:40
Sparse Core Ops, SparseCore 0:
  62.6 122.6 all-gather.2

commit v6 on v4

--- a/solution.py
+++ b/solution.py
@@ -192,6 +192,66 @@
     )(own, other, keep, given, pieces, scale)
 
 
+def sum_kernel(spread_ref, out_ref, acc_ref):
+    step = pl.program_id(0)
+    part = spread_ref[0].astype(f32)
+    for place in range(1, spread_ref.shape[0]):
+        part = part + spread_ref[place].astype(f32)
+
+    @pl.when(step == 0)
+    def _():
+        acc_ref[...] = part
+
+    @pl.when(step > 0)
+    def _():
+        acc_ref[...] += part
+
+    @pl.when(step == NX - 1)
+    def _():
+        for block in range(NR):
+            out_ref[block] = acc_ref[block * SLICE : (block + 1) * SLICE, :].astype(bf16)
+
+
+def sum_senders(spread):
+    return pl.pallas_call(
+        sum_kernel,
+        grid=(NX,),
+        out_shape=jax.ShapeDtypeStruct((NR, SLICE, COLS), bf16),
+        in_specs=[pl.BlockSpec((NY, NR * SLICE, COLS), lambda step: (step, 0, 0))],
+        out_specs=pl.BlockSpec((NR, SLICE, COLS), lambda step: (0, 0, 0)),
+        scratch_shapes=[pltpu.VMEM((NR * SLICE, COLS), f32)],
+        compiler_params=pltpu.CompilerParams(vmem_limit_bytes=16 * 1024 * 1024),
+        cost_estimate=pl.CostEstimate(
+            flops=NX * NY * NR * SLICE * COLS, bytes_accessed=4 * 1024 * 1024, transcendentals=0
+        ),
+        name="sum_senders",
+    )(spread)
+
+
+def join_kernel(core_ref, mine_ref, other_ref, out_ref):
+    core = core_ref[0]
+    for which, ref in ((core, mine_ref), (1 - core, other_ref)):
+        rows = [ref[place].astype(f32) for place in range(NX * NY)]
+        out_ref[pl.ds(pl.multiple_of(which * HALF, HALF), HALF), :] = jnp.concatenate(
+            rows, 0
+        ).astype(bf16)
+
+
+def join_halves(core, mine, other):
+    spec = pl.BlockSpec(memory_space=pltpu.VMEM)
+    return pl.pallas_call(
+        join_kernel,
+        out_shape=jax.ShapeDtypeStruct((FEAT, COLS), bf16),
+        in_specs=[pl.BlockSpec(memory_space=pltpu.SMEM), spec, spec],
+        out_specs=spec,
+        compiler_params=pltpu.CompilerParams(vmem_limit_bytes=16 * 1024 * 1024),
+        cost_estimate=pl.CostEstimate(
+            flops=0, bytes_accessed=4 * 1024 * 1024, transcendentals=0
+        ),
+        name="join_halves",
+    )(core, mine, other)
+
+
 def attn_kernel(
     shift_ref, own_ref, other_ref, pieces_ref, w_ref, coef_ref, first_ref, keep_ref, give_ref
 ):
@@ -257,7 +317,6 @@
     attn_pool = jnp.sum(pool_weight[..., None] * attn.astype(f32).reshape(2, SEQ, FEAT), 1)
 
     near = jnp.concatenate([pooled, norm_gain[None]], 0)
-    near, w_moved = lax.optimization_barrier((near, w_moved))
     near = lax.all_to_all(jnp.broadcast_to(near[None], (NT, 3, FEAT)), "t", 0, 0)
     pooled_row = near[:, :2].transpose(1, 0, 2).reshape(2, D)
     gain = near[:, 2].reshape(1, D)
@@ -278,10 +337,7 @@
         -1,
     )
     got = lax.all_to_all(send, DP, 0, 0)
-    got, state_all, w_moved, attn_other = lax.optimization_barrier(
-        (got, state_all, w_moved, attn_other)
-    )
-    w_all = lax.all_gather(w_moved, PLANE).reshape(NX, HALF, COLS)
+    got, state_all, attn_other = lax.optimization_barrier((got, state_all, attn_other))
 
     other_index = dp_index + 1 - 2 * ic
     state_other = swap_core(state_all)
@@ -292,7 +348,8 @@
     partial, coef = weight_partials(
         state_all, state_other, attn_keep, attn_other, pieces, scale
     )
-    partial, first = lax.optimization_barrier((partial, first))
+    partial, first, w_moved = lax.optimization_barrier((partial, first, w_moved))
+    w_all = lax.all_gather(w_moved, PLANE).reshape(NX, HALF, COLS)
     spread = lax.all_to_all(partial, PLANE, 0, 0)
 
     gain_mine = lax.dynamic_index_in_dim(gain_part, it, 0, keepdims=False)
@@ -316,8 +373,7 @@
         )
 
     spread, first_sum, totals = lax.optimization_barrier((spread, first_sum, totals))
-    second = jnp.sum(spread.astype(f32), 0).reshape(NR, SLICE, COLS)
-    second = lax.all_to_all(second.astype(bf16), "r", 0, 0)
+    second = lax.all_to_all(sum_senders(spread), "r", 0, 0)
 
     row_here = lax.dynamic_slice(scaled, (0, dp_index, it * FEAT), (2, 1, FEAT))
     state_grad = first_col[0].reshape(2, SEQ, 1) * row_here - states * coef[0].reshape(2, SEQ, 1)
@@ -326,25 +382,19 @@
         ir.reshape(1), state_all, state_other, pieces, w_all, coef, first_col
     )
 
-    second, keep, give = lax.optimization_barrier((second, keep, give))
     second_sum = jnp.sum(second.astype(f32), 0)
     total = first_sum - second_sum
     done = jnp.broadcast_to(total.astype(bf16)[None], (NX * NY, SLICE, COLS))
-    half = lax.all_to_all(done, PLANE, 0, 0).reshape(HALF, COLS)
+    half = lax.all_to_all(done, PLANE, 0, 0)
+    half, keep, give, grad_hidden, totals = lax.optimization_barrier(
+        (half, keep, give, grad_hidden, totals)
+    )
+    half_other = swap_core(half)
     arrived = swap_core(give)
     grad_attn = jnp.where(
         ic == 0, jnp.concatenate([keep, arrived], 1), jnp.concatenate([arrived, keep], 1)
     ).reshape(1, 2, SEQ, FEAT)
-    half, grad_attn, grad_hidden, totals = lax.optimization_barrier(
-        (half, grad_attn, grad_hidden, totals)
-    )
-    half_other = swap_core(half)
-    grad_weight = jnp.where(
-        ic == 0,
-        jnp.concatenate([half, half_other], 0),
-        jnp.concatenate([half_other, half], 0),
-    )
-
+    grad_weight = join_halves(ic.reshape(1), half, half_other)
     return (grad_hidden, grad_attn, grad_weight, totals[0], totals[1, 0])
 
 

time: 238 us -> 220 us (0.924)
  starting transfers between devices: 103 us -> 75.2 us
  blocking collectives: 11.8 us -> 35.9 us
  other arithmetic: 14.7 us -> 8.29 us
  waiting for transfers between devices: 48.9 us -> 42.9 us
  local copies, waits for them, and re-layouts: 27.9 us -> 22.3 us
  Pallas kernels: 14.8 us -> 19.1 us
    all_to_all x1, starting transfers between devices: 42.3 us -> 11 us  [body(): got = lax.all_to_all(send, DP, 0, 0)]
    all_to_all x0 -> x1, blocking collectives: none -> 24.1 us  [body(): second = lax.all_to_all(sum_senders(spread), 'r', 0, 0)]
    all_to_all x1, starting transfers between devices: 4.49 us -> 14.5 us  [body(): spread = lax.all_to_all(partial, PLANE, 0, 0)]
    all_to_all x2 -> x1, starting transfers between devices: 20.6 us -> 10.7 us  [body(): half = lax.all_to_all(done, PLANE, 0, 0)]
    ppermute x3, starting transfers between devices: 13.8 us -> 19.4 us  [body(): lax.ppermute(jnp.concatenate([outgoing, tail], 0), 'r', [(j, (j + step) %...]
    ppermute x4, starting transfers between devices: 17.5 us -> 12.8 us  [swap_core(): return lax.ppermute(value, 'c', [(0, 1), (1, 0)])]
    pallas_call x0 -> x2, Pallas kernels: none -> 4.4 us  [the longest x1 2.99 us: sum_senders(): pl.pallas_call(sum_kernel, grid=(NX,), out_shape=jax.ShapeDtypeStruct((NR...]
    all_to_all x2 -> x1, waiting for transfers between devices: 3.48 us -> 0.01 us  [body(): half = lax.all_to_all(done, PLANE, 0, 0)]
  transfers between devices with their start and end apart: 15 -> 14, of which waited for: 11 -> 8; matrix products, arithmetic and copies ran while one was open for 10% -> 9% of each run, Pallas kernels for 6% -> 8%
where the time goes in v6:
time: 220 us; the launch traced here: 219 us
  starting transfers between devices  75.2 us (34%)
  waiting for transfers between devices  42.9 us (20%)
  blocking collectives  35.9 us (16%)
  local copies, waits for them, and re-layouts  22.3 us (10%)
  Pallas kernels  19.1 us (9%)
  between operations  15.2 us (7%)
  other arithmetic  8.29 us (4%)
    all_to_all x1, blocking collectives, body(): second = lax.all_to_all(sum_senders(spread), 'r', 0, 0)  24.1 us
    ppermute x3, starting transfers between devices, body(): lax.ppermute(jnp.concatenate([outgoing, tail], 0), 'r', [(j, (j + step) %...  19.4 us
    ppermute x3, waiting for transfers between devices, body(): lax.ppermute(jnp.concatenate([outgoing, tail], 0), 'r', [(j, (j + step) %...  17.7 us
    all_to_all x1, starting transfers between devices, body(): spread = lax.all_to_all(partial, PLANE, 0, 0)  14.5 us
    ppermute x4, starting transfers between devices, swap_core(): return lax.ppermute(value, 'c', [(0, 1), (1, 0)])  12.8 us
    psum x1, blocking collectives, body(): square = lax.psum(jnp.sum(states * states, -1), 't') / D  11.8 us
    all_to_all x1, waiting for transfers between devices, body(): got = lax.all_to_all(send, DP, 0, 0)  11.2 us
    all_to_all x1, starting transfers between devices, body(): got = lax.all_to_all(send, DP, 0, 0)  11 us
  transfers between devices with their start and end apart: 14, of which 8 were waited for; matrix products, arithmetic and copies ran while one was open for 9% of the time, Pallas kernels for 8%

profile of v6, /device:TPU:1, one launch (start us, length us, event | category | flops | bytes accessed | tf_op | source)
XLA Modules:
  0.0 218.9 jit_solution(7758496159762667326)
XLA Ops:
  8.6 1.2 fusion.2
  9.8 11.8 %psum.7 = f32[2,128]{1,0:T(2,128)S(1)} all-reduce(f32[2,128]{1,0:T(2,128)S(1)} %fusion.2), channel_id=1, replica_groups=mesh['x'=4,'y'=4,'c'=2,'t'=4,'r'=4] {'t'}, use_global_device_ids=true, to_apply=%region_1.2 | all-reduce | flops 256 | bytes 2048 | tf_op jit(solution)/shard_map/psum | solution.py:311
  21.6 0.7 convert_bitcast_fusion.1
  22.3 0.7 fusion.10
  23.1 1.4 fusion.6
  25.1 3.3 %all-to-all-start = ((f32[4,3,896]{2,1,0:T(4,128)}), f32[4,3,896]{2,1,0:T(4,128)S(1)}, u32[]{:S(2)}, u32[]{:S(2)}) async-start(f32[4,3,896]{2,1,0:T(4,128)} %broadcast_in_dim.17), calls=%async_computation | async-start | bytes 114688 | tf_op jit(solution)/shard_map/all_to_all | solution.py:320
  29.4 3.6 %all-to-all-done = f32[4,3,896]{2,1,0:T(4,128)S(1)} async-done(((f32[4,3,896]{2,1,0:T(4,128)}), f32[4,3,896]{2,1,0:T(4,128)S(1)}, u32[]{:S(2)}, u32[]{:S(2)}) %all-to-all-start) | async-done | bytes 43040 | tf_op jit(solution)/shard_map/all_to_all | solution.py:320
  33.3 2.2 %concatenate.50 = f32[32,2,3840]{2,1,0:T(2,128)} concatenate(f32[32,2,3712]{2,1,0:T(2,128)S(1)} %broadcast_in_dim.18, f32[32,2,28]{2,1,0:T(2,128)S(1)} %copy.20, f32[32,2,2]{2,1,0:T(2,128)S(1)} %broadcast_in_dim.19, f32[32,2,98]{2,1,0:T(2,128)S(1)} %broadcast_in_dim.20), dimensions={2} | concatenate | bytes 1966080 | tf_op jit(solution)/shard_map/concatenate | solution.py:330
  35.5 11.0 %all-to-all-start.1 = ((f32[32,2,3840]{2,1,0:T(2,128)}), f32[32,2,3840]{2,1,0:T(2,128)S(1)}, u32[]{:S(2)}, u32[]{:S(2)}) async-start(f32[32,2,3840]{2,1,0:T(2,128)} %concatenate.50), calls=%async_computation.1 | async-start | bytes 1966080 | tf_op jit(solution)/shard_map/all_to_all | solution.py:339
  46.7 0.8 broadcast_select_fusion
  47.5 2.1 collective-permute-start
  49.6 1.3 collective-permute-done.given_ref
  50.9 0.7 copy-done.15
  51.6 11.2 %all-to-all-done.1 = f32[32,2,3840]{2,1,0:T(2,128)S(1)} async-done(((f32[32,2,3840]{2,1,0:T(2,128)}), f32[32,2,3840]{2,1,0:T(2,128)S(1)}, u32[]{:S(2)}, u32[]{:S(2)}) %all-to-all-start.1) | async-done | bytes 983072 | tf_op jit(solution)/shard_map/all_to_all | solution.py:339
  62.8 0.9 copy-done.18
  63.7 2.4 %all-gather.4.cloned.1.call-done.own_ref = bf16[4,256,896]{2,1,0:T(8,128)(2,1)} async-done(((bf16[1,256,896]{2,1,0:T(8,128)(2,1)}), bf16[4,256,896]{2,1,0:T(8,128)(2,1)}) %all-gather.4.cloned.1.call-update) | async-done | bytes 1835024 | tf_op jit(solution)/shard_map/all_gather | solution.py:298
  66.1 3.0 %collective-permute-start.1 = (bf16[4,256,896]{2,1,0:T(8,128)(2,1)}, bf16[4,256,896]{2,1,0:T(8,128)(2,1)}, u32[]{:S(2)}, u32[]{:S(2)}) collective-permute-start(bf16[4,256,896]{2,1,0:T(8,128)(2,1)} %all-gather.4.cloned.1.call-done.own_ref), channel_id=1, source_target_pairs={{0,16},{16,0},{1,17},{17,1},{2,18},{18,2},{3,19},{19,3},{4,20},{20... | collective-permute-start | bytes 5505032 | tf_op jit(solution)/shard_map/ppermute | solution.py:38
  69.1 0.7 constant_dynamic-slice_fusion.1
  69.8 3.4 %collective-permute-start.2 = (bf16[112,896]{1,0:T(8,128)(2,1)}, bf16[112,896]{1,0:T(8,128)(2,1)}, u32[]{:S(2)}, u32[]{:S(2)}) collective-permute-start(bf16[112,896]{1,0:T(8,128)(2,1)} %constant_dynamic-slice_fusion.1), channel_id=1, source_target_pairs={{0,0},{1,1},{2,2},{3,3},{129,128},{130,129},{131,130},{128,131},{2... | collective-permute-start | bytes 602120 | tf_op jit(solution)/shard_map/ppermute | solution.py:301
  73.3 1.3 copy.28
  74.6 4.2 %group_math.1 = (f32[2,32,3584]{2,1,0:T(8,128)S(1)}, f32[4,28,896]{2,1,0:T(8,128)S(1)}, f32[4,1,896]{2,1,0:T(1,128)S(1)}, f32[8,128]{1,0:T(8,128)S(1)}, bf16[2,4...) custom-call(s32[2]{0:T(128)S(1)} %pad_add_fusion.index_ref, ...), custom_call_target="tpu_custom_call" | custom-call | flops 183500800 | bytes 3145728 | tf_op jit(solution)/shard_map/group_math/pallas_call | solution.py:124
  79.5 0.8 copy-done.9
  80.3 0.9 copy-done.14
  81.2 5.0 %weight_partials.1 = (bf16[16,112,896]{2,1,0:T(8,128)(2,1)S(1)}, f32[2,256,1]{2,1,0:T(8,128)S(1)}) custom-call(bf16[4,256,896]{2,1,0:T(8,128)(2,1)S(1)} %copy-done.3, bf16[4,256,896]{2,1,0:T(8,128)(2,1)} %collective-permute-done.1.other_ref, bf16[256,448]{1,0:T(8,128)(2,1)S(1)} %copy-done.11, bf16[256,448]{1,0:T(8,128)(2,1)S(1)} %copy-done.16, ...), custom_call_target="tpu_custom_call" | custom-call | flops 1644167168 | bytes 8388608 | tf_op jit(solution)/shard_map/weight_partials/pallas_call | solution.py:178
  86.2 1.7 copy-done.1
  87.9 0.7 copy-done.7
  88.6 14.5 %all-to-all-start.2 = ((bf16[16,112,896]{2,1,0:T(8,128)(2,1)}), bf16[16,112,896]{2,1,0:T(8,128)(2,1)}, u32[]{:S(2)}, u32[]{:S(2)}) async-start(bf16[16,112,896]{2,1,0:T(8,128)(2,1)} %copy-done.1), calls=%async_computation.2 | async-start | bytes 6422528 | tf_op jit(solution)/shard_map/all_to_all | solution.py:353
  103.8 0.7 pad.18.clone
  104.6 7.4 %collective-permute-start.3 = (f32[30,896]{1,0:T(8,128)S(1)}, f32[30,896]{1,0:T(8,128)S(1)}, u32[]{:S(2)}, u32[]{:S(2)}) collective-permute-start(f32[30,896]{1,0:T(8,128)S(1)} %get-tuple-element.62), channel_id=1, source_target_pairs={{0,1},{1,2},{2,3},{3,0},{4,5},{5,6},{6,7},{7,4},{8,9},{9,10},{10,1... | collective-permute-start | bytes 322568 | tf_op jit(solution)/shard_map/ppermute | solution.py:361
  112.6 5.2 %collective-permute-start.4 = (f32[30,896]{1,0:T(8,128)S(1)}, f32[30,896]{1,0:T(8,128)S(1)}, u32[]{:S(2)}, u32[]{:S(2)}) collective-permute-start(f32[30,896]{1,0:T(8,128)S(1)} %get-tuple-element.63), channel_id=1, source_target_pairs={{0,2},{1,3},{2,0},{3,1},{4,6},{5,7},{6,4},{7,5},{8,10},{9,11},{10,... | collective-permute-start | bytes 322568 | tf_op jit(solution)/shard_map/ppermute | solution.py:361
  117.8 6.9 %collective-permute-start.5 = (f32[30,896]{1,0:T(8,128)S(1)}, f32[30,896]{1,0:T(8,128)S(1)}, u32[]{:S(2)}, u32[]{:S(2)}) collective-permute-start(f32[30,896]{1,0:T(8,128)S(1)} %get-tuple-element.64), channel_id=1, source_target_pairs={{0,3},{1,0},{2,1},{3,2},{4,7},{5,4},{6,5},{7,6},{8,11},{9,8},{10,9... | collective-permute-start | bytes 322568 | tf_op jit(solution)/shard_map/ppermute | solution.py:361
  124.7 12.9 %collective-permute-done.4 = f32[30,896]{1,0:T(8,128)S(1)} collective-permute-done((f32[30,896]{1,0:T(8,128)S(1)}, f32[30,896]{1,0:T(8,128)S(1)}, u32[]{:S(2)}, u32[]{:S(2)}) %collective-permute-start.4) | collective-permute-done | bytes 107552 | tf_op jit(solution)/shard_map/ppermute | solution.py:361
  137.6 4.8 %collective-permute-done.5 = f32[30,896]{1,0:T(8,128)S(1)} collective-permute-done((f32[30,896]{1,0:T(8,128)S(1)}, f32[30,896]{1,0:T(8,128)S(1)}, u32[]{:S(2)}, u32[]{:S(2)}) %collective-permute-start.5) | collective-permute-done | bytes 107552 | tf_op jit(solution)/shard_map/ppermute | solution.py:361
  142.5 5.5 %all-to-all-done.2.spread_ref = bf16[16,112,896]{2,1,0:T(8,128)(2,1)} async-done(((bf16[16,112,896]{2,1,0:T(8,128)(2,1)}), bf16[16,112,896]{2,1,0:T(8,128)(2,1)}, u32[]{:S(2)}, u32[]{:S(2)}) %all-to-all-start.2) | async-done | bytes 3211296 | tf_op jit(solution)/shard_map/all_to_all | solution.py:353
  148.0 3.0 %sum_senders.1 = bf16[4,28,896]{2,1,0:T(8,128)(2,1)S(1)} custom-call(bf16[16,112,896]{2,1,0:T(8,128)(2,1)} %all-to-all-done.2.spread_ref), custom_call_target="tpu_custom_call" | custom-call | flops 1605632 | bytes 4194304 | tf_op jit(solution)/shard_map/sum_senders/pallas_call | solution.py:216
  151.0 24.1 %all_to_all.25 = bf16[4,28,896]{2,1,0:T(8,128)(2,1)S(1)} all-to-all(bf16[4,28,896]{2,1,0:T(8,128)(2,1)S(1)} %sum_senders.1), channel_id=1, replica_groups=mesh['x'=4,'y'=4,'c'=2,'t'=4,'r'=4] {'r'}, dimensions={0} | all-to-all | bytes 401408 | tf_op jit(solution)/shard_map/all_to_all | solution.py:376
  175.2 1.0 broadcast_in_dim.23
  176.2 10.7 %all-to-all-start.4 = ((bf16[16,28,896]{2,1,0:T(8,128)(2,1)}), bf16[16,28,896]{2,1,0:T(8,128)(2,1)S(1)}, u32[]{:S(2)}, u32[]{:S(2)}) async-start(bf16[16,28,896]{2,1,0:T(8,128)(2,1)} %broadcast_in_dim.23), calls=%async_computation.4 | async-start | bytes 1835008 | tf_op jit(solution)/shard_map/all_to_all | solution.py:388
  186.9 0.9 constant_dynamic-slice_fusion
  188.0 2.0 fusion.5
  190.0 1.9 copy-done.2
  191.9 1.5 copy-done.4
  193.4 5.6 %attn_grads.1 = (bf16[256,448]{1,0:T(8,128)(2,1)S(1)}, bf16[256,448]{1,0:T(8,128)(2,1)S(1)}) custom-call(s32[1]{0:T(128)} %bitcast.26.shift_ref, bf16[4,256,896]{2,1,0:T(8,128)(2,1)S(1)} %copy-done.4, bf16[4,256,896]{2,1,0:T(8,128)(2,1)} %collective-permute-done.1.other_ref, bf16[2,4,16,896]{3,2,1,0:T(8,128)(2,1)S(1)} %copy-done.13, ...), custom_call_target="tpu_custom_call" | custom-call | flops 1644167168 | bytes 8388608 | tf_op jit(solution)/shard_map/attn_grads/pallas_call | solution.py:278
  199.1 0.7 copy-done.17
  200.0 5.8 %collective-permute-start.7 = (bf16[16,28,896]{2,0,1:T(8,128)(2,1)S(1)}, bf16[16,28,896]{2,0,1:T(8,128)(2,1)S(1)}, u32[]{:S(2)}, u32[]{:S(2)}) collective-permute-start(bf16[16,28,896]{2,0,1:T(8,128)(2,1)S(1)} %copy.22), channel_id=1, source_target_pairs={{0,16},{16,0},{1,17},{17,1},{2,18},{18,2},{3,19},{19,3},{4,20},{20... | collective-permute-start | bytes 2408456 | tf_op jit(solution)/shard_map/ppermute | solution.py:38
  205.9 1.9 collective-permute-start.6
  209.5 1.1 maximum_select_fusion
  210.7 1.4 join_halves.1
  (77 shorter events, 7.3 us)
Async XLA Ops:
  7.2 61.9 %copy-start = (bf16[896,896]{1,0:T(8,128)(2,1)S(1)}, bf16[896,896]{1,0:T(8,128)(2,1)}, u32[]{:S(2)}) copy-start(bf16[896,896]{1,0:T(8,128)(2,1)} %param.8) | copy-start | bytes 4816900
  7.2 58.9 %all-gather.4.cloned.1.call-start = ((), (), s32[]{:S(2)}) async-start(), calls=%async_computation.5 | async-start | bytes 2293760 | tf_op jit(solution)/shard_map/all_gather | solution.py:298
  25.1 7.8 %all-to-all-start = ((f32[4,3,896]{2,1,0:T(4,128)}), f32[4,3,896]{2,1,0:T(4,128)S(1)}, u32[]{:S(2)}, u32[]{:S(2)}) async-start(f32[4,3,896]{2,1,0:T(4,128)} %broadcast_in_dim.17), calls=%async_computation | async-start | bytes 114688 | tf_op jit(solution)/shard_map/all_to_all | solution.py:320
  33.3 13.3 %copy-start.19 = (bf16[1,2,128,896]{3,2,1,0:T(8,128)(2,1)S(1)}, bf16[1,2,128,896]{3,2,1,0:T(8,128)(2,1)}, u32[]{:S(2)}) copy-start(bf16[1,2,128,896]{3,2,1,0:T(8,128)(2,1)} %param.7) | copy-start | bytes 1376260
  35.5 27.2 %all-to-all-start.1 = ((f32[32,2,3840]{2,1,0:T(2,128)}), f32[32,2,3840]{2,1,0:T(2,128)S(1)}, u32[]{:S(2)}, u32[]{:S(2)}) async-start(f32[32,2,3840]{2,1,0:T(2,128)} %concatenate.50), calls=%async_computation.1 | async-start | bytes 1966080 | tf_op jit(solution)/shard_map/all_to_all | solution.py:339
  46.6 143.4 %all-gather.6.cloned.1.call-start = ((), (), s32[]{:S(2)}) async-start(), calls=%async_computation.6 | async-start | bytes 3411968 | tf_op jit(solution)/shard_map/all_gather | solution.py:352
  47.5 3.4 %collective-permute-start = (bf16[256,448]{1,0:T(8,128)(2,1)S(1)}, bf16[256,448]{1,0:T(8,128)(2,1)S(1)}, u32[]{:S(2)}, u32[]{:S(2)}) collective-permute-start(bf16[256,448]{1,0:T(8,128)(2,1)S(1)} %get-tuple-element.61), channel_id=1, source_target_pairs={{0,16},{16,0},{1,17},{17,1},{2,18},{18,2},{3,19},{19,3},{4,20},{20... | collective-permute-start | bytes 688136 | tf_op jit(solution)/shard_map/ppermute | solution.py:38
  50.9 0.7 copy-start.15
  62.8 0.9 copy-start.18
  66.1 15.1 %copy-start.3 = (bf16[4,256,896]{2,1,0:T(8,128)(2,1)S(1)}, bf16[4,256,896]{2,1,0:T(8,128)(2,1)}, u32[]{:S(2)}) copy-start(bf16[4,256,896]{2,1,0:T(8,128)(2,1)} %all-gather.4.cloned.1.call-done.own_ref) | copy-start | bytes 5505028
  66.1 14.1 %collective-permute-start.1 = (bf16[4,256,896]{2,1,0:T(8,128)(2,1)}, bf16[4,256,896]{2,1,0:T(8,128)(2,1)}, u32[]{:S(2)}, u32[]{:S(2)}) collective-permute-start(bf16[4,256,896]{2,1,0:T(8,128)(2,1)} %all-gather.4.cloned.1.call-done.own_ref), channel_id=1, source_target_pairs={{0,16},{16,0},{1,17},{17,1},{2,18},{18,2},{3,19},{19,3},{4,20},{20... | collective-permute-start | bytes 5505032 | tf_op jit(solution)/shard_map/ppermute | solution.py:38
  69.8 18.8 %collective-permute-start.2 = (bf16[112,896]{1,0:T(8,128)(2,1)}, bf16[112,896]{1,0:T(8,128)(2,1)}, u32[]{:S(2)}, u32[]{:S(2)}) collective-permute-start(bf16[112,896]{1,0:T(8,128)(2,1)} %constant_dynamic-slice_fusion.1), channel_id=1, source_target_pairs={{0,0},{1,1},{2,2},{3,3},{129,128},{130,129},{131,130},{128,131},{2... | collective-permute-start | bytes 602120 | tf_op jit(solution)/shard_map/ppermute | solution.py:301
  73.2 8.0 %copy-start.11 = (bf16[256,448]{1,0:T(8,128)(2,1)S(1)}, bf16[256,448]{1,0:T(8,128)(2,1)}, u32[]{:S(2)}) copy-start(bf16[256,448]{1,0:T(8,128)(2,1)} %get-tuple-element.60.keep_ref) | copy-start | bytes 688132
  73.2 8.0 %copy-start.16 = (bf16[256,448]{1,0:T(8,128)(2,1)S(1)}, bf16[256,448]{1,0:T(8,128)(2,1)}, u32[]{:S(2)}) copy-start(bf16[256,448]{1,0:T(8,128)(2,1)} %copy-done.15) | copy-start | bytes 688132
  78.8 0.7 copy-start.5
  79.5 0.8 copy-start.9
  80.2 0.9 copy-start.14
  80.2 5.9 %copy-start.12 = (bf16[2,4,16,896]{3,2,1,0:T(8,128)(2,1)}, bf16[2,4,16,896]{3,2,1,0:T(8,128)(2,1)S(1)}, u32[]{:S(2)}) copy-start(bf16[2,4,16,896]{3,2,1,0:T(8,128)(2,1)S(1)} %get-tuple-element.33.pieces_ref) | copy-start | bytes 688132
  86.2 1.7 copy-start.1
  87.9 0.7 copy-start.7
  88.6 15.9 %copy-start.10 = (f32[4,28,896]{2,1,0:T(8,128)S(1)}, f32[4,28,896]{2,1,0:T(8,128)}, u32[]{:S(2)}) copy-start(f32[4,28,896]{2,1,0:T(8,128)} %copy-done.9) | copy-start | bytes 1204228
  88.6 59.4 %all-to-all-start.2 = ((bf16[16,112,896]{2,1,0:T(8,128)(2,1)}), bf16[16,112,896]{2,1,0:T(8,128)(2,1)}, u32[]{:S(2)}, u32[]{:S(2)}) async-start(bf16[16,112,896]{2,1,0:T(8,128)(2,1)} %copy-done.1), calls=%async_computation.2 | async-start | bytes 6422528 | tf_op jit(solution)/shard_map/all_to_all | solution.py:353
  104.6 20.1 %collective-permute-start.3 = (f32[30,896]{1,0:T(8,128)S(1)}, f32[30,896]{1,0:T(8,128)S(1)}, u32[]{:S(2)}, u32[]{:S(2)}) collective-permute-start(f32[30,896]{1,0:T(8,128)S(1)} %get-tuple-element.62), channel_id=1, source_target_pairs={{0,1},{1,2},{2,3},{3,0},{4,5},{5,6},{6,7},{7,4},{8,9},{9,10},{10,1... | collective-permute-start | bytes 322568 | tf_op jit(solution)/shard_map/ppermute | solution.py:361
  112.6 25.0 %collective-permute-start.4 = (f32[30,896]{1,0:T(8,128)S(1)}, f32[30,896]{1,0:T(8,128)S(1)}, u32[]{:S(2)}, u32[]{:S(2)}) collective-permute-start(f32[30,896]{1,0:T(8,128)S(1)} %get-tuple-element.63), channel_id=1, source_target_pairs={{0,2},{1,3},{2,0},{3,1},{4,6},{5,7},{6,4},{7,5},{8,10},{9,11},{10,... | collective-permute-start | bytes 322568 | tf_op jit(solution)/shard_map/ppermute | solution.py:361
  117.8 24.6 %collective-permute-start.5 = (f32[30,896]{1,0:T(8,128)S(1)}, f32[30,896]{1,0:T(8,128)S(1)}, u32[]{:S(2)}, u32[]{:S(2)}) collective-permute-start(f32[30,896]{1,0:T(8,128)S(1)} %get-tuple-element.64), channel_id=1, source_target_pairs={{0,3},{1,0},{2,1},{3,2},{4,7},{5,4},{6,5},{7,6},{8,11},{9,8},{10,9... | collective-permute-start | bytes 322568 | tf_op jit(solution)/shard_map/ppermute | solution.py:361
  175.1 12.7 %copy-start.6 = (f32[2,256,1]{2,1,0:T(8,128)S(1)}, f32[2,256,1]{2,1,0:T(8,128)}, u32[]{:S(2)}) copy-start(f32[2,256,1]{2,1,0:T(8,128)} %copy-done.5) | copy-start | bytes 6148
  175.1 12.8 %copy-start.8 = (f32[2,256,1]{2,1,0:T(8,128)S(1)}, f32[2,256,1]{2,1,0:T(8,128)}, u32[]{:S(2)}) copy-start(f32[2,256,1]{2,1,0:T(8,128)} %copy-done.7) | copy-start | bytes 6148
  175.2 14.8 %copy-start.13 = (bf16[2,4,16,896]{3,2,1,0:T(8,128)(2,1)S(1)}, bf16[2,4,16,896]{3,2,1,0:T(8,128)(2,1)}, u32[]{:S(2)}) copy-start(bf16[2,4,16,896]{3,2,1,0:T(8,128)(2,1)} %copy-done.12) | copy-start | bytes 688132
  176.2 23.6 %all-to-all-start.4 = ((bf16[16,28,896]{2,1,0:T(8,128)(2,1)}), bf16[16,28,896]{2,1,0:T(8,128)(2,1)S(1)}, u32[]{:S(2)}, u32[]{:S(2)}) async-start(bf16[16,28,896]{2,1,0:T(8,128)(2,1)} %broadcast_in_dim.23), calls=%async_computation.4 | async-start | bytes 1835008 | tf_op jit(solution)/shard_map/all_to_all | solution.py:388
  190.0 1.9 copy-start.2
  191.9 1.5 copy-start.4
  199.1 0.7 copy-start.17
  200.0 10.5 %collective-permute-start.7 = (bf16[16,28,896]{2,0,1:T(8,128)(2,1)S(1)}, bf16[16,28,896]{2,0,1:T(8,128)(2,1)S(1)}, u32[]{:S(2)}, u32[]{:S(2)}) collective-permute-start(bf16[16,28,896]{2,0,1:T(8,128)(2,1)S(1)} %copy.22), channel_id=1, source_target_pairs={{0,16},{16,0},{1,17},{17,1},{2,18},{18,2},{3,19},{19,3},{4,20},{20... | collective-permute-start | bytes 2408456 | tf_op jit(solution)/shard_map/ppermute | solution.py:38
  205.9 3.6 %collective-permute-start.6 = (bf16[256,448]{1,0:T(8,128)(2,1)}, bf16[256,448]{1,0:T(8,128)(2,1)S(1)}, u32[]{:S(2)}, u32[]{:S(2)}) collective-permute-start(bf16[256,448]{1,0:T(8,128)(2,1)} %copy-done.17), channel_id=1, source_target_pairs={{0,16},{16,0},{1,17},{17,1},{2,18},{18,2},{3,19},{19,3},{4,20},{20... | collective-permute-start | bytes 688136 | tf_op jit(solution)/shard_map/ppermute | solution.py:38
Sparse Core Ops, SparseCore 0:
  10.1 55.9 all-gather.3
  88.7 95.7 all-gather.5

commit v7 on v6

--- a/solution.py
+++ b/solution.py
@@ -300,8 +300,13 @@
     w_mine = lax.dynamic_slice(o_weight, (w_start, 0), (W_ROWS, COLS))
     w_moved = lax.ppermute(
         w_mine,
-        ("x", "r"),
-        [(i * NR + (j + i) % NR, i * NR + j) for i in range(NX) for j in range(NR)],
+        ("x", "c", "r"),
+        [
+            ((i * NC + k) * NR + (j + i + 2 * k) % NR, (i * NC + k) * NR + j)
+            for i in range(NX)
+            for k in range(NC)
+            for j in range(NR)
+        ],
     )
     attn_keep = jnp.where(ic == 0, attn[:, :HALF], attn[:, HALF:])
     attn_give = jnp.where(ic == 0, attn[:, HALF:], attn[:, :HALF])
@@ -341,6 +346,8 @@
 
     other_index = dp_index + 1 - 2 * ic
     state_other = swap_core(state_all)
+    got, w_moved = lax.optimization_barrier((got, w_moved))
+    w_all = lax.all_gather(w_moved, PLANE).reshape(NX, HALF, COLS)
     scaled, first, gain_part, loss_part, pieces, scale, first_col = group_math(
         jnp.stack([dp_index, other_index]), got.transpose(1, 0, 2), gain
     )
@@ -348,8 +355,7 @@
     partial, coef = weight_partials(
         state_all, state_other, attn_keep, attn_other, pieces, scale
     )
-    partial, first, w_moved = lax.optimization_barrier((partial, first, w_moved))
-    w_all = lax.all_gather(w_moved, PLANE).reshape(NX, HALF, COLS)
+    partial, first = lax.optimization_barrier((partial, first))
     spread = lax.all_to_all(partial, PLANE, 0, 0)
 
     gain_mine = lax.dynamic_index_in_dim(gain_part, it, 0, keepdims=False)
@@ -379,21 +385,22 @@
     state_grad = first_col[0].reshape(2, SEQ, 1) * row_here - states * coef[0].reshape(2, SEQ, 1)
     grad_hidden = state_grad.astype(bf16).reshape(1, 2, SEQ, FEAT)
     keep, give = attn_grads(
-        ir.reshape(1), state_all, state_other, pieces, w_all, coef, first_col
-    )
-
+        (ir + 2 * ic).reshape(1), state_all, state_other, pieces, w_all, coef, first_col
+    )
+
+    second, keep, give = lax.optimization_barrier((second, keep, give))
     second_sum = jnp.sum(second.astype(f32), 0)
     total = first_sum - second_sum
     done = jnp.broadcast_to(total.astype(bf16)[None], (NX * NY, SLICE, COLS))
     half = lax.all_to_all(done, PLANE, 0, 0)
-    half, keep, give, grad_hidden, totals = lax.optimization_barrier(
-        (half, keep, give, grad_hidden, totals)
-    )
-    half_other = swap_core(half)
     arrived = swap_core(give)
     grad_attn = jnp.where(
         ic == 0, jnp.concatenate([keep, arrived], 1), jnp.concatenate([arrived, keep], 1)
     ).reshape(1, 2, SEQ, FEAT)
+    half, grad_attn, grad_hidden, totals = lax.optimization_barrier(
+        (half, grad_attn, grad_hidden, totals)
+    )
+    half_other = swap_core(half)
     grad_weight = join_halves(ic.reshape(1), half, half_other)
     return (grad_hidden, grad_attn, grad_weight, totals[0], totals[1, 0])
 

time: 220 us -> 221 us (level)
  the two profiles are of different devices: /device:TPU:1 before, /device:TPU:33 now
where the time goes in v7:
time: 221 us; the launch traced here: 219 us
  starting transfers between devices  85.4 us (39%)
  waiting for transfers between devices  54.8 us (25%)
  local copies, waits for them, and re-layouts  26 us (12%)
  Pallas kernels  19.2 us (9%)
  between operations  15.3 us (7%)
  other arithmetic  10.9 us (5%)
  blocking collectives  7.5 us (3%)
    ppermute x4, starting transfers between devices, swap_core(): return lax.ppermute(value, 'c', [(0, 1), (1, 0)])  19.4 us
    ppermute x3, waiting for transfers between devices, body(): lax.ppermute(jnp.concatenate([outgoing, tail], 0), 'r', [(j, (j + step) %...  18 us
    ppermute x3, starting transfers between devices, body(): lax.ppermute(jnp.concatenate([outgoing, tail], 0), 'r', [(j, (j + step) %...  14.5 us
    ppermute x1, starting transfers between devices, body(): lax.ppermute(w_mine, ('x', 'c', 'r'), [((i * NC + k) * NR + (j + i + 2 *...  13.5 us
    unnamed x50, local copies, waits for them, and re-layouts  13.4 us
    ppermute x1, waiting for transfers between devices, body(): lax.ppermute(w_mine, ('x', 'c', 'r'), [((i * NC + k) * NR + (j + i + 2 *...  13.2 us
    all_to_all x1, starting transfers between devices, body(): got = lax.all_to_all(send, DP, 0, 0)  10.9 us
    all_to_all x1, starting transfers between devices, body(): half = lax.all_to_all(done, PLANE, 0, 0)  9.12 us
  transfers between devices with their start and end apart: 15, of which 8 were waited for; matrix products, arithmetic and copies ran while one was open for 10% of the time, Pallas kernels for 8%

profile of v7, /device:TPU:33, one launch (start us, length us, event | category | flops | bytes accessed | tf_op | source)
XLA Modules:
  0.0 219.1 jit_solution(10958411086934800951)
XLA Ops:
  8.6 1.2 fusion.2
  9.8 7.5 %psum.7 = f32[2,128]{1,0:T(2,128)S(1)} all-reduce(f32[2,128]{1,0:T(2,128)S(1)} %fusion.2), channel_id=1, replica_groups=mesh['x'=4,'y'=4,'c'=2,'t'=4,'r'=4] {'t'}, use_global_device_ids=true, to_apply=%region_1.2 | all-reduce | flops 256 | bytes 2048 | tf_op jit(solution)/shard_map/psum | solution.py:316
  17.3 0.7 convert_bitcast_fusion.1
  18.8 1.4 fusion.6
  20.8 6.5 %all-to-all-start = ((f32[4,3,896]{2,1,0:T(4,128)}), f32[4,3,896]{2,1,0:T(4,128)S(1)}, u32[]{:S(2)}, u32[]{:S(2)}) async-start(f32[4,3,896]{2,1,0:T(4,128)} %broadcast_in_dim.17), calls=%async_computation | async-start | bytes 114688 | tf_op jit(solution)/shard_map/all_to_all | solution.py:325
  28.3 2.8 %all-to-all-done = f32[4,3,896]{2,1,0:T(4,128)S(1)} async-done(((f32[4,3,896]{2,1,0:T(4,128)}), f32[4,3,896]{2,1,0:T(4,128)S(1)}, u32[]{:S(2)}, u32[]{:S(2)}) %all-to-all-start) | async-done | bytes 43040 | tf_op jit(solution)/shard_map/all_to_all | solution.py:325
  31.4 2.2 %concatenate.50 = f32[32,2,3840]{2,1,0:T(2,128)} concatenate(f32[32,2,3712]{2,1,0:T(2,128)S(1)} %broadcast_in_dim.18, f32[32,2,28]{2,1,0:T(2,128)S(1)} %copy.20, f32[32,2,2]{2,1,0:T(2,128)S(1)} %broadcast_in_dim.19, f32[32,2,98]{2,1,0:T(2,128)S(1)} %broadcast_in_dim.20), dimensions={2} | concatenate | bytes 1966080 | tf_op jit(solution)/shard_map/concatenate | solution.py:335
  33.7 10.9 %all-to-all-start.1 = ((f32[32,2,3840]{2,1,0:T(2,128)}), f32[32,2,3840]{2,1,0:T(2,128)S(1)}, u32[]{:S(2)}, u32[]{:S(2)}) async-start(f32[32,2,3840]{2,1,0:T(2,128)} %concatenate.50), calls=%async_computation.1 | async-start | bytes 1966080 | tf_op jit(solution)/shard_map/all_to_all | solution.py:344
  44.7 0.9 broadcast_select_fusion
  45.6 2.1 collective-permute-start
  48.5 13.5 %collective-permute-start.2 = (bf16[112,896]{1,0:T(8,128)(2,1)}, bf16[112,896]{1,0:T(8,128)(2,1)}, u32[]{:S(2)}, u32[]{:S(2)}) collective-permute-start(bf16[112,896]{1,0:T(8,128)(2,1)} %constant_dynamic-slice_fusion.1), channel_id=1, source_target_pairs={{0,0},{1,1},{2,2},{3,3},{18,16},{19,17},{16,18},{17,19},{129,128},... | collective-permute-start | bytes 602120 | tf_op jit(solution)/shard_map/ppermute | solution.py:301
  62.7 0.9 copy-done.21
  63.7 2.0 all-gather.4.cloned.1.call-done.own_ref
  65.7 13.2 %collective-permute-done.2 = bf16[112,896]{1,0:T(8,128)(2,1)} collective-permute-done((bf16[112,896]{1,0:T(8,128)(2,1)}, bf16[112,896]{1,0:T(8,128)(2,1)}, u32[]{:S(2)}, u32[]{:S(2)}) %collective-permute-start.2) | collective-permute-done | bytes 200736 | tf_op jit(solution)/shard_map/ppermute | solution.py:301
  78.9 1.9 collective-permute-start.1
  80.9 1.3 copy.28
  82.2 4.2 %group_math.1 = (f32[2,32,3584]{2,1,0:T(8,128)S(1)}, f32[4,28,896]{2,1,0:T(8,128)S(1)}, f32[4,1,896]{2,1,0:T(1,128)S(1)}, f32[8,128]{1,0:T(8,128)S(1)}, bf16[2,4...) custom-call(s32[2]{0:T(128)S(1)} %pad_add_fusion.index_ref, ...), custom_call_target="tpu_custom_call" | custom-call | flops 183500800 | bytes 3145728 | tf_op jit(solution)/shard_map/group_math/pallas_call | solution.py:124
  87.1 0.8 copy-done.11
  87.9 0.9 copy-done.17
  88.9 5.0 %weight_partials.1 = (bf16[16,112,896]{2,1,0:T(8,128)(2,1)S(1)}, f32[2,256,1]{2,1,0:T(8,128)S(1)}) custom-call(bf16[4,256,896]{2,1,0:T(8,128)(2,1)S(1)} %copy-done.3, bf16[4,256,896]{2,1,0:T(8,128)(2,1)} %collective-permute-done.1.other_ref, bf16[256,448]{1,0:T(8,128)(2,1)S(1)} %copy-done.14, bf16[256,448]{1,0:T(8,128)(2,1)S(1)} %copy-done.19, ...), custom_call_target="tpu_custom_call" | custom-call | flops 1644167168 | bytes 8388608 | tf_op jit(solution)/shard_map/weight_partials/pallas_call | solution.py:178
  93.9 1.7 copy-done.1
  96.3 7.2 %all-to-all-start.2 = ((bf16[16,112,896]{2,1,0:T(8,128)(2,1)}), bf16[16,112,896]{2,1,0:T(8,128)(2,1)}, u32[]{:S(2)}, u32[]{:S(2)}) async-start(bf16[16,112,896]{2,1,0:T(8,128)(2,1)} %copy-done.1), calls=%async_computation.2 | async-start | bytes 6422528 | tf_op jit(solution)/shard_map/all_to_all | solution.py:359
  104.9 1.0 dynamic-slice_bitcast_fusion.2
  106.0 5.4 %collective-permute-start.3 = (f32[30,896]{1,0:T(8,128)S(1)}, f32[30,896]{1,0:T(8,128)S(1)}, u32[]{:S(2)}, u32[]{:S(2)}) collective-permute-start(f32[30,896]{1,0:T(8,128)S(1)} %get-tuple-element.68), channel_id=1, source_target_pairs={{0,1},{1,2},{2,3},{3,0},{4,5},{5,6},{6,7},{7,4},{8,9},{9,10},{10,1... | collective-permute-start | bytes 322568 | tf_op jit(solution)/shard_map/ppermute | solution.py:367
  112.1 6.6 %collective-permute-start.4 = (f32[30,896]{1,0:T(8,128)S(1)}, f32[30,896]{1,0:T(8,128)S(1)}, u32[]{:S(2)}, u32[]{:S(2)}) collective-permute-start(f32[30,896]{1,0:T(8,128)S(1)} %get-tuple-element.69), channel_id=1, source_target_pairs={{0,2},{1,3},{2,0},{3,1},{4,6},{5,7},{6,4},{7,5},{8,10},{9,11},{10,... | collective-permute-start | bytes 322568 | tf_op jit(solution)/shard_map/ppermute | solution.py:367
  118.7 2.4 %collective-permute-start.5 = (f32[30,896]{1,0:T(8,128)S(1)}, f32[30,896]{1,0:T(8,128)S(1)}, u32[]{:S(2)}, u32[]{:S(2)}) collective-permute-start(f32[30,896]{1,0:T(8,128)S(1)} %get-tuple-element.70), channel_id=1, source_target_pairs={{0,3},{1,0},{2,1},{3,2},{4,7},{5,4},{6,5},{7,6},{8,11},{9,8},{10,9... | collective-permute-start | bytes 322568 | tf_op jit(solution)/shard_map/ppermute | solution.py:367
  121.2 14.7 %collective-permute-done.4 = f32[30,896]{1,0:T(8,128)S(1)} collective-permute-done((f32[30,896]{1,0:T(8,128)S(1)}, f32[30,896]{1,0:T(8,128)S(1)}, u32[]{:S(2)}, u32[]{:S(2)}) %collective-permute-start.4) | collective-permute-done | bytes 107552 | tf_op jit(solution)/shard_map/ppermute | solution.py:367
  135.9 3.2 %collective-permute-done.5 = f32[30,896]{1,0:T(8,128)S(1)} collective-permute-done((f32[30,896]{1,0:T(8,128)S(1)}, f32[30,896]{1,0:T(8,128)S(1)}, u32[]{:S(2)}, u32[]{:S(2)}) %collective-permute-start.5) | collective-permute-done | bytes 107552 | tf_op jit(solution)/shard_map/ppermute | solution.py:367
  139.8 0.9 slice_add_fusion
  140.7 8.8 %all-to-all-done.2.spread_ref = bf16[16,112,896]{2,1,0:T(8,128)(2,1)} async-done(((bf16[16,112,896]{2,1,0:T(8,128)(2,1)}), bf16[16,112,896]{2,1,0:T(8,128)(2,1)}, u32[]{:S(2)}, u32[]{:S(2)}) %all-to-all-start.2) | async-done | bytes 3211296 | tf_op jit(solution)/shard_map/all_to_all | solution.py:359
  149.5 3.0 %sum_senders.1 = bf16[4,28,896]{2,1,0:T(8,128)(2,1)S(1)} custom-call(bf16[16,112,896]{2,1,0:T(8,128)(2,1)} %all-to-all-done.2.spread_ref), custom_call_target="tpu_custom_call" | custom-call | flops 1605632 | bytes 4194304 | tf_op jit(solution)/shard_map/sum_senders/pallas_call | solution.py:216
  153.2 4.2 %all-to-all-start.3 = ((bf16[4,28,896]{2,1,0:T(8,128)(2,1)}), bf16[4,28,896]{2,1,0:T(8,128)(2,1)}, u32[]{:S(2)}, u32[]{:S(2)}) async-start(bf16[4,28,896]{2,1,0:T(8,128)(2,1)} %copy-done.4), calls=%async_computation.3 | async-start | bytes 458752 | tf_op jit(solution)/shard_map/all_to_all | solution.py:382
  157.4 8.6 %all-gather.6.cloned.1.call-done = bf16[1792,896]{1,0:T(8,128)(2,1)} async-done(((bf16[112,896]{1,0:T(8,128)(2,1)}), bf16[1792,896]{1,0:T(8,128)(2,1)}) %all-gather.6.cloned.1.call-update) | async-done | bytes 3211280 | tf_op jit(solution)/shard_map/all_gather | solution.py:350
  166.0 1.9 copy-done.2
  167.9 0.9 copy-done.6
  168.8 0.9 copy-done.9
  169.8 0.9 copy-done.16
  170.7 5.6 %attn_grads.1 = (bf16[256,448]{1,0:T(8,128)(2,1)S(1)}, bf16[256,448]{1,0:T(8,128)(2,1)S(1)}) custom-call(s32[1]{0:T(128)} %bitcast.26.shift_ref, bf16[4,256,896]{2,1,0:T(8,128)(2,1)S(1)} %copy-done.3, bf16[4,256,896]{2,1,0:T(8,128)(2,1)} %collective-permute-done.1.other_ref, bf16[2,4,16,896]{3,2,1,0:T(8,128)(2,1)S(1)} %copy-done.16, ...), custom_call_target="tpu_custom_call" | custom-call | flops 1644167168 | bytes 8388608 | tf_op jit(solution)/shard_map/attn_grads/pallas_call | solution.py:278
  177.8 1.0 convert_reduce_fusion
  178.8 1.0 broadcast_in_dim.23
  179.9 9.1 %all-to-all-start.4 = ((bf16[16,28,896]{2,1,0:T(8,128)(2,1)}), bf16[16,28,896]{2,1,0:T(8,128)(2,1)S(1)}, u32[]{:S(2)}, u32[]{:S(2)}) async-start(bf16[16,28,896]{2,1,0:T(8,128)(2,1)} %broadcast_in_dim.23), calls=%async_computation.4 | async-start | bytes 1835008 | tf_op jit(solution)/shard_map/all_to_all | solution.py:395
  189.0 0.9 constant_dynamic-slice_fusion
  190.1 7.5 %collective-permute-start.6 = (bf16[256,448]{1,0:T(8,128)(2,1)}, bf16[256,448]{1,0:T(8,128)(2,1)S(1)}, u32[]{:S(2)}, u32[]{:S(2)}) collective-permute-start(bf16[256,448]{1,0:T(8,128)(2,1)} %copy-done.20), channel_id=1, source_target_pairs={{0,16},{16,0},{1,17},{17,1},{2,18},{18,2},{3,19},{19,3},{4,20},{20... | collective-permute-start | bytes 688136 | tf_op jit(solution)/shard_map/ppermute | solution.py:38
  197.6 2.0 fusion.5
  199.6 1.1 maximum_select_fusion
  200.9 7.8 %collective-permute-start.7 = (bf16[16,28,896]{2,0,1:T(8,128)(2,1)S(1)}, bf16[16,28,896]{2,0,1:T(8,128)(2,1)S(1)}, u32[]{:S(2)}, u32[]{:S(2)}) collective-permute-start(bf16[16,28,896]{2,0,1:T(8,128)(2,1)S(1)} %copy.22), channel_id=1, source_target_pairs={{0,16},{16,0},{1,17},{17,1},{2,18},{18,2},{3,19},{19,3},{4,20},{20... | collective-permute-start | bytes 2408456 | tf_op jit(solution)/shard_map/ppermute | solution.py:38
  209.9 0.8 collective-permute-done.7
  210.8 1.4 join_halves.1
  (86 shorter events, 12.8 us)
Async XLA Ops:
  7.2 40.6 %copy-start = (bf16[896,896]{1,0:T(8,128)(2,1)S(1)}, bf16[896,896]{1,0:T(8,128)(2,1)}, u32[]{:S(2)}) copy-start(bf16[896,896]{1,0:T(8,128)(2,1)} %param.8) | copy-start | bytes 4816900
  7.2 58.5 %all-gather.4.cloned.1.call-start = ((), (), s32[]{:S(2)}) async-start(), calls=%async_computation.5 | async-start | bytes 2293760 | tf_op jit(solution)/shard_map/all_gather | solution.py:298
  20.8 10.2 %all-to-all-start = ((f32[4,3,896]{2,1,0:T(4,128)}), f32[4,3,896]{2,1,0:T(4,128)S(1)}, u32[]{:S(2)}, u32[]{:S(2)}) async-start(f32[4,3,896]{2,1,0:T(4,128)} %broadcast_in_dim.17), calls=%async_computation | async-start | bytes 114688 | tf_op jit(solution)/shard_map/all_to_all | solution.py:325
  31.4 13.2 %copy-start.22 = (bf16[1,2,128,896]{3,2,1,0:T(8,128)(2,1)S(1)}, bf16[1,2,128,896]{3,2,1,0:T(8,128)(2,1)}, u32[]{:S(2)}) copy-start(bf16[1,2,128,896]{3,2,1,0:T(8,128)(2,1)} %param.7) | copy-start | bytes 1376260
  33.7 29.1 %all-to-all-start.1 = ((f32[32,2,3840]{2,1,0:T(2,128)}), f32[32,2,3840]{2,1,0:T(2,128)S(1)}, u32[]{:S(2)}, u32[]{:S(2)}) async-start(f32[32,2,3840]{2,1,0:T(2,128)} %concatenate.50), calls=%async_computation.1 | async-start | bytes 1966080 | tf_op jit(solution)/shard_map/all_to_all | solution.py:344
  44.6 121.4 %all-gather.6.cloned.1.call-start = ((), (), s32[]{:S(2)}) async-start(), calls=%async_computation.6 | async-start | bytes 3411968 | tf_op jit(solution)/shard_map/all_gather | solution.py:350
  45.6 16.4 %collective-permute-start = (bf16[256,448]{1,0:T(8,128)(2,1)}, bf16[256,448]{1,0:T(8,128)(2,1)S(1)}, u32[]{:S(2)}, u32[]{:S(2)}) collective-permute-start(bf16[256,448]{1,0:T(8,128)(2,1)} %get-tuple-element.67), channel_id=1, source_target_pairs={{0,16},{16,0},{1,17},{17,1},{2,18},{18,2},{3,19},{19,3},{4,20},{20... | collective-permute-start | bytes 688136 | tf_op jit(solution)/shard_map/ppermute | solution.py:38
  48.5 30.4 %collective-permute-start.2 = (bf16[112,896]{1,0:T(8,128)(2,1)}, bf16[112,896]{1,0:T(8,128)(2,1)}, u32[]{:S(2)}, u32[]{:S(2)}) collective-permute-start(bf16[112,896]{1,0:T(8,128)(2,1)} %constant_dynamic-slice_fusion.1), channel_id=1, source_target_pairs={{0,0},{1,1},{2,2},{3,3},{18,16},{19,17},{16,18},{17,19},{129,128},... | collective-permute-start | bytes 602120 | tf_op jit(solution)/shard_map/ppermute | solution.py:301
  62.0 0.7 copy-start.18
  62.7 0.9 copy-start.21
  65.7 23.2 %copy-start.3 = (bf16[4,256,896]{2,1,0:T(8,128)(2,1)S(1)}, bf16[4,256,896]{2,1,0:T(8,128)(2,1)}, u32[]{:S(2)}) copy-start(bf16[4,256,896]{2,1,0:T(8,128)(2,1)} %all-gather.4.cloned.1.call-done.own_ref) | copy-start | bytes 5505028
  78.9 10.0 %collective-permute-start.1 = (bf16[4,256,896]{2,1,0:T(8,128)(2,1)}, bf16[4,256,896]{2,1,0:T(8,128)(2,1)}, u32[]{:S(2)}, u32[]{:S(2)}) collective-permute-start(bf16[4,256,896]{2,1,0:T(8,128)(2,1)} %all-gather.4.cloned.1.call-done.own_ref), channel_id=1, source_target_pairs={{0,16},{16,0},{1,17},{17,1},{2,18},{18,2},{3,19},{19,3},{4,20},{20... | collective-permute-start | bytes 5505032 | tf_op jit(solution)/shard_map/ppermute | solution.py:38
  80.8 8.0 %copy-start.14 = (bf16[256,448]{1,0:T(8,128)(2,1)S(1)}, bf16[256,448]{1,0:T(8,128)(2,1)}, u32[]{:S(2)}) copy-start(bf16[256,448]{1,0:T(8,128)(2,1)} %get-tuple-element.66.keep_ref) | copy-start | bytes 688132
  80.8 8.0 %copy-start.19 = (bf16[256,448]{1,0:T(8,128)(2,1)S(1)}, bf16[256,448]{1,0:T(8,128)(2,1)}, u32[]{:S(2)}) copy-start(bf16[256,448]{1,0:T(8,128)(2,1)} %copy-done.18) | copy-start | bytes 688132
  86.4 0.7 copy-start.5
  87.1 0.8 copy-start.11
  87.9 0.9 copy-start.17
  88.8 5.1 %copy-start.15 = (bf16[2,4,16,896]{3,2,1,0:T(8,128)(2,1)}, bf16[2,4,16,896]{3,2,1,0:T(8,128)(2,1)S(1)}, u32[]{:S(2)}) copy-start(bf16[2,4,16,896]{3,2,1,0:T(8,128)(2,1)S(1)} %get-tuple-element.37.pieces_ref) | copy-start | bytes 688132
  93.9 1.7 copy-start.1
  95.6 0.7 copy-start.8
  96.3 53.2 %all-to-all-start.2 = ((bf16[16,112,896]{2,1,0:T(8,128)(2,1)}), bf16[16,112,896]{2,1,0:T(8,128)(2,1)}, u32[]{:S(2)}, u32[]{:S(2)}) async-start(bf16[16,112,896]{2,1,0:T(8,128)(2,1)} %copy-done.1), calls=%async_computation.2 | async-start | bytes 6422528 | tf_op jit(solution)/shard_map/all_to_all | solution.py:359
  106.0 15.1 %collective-permute-start.3 = (f32[30,896]{1,0:T(8,128)S(1)}, f32[30,896]{1,0:T(8,128)S(1)}, u32[]{:S(2)}, u32[]{:S(2)}) collective-permute-start(f32[30,896]{1,0:T(8,128)S(1)} %get-tuple-element.68), channel_id=1, source_target_pairs={{0,1},{1,2},{2,3},{3,0},{4,5},{5,6},{6,7},{7,4},{8,9},{9,10},{10,1... | collective-permute-start | bytes 322568 | tf_op jit(solution)/shard_map/ppermute | solution.py:367
  112.1 23.8 %collective-permute-start.4 = (f32[30,896]{1,0:T(8,128)S(1)}, f32[30,896]{1,0:T(8,128)S(1)}, u32[]{:S(2)}, u32[]{:S(2)}) collective-permute-start(f32[30,896]{1,0:T(8,128)S(1)} %get-tuple-element.69), channel_id=1, source_target_pairs={{0,2},{1,3},{2,0},{3,1},{4,6},{5,7},{6,4},{7,5},{8,10},{9,11},{10,... | collective-permute-start | bytes 322568 | tf_op jit(solution)/shard_map/ppermute | solution.py:367
  118.7 20.4 %collective-permute-start.5 = (f32[30,896]{1,0:T(8,128)S(1)}, f32[30,896]{1,0:T(8,128)S(1)}, u32[]{:S(2)}, u32[]{:S(2)}) collective-permute-start(f32[30,896]{1,0:T(8,128)S(1)} %get-tuple-element.70), channel_id=1, source_target_pairs={{0,3},{1,0},{2,1},{3,2},{4,7},{5,4},{6,5},{7,6},{8,11},{9,8},{10,9... | collective-permute-start | bytes 322568 | tf_op jit(solution)/shard_map/ppermute | solution.py:367
  152.5 0.7 copy-start.4
  153.2 24.6 %all-to-all-start.3 = ((bf16[4,28,896]{2,1,0:T(8,128)(2,1)}), bf16[4,28,896]{2,1,0:T(8,128)(2,1)}, u32[]{:S(2)}, u32[]{:S(2)}) async-start(bf16[4,28,896]{2,1,0:T(8,128)(2,1)} %copy-done.4), calls=%async_computation.3 | async-start | bytes 458752 | tf_op jit(solution)/shard_map/all_to_all | solution.py:382
  166.0 1.9 copy-start.2
  167.9 0.9 copy-start.6
  168.8 0.9 copy-start.9
  169.8 0.9 copy-start.16
  176.4 0.7 copy-start.12
  177.1 0.7 copy-start.20
  177.8 12.1 %copy-start.7 = (f32[2,256,1]{2,1,0:T(8,128)S(1)}, f32[2,256,1]{2,1,0:T(8,128)}, u32[]{:S(2)}) copy-start(f32[2,256,1]{2,1,0:T(8,128)} %copy-done.5) | copy-start | bytes 6148
  177.8 12.3 %copy-start.10 = (f32[2,256,1]{2,1,0:T(8,128)S(1)}, f32[2,256,1]{2,1,0:T(8,128)}, u32[]{:S(2)}) copy-start(f32[2,256,1]{2,1,0:T(8,128)} %copy-done.8) | copy-start | bytes 6148
  178.8 20.8 %copy-start.13 = (bf16[256,448]{1,0:T(8,128)(2,1)S(1)}, bf16[256,448]{1,0:T(8,128)(2,1)}, u32[]{:S(2)}) copy-start(bf16[256,448]{1,0:T(8,128)(2,1)} %copy-done.12) | copy-start | bytes 688132
  179.9 20.8 %all-to-all-start.4 = ((bf16[16,28,896]{2,1,0:T(8,128)(2,1)}), bf16[16,28,896]{2,1,0:T(8,128)(2,1)S(1)}, u32[]{:S(2)}, u32[]{:S(2)}) async-start(bf16[16,28,896]{2,1,0:T(8,128)(2,1)} %broadcast_in_dim.23), calls=%async_computation.4 | async-start | bytes 1835008 | tf_op jit(solution)/shard_map/all_to_all | solution.py:395
  190.1 18.6 %copy-start.23 = (f32[2,896]{1,0:T(2,128)S(1)}, f32[2,896]{1,0:T(2,128)}, u32[]{:S(2)}) copy-start(f32[2,896]{1,0:T(2,128)} %add_bitcast_fusion) | copy-start | bytes 21508
  190.1 9.5 %collective-permute-start.6 = (bf16[256,448]{1,0:T(8,128)(2,1)}, bf16[256,448]{1,0:T(8,128)(2,1)S(1)}, u32[]{:S(2)}, u32[]{:S(2)}) collective-permute-start(bf16[256,448]{1,0:T(8,128)(2,1)} %copy-done.20), channel_id=1, source_target_pairs={{0,16},{16,0},{1,17},{17,1},{2,18},{18,2},{3,19},{19,3},{4,20},{20... | collective-permute-start | bytes 688136 | tf_op jit(solution)/shard_map/ppermute | solution.py:38
  200.9 9.8 %collective-permute-start.7 = (bf16[16,28,896]{2,0,1:T(8,128)(2,1)S(1)}, bf16[16,28,896]{2,0,1:T(8,128)(2,1)S(1)}, u32[]{:S(2)}, u32[]{:S(2)}) collective-permute-start(bf16[16,28,896]{2,0,1:T(8,128)(2,1)S(1)} %copy.22), channel_id=1, source_target_pairs={{0,16},{16,0},{1,17},{17,1},{2,18},{18,2},{3,19},{19,3},{4,20},{20... | collective-permute-start | bytes 2408456 | tf_op jit(solution)/shard_map/ppermute | solution.py:38
Sparse Core Ops, SparseCore 0:
  10.1 55.5 all-gather.3
  79.0 86.9 all-gather.5

commit v8 on v7

--- a/solution.py
+++ b/solution.py
@@ -142,29 +142,30 @@
     )(index, got, gain)
 
 
-def weight_kernel(
-    own_ref, other_ref, keep_ref, given_ref, pieces_ref, scale_ref, out_ref, coef_ref, acc_ref
-):
+def weight_kernel(index_ref, *refs):
+    states, (keep_ref, given_ref, pieces_ref, scale_ref) = refs[: 2 * NT], refs[2 * NT : 2 * NT + 4]
+    out_ref, coef_ref, acc_ref = refs[2 * NT + 4 :]
+    blocks = [lax.rem(index_ref[0] + NT - step, NT) for step in range(NT)]
     token = lax.broadcasted_iota(jnp.int32, (TOK, PIECES), 0)
     part = lax.broadcasted_iota(jnp.int32, (TOK, PIECES), 1)
     part = part - jnp.where(token < SEQ, 0, 3)
     mask = (part >= 0) & (part < 3)
     scaled = []
-    for pair, (state_ref, attn_ref) in enumerate(
-        ((own_ref, keep_ref), (other_ref, given_ref))
-    ):
+    for pair, attn_ref in enumerate((keep_ref, given_ref)):
         inner = jnp.zeros((TOK, PIECES), f32)
-        for block in range(NT):
-            inner = inner + dot_last(state_ref[block], pieces_ref[pair, block])
+        for step in range(NT):
+            inner = inner + dot_last(
+                states[pair * NT + step][...], pieces_ref[pair, blocks[step]]
+            )
         inner = jnp.sum(jnp.where(mask, inner, 0.0), -1, keepdims=True)
         coef = scale_ref[pair] * inner
         coef_ref[pair] = coef
         scaled.append((attn_ref[...].astype(f32) * coef).astype(bf16))
-    for block in range(NT):
-        acc_ref[block] = lax.dot_general(
-            scaled[0], own_ref[block], contract_first, preferred_element_type=f32
+    for step in range(NT):
+        acc_ref[blocks[step]] = lax.dot_general(
+            scaled[0], states[step][...], contract_first, preferred_element_type=f32
         ) + lax.dot_general(
-            scaled[1], other_ref[block], contract_first, preferred_element_type=f32
+            scaled[1], states[NT + step][...], contract_first, preferred_element_type=f32
         )
     for place in range(NX * NY):
         rows = [
@@ -173,7 +174,7 @@
         out_ref[place] = jnp.concatenate(rows, 0).astype(bf16)
 
 
-def weight_partials(own, other, keep, given, pieces, scale):
+def weight_partials(index, states, keep, given, pieces, scale):
     spec = pl.BlockSpec(memory_space=pltpu.VMEM)
     return pl.pallas_call(
         weight_kernel,
@@ -181,7 +182,7 @@
             jax.ShapeDtypeStruct((NX * NY, NR * SLICE, COLS), bf16),
             jax.ShapeDtypeStruct((NC, TOK, 1), f32),
         ),
-        in_specs=[spec] * 6,
+        in_specs=[pl.BlockSpec(memory_space=pltpu.SMEM)] + [spec] * (2 * NT + 4),
         out_specs=(spec, spec),
         scratch_shapes=[pltpu.VMEM((NR, HALF, COLS), f32)],
         compiler_params=pltpu.CompilerParams(vmem_limit_bytes=24 * 1024 * 1024),
@@ -189,7 +190,7 @@
             flops=4 * TOK * HALF * D, bytes_accessed=8 * 1024 * 1024, transcendentals=0
         ),
         name="weight_partials",
-    )(own, other, keep, given, pieces, scale)
+    )(index, *states, keep, given, pieces, scale)
 
 
 def sum_kernel(spread_ref, out_ref, acc_ref):
@@ -252,17 +253,17 @@
     )(core, mine, other)
 
 
-def attn_kernel(
-    shift_ref, own_ref, other_ref, pieces_ref, w_ref, coef_ref, first_ref, keep_ref, give_ref
-):
-    shift = shift_ref[0]
-    for pair, (state_ref, out_ref) in enumerate(((own_ref, keep_ref), (other_ref, give_ref))):
+def attn_kernel(index_ref, *refs):
+    states, (pieces_ref, w_ref, coef_ref, first_ref) = refs[: 2 * NT], refs[2 * NT : 2 * NT + 4]
+    blocks = [lax.rem(index_ref[0] + NT - step, NT) for step in range(NT)]
+    places = [lax.rem(blocks[step] + 2 * NR - index_ref[1], NR) for step in range(NT)]
+    for pair, out_ref in enumerate(refs[2 * NT + 4 :]):
         tokens = jnp.zeros((TOK, HALF), f32)
         rows = jnp.zeros((PIECES, HALF), f32)
-        for block in range(NX):
-            which = lax.rem(shift + block, NR)
-            tokens = tokens + dot_last(state_ref[which], w_ref[block])
-            rows = rows + dot_last(pieces_ref[pair, which], w_ref[block])
+        for step in range(NT):
+            weight = w_ref[places[step]]
+            tokens = tokens + dot_last(states[pair * NT + step][...], weight)
+            rows = rows + dot_last(pieces_ref[pair, blocks[step]], weight)
         for side in range(2):
             row = rows[3 * side + 2 : 3 * side + 3] + rows[3 * side + 1 : 3 * side + 2]
             row = row + rows[3 * side : 3 * side + 1]
@@ -272,20 +273,20 @@
             ).astype(bf16)
 
 
-def attn_grads(shift, own, other, pieces, w_all, coef, first):
+def attn_grads(index, states, pieces, w_all, coef, first):
     spec = pl.BlockSpec(memory_space=pltpu.VMEM)
     out = jax.ShapeDtypeStruct((TOK, HALF), bf16)
     return pl.pallas_call(
         attn_kernel,
         out_shape=(out, out),
-        in_specs=[pl.BlockSpec(memory_space=pltpu.SMEM)] + [spec] * 6,
+        in_specs=[pl.BlockSpec(memory_space=pltpu.SMEM)] + [spec] * (2 * NT + 4),
         out_specs=(spec, spec),
         compiler_params=pltpu.CompilerParams(vmem_limit_bytes=24 * 1024 * 1024),
         cost_estimate=pl.CostEstimate(
             flops=4 * TOK * HALF * D, bytes_accessed=8 * 1024 * 1024, transcendentals=0
         ),
         name="attn_grads",
-    )(shift, own, other, pieces, w_all, coef, first)
+    )(index, *states, pieces, w_all, coef, first)
 
 
 def body(hidden_state, attn_out, o_weight, norm_gain, lengths, positive):
@@ -295,7 +296,6 @@
 
     state = hidden_state.reshape(TOK, FEAT)
     attn = attn_out.reshape(TOK, FEAT)
-    state_all = lax.all_gather(state, "t")
     w_start = (ic * NY + iy) * W_ROWS
     w_mine = lax.dynamic_slice(o_weight, (w_start, 0), (W_ROWS, COLS))
     w_moved = lax.ppermute(
@@ -322,7 +322,13 @@
     attn_pool = jnp.sum(pool_weight[..., None] * attn.astype(f32).reshape(2, SEQ, FEAT), 1)
 
     near = jnp.concatenate([pooled, norm_gain[None]], 0)
+    near, w_moved = lax.optimization_barrier((near, w_moved))
+    w_all = lax.all_gather(w_moved, PLANE).reshape(NX, HALF, COLS)
     near = lax.all_to_all(jnp.broadcast_to(near[None], (NT, 3, FEAT)), "t", 0, 0)
+    near, later = lax.optimization_barrier((near, state))
+    own = [state]
+    for step in range(1, NT):
+        own.append(lax.ppermute(later, "t", [(j, (j + step) % NT) for j in range(NT)]))
     pooled_row = near[:, :2].transpose(1, 0, 2).reshape(2, D)
     gain = near[:, 2].reshape(1, D)
 
@@ -342,18 +348,18 @@
         -1,
     )
     got = lax.all_to_all(send, DP, 0, 0)
-    got, state_all, attn_other = lax.optimization_barrier((got, state_all, attn_other))
+    got, attn_other = lax.optimization_barrier((got, attn_other))
 
     other_index = dp_index + 1 - 2 * ic
-    state_other = swap_core(state_all)
-    got, w_moved = lax.optimization_barrier((got, w_moved))
-    w_all = lax.all_gather(w_moved, PLANE).reshape(NX, HALF, COLS)
     scaled, first, gain_part, loss_part, pieces, scale, first_col = group_math(
         jnp.stack([dp_index, other_index]), got.transpose(1, 0, 2), gain
     )
 
+    for step in range(NT - 1, 0, -1):
+        scale, own[step] = lax.optimization_barrier((scale, own[step]))
+    other = [swap_core(block) for block in own]
     partial, coef = weight_partials(
-        state_all, state_other, attn_keep, attn_other, pieces, scale
+        it.reshape(1), own + other, attn_keep, attn_other, pieces, scale
     )
     partial, first = lax.optimization_barrier((partial, first))
     spread = lax.all_to_all(partial, PLANE, 0, 0)
@@ -378,28 +384,25 @@
             tails, (ir - source) % NR, 0, keepdims=False
         )
 
-    spread, first_sum, totals = lax.optimization_barrier((spread, first_sum, totals))
-    second = lax.all_to_all(sum_senders(spread), "r", 0, 0)
-
     row_here = lax.dynamic_slice(scaled, (0, dp_index, it * FEAT), (2, 1, FEAT))
     state_grad = first_col[0].reshape(2, SEQ, 1) * row_here - states * coef[0].reshape(2, SEQ, 1)
     grad_hidden = state_grad.astype(bf16).reshape(1, 2, SEQ, FEAT)
     keep, give = attn_grads(
-        (ir + 2 * ic).reshape(1), state_all, state_other, pieces, w_all, coef, first_col
-    )
-
-    second, keep, give = lax.optimization_barrier((second, keep, give))
+        jnp.stack([it, ir + 2 * ic]), own + other, pieces, w_all, coef, first_col
+    )
+    arrived = swap_core(give)
+    grad_attn = jnp.where(
+        ic == 0, jnp.concatenate([keep, arrived], 1), jnp.concatenate([arrived, keep], 1)
+    ).reshape(1, 2, SEQ, FEAT)
+    spread, first_sum, totals, grad_attn, grad_hidden = lax.optimization_barrier(
+        (spread, first_sum, totals, grad_attn, grad_hidden)
+    )
+    second = lax.all_to_all(sum_senders(spread), "r", 0, 0)
+
     second_sum = jnp.sum(second.astype(f32), 0)
     total = first_sum - second_sum
     done = jnp.broadcast_to(total.astype(bf16)[None], (NX * NY, SLICE, COLS))
     half = lax.all_to_all(done, PLANE, 0, 0)
-    arrived = swap_core(give)
-    grad_attn = jnp.where(
-        ic == 0, jnp.concatenate([keep, arrived], 1), jnp.concatenate([arrived, keep], 1)
-    ).reshape(1, 2, SEQ, FEAT)
-    half, grad_attn, grad_hidden, totals = lax.optimization_barrier(
-        (half, grad_attn, grad_hidden, totals)
-    )
     half_other = swap_core(half)
     grad_weight = join_halves(ic.reshape(1), half, half_other)
     return (grad_hidden, grad_attn, grad_weight, totals[0], totals[1, 0])

time: 221 us -> 245 us (1.11)
  blocking collectives: 7.5 us -> 48.9 us
  waiting for transfers between devices: 54.8 us -> 44.7 us
  starting transfers between devices: 85.4 us -> 79.2 us
  other arithmetic: 10.9 us -> 7.52 us
    all_to_all x0 -> x2, blocking collectives: none -> 38 us  [the longest x1 19.8 us: body(): half = lax.all_to_all(done, PLANE, 0, 0)]
    ppermute x0 -> x3, waiting for transfers between devices: none -> 21.5 us  [body(): lax.ppermute(later, 't', [(j, (j + step) % NT) for j in range(NT)])]
    all_to_all x2 -> x0, starting transfers between devices: 13.3 us -> none  [the longest x1 9.12 us: body(): half = lax.all_to_all(done, PLANE, 0, 0)]
    ppermute x1, waiting for transfers between devices: 13.2 us -> 0.01 us  [body(): lax.ppermute(w_mine, ('x', 'c', 'r'), [((i * NC + k) * NR + (j + i + 2 *...]
    all_to_all x1, waiting for transfers between devices: 8.81 us -> 0.01 us  [body(): spread = lax.all_to_all(partial, PLANE, 0, 0)]
    ppermute x0 -> x3, starting transfers between devices: none -> 8.69 us  [body(): lax.ppermute(later, 't', [(j, (j + step) % NT) for j in range(NT)])]
    all_gather x1, waiting for transfers between devices: 8.56 us -> 0.02 us  [body(): w_all = lax.all_gather(w_moved, PLANE).reshape(NX, HALF, COLS)]
    psum x1, blocking collectives: 7.5 us -> 10.9 us  [body(): square = lax.psum(jnp.sum(states * states, -1), 't') / D]
  transfers between devices with their start and end apart: 15 -> 18, of which waited for: 8 -> 9; matrix products, arithmetic and copies ran while one was open for 10% -> 8% of each run, Pallas kernels for 8% -> 7%
where the time goes in v8:
time: 245 us; the launch traced here: 244 us
  starting transfers between devices  79.2 us (32%)
  blocking collectives  48.9 us (20%)
  waiting for transfers between devices  44.7 us (18%)
  local copies, waits for them, and re-layouts  27.8 us (11%)
  Pallas kernels  20.3 us (8%)
  between operations  15.3 us (6%)
  other arithmetic  7.52 us (3%)
    ppermute x3, waiting for transfers between devices, body(): lax.ppermute(later, 't', [(j, (j + step) % NT) for j in range(NT)])  21.5 us
    all_to_all x1, blocking collectives, body(): half = lax.all_to_all(done, PLANE, 0, 0)  19.8 us
    ppermute x7, starting transfers between devices, swap_core(): return lax.ppermute(value, 'c', [(0, 1), (1, 0)])  19.2 us
    all_to_all x1, blocking collectives, body(): second = lax.all_to_all(sum_senders(spread), 'r', 0, 0)  18.1 us
    ppermute x3, waiting for transfers between devices, body(): lax.ppermute(jnp.concatenate([outgoing, tail], 0), 'r', [(j, (j + step) %...  15.9 us
    unnamed x46, local copies, waits for them, and re-layouts  15.3 us
    ppermute x1, starting transfers between devices, body(): lax.ppermute(w_mine, ('x', 'c', 'r'), [((i * NC + k) * NR + (j + i + 2 *...  14.5 us
    ppermute x3, starting transfers between devices, body(): lax.ppermute(jnp.concatenate([outgoing, tail], 0), 'r', [(j, (j + step) %...  14.4 us
  transfers between devices with their start and end apart: 18, of which 9 were waited for; matrix products, arithmetic and copies ran while one was open for 8% of the time, Pallas kernels for 7%

profile of v8, /device:TPU:33, one launch (start us, length us, event | category | flops | bytes accessed | tf_op | source)
XLA Modules:
  0.0 243.7 jit_solution(5524719348755298774)
XLA Ops:
  7.2 1.4 copy-done
  8.6 14.5 %collective-permute-start = (bf16[112,896]{1,0:T(8,128)(2,1)S(1)}, bf16[112,896]{1,0:T(8,128)(2,1)S(1)}, u32[]{:S(2)}, u32[]{:S(2)}) collective-permute-start(bf16[112,896]{1,0:T(8,128)(2,1)S(1)} %constant_dynamic-slice_fusion.1), channel_id=1, source_target_pairs={{0,0},{1,1},{2,2},{3,3},{18,16},{19,17},{16,18},{17,19},{129,128},... | collective-permute-start | bytes 602120 | tf_op jit(solution)/shard_map/ppermute | solution.py:301
  23.2 1.2 fusion.2
  24.4 10.9 %psum.7 = f32[2,128]{1,0:T(2,128)S(1)} all-reduce(f32[2,128]{1,0:T(2,128)S(1)} %fusion.2), channel_id=1, replica_groups=mesh['x'=4,'y'=4,'c'=2,'t'=4,'r'=4] {'t'}, use_global_device_ids=true, to_apply=%region_1.2 | all-reduce | flops 256 | bytes 2048 | tf_op jit(solution)/shard_map/psum | solution.py:316
  37.4 1.5 fusion.6
  40.3 4.1 %all-to-all-start = ((f32[4,3,896]{2,1,0:T(4,128)}), f32[4,3,896]{2,1,0:T(4,128)S(1)}, u32[]{:S(2)}, u32[]{:S(2)}) async-start(f32[4,3,896]{2,1,0:T(4,128)} %broadcast_in_dim.17), calls=%async_computation | async-start | bytes 114688 | tf_op jit(solution)/shard_map/all_to_all | solution.py:327
  45.4 2.8 %all-to-all-done = f32[4,3,896]{2,1,0:T(4,128)S(1)} async-done(((f32[4,3,896]{2,1,0:T(4,128)}), f32[4,3,896]{2,1,0:T(4,128)S(1)}, u32[]{:S(2)}, u32[]{:S(2)}) %all-to-all-start) | async-done | bytes 43040 | tf_op jit(solution)/shard_map/all_to_all | solution.py:327
  49.6 3.3 %concatenate.50 = f32[32,2,3840]{2,1,0:T(2,128)} concatenate(f32[32,2,3712]{2,1,0:T(2,128)S(1)} %broadcast_in_dim.18, f32[32,2,28]{2,1,0:T(2,128)S(1)} %copy.20, f32[32,2,2]{2,1,0:T(2,128)S(1)} %broadcast_in_dim.19, f32[32,2,98]{2,1,0:T(2,128)} %broadcast_in_dim.20), dimensions={2} | concatenate | bytes 1966080 | tf_op jit(solution)/shard_map/concatenate | solution.py:341
  53.0 11.5 %all-to-all-start.1 = ((f32[32,2,3840]{2,1,0:T(2,128)}), f32[32,2,3840]{2,1,0:T(2,128)}, u32[]{:S(2)}, u32[]{:S(2)}) async-start(f32[32,2,3840]{2,1,0:T(2,128)} %concatenate.50), calls=%async_computation.1 | async-start | bytes 1966080 | tf_op jit(solution)/shard_map/all_to_all | solution.py:350
  64.5 2.0 collective-permute-start.4
  66.5 4.7 %collective-permute-start.3 = (bf16[256,896]{1,0:T(8,128)(2,1)S(1)}, bf16[256,896]{1,0:T(8,128)(2,1)}, u32[]{:S(2)}, u32[]{:S(2)}) collective-permute-start(bf16[256,896]{1,0:T(8,128)(2,1)S(1)} %bitcast.67), channel_id=1, source_target_pairs={{0,8},{4,12},{8,0},{12,4},{1,9},{5,13},{9,1},{13,5},{2,10},{6,14},... | collective-permute-start | bytes 1376264 | tf_op jit(solution)/shard_map/ppermute | solution.py:331
  71.2 1.9 collective-permute-start.2
  73.2 0.9 broadcast_select_fusion
  74.1 2.8 %collective-permute-start.1 = (bf16[256,448]{1,0:T(8,128)(2,1)}, bf16[256,448]{1,0:T(8,128)(2,1)S(1)}, u32[]{:S(2)}, u32[]{:S(2)}) collective-permute-start(bf16[256,448]{1,0:T(8,128)(2,1)} %get-tuple-element.71), channel_id=1, source_target_pairs={{0,16},{16,0},{1,17},{17,1},{2,18},{18,2},{3,19},{19,3},{4,20},{20... | collective-permute-start | bytes 688136 | tf_op jit(solution)/shard_map/ppermute | solution.py:38
  76.9 1.9 collective-permute-start.5
  79.8 0.9 all-to-all-done.1
  80.7 1.3 copy.28
  82.0 4.2 %group_math.1 = (f32[2,32,3584]{2,1,0:T(8,128)S(1)}, f32[4,28,896]{2,1,0:T(8,128)S(1)}, f32[4,1,896]{2,1,0:T(1,128)S(1)}, f32[8,128]{1,0:T(8,128)S(1)}, bf16[2,4...) custom-call(s32[2]{0:T(128)S(1)} %pad_add_fusion.index_ref, ...), custom_call_target="tpu_custom_call" | custom-call | flops 183500800 | bytes 3145728 | tf_op jit(solution)/shard_map/group_math/pallas_call | solution.py:124
  88.5 21.4 %collective-permute-done.2.refs_3_ = bf16[256,896]{1,0:T(8,128)(2,1)} collective-permute-done((bf16[256,896]{1,0:T(8,128)(2,1)S(1)}, bf16[256,896]{1,0:T(8,128)(2,1)}, u32[]{:S(2)}, u32[]{:S(2)}) %collective-permute-start.2) | collective-permute-done | bytes 458784 | tf_op jit(solution)/shard_map/ppermute | solution.py:331
  109.9 2.4 collective-permute-start.6
  112.3 1.9 collective-permute-start.7
  114.3 2.4 collective-permute-start.8
  116.7 1.7 collective-permute-done.8.refs_7_
  118.4 0.9 copy-done.4
  119.4 0.9 copy-done.6
  120.3 0.9 copy-done.10
  121.3 0.9 copy-done.12
  122.2 5.9 %weight_partials.1 = (bf16[16,112,896]{2,1,0:T(8,128)(2,1)S(1)}, f32[2,256,1]{2,1,0:T(8,128)S(1)}) custom-call(s32[1]{0:T(128)} %bitcast.index_ref, bf16[256,896]{1,0:T(8,128)(2,1)S(1)} %bitcast.70, bf16[256,896]{1,0:T(8,128)(2,1)S(1)} %collective-permute-done.4.refs_1_, bf16[256,896]{1,0:T(8,128)(2,1)} %collective-permute-done.3.refs_2_, ...), custom_call_target="tpu_custom_call" | custom-call | flops 1644167168 | bytes 8388608 | tf_op jit(solution)/shard_map/weight_partials/pallas_call | solution.py:179
  128.1 1.7 copy-done.2
  129.8 6.7 %all-to-all-start.2 = ((bf16[16,112,896]{2,1,0:T(8,128)(2,1)}), bf16[16,112,896]{2,1,0:T(8,128)(2,1)}, u32[]{:S(2)}, u32[]{:S(2)}) async-start(bf16[16,112,896]{2,1,0:T(8,128)(2,1)} %copy-done.2), calls=%async_computation.2 | async-start | bytes 6422528 | tf_op jit(solution)/shard_map/all_to_all | solution.py:365
  139.8 4.1 %collective-permute-start.9 = (f32[30,896]{1,0:T(8,128)S(1)}, f32[30,896]{1,0:T(8,128)S(1)}, u32[]{:S(2)}, u32[]{:S(2)}) collective-permute-start(f32[30,896]{1,0:T(8,128)S(1)} %get-tuple-element.72), channel_id=1, source_target_pairs={{0,1},{1,2},{2,3},{3,0},{4,5},{5,6},{6,7},{7,4},{8,9},{9,10},{10,1... | collective-permute-start | bytes 322568 | tf_op jit(solution)/shard_map/ppermute | solution.py:373
  143.9 4.5 %collective-permute-start.10 = (f32[30,896]{1,0:T(8,128)S(1)}, f32[30,896]{1,0:T(8,128)S(1)}, u32[]{:S(2)}, u32[]{:S(2)}) collective-permute-start(f32[30,896]{1,0:T(8,128)S(1)} %get-tuple-element.73), channel_id=1, source_target_pairs={{0,2},{1,3},{2,0},{3,1},{4,6},{5,7},{6,4},{7,5},{8,10},{9,11},{10,... | collective-permute-start | bytes 322568 | tf_op jit(solution)/shard_map/ppermute | solution.py:373
  148.5 5.8 %collective-permute-start.11 = (f32[30,896]{1,0:T(8,128)S(1)}, f32[30,896]{1,0:T(8,128)S(1)}, u32[]{:S(2)}, u32[]{:S(2)}) collective-permute-start(f32[30,896]{1,0:T(8,128)S(1)} %get-tuple-element.74), channel_id=1, source_target_pairs={{0,3},{1,0},{2,1},{3,2},{4,7},{5,4},{6,5},{7,6},{8,11},{9,8},{10,9... | collective-permute-start | bytes 322568 | tf_op jit(solution)/shard_map/ppermute | solution.py:373
  154.4 1.0 fusion.5
  155.4 1.4 collective-permute-done.9
  157.5 12.3 %collective-permute-done.10 = f32[30,896]{1,0:T(8,128)S(1)} collective-permute-done((f32[30,896]{1,0:T(8,128)S(1)}, f32[30,896]{1,0:T(8,128)S(1)}, u32[]{:S(2)}, u32[]{:S(2)}) %collective-permute-start.10) | collective-permute-done | bytes 107552 | tf_op jit(solution)/shard_map/ppermute | solution.py:373
  170.4 2.2 collective-permute-done.11
  173.3 1.9 copy-done.3
  175.2 0.9 copy-done.7
  176.2 5.9 %attn_grads.1 = (bf16[256,448]{1,0:T(8,128)(2,1)S(1)}, bf16[256,448]{1,0:T(8,128)(2,1)S(1)}) custom-call(s32[2]{0:T(128)S(1)} %pad_add_fusion.1.index_ref, bf16[256,896]{1,0:T(8,128)(2,1)S(1)} %bitcast.71, bf16[256,896]{1,0:T(8,128)(2,1)S(1)} %collective-permute-done.4.refs_1_, bf16[256,896]{1,0:T(8,128)(2,1)} %collective-permute-done.3.refs_2_, ...), custom_call_target="tpu_custom_call" | custom-call | flops 1644167168 | bytes 8388608 | tf_op jit(solution)/shard_map/attn_grads/pallas_call | solution.py:279
  182.1 2.4 collective-permute-start.12
  184.6 1.1 collective-permute-done.12
  185.6 1.1 maximum_select_fusion
  186.7 3.0 %sum_senders.1 = bf16[4,28,896]{2,1,0:T(8,128)(2,1)S(1)} custom-call(bf16[16,112,896]{2,1,0:T(8,128)(2,1)} %all-to-all-done.2.spread_ref), custom_call_target="tpu_custom_call" | custom-call | flops 1605632 | bytes 4194304 | tf_op jit(solution)/shard_map/sum_senders/pallas_call | solution.py:217
  189.7 18.1 %all_to_all.25 = bf16[4,28,896]{2,1,0:T(8,128)(2,1)S(1)} all-to-all(bf16[4,28,896]{2,1,0:T(8,128)(2,1)S(1)} %sum_senders.1), channel_id=1, replica_groups=mesh['x'=4,'y'=4,'c'=2,'t'=4,'r'=4] {'r'}, dimensions={0} | all-to-all | bytes 401408 | tf_op jit(solution)/shard_map/all_to_all | solution.py:400
  208.0 19.8 %all_to_all.26.mine_ref = bf16[16,28,896]{2,1,0:T(8,128)(2,1)S(1)} all-to-all(bf16[16,28,896]{2,1,0:T(8,128)(2,1)S(1)} %broadcast_in_dim.23), channel_id=1, replica_groups=mesh['x'=4,'y'=4,'c'=2,'t'=4,'r'=4] {'x','y'}, dimensions={0} | all-to-all | bytes 1605632 | tf_op jit(solution)/shard_map/all_to_all | solution.py:405
  228.1 5.3 %collective-permute-start.13 = (bf16[16,28,896]{2,0,1:T(8,128)(2,1)S(1)}, bf16[16,28,896]{2,0,1:T(8,128)(2,1)S(1)}, u32[]{:S(2)}, u32[]{:S(2)}) collective-permute-start(bf16[16,28,896]{2,0,1:T(8,128)(2,1)S(1)} %copy.22), channel_id=1, source_target_pairs={{0,16},{16,0},{1,17},{17,1},{2,18},{18,2},{3,19},{19,3},{4,20},{20... | collective-permute-start | bytes 2408456 | tf_op jit(solution)/shard_map/ppermute | solution.py:38
  235.5 1.4 join_halves.1
  (90 shorter events, 16.2 us)
Async XLA Ops:
  7.2 1.4 copy-start
  7.2 166.1 %all-gather.3.cloned.1.call-start = ((), (), s32[]{:S(2)}) async-start(), calls=%async_computation.5 | async-start | bytes 3411968 | tf_op jit(solution)/shard_map/all_gather | solution.py:326
  8.6 30.3 %collective-permute-start = (bf16[112,896]{1,0:T(8,128)(2,1)S(1)}, bf16[112,896]{1,0:T(8,128)(2,1)S(1)}, u32[]{:S(2)}, u32[]{:S(2)}) collective-permute-start(bf16[112,896]{1,0:T(8,128)(2,1)S(1)} %constant_dynamic-slice_fusion.1), channel_id=1, source_target_pairs={{0,0},{1,1},{2,2},{3,3},{18,16},{19,17},{16,18},{17,19},{129,128},... | collective-permute-start | bytes 602120 | tf_op jit(solution)/shard_map/ppermute | solution.py:301
  37.4 27.0 %copy-start.1 = (bf16[1,2,128,896]{3,2,1,0:T(8,128)(2,1)S(1)}, bf16[1,2,128,896]{3,2,1,0:T(8,128)(2,1)}, u32[]{:S(2)}) copy-start(bf16[1,2,128,896]{3,2,1,0:T(8,128)(2,1)} %param.6) | copy-start | bytes 1376260
  37.4 35.8 %copy-start.13 = (bf16[1,2,128,896]{3,2,1,0:T(8,128)(2,1)S(1)}, bf16[1,2,128,896]{3,2,1,0:T(8,128)(2,1)}, u32[]{:S(2)}) copy-start(bf16[1,2,128,896]{3,2,1,0:T(8,128)(2,1)} %param.7) | copy-start | bytes 1376260
  39.0 0.7 copy-start.14
  40.3 7.8 %all-to-all-start = ((f32[4,3,896]{2,1,0:T(4,128)}), f32[4,3,896]{2,1,0:T(4,128)S(1)}, u32[]{:S(2)}, u32[]{:S(2)}) async-start(f32[4,3,896]{2,1,0:T(4,128)} %broadcast_in_dim.17), calls=%async_computation | async-start | bytes 114688 | tf_op jit(solution)/shard_map/all_to_all | solution.py:327
  48.1 0.6 copy-start.15
  53.0 27.7 %all-to-all-start.1 = ((f32[32,2,3840]{2,1,0:T(2,128)}), f32[32,2,3840]{2,1,0:T(2,128)}, u32[]{:S(2)}, u32[]{:S(2)}) async-start(f32[32,2,3840]{2,1,0:T(2,128)} %concatenate.50), calls=%async_computation.1 | async-start | bytes 1966080 | tf_op jit(solution)/shard_map/all_to_all | solution.py:350
  64.5 45.5 %collective-permute-start.4 = (bf16[256,896]{1,0:T(8,128)(2,1)S(1)}, bf16[256,896]{1,0:T(8,128)(2,1)S(1)}, u32[]{:S(2)}, u32[]{:S(2)}) collective-permute-start(bf16[256,896]{1,0:T(8,128)(2,1)S(1)} %bitcast.66), channel_id=1, source_target_pairs={{0,4},{4,8},{8,12},{12,0},{1,5},{5,9},{9,13},{13,1},{2,6},{6,10},{... | collective-permute-start | bytes 1376264 | tf_op jit(solution)/shard_map/ppermute | solution.py:331
  66.5 43.4 %collective-permute-start.3 = (bf16[256,896]{1,0:T(8,128)(2,1)S(1)}, bf16[256,896]{1,0:T(8,128)(2,1)}, u32[]{:S(2)}, u32[]{:S(2)}) collective-permute-start(bf16[256,896]{1,0:T(8,128)(2,1)S(1)} %bitcast.67), channel_id=1, source_target_pairs={{0,8},{4,12},{8,0},{12,4},{1,9},{5,13},{9,1},{13,5},{2,10},{6,14},... | collective-permute-start | bytes 1376264 | tf_op jit(solution)/shard_map/ppermute | solution.py:331
  71.2 38.7 %collective-permute-start.2 = (bf16[256,896]{1,0:T(8,128)(2,1)S(1)}, bf16[256,896]{1,0:T(8,128)(2,1)}, u32[]{:S(2)}, u32[]{:S(2)}) collective-permute-start(bf16[256,896]{1,0:T(8,128)(2,1)S(1)} %bitcast.68), channel_id=1, source_target_pairs={{0,12},{4,0},{8,4},{12,8},{1,13},{5,1},{9,5},{13,9},{2,14},{6,2},{... | collective-permute-start | bytes 1376264 | tf_op jit(solution)/shard_map/ppermute | solution.py:331
  74.1 5.6 %collective-permute-start.1 = (bf16[256,448]{1,0:T(8,128)(2,1)}, bf16[256,448]{1,0:T(8,128)(2,1)S(1)}, u32[]{:S(2)}, u32[]{:S(2)}) collective-permute-start(bf16[256,448]{1,0:T(8,128)(2,1)} %get-tuple-element.71), channel_id=1, source_target_pairs={{0,16},{16,0},{1,17},{17,1},{2,18},{18,2},{3,19},{19,3},{4,20},{20... | collective-permute-start | bytes 688136 | tf_op jit(solution)/shard_map/ppermute | solution.py:38
  76.9 39.8 %collective-permute-start.5 = (bf16[256,896]{1,0:T(8,128)(2,1)S(1)}, bf16[256,896]{1,0:T(8,128)(2,1)}, u32[]{:S(2)}, u32[]{:S(2)}) collective-permute-start(bf16[256,896]{1,0:T(8,128)(2,1)S(1)} %bitcast.69), channel_id=1, source_target_pairs={{0,16},{16,0},{1,17},{17,1},{2,18},{18,2},{3,19},{19,3},{4,20},{20... | collective-permute-start | bytes 1376264 | tf_op jit(solution)/shard_map/ppermute | solution.py:38
  79.8 2.2 copy-start.9
  86.1 0.7 copy-start.5
  86.9 0.9 copy-start.8
  87.8 0.7 copy-start.11
  109.9 6.8 %collective-permute-start.6 = (bf16[256,896]{1,0:T(8,128)(2,1)S(1)}, bf16[256,896]{1,0:T(8,128)(2,1)}, u32[]{:S(2)}, u32[]{:S(2)}) collective-permute-start(bf16[256,896]{1,0:T(8,128)(2,1)S(1)} %collective-permute-done.4.refs_1_), channel_id=1, source_target_pairs={{0,16},{16,0},{1,17},{17,1},{2,18},{18,2},{3,19},{19,3},{4,20},{20... | collective-permute-start | bytes 1376264 | tf_op jit(solution)/shard_map/ppermute | solution.py:38
  112.3 4.4 %collective-permute-start.7 = (bf16[256,896]{1,0:T(8,128)(2,1)}, bf16[256,896]{1,0:T(8,128)(2,1)}, u32[]{:S(2)}, u32[]{:S(2)}) collective-permute-start(bf16[256,896]{1,0:T(8,128)(2,1)} %collective-permute-done.3.refs_2_), channel_id=1, source_target_pairs={{0,16},{16,0},{1,17},{17,1},{2,18},{18,2},{3,19},{19,3},{4,20},{20... | collective-permute-start | bytes 1376264 | tf_op jit(solution)/shard_map/ppermute | solution.py:38
  114.3 4.2 %collective-permute-start.8 = (bf16[256,896]{1,0:T(8,128)(2,1)}, bf16[256,896]{1,0:T(8,128)(2,1)}, u32[]{:S(2)}, u32[]{:S(2)}) collective-permute-start(bf16[256,896]{1,0:T(8,128)(2,1)} %collective-permute-done.2.refs_3_), channel_id=1, source_target_pairs={{0,16},{16,0},{1,17},{17,1},{2,18},{18,2},{3,19},{19,3},{4,20},{20... | collective-permute-start | bytes 1376264 | tf_op jit(solution)/shard_map/ppermute | solution.py:38
  118.4 0.9 copy-start.4
  119.4 0.9 copy-start.6
  120.3 0.9 copy-start.10
  121.3 0.9 copy-start.12
  128.1 1.7 copy-start.2
  129.8 56.9 %all-to-all-start.2 = ((bf16[16,112,896]{2,1,0:T(8,128)(2,1)}), bf16[16,112,896]{2,1,0:T(8,128)(2,1)}, u32[]{:S(2)}, u32[]{:S(2)}) async-start(bf16[16,112,896]{2,1,0:T(8,128)(2,1)} %copy-done.2), calls=%async_computation.2 | async-start | bytes 6422528 | tf_op jit(solution)/shard_map/all_to_all | solution.py:365
  139.8 17.0 %collective-permute-start.9 = (f32[30,896]{1,0:T(8,128)S(1)}, f32[30,896]{1,0:T(8,128)S(1)}, u32[]{:S(2)}, u32[]{:S(2)}) collective-permute-start(f32[30,896]{1,0:T(8,128)S(1)} %get-tuple-element.72), channel_id=1, source_target_pairs={{0,1},{1,2},{2,3},{3,0},{4,5},{5,6},{6,7},{7,4},{8,9},{9,10},{10,1... | collective-permute-start | bytes 322568 | tf_op jit(solution)/shard_map/ppermute | solution.py:373
  143.9 25.8 %collective-permute-start.10 = (f32[30,896]{1,0:T(8,128)S(1)}, f32[30,896]{1,0:T(8,128)S(1)}, u32[]{:S(2)}, u32[]{:S(2)}) collective-permute-start(f32[30,896]{1,0:T(8,128)S(1)} %get-tuple-element.73), channel_id=1, source_target_pairs={{0,2},{1,3},{2,0},{3,1},{4,6},{5,7},{6,4},{7,5},{8,10},{9,11},{10,... | collective-permute-start | bytes 322568 | tf_op jit(solution)/shard_map/ppermute | solution.py:373
  148.5 24.1 %collective-permute-start.11 = (f32[30,896]{1,0:T(8,128)S(1)}, f32[30,896]{1,0:T(8,128)S(1)}, u32[]{:S(2)}, u32[]{:S(2)}) collective-permute-start(f32[30,896]{1,0:T(8,128)S(1)} %get-tuple-element.74), channel_id=1, source_target_pairs={{0,3},{1,0},{2,1},{3,2},{4,7},{5,4},{6,5},{7,6},{8,11},{9,8},{10,9... | collective-permute-start | bytes 322568 | tf_op jit(solution)/shard_map/ppermute | solution.py:373
  156.8 0.7 copy-start.16
  169.7 0.6 copy-start.18
  172.6 0.6 copy-start.20
  173.3 1.9 copy-start.3
  175.2 0.9 copy-start.7
  176.2 8.3 %copy-start.17 = (f32[30,896]{1,0:T(8,128)S(1)}, f32[30,896]{1,0:T(8,128)}, u32[]{:S(2)}) copy-start(f32[30,896]{1,0:T(8,128)} %copy-done.16) | copy-start | bytes 322564
  176.2 8.3 %copy-start.19 = (f32[30,896]{1,0:T(8,128)S(1)}, f32[30,896]{1,0:T(8,128)}, u32[]{:S(2)}) copy-start(f32[30,896]{1,0:T(8,128)} %copy-done.18) | copy-start | bytes 322564
  176.2 8.3 %copy-start.21 = (f32[30,896]{1,0:T(8,128)S(1)}, f32[30,896]{1,0:T(8,128)}, u32[]{:S(2)}) copy-start(f32[30,896]{1,0:T(8,128)} %copy-done.20) | copy-start | bytes 322564
  182.1 3.6 %collective-permute-start.12 = (bf16[256,448]{1,0:T(8,128)(2,1)S(1)}, bf16[256,448]{1,0:T(8,128)(2,1)S(1)}, u32[]{:S(2)}, u32[]{:S(2)}) collective-permute-start(bf16[256,448]{1,0:T(8,128)(2,1)S(1)} %get-tuple-element.58), channel_id=1, source_target_pairs={{0,16},{16,0},{1,17},{17,1},{2,18},{18,2},{3,19},{19,3},{4,20},{20... | collective-permute-start | bytes 688136 | tf_op jit(solution)/shard_map/ppermute | solution.py:38
  228.1 7.3 %collective-permute-start.13 = (bf16[16,28,896]{2,0,1:T(8,128)(2,1)S(1)}, bf16[16,28,896]{2,0,1:T(8,128)(2,1)S(1)}, u32[]{:S(2)}, u32[]{:S(2)}) collective-permute-start(bf16[16,28,896]{2,0,1:T(8,128)(2,1)S(1)} %copy.22), channel_id=1, source_target_pairs={{0,16},{16,0},{1,17},{17,1},{2,18},{18,2},{3,19},{19,3},{4,20},{20... | collective-permute-start | bytes 2408456 | tf_op jit(solution)/shard_map/ppermute | solution.py:38
Sparse Core Ops, SparseCore 0:
  39.8 66.8 all-gather.2

commit v9 on v7

--- a/solution.py
+++ b/solution.py
@@ -143,28 +143,27 @@
 
 
 def weight_kernel(
-    own_ref, other_ref, keep_ref, given_ref, pieces_ref, scale_ref, out_ref, coef_ref, acc_ref
+    core_ref, state_ref, keep_ref, given_ref, pieces_ref, scale_ref, out_ref, coef_ref, acc_ref
 ):
+    bases = (NT * core_ref[0], NT * (1 - core_ref[0]))
     token = lax.broadcasted_iota(jnp.int32, (TOK, PIECES), 0)
     part = lax.broadcasted_iota(jnp.int32, (TOK, PIECES), 1)
     part = part - jnp.where(token < SEQ, 0, 3)
     mask = (part >= 0) & (part < 3)
     scaled = []
-    for pair, (state_ref, attn_ref) in enumerate(
-        ((own_ref, keep_ref), (other_ref, given_ref))
-    ):
+    for pair, attn_ref in enumerate((keep_ref, given_ref)):
         inner = jnp.zeros((TOK, PIECES), f32)
         for block in range(NT):
-            inner = inner + dot_last(state_ref[block], pieces_ref[pair, block])
+            inner = inner + dot_last(state_ref[bases[pair] + block], pieces_ref[pair, block])
         inner = jnp.sum(jnp.where(mask, inner, 0.0), -1, keepdims=True)
         coef = scale_ref[pair] * inner
         coef_ref[pair] = coef
         scaled.append((attn_ref[...].astype(f32) * coef).astype(bf16))
     for block in range(NT):
         acc_ref[block] = lax.dot_general(
-            scaled[0], own_ref[block], contract_first, preferred_element_type=f32
+            scaled[0], state_ref[bases[0] + block], contract_first, preferred_element_type=f32
         ) + lax.dot_general(
-            scaled[1], other_ref[block], contract_first, preferred_element_type=f32
+            scaled[1], state_ref[bases[1] + block], contract_first, preferred_element_type=f32
         )
     for place in range(NX * NY):
         rows = [
@@ -173,7 +172,7 @@
         out_ref[place] = jnp.concatenate(rows, 0).astype(bf16)
 
 
-def weight_partials(own, other, keep, given, pieces, scale):
+def weight_partials(core, states, keep, given, pieces, scale):
     spec = pl.BlockSpec(memory_space=pltpu.VMEM)
     return pl.pallas_call(
         weight_kernel,
@@ -181,7 +180,7 @@
             jax.ShapeDtypeStruct((NX * NY, NR * SLICE, COLS), bf16),
             jax.ShapeDtypeStruct((NC, TOK, 1), f32),
         ),
-        in_specs=[spec] * 6,
+        in_specs=[pl.BlockSpec(memory_space=pltpu.SMEM)] + [spec] * 5,
         out_specs=(spec, spec),
         scratch_shapes=[pltpu.VMEM((NR, HALF, COLS), f32)],
         compiler_params=pltpu.CompilerParams(vmem_limit_bytes=24 * 1024 * 1024),
@@ -189,7 +188,7 @@
             flops=4 * TOK * HALF * D, bytes_accessed=8 * 1024 * 1024, transcendentals=0
         ),
         name="weight_partials",
-    )(own, other, keep, given, pieces, scale)
+    )(core, states, keep, given, pieces, scale)
 
 
 def sum_kernel(spread_ref, out_ref, acc_ref):
@@ -253,15 +252,16 @@
 
 
 def attn_kernel(
-    shift_ref, own_ref, other_ref, pieces_ref, w_ref, coef_ref, first_ref, keep_ref, give_ref
+    index_ref, state_ref, pieces_ref, w_ref, coef_ref, first_ref, keep_ref, give_ref
 ):
-    shift = shift_ref[0]
-    for pair, (state_ref, out_ref) in enumerate(((own_ref, keep_ref), (other_ref, give_ref))):
+    core, shift = index_ref[0], index_ref[1]
+    bases = (NT * core, NT * (1 - core))
+    for pair, out_ref in enumerate((keep_ref, give_ref)):
         tokens = jnp.zeros((TOK, HALF), f32)
         rows = jnp.zeros((PIECES, HALF), f32)
         for block in range(NX):
             which = lax.rem(shift + block, NR)
-            tokens = tokens + dot_last(state_ref[which], w_ref[block])
+            tokens = tokens + dot_last(state_ref[bases[pair] + which], w_ref[block])
             rows = rows + dot_last(pieces_ref[pair, which], w_ref[block])
         for side in range(2):
             row = rows[3 * side + 2 : 3 * side + 3] + rows[3 * side + 1 : 3 * side + 2]
@@ -272,20 +272,20 @@
             ).astype(bf16)
 
 
-def attn_grads(shift, own, other, pieces, w_all, coef, first):
+def attn_grads(index, states, pieces, w_all, coef, first):
     spec = pl.BlockSpec(memory_space=pltpu.VMEM)
     out = jax.ShapeDtypeStruct((TOK, HALF), bf16)
     return pl.pallas_call(
         attn_kernel,
         out_shape=(out, out),
-        in_specs=[pl.BlockSpec(memory_space=pltpu.SMEM)] + [spec] * 6,
+        in_specs=[pl.BlockSpec(memory_space=pltpu.SMEM)] + [spec] * 5,
         out_specs=(spec, spec),
         compiler_params=pltpu.CompilerParams(vmem_limit_bytes=24 * 1024 * 1024),
         cost_estimate=pl.CostEstimate(
             flops=4 * TOK * HALF * D, bytes_accessed=8 * 1024 * 1024, transcendentals=0
         ),
         name="attn_grads",
-    )(shift, own, other, pieces, w_all, coef, first)
+    )(index, states, pieces, w_all, coef, first)
 
 
 def body(hidden_state, attn_out, o_weight, norm_gain, lengths, positive):
@@ -295,7 +295,7 @@
 
     state = hidden_state.reshape(TOK, FEAT)
     attn = attn_out.reshape(TOK, FEAT)
-    state_all = lax.all_gather(state, "t")
+    state_all = lax.all_gather(state, ("c", "t"))
     w_start = (ic * NY + iy) * W_ROWS
     w_mine = lax.dynamic_slice(o_weight, (w_start, 0), (W_ROWS, COLS))
     w_moved = lax.ppermute(
@@ -342,18 +342,17 @@
         -1,
     )
     got = lax.all_to_all(send, DP, 0, 0)
-    got, state_all, attn_other = lax.optimization_barrier((got, state_all, attn_other))
+    got, attn_other = lax.optimization_barrier((got, attn_other))
 
     other_index = dp_index + 1 - 2 * ic
-    state_other = swap_core(state_all)
-    got, w_moved = lax.optimization_barrier((got, w_moved))
-    w_all = lax.all_gather(w_moved, PLANE).reshape(NX, HALF, COLS)
     scaled, first, gain_part, loss_part, pieces, scale, first_col = group_math(
         jnp.stack([dp_index, other_index]), got.transpose(1, 0, 2), gain
     )
 
+    scale, w_moved = lax.optimization_barrier((scale, w_moved))
+    w_all = lax.all_gather(w_moved, PLANE).reshape(NX, HALF, COLS)
     partial, coef = weight_partials(
-        state_all, state_other, attn_keep, attn_other, pieces, scale
+        ic.reshape(1), state_all, attn_keep, attn_other, pieces, scale
     )
     partial, first = lax.optimization_barrier((partial, first))
     spread = lax.all_to_all(partial, PLANE, 0, 0)
@@ -385,22 +384,21 @@
     state_grad = first_col[0].reshape(2, SEQ, 1) * row_here - states * coef[0].reshape(2, SEQ, 1)
     grad_hidden = state_grad.astype(bf16).reshape(1, 2, SEQ, FEAT)
     keep, give = attn_grads(
-        (ir + 2 * ic).reshape(1), state_all, state_other, pieces, w_all, coef, first_col
-    )
-
-    second, keep, give = lax.optimization_barrier((second, keep, give))
+        jnp.stack([ic, ir + 2 * ic]), state_all, pieces, w_all, coef, first_col
+    )
+
     second_sum = jnp.sum(second.astype(f32), 0)
     total = first_sum - second_sum
     done = jnp.broadcast_to(total.astype(bf16)[None], (NX * NY, SLICE, COLS))
     half = lax.all_to_all(done, PLANE, 0, 0)
+    half, keep, give, grad_hidden, totals = lax.optimization_barrier(
+        (half, keep, give, grad_hidden, totals)
+    )
+    half_other = swap_core(half)
     arrived = swap_core(give)
     grad_attn = jnp.where(
         ic == 0, jnp.concatenate([keep, arrived], 1), jnp.concatenate([arrived, keep], 1)
     ).reshape(1, 2, SEQ, FEAT)
-    half, grad_attn, grad_hidden, totals = lax.optimization_barrier(
-        (half, grad_attn, grad_hidden, totals)
-    )
-    half_other = swap_core(half)
     grad_weight = join_halves(ic.reshape(1), half, half_other)
     return (grad_hidden, grad_attn, grad_weight, totals[0], totals[1, 0])
 

time: 221 us -> 243 us (1.100)
  the two profiles are of different devices: /device:TPU:33 before, /device:TPU:1 now
where the time goes in v9:
time: 243 us; the launch traced here: 242 us
  starting transfers between devices  84.8 us (35%)
  waiting for transfers between devices  81.8 us (34%)
  local copies, waits for them, and re-layouts  23.3 us (10%)
  Pallas kernels  17.4 us (7%)
  between operations  15.2 us (6%)
  blocking collectives  11.8 us (5%)
  other arithmetic  7.72 us (3%)
    all_gather x1, waiting for transfers between devices, body(): state_all = lax.all_gather(state, ('c', 't'))  38.1 us
    ppermute x3, starting transfers between devices, body(): lax.ppermute(jnp.concatenate([outgoing, tail], 0), 'r', [(j, (j + step) %...  20.1 us
    ppermute x3, waiting for transfers between devices, body(): lax.ppermute(jnp.concatenate([outgoing, tail], 0), 'r', [(j, (j + step) %...  15.8 us
    ppermute x1, starting transfers between devices, body(): lax.ppermute(w_mine, ('x', 'c', 'r'), [((i * NC + k) * NR + (j + i + 2 *...  13.2 us
    all_to_all x1, waiting for transfers between devices, body(): second = lax.all_to_all(sum_senders(spread), 'r', 0, 0)  12.6 us
    all_to_all x1, starting transfers between devices, body(): got = lax.all_to_all(send, DP, 0, 0)  11.9 us
    psum x1, blocking collectives, body(): square = lax.psum(jnp.sum(states * states, -1), 't') / D  11.8 us
    unnamed x24, local copies, waits for them, and re-layouts  11.8 us
  transfers between devices with their start and end apart: 14, of which 8 were waited for; matrix products, arithmetic and copies ran while one was open for 8% of the time, Pallas kernels for 7%

profile of v9, /device:TPU:1, one launch (start us, length us, event | category | flops | bytes accessed | tf_op | source)
XLA Modules:
  0.0 242.1 jit_solution(17031852429192943696)
XLA Ops:
  7.2 0.7 all-gather.4.cloned.1.call-update
  7.9 0.7 broadcast_in_dim.16
  8.6 1.2 fusion.2
  9.8 11.8 %psum.7 = f32[2,128]{1,0:T(2,128)S(1)} all-reduce(f32[2,128]{1,0:T(2,128)S(1)} %fusion.2), channel_id=1, replica_groups=mesh['x'=4,'y'=4,'c'=2,'t'=4,'r'=4] {'t'}, use_global_device_ids=true, to_apply=%region_1.2 | all-reduce | flops 256 | bytes 2048 | tf_op jit(solution)/shard_map/psum | solution.py:316
  21.6 0.7 convert_bitcast_fusion.1
  22.3 0.7 fusion.10
  23.1 1.5 fusion.6
  25.2 3.3 %all-to-all-start = ((f32[4,3,896]{2,1,0:T(4,128)}), f32[4,3,896]{2,1,0:T(4,128)S(1)}, u32[]{:S(2)}, u32[]{:S(2)}) async-start(f32[4,3,896]{2,1,0:T(4,128)} %broadcast_in_dim.17), calls=%async_computation | async-start | bytes 114688 | tf_op jit(solution)/shard_map/all_to_all | solution.py:325
  29.4 3.6 %all-to-all-done = f32[4,3,896]{2,1,0:T(4,128)S(1)} async-done(((f32[4,3,896]{2,1,0:T(4,128)}), f32[4,3,896]{2,1,0:T(4,128)S(1)}, u32[]{:S(2)}, u32[]{:S(2)}) %all-to-all-start) | async-done | bytes 43040 | tf_op jit(solution)/shard_map/all_to_all | solution.py:325
  33.4 2.2 concatenate.50
  35.6 11.9 %all-to-all-start.1 = ((f32[32,2,3840]{2,1,0:T(2,128)}), f32[32,2,3840]{2,1,0:T(2,128)}, u32[]{:S(2)}, u32[]{:S(2)}) async-start(f32[32,2,3840]{2,1,0:T(2,128)} %concatenate.50), calls=%async_computation.1 | async-start | bytes 1966080 | tf_op jit(solution)/shard_map/all_to_all | solution.py:344
  47.7 2.2 collective-permute-start
  49.9 0.7 constant_dynamic-slice_fusion.1
  50.6 13.2 %collective-permute-start.1 = (bf16[112,896]{1,0:T(8,128)(2,1)}, bf16[112,896]{1,0:T(8,128)(2,1)S(1)}, u32[]{:S(2)}, u32[]{:S(2)}) collective-permute-start(bf16[112,896]{1,0:T(8,128)(2,1)} %constant_dynamic-slice_fusion.1), channel_id=1, source_target_pairs={{0,0},{1,1},{2,2},{3,3},{18,16},{19,17},{16,18},{17,19},{129,128},... | collective-permute-start | bytes 602120 | tf_op jit(solution)/shard_map/ppermute | solution.py:301
  64.0 1.3 copy.28
  65.2 4.2 %group_math.1 = (f32[2,32,3584]{2,1,0:T(8,128)S(1)}, f32[4,28,896]{2,1,0:T(8,128)S(1)}, f32[4,1,896]{2,1,0:T(1,128)S(1)}, f32[8,128]{1,0:T(8,128)S(1)}, bf16[2,4...) custom-call(s32[2]{0:T(128)S(1)} %pad_add_fusion.index_ref, ...), custom_call_target="tpu_custom_call" | custom-call | flops 183500800 | bytes 3145728 | tf_op jit(solution)/shard_map/group_math/pallas_call | solution.py:124
  69.4 0.9 copy-done.5
  70.3 0.7 copy-done.6
  71.0 3.3 %collective-permute-done.1 = bf16[112,896]{1,0:T(8,128)(2,1)S(1)} collective-permute-done((bf16[112,896]{1,0:T(8,128)(2,1)}, bf16[112,896]{1,0:T(8,128)(2,1)S(1)}, u32[]{:S(2)}, u32[]{:S(2)}) %collective-permute-start.1) | collective-permute-done | bytes 200736 | tf_op jit(solution)/shard_map/ppermute | solution.py:301
  74.3 0.7 copy-done.10
  75.0 38.1 %all-gather.4.cloned.1.call-done.state_ref = bf16[8,256,896]{2,1,0:T(8,128)(2,1)} async-done(((bf16[1,256,896]{2,1,0:T(8,128)(2,1)}), bf16[8,256,896]{2,1,0:T(8,128)(2,1)}) %all-gather.4.cloned.1.call-update) | async-done | bytes 3670032 | tf_op jit(solution)/shard_map/all_gather | solution.py:298
  113.2 2.0 copy-done.1
  115.2 0.9 copy-done.7
  116.2 3.5 %weight_partials.1 = (bf16[16,112,896]{2,1,0:T(8,128)(2,1)S(1)}, f32[2,256,1]{2,1,0:T(8,128)S(1)}) custom-call(s32[1]{0:T(128)} %bitcast.core_ref, bf16[8,256,896]{2,1,0:T(8,128)(2,1)S(1)} %copy-done.1, bf16[256,448]{1,0:T(8,128)(2,1)S(1)} %get-tuple-element.61.keep_ref, bf16[256,448]{1,0:T(8,128)(2,1)S(1)} %collective-permute-done.given_ref, ...), custom_call_target="tpu_custom_call" | custom-call | flops 1644167168 | bytes 8388608 | tf_op jit(solution)/shard_map/weight_partials/pallas_call | solution.py:177
  119.6 1.8 copy-done.3
  121.4 6.5 %all-to-all-start.2 = ((bf16[16,112,896]{2,1,0:T(8,128)(2,1)}), bf16[16,112,896]{2,1,0:T(8,128)(2,1)}, u32[]{:S(2)}, u32[]{:S(2)}) async-start(bf16[16,112,896]{2,1,0:T(8,128)(2,1)} %copy-done.3), calls=%async_computation.2 | async-start | bytes 6422528 | tf_op jit(solution)/shard_map/all_to_all | solution.py:358
  128.6 0.7 pad.20.clone
  129.4 7.4 %collective-permute-start.2 = (f32[30,896]{1,0:T(8,128)S(1)}, f32[30,896]{1,0:T(8,128)S(1)}, u32[]{:S(2)}, u32[]{:S(2)}) collective-permute-start(f32[30,896]{1,0:T(8,128)S(1)} %get-tuple-element.62), channel_id=1, source_target_pairs={{0,1},{1,2},{2,3},{3,0},{4,5},{5,6},{6,7},{7,4},{8,9},{9,10},{10,1... | collective-permute-start | bytes 322568 | tf_op jit(solution)/shard_map/ppermute | solution.py:366
  137.5 6.4 %collective-permute-start.3 = (f32[30,896]{1,0:T(8,128)S(1)}, f32[30,896]{1,0:T(8,128)S(1)}, u32[]{:S(2)}, u32[]{:S(2)}) collective-permute-start(f32[30,896]{1,0:T(8,128)S(1)} %get-tuple-element.63), channel_id=1, source_target_pairs={{0,2},{1,3},{2,0},{3,1},{4,6},{5,7},{6,4},{7,5},{8,10},{9,11},{10,... | collective-permute-start | bytes 322568 | tf_op jit(solution)/shard_map/ppermute | solution.py:366
  143.9 6.3 %collective-permute-start.4 = (f32[30,896]{1,0:T(8,128)S(1)}, f32[30,896]{1,0:T(8,128)S(1)}, u32[]{:S(2)}, u32[]{:S(2)}) collective-permute-start(f32[30,896]{1,0:T(8,128)S(1)} %get-tuple-element.64), channel_id=1, source_target_pairs={{0,3},{1,0},{2,1},{3,2},{4,7},{5,4},{6,5},{7,6},{8,11},{9,8},{10,9... | collective-permute-start | bytes 322568 | tf_op jit(solution)/shard_map/ppermute | solution.py:366
  150.2 13.0 %collective-permute-done.3 = f32[30,896]{1,0:T(8,128)S(1)} collective-permute-done((f32[30,896]{1,0:T(8,128)S(1)}, f32[30,896]{1,0:T(8,128)S(1)}, u32[]{:S(2)}, u32[]{:S(2)}) %collective-permute-start.3) | collective-permute-done | bytes 107552 | tf_op jit(solution)/shard_map/ppermute | solution.py:366
  163.2 2.8 %collective-permute-done.4 = f32[30,896]{1,0:T(8,128)S(1)} collective-permute-done((f32[30,896]{1,0:T(8,128)S(1)}, f32[30,896]{1,0:T(8,128)S(1)}, u32[]{:S(2)}, u32[]{:S(2)}) %collective-permute-start.4) | collective-permute-done | bytes 107552 | tf_op jit(solution)/shard_map/ppermute | solution.py:366
  166.1 7.1 %all-to-all-done.2.spread_ref = bf16[16,112,896]{2,1,0:T(8,128)(2,1)} async-done(((bf16[16,112,896]{2,1,0:T(8,128)(2,1)}), bf16[16,112,896]{2,1,0:T(8,128)(2,1)}, u32[]{:S(2)}, u32[]{:S(2)}) %all-to-all-start.2) | async-done | bytes 3211296 | tf_op jit(solution)/shard_map/all_to_all | solution.py:358
  173.2 3.7 %sum_senders.1 = bf16[4,28,896]{2,1,0:T(8,128)(2,1)} custom-call(bf16[16,112,896]{2,1,0:T(8,128)(2,1)} %all-to-all-done.2.spread_ref), custom_call_target="tpu_custom_call" | custom-call | flops 1605632 | bytes 4194304 | tf_op jit(solution)/shard_map/sum_senders/pallas_call | solution.py:215
  176.9 10.1 %all-to-all-start.3 = ((bf16[4,28,896]{2,1,0:T(8,128)(2,1)}), bf16[4,28,896]{2,1,0:T(8,128)(2,1)S(1)}, u32[]{:S(2)}, u32[]{:S(2)}) async-start(bf16[4,28,896]{2,1,0:T(8,128)(2,1)} %sum_senders.1), calls=%async_computation.3 | async-start | bytes 458752 | tf_op jit(solution)/shard_map/all_to_all | solution.py:381
  187.0 12.6 %all-to-all-done.3 = bf16[4,28,896]{2,1,0:T(8,128)(2,1)S(1)} async-done(((bf16[4,28,896]{2,1,0:T(8,128)(2,1)}), bf16[4,28,896]{2,1,0:T(8,128)(2,1)S(1)}, u32[]{:S(2)}, u32[]{:S(2)}) %all-to-all-start.3) | async-done | bytes 200736 | tf_op jit(solution)/shard_map/all_to_all | solution.py:381
  199.7 1.0 broadcast_in_dim.23
  200.7 8.7 %all-to-all-start.4 = ((bf16[16,28,896]{2,1,0:T(8,128)(2,1)}), bf16[16,28,896]{2,1,0:T(8,128)(2,1)S(1)}, u32[]{:S(2)}, u32[]{:S(2)}) async-start(bf16[16,28,896]{2,1,0:T(8,128)(2,1)} %broadcast_in_dim.23), calls=%async_computation.4 | async-start | bytes 1835008 | tf_op jit(solution)/shard_map/all_to_all | solution.py:393
  209.5 0.9 constant_dynamic-slice_fusion
  210.6 2.0 fusion.5
  212.6 2.0 copy-done.2
  214.7 1.9 copy-done.4
  216.6 4.7 %attn_grads.1 = (bf16[256,448]{1,0:T(8,128)(2,1)S(1)}, bf16[256,448]{1,0:T(8,128)(2,1)S(1)}) custom-call(s32[2]{0:T(128)S(1)} %pad_add_fusion.1.index_ref, bf16[8,256,896]{2,1,0:T(8,128)(2,1)S(1)} %copy-done.2, bf16[2,4,16,896]{3,2,1,0:T(8,128)(2,1)S(1)} %get-tuple-element.32.pieces_ref, bf16[4,448,896]{2,1,0:T(8,128)(2,1)S(1)} %bitcast.66, ...), custom_call_target="tpu_custom_call" | custom-call | flops 1644167168 | bytes 8388608 | tf_op jit(solution)/shard_map/attn_grads/pallas_call | solution.py:278
  221.3 0.7 copy-done.8
  222.2 6.8 %collective-permute-start.6 = (bf16[16,28,896]{2,0,1:T(8,128)(2,1)S(1)}, bf16[16,28,896]{2,0,1:T(8,128)(2,1)S(1)}, u32[]{:S(2)}, u32[]{:S(2)}) collective-permute-start(bf16[16,28,896]{2,0,1:T(8,128)(2,1)S(1)} %copy.22), channel_id=1, source_target_pairs={{0,16},{16,0},{1,17},{17,1},{2,18},{18,2},{3,19},{19,3},{4,20},{20... | collective-permute-start | bytes 2408456 | tf_op jit(solution)/shard_map/ppermute | solution.py:38
  229.0 1.9 collective-permute-start.5
  232.6 1.1 maximum_select_fusion
  233.9 1.4 join_halves.1
  (59 shorter events, 5.4 us)
Async XLA Ops:
  7.2 42.7 %copy-start = (bf16[896,896]{1,0:T(8,128)(2,1)S(1)}, bf16[896,896]{1,0:T(8,128)(2,1)}, u32[]{:S(2)}) copy-start(bf16[896,896]{1,0:T(8,128)(2,1)} %param.8) | copy-start | bytes 4816900
  7.2 106.0 %all-gather.4.cloned.1.call-start = ((), (), s32[]{:S(2)}) async-start(), calls=%async_computation.5 | async-start | bytes 4128768 | tf_op jit(solution)/shard_map/all_gather | solution.py:298
  23.1 24.5 %copy-start.9 = (bf16[1,2,128,896]{3,2,1,0:T(8,128)(2,1)S(1)}, bf16[1,2,128,896]{3,2,1,0:T(8,128)(2,1)}, u32[]{:S(2)}) copy-start(bf16[1,2,128,896]{3,2,1,0:T(8,128)(2,1)} %param.7) | copy-start | bytes 1376260
  25.2 7.8 %all-to-all-start = ((f32[4,3,896]{2,1,0:T(4,128)}), f32[4,3,896]{2,1,0:T(4,128)S(1)}, u32[]{:S(2)}, u32[]{:S(2)}) async-start(f32[4,3,896]{2,1,0:T(4,128)} %broadcast_in_dim.17), calls=%async_computation | async-start | bytes 114688 | tf_op jit(solution)/shard_map/all_to_all | solution.py:325
  35.6 28.4 %all-to-all-start.1 = ((f32[32,2,3840]{2,1,0:T(2,128)}), f32[32,2,3840]{2,1,0:T(2,128)}, u32[]{:S(2)}, u32[]{:S(2)}) async-start(f32[32,2,3840]{2,1,0:T(2,128)} %concatenate.50), calls=%async_computation.1 | async-start | bytes 1966080 | tf_op jit(solution)/shard_map/all_to_all | solution.py:344
  47.4 165.2 %all-gather.6.cloned.1.call-start = ((), (), s32[]{:S(2)}) async-start(), calls=%async_computation.6 | async-start | bytes 3411968 | tf_op jit(solution)/shard_map/all_gather | solution.py:353
  47.7 16.3 %collective-permute-start = (bf16[256,448]{1,0:T(8,128)(2,1)S(1)}, bf16[256,448]{1,0:T(8,128)(2,1)S(1)}, u32[]{:S(2)}, u32[]{:S(2)}) collective-permute-start(bf16[256,448]{1,0:T(8,128)(2,1)S(1)} %get-tuple-element.60), channel_id=1, source_target_pairs={{0,16},{16,0},{1,17},{17,1},{2,18},{18,2},{3,19},{19,3},{4,20},{20... | collective-permute-start | bytes 688136 | tf_op jit(solution)/shard_map/ppermute | solution.py:38
  50.6 23.7 %collective-permute-start.1 = (bf16[112,896]{1,0:T(8,128)(2,1)}, bf16[112,896]{1,0:T(8,128)(2,1)S(1)}, u32[]{:S(2)}, u32[]{:S(2)}) collective-permute-start(bf16[112,896]{1,0:T(8,128)(2,1)} %constant_dynamic-slice_fusion.1), channel_id=1, source_target_pairs={{0,0},{1,1},{2,2},{3,3},{18,16},{19,17},{16,18},{17,19},{129,128},... | collective-permute-start | bytes 602120 | tf_op jit(solution)/shard_map/ppermute | solution.py:301
  69.4 0.9 copy-start.5
  70.3 0.7 copy-start.6
  74.3 0.7 copy-start.10
  113.2 2.0 copy-start.1
  115.2 0.9 copy-start.7
  119.6 1.8 copy-start.3
  121.4 51.8 %all-to-all-start.2 = ((bf16[16,112,896]{2,1,0:T(8,128)(2,1)}), bf16[16,112,896]{2,1,0:T(8,128)(2,1)}, u32[]{:S(2)}, u32[]{:S(2)}) async-start(bf16[16,112,896]{2,1,0:T(8,128)(2,1)} %copy-done.3), calls=%async_computation.2 | async-start | bytes 6422528 | tf_op jit(solution)/shard_map/all_to_all | solution.py:358
  129.4 20.8 %collective-permute-start.2 = (f32[30,896]{1,0:T(8,128)S(1)}, f32[30,896]{1,0:T(8,128)S(1)}, u32[]{:S(2)}, u32[]{:S(2)}) collective-permute-start(f32[30,896]{1,0:T(8,128)S(1)} %get-tuple-element.62), channel_id=1, source_target_pairs={{0,1},{1,2},{2,3},{3,0},{4,5},{5,6},{6,7},{7,4},{8,9},{9,10},{10,1... | collective-permute-start | bytes 322568 | tf_op jit(solution)/shard_map/ppermute | solution.py:366
  137.5 25.7 %collective-permute-start.3 = (f32[30,896]{1,0:T(8,128)S(1)}, f32[30,896]{1,0:T(8,128)S(1)}, u32[]{:S(2)}, u32[]{:S(2)}) collective-permute-start(f32[30,896]{1,0:T(8,128)S(1)} %get-tuple-element.63), channel_id=1, source_target_pairs={{0,2},{1,3},{2,0},{3,1},{4,6},{5,7},{6,4},{7,5},{8,10},{9,11},{10,... | collective-permute-start | bytes 322568 | tf_op jit(solution)/shard_map/ppermute | solution.py:366
  143.9 22.1 %collective-permute-start.4 = (f32[30,896]{1,0:T(8,128)S(1)}, f32[30,896]{1,0:T(8,128)S(1)}, u32[]{:S(2)}, u32[]{:S(2)}) collective-permute-start(f32[30,896]{1,0:T(8,128)S(1)} %get-tuple-element.64), channel_id=1, source_target_pairs={{0,3},{1,0},{2,1},{3,2},{4,7},{5,4},{6,5},{7,6},{8,11},{9,8},{10,9... | collective-permute-start | bytes 322568 | tf_op jit(solution)/shard_map/ppermute | solution.py:366
  176.9 22.7 %all-to-all-start.3 = ((bf16[4,28,896]{2,1,0:T(8,128)(2,1)}), bf16[4,28,896]{2,1,0:T(8,128)(2,1)S(1)}, u32[]{:S(2)}, u32[]{:S(2)}) async-start(bf16[4,28,896]{2,1,0:T(8,128)(2,1)} %sum_senders.1), calls=%async_computation.3 | async-start | bytes 458752 | tf_op jit(solution)/shard_map/all_to_all | solution.py:381
  200.7 21.3 %all-to-all-start.4 = ((bf16[16,28,896]{2,1,0:T(8,128)(2,1)}), bf16[16,28,896]{2,1,0:T(8,128)(2,1)S(1)}, u32[]{:S(2)}, u32[]{:S(2)}) async-start(bf16[16,28,896]{2,1,0:T(8,128)(2,1)} %broadcast_in_dim.23), calls=%async_computation.4 | async-start | bytes 1835008 | tf_op jit(solution)/shard_map/all_to_all | solution.py:393
  212.6 2.0 copy-start.2
  214.7 1.9 copy-start.4
  221.3 0.7 copy-start.8
  222.2 11.5 %collective-permute-start.6 = (bf16[16,28,896]{2,0,1:T(8,128)(2,1)S(1)}, bf16[16,28,896]{2,0,1:T(8,128)(2,1)S(1)}, u32[]{:S(2)}, u32[]{:S(2)}) collective-permute-start(bf16[16,28,896]{2,0,1:T(8,128)(2,1)S(1)} %copy.22), channel_id=1, source_target_pairs={{0,16},{16,0},{1,17},{17,1},{2,18},{18,2},{3,19},{19,3},{4,20},{20... | collective-permute-start | bytes 2408456 | tf_op jit(solution)/shard_map/ppermute | solution.py:38
  229.0 3.6 %collective-permute-start.5 = (bf16[256,448]{1,0:T(8,128)(2,1)}, bf16[256,448]{1,0:T(8,128)(2,1)S(1)}, u32[]{:S(2)}, u32[]{:S(2)}) collective-permute-start(bf16[256,448]{1,0:T(8,128)(2,1)} %copy-done.8), channel_id=1, source_target_pairs={{0,16},{16,0},{1,17},{17,1},{2,18},{18,2},{3,19},{19,3},{4,20},{20... | collective-permute-start | bytes 688136 | tf_op jit(solution)/shard_map/ppermute | solution.py:38
Sparse Core Ops, SparseCore 0:
  10.1 103.0 all-gather.3
  116.2 91.0 all-gather.5

commit v10 on v7

--- a/solution.py
+++ b/solution.py
@@ -54,7 +54,7 @@
 
 def group_kernel(
     index_ref, got_ref, gain_ref,
-    scaled_ref, first_ref, gain_out_ref, loss_ref, pieces_ref, scale_ref, column_ref,
+    first_ref, gain_out_ref, loss_ref, pieces_ref, scale_ref, column_ref, scaled_ref,
 ):
     gain = gain_ref[...]
     raw, unit, inv_norm = [], [], []
@@ -124,7 +124,6 @@
     return pl.pallas_call(
         group_kernel,
         out_shape=(
-            jax.ShapeDtypeStruct((2, GROUP, D), f32),
             jax.ShapeDtypeStruct((NR, SLICE, COLS), f32),
             jax.ShapeDtypeStruct((NR, 1, COLS), f32),
             jax.ShapeDtypeStruct((8, 128), f32),
@@ -133,7 +132,8 @@
             jax.ShapeDtypeStruct((NC, TOK, 1), f32),
         ),
         in_specs=[pl.BlockSpec(memory_space=pltpu.SMEM), spec, spec],
-        out_specs=(spec,) * 7,
+        out_specs=(spec,) * 6,
+        scratch_shapes=[pltpu.VMEM((2, GROUP, D), f32)],
         compiler_params=pltpu.CompilerParams(vmem_limit_bytes=16 * 1024 * 1024),
         cost_estimate=pl.CostEstimate(
             flops=50 * GROUP * GROUP * D, bytes_accessed=3 * 1024 * 1024, transcendentals=4096
@@ -143,48 +143,71 @@
 
 
 def weight_kernel(
-    own_ref, other_ref, keep_ref, given_ref, pieces_ref, scale_ref, out_ref, coef_ref, acc_ref
+    own_hbm, other_hbm, keep_ref, given_ref, pieces_ref, scale_ref, out_ref, coef_ref, acc_ref,
+    state_ref, stage_ref, in_sems, out_sems,
 ):
+    loads = [
+        pltpu.make_async_copy(
+            source.at[block], state_ref.at[pair * NT + block], in_sems.at[pair * NT + block]
+        )
+        for pair, source in enumerate((own_hbm, other_hbm))
+        for block in range(NT)
+    ]
+    for load in loads:
+        load.start()
     token = lax.broadcasted_iota(jnp.int32, (TOK, PIECES), 0)
     part = lax.broadcasted_iota(jnp.int32, (TOK, PIECES), 1)
     part = part - jnp.where(token < SEQ, 0, 3)
     mask = (part >= 0) & (part < 3)
     scaled = []
-    for pair, (state_ref, attn_ref) in enumerate(
-        ((own_ref, keep_ref), (other_ref, given_ref))
-    ):
+    for pair, attn_ref in enumerate((keep_ref, given_ref)):
         inner = jnp.zeros((TOK, PIECES), f32)
         for block in range(NT):
-            inner = inner + dot_last(state_ref[block], pieces_ref[pair, block])
+            loads[pair * NT + block].wait()
+            inner = inner + dot_last(state_ref[pair * NT + block], pieces_ref[pair, block])
         inner = jnp.sum(jnp.where(mask, inner, 0.0), -1, keepdims=True)
         coef = scale_ref[pair] * inner
         coef_ref[pair] = coef
         scaled.append((attn_ref[...].astype(f32) * coef).astype(bf16))
     for block in range(NT):
         acc_ref[block] = lax.dot_general(
-            scaled[0], own_ref[block], contract_first, preferred_element_type=f32
+            scaled[0], state_ref[block], contract_first, preferred_element_type=f32
         ) + lax.dot_general(
-            scaled[1], other_ref[block], contract_first, preferred_element_type=f32
-        )
+            scaled[1], state_ref[NT + block], contract_first, preferred_element_type=f32
+        )
+    stores = []
     for place in range(NX * NY):
         rows = [
             acc_ref[block, place * SLICE : (place + 1) * SLICE, :] for block in range(NR)
         ]
-        out_ref[place] = jnp.concatenate(rows, 0).astype(bf16)
+        stage_ref[place] = jnp.concatenate(rows, 0).astype(bf16)
+        stores.append(
+            pltpu.make_async_copy(stage_ref.at[place], out_ref.at[place], out_sems.at[place])
+        )
+        stores[place].start()
+    for store in stores:
+        store.wait()
 
 
 def weight_partials(own, other, keep, given, pieces, scale):
     spec = pl.BlockSpec(memory_space=pltpu.VMEM)
+    hbm = pl.BlockSpec(memory_space=pltpu.HBM)
     return pl.pallas_call(
         weight_kernel,
         out_shape=(
             jax.ShapeDtypeStruct((NX * NY, NR * SLICE, COLS), bf16),
             jax.ShapeDtypeStruct((NC, TOK, 1), f32),
         ),
-        in_specs=[spec] * 6,
-        out_specs=(spec, spec),
-        scratch_shapes=[pltpu.VMEM((NR, HALF, COLS), f32)],
-        compiler_params=pltpu.CompilerParams(vmem_limit_bytes=24 * 1024 * 1024),
+        in_specs=[hbm, hbm] + [spec] * 4,
+        out_specs=(hbm, spec),
+        scratch_shapes=[
+            pltpu.VMEM((NR, HALF, COLS), f32),
+            pltpu.VMEM((NC * NT, TOK, FEAT), bf16),
+            pltpu.VMEM((NX * NY, NR * SLICE, COLS), bf16),
+            pltpu.SemaphoreType.DMA((NC * NT,)),
+            pltpu.SemaphoreType.DMA((NX * NY,)),
+        ],
+        compiler_params=pltpu.CompilerParams(vmem_limit_bytes=58 * 1024 * 1024),
         cost_estimate=pl.CostEstimate(
             flops=4 * TOK * HALF * D, bytes_accessed=8 * 1024 * 1024, transcendentals=0
         ),
@@ -253,34 +276,62 @@
 
 
 def attn_kernel(
-    shift_ref, own_ref, other_ref, pieces_ref, w_ref, coef_ref, first_ref, keep_ref, give_ref
+    shift_ref, own_hbm, other_hbm, pieces_ref, w_hbm, coef_ref, first_ref, keep_ref, give_ref,
+    state_ref, w_ref, state_sems, w_sems,
 ):
     shift = shift_ref[0]
-    for pair, (state_ref, out_ref) in enumerate(((own_ref, keep_ref), (other_ref, give_ref))):
-        tokens = jnp.zeros((TOK, HALF), f32)
-        rows = jnp.zeros((PIECES, HALF), f32)
-        for block in range(NX):
-            which = lax.rem(shift + block, NR)
-            tokens = tokens + dot_last(state_ref[which], w_ref[block])
-            rows = rows + dot_last(pieces_ref[pair, which], w_ref[block])
+    loads = []
+    for block in range(NX):
+        which = lax.rem(shift + block, NR)
+        loads.append(
+            [pltpu.make_async_copy(w_hbm.at[block], w_ref.at[block], w_sems.at[block])]
+            + [
+                pltpu.make_async_copy(
+                    source.at[which],
+                    state_ref.at[pair * NX + block],
+                    state_sems.at[pair * NX + block],
+                )
+                for pair, source in enumerate((own_hbm, other_hbm))
+            ]
+        )
+        for load in loads[block]:
+            load.start()
+    tokens = [jnp.zeros((TOK, HALF), f32) for pair in range(NC)]
+    rows = [jnp.zeros((PIECES, HALF), f32) for pair in range(NC)]
+    for block in range(NX):
+        which = lax.rem(shift + block, NR)
+        for load in loads[block]:
+            load.wait()
+        for pair in range(NC):
+            tokens[pair] = tokens[pair] + dot_last(state_ref[pair * NX + block], w_ref[block])
+            rows[pair] = rows[pair] + dot_last(pieces_ref[pair, which], w_ref[block])
+    for pair, out_ref in enumerate((keep_ref, give_ref)):
         for side in range(2):
-            row = rows[3 * side + 2 : 3 * side + 3] + rows[3 * side + 1 : 3 * side + 2]
-            row = row + rows[3 * side : 3 * side + 1]
+            at = 3 * side
+            row = rows[pair][at + 2 : at + 3] + rows[pair][at + 1 : at + 2]
+            row = row + rows[pair][at : at + 1]
             here = slice(side * SEQ, (side + 1) * SEQ)
             out_ref[here, :] = (
-                first_ref[pair, here, :] * row - coef_ref[pair, here, :] * tokens[here]
+                first_ref[pair, here, :] * row - coef_ref[pair, here, :] * tokens[pair][here]
             ).astype(bf16)
 
 
 def attn_grads(shift, own, other, pieces, w_all, coef, first):
     spec = pl.BlockSpec(memory_space=pltpu.VMEM)
+    hbm = pl.BlockSpec(memory_space=pltpu.HBM)
     out = jax.ShapeDtypeStruct((TOK, HALF), bf16)
     return pl.pallas_call(
         attn_kernel,
         out_shape=(out, out),
-        in_specs=[pl.BlockSpec(memory_space=pltpu.SMEM)] + [spec] * 6,
+        in_specs=[pl.BlockSpec(memory_space=pltpu.SMEM), hbm, hbm, spec, hbm, spec, spec],
         out_specs=(spec, spec),
-        compiler_params=pltpu.CompilerParams(vmem_limit_bytes=24 * 1024 * 1024),
+        scratch_shapes=[
+            pltpu.VMEM((NC * NX, TOK, FEAT), bf16),
+            pltpu.VMEM((NX, HALF, COLS), bf16),
+            pltpu.SemaphoreType.DMA((NC * NX,)),
+            pltpu.SemaphoreType.DMA((NX,)),
+        ],
+        compiler_params=pltpu.CompilerParams(vmem_limit_bytes=58 * 1024 * 1024),
         cost_estimate=pl.CostEstimate(
             flops=4 * TOK * HALF * D, bytes_accessed=8 * 1024 * 1024, transcendentals=0
         ),
@@ -342,16 +393,17 @@
         -1,
     )
     got = lax.all_to_all(send, DP, 0, 0)
-    got, state_all, attn_other = lax.optimization_barrier((got, state_all, attn_other))
+    got, attn_other = lax.optimization_barrier((got, attn_other))
 
     other_index = dp_index + 1 - 2 * ic
+    first, gain_part, loss_part, pieces, scale, first_col = group_math(
+        jnp.stack([dp_index, other_index]), got.transpose(1, 0, 2), gain
+    )
+
+    scale, state_all = lax.optimization_barrier((scale, state_all))
     state_other = swap_core(state_all)
-    got, w_moved = lax.optimization_barrier((got, w_moved))
+    scale, w_moved = lax.optimization_barrier((scale, w_moved))
     w_all = lax.all_gather(w_moved, PLANE).reshape(NX, HALF, COLS)
-    scaled, first, gain_part, loss_part, pieces, scale, first_col = group_math(
-        jnp.stack([dp_index, other_index]), got.transpose(1, 0, 2), gain
-    )
-
     partial, coef = weight_partials(
         state_all, state_other, attn_keep, attn_other, pieces, scale
     )
@@ -381,7 +433,9 @@
     spread, first_sum, totals = lax.optimization_barrier((spread, first_sum, totals))
     second = lax.all_to_all(sum_senders(spread), "r", 0, 0)
 
-    row_here = lax.dynamic_slice(scaled, (0, dp_index, it * FEAT), (2, 1, FEAT))
+    row_here = lax.dynamic_index_in_dim(pieces[0], it, 0, keepdims=False)[:6]
+    row_here = row_here.astype(f32).reshape(2, 3, FEAT)
+    row_here = (row_here[:, :1] + row_here[:, 1:2]) + row_here[:, 2:]
     state_grad = first_col[0].reshape(2, SEQ, 1) * row_here - states * coef[0].reshape(2, SEQ, 1)
     grad_hidden = state_grad.astype(bf16).reshape(1, 2, SEQ, FEAT)
     keep, give = attn_grads(

time: 221 us -> 219 us (level)
  the two profiles are of different devices: /device:TPU:33 before, /device:TPU:1 now
where the time goes in v10:
time: 219 us; the launch traced here: 218 us
  starting transfers between devices  94.4 us (43%)
  waiting for transfers between devices  45.9 us (21%)
  Pallas kernels  26.9 us (12%)
  local copies, waits for them, and re-layouts  15.4 us (7%)
  between operations  15.3 us (7%)
  blocking collectives  11.8 us (5%)
  other arithmetic  8.33 us (4%)
    ppermute x3, starting transfers between devices, body(): lax.ppermute(jnp.concatenate([outgoing, tail], 0), 'r', [(j, (j + step) %...  22.4 us
    ppermute x4, starting transfers between devices, swap_core(): return lax.ppermute(value, 'c', [(0, 1), (1, 0)])  20 us
    all_to_all x1, waiting for transfers between devices, body(): spread = lax.all_to_all(partial, PLANE, 0, 0)  14.1 us
    ppermute x3, waiting for transfers between devices, body(): lax.ppermute(jnp.concatenate([outgoing, tail], 0), 'r', [(j, (j + step) %...  13.7 us
    ppermute x1, starting transfers between devices, body(): lax.ppermute(w_mine, ('x', 'c', 'r'), [((i * NC + k) * NR + (j + i + 2 *...  13.1 us
    all_to_all x1, starting transfers between devices, body(): half = lax.all_to_all(done, PLANE, 0, 0)  12.1 us
    psum x1, blocking collectives, body(): square = lax.psum(jnp.sum(states * states, -1), 't') / D  11.8 us
    all_to_all x1, starting transfers between devices, body(): got = lax.all_to_all(send, DP, 0, 0)  11 us
  transfers between devices with their start and end apart: 15, of which 9 were waited for; matrix products, arithmetic and copies ran while one was open for 8% of the time, Pallas kernels for 12%

profile of v10, /device:TPU:1, one launch (start us, length us, event | category | flops | bytes accessed | tf_op | source)
XLA Modules:
  0.0 218.1 jit_solution(12346837725033350103)
XLA Ops:
  7.2 0.7 all-gather.4.cloned.1.call-update
  7.9 0.7 broadcast_in_dim.16
  8.6 1.2 fusion.2
  9.8 11.8 %psum.7 = f32[2,128]{1,0:T(2,128)S(1)} all-reduce(f32[2,128]{1,0:T(2,128)S(1)} %fusion.2), channel_id=1, replica_groups=mesh['x'=4,'y'=4,'c'=2,'t'=4,'r'=4] {'t'}, use_global_device_ids=true, to_apply=%region_1.2 | all-reduce | flops 256 | bytes 2048 | tf_op jit(solution)/shard_map/psum | solution.py:367
  21.6 0.7 convert_bitcast_fusion.1
  22.3 0.7 fusion.10
  23.1 1.4 fusion.6
  24.5 0.6 broadcast_in_dim.17
  25.1 3.3 %all-to-all-start = ((f32[4,3,896]{2,1,0:T(4,128)}), f32[4,3,896]{2,1,0:T(4,128)S(1)}, u32[]{:S(2)}, u32[]{:S(2)}) async-start(f32[4,3,896]{2,1,0:T(4,128)} %broadcast_in_dim.17), calls=%async_computation | async-start | bytes 114688 | tf_op jit(solution)/shard_map/all_to_all | solution.py:376
  29.4 3.6 %all-to-all-done = f32[4,3,896]{2,1,0:T(4,128)S(1)} async-done(((f32[4,3,896]{2,1,0:T(4,128)}), f32[4,3,896]{2,1,0:T(4,128)S(1)}, u32[]{:S(2)}, u32[]{:S(2)}) %all-to-all-start) | async-done | bytes 43040 | tf_op jit(solution)/shard_map/all_to_all | solution.py:376
  33.6 2.2 %concatenate.50 = f32[32,2,3840]{2,1,0:T(2,128)} concatenate(f32[32,2,3712]{2,1,0:T(2,128)S(1)} %broadcast_in_dim.18, f32[32,2,28]{2,1,0:T(2,128)S(1)} %copy.20, f32[32,2,2]{2,1,0:T(2,128)S(1)} %broadcast_in_dim.19, f32[32,2,98]{2,1,0:T(2,128)S(1)} %broadcast_in_dim.20), dimensions={2} | concatenate | bytes 1966080 | tf_op jit(solution)/shard_map/concatenate | solution.py:386
  35.9 11.0 %all-to-all-start.1 = ((f32[32,2,3840]{2,1,0:T(2,128)}), f32[32,2,3840]{2,1,0:T(2,128)S(1)}, u32[]{:S(2)}, u32[]{:S(2)}) async-start(f32[32,2,3840]{2,1,0:T(2,128)} %concatenate.50), calls=%async_computation.1 | async-start | bytes 1966080 | tf_op jit(solution)/shard_map/all_to_all | solution.py:395
  47.0 0.8 broadcast_select_fusion
  47.8 2.1 collective-permute-start
  50.0 0.7 constant_dynamic-slice_fusion
  50.7 13.1 %collective-permute-start.2 = (bf16[112,896]{1,0:T(8,128)(2,1)}, bf16[112,896]{1,0:T(8,128)(2,1)S(1)}, u32[]{:S(2)}, u32[]{:S(2)}) collective-permute-start(bf16[112,896]{1,0:T(8,128)(2,1)} %constant_dynamic-slice_fusion), channel_id=1, source_target_pairs={{0,0},{1,1},{2,2},{3,3},{18,16},{19,17},{16,18},{17,19},{129,128},... | collective-permute-start | bytes 602120 | tf_op jit(solution)/shard_map/ppermute | solution.py:352
  63.9 0.8 slice.86
  65.5 4.2 %group_math.1 = (f32[4,28,896]{2,1,0:T(8,128)S(1)}, f32[4,1,896]{2,1,0:T(1,128)S(1)}, f32[8,128]{1,0:T(8,128)S(1)}, bf16[2,4,16,896]{3,2,1,0:T(8,128)(2,1)S(1)},...) custom-call(s32[2]{0:T(128)S(1)} %pad_add_fusion.index_ref, f32[2,32,3840]{2,1,0:T(8,128)S(1)} %bitcast.65, ...), custom_call_target="tpu_custom_call" | custom-call | flops 183500800 | bytes 3145728 | tf_op jit(solution)/shard_map/group_math/pallas_call | solution.py:124
  69.6 0.7 copy-done.1
  70.3 0.7 copy-done.3
  71.0 0.7 copy-done.5
  71.7 0.7 copy-done.10
  72.4 1.9 collective-permute-start.1
  74.4 4.0 %collective-permute-done.1.other_hbm = bf16[4,256,896]{2,1,0:T(8,128)(2,1)S(1)} collective-permute-done((bf16[4,256,896]{2,1,0:T(8,128)(2,1)}, bf16[4,256,896]{2,1,0:T(8,128)(2,1)S(1)}, u32[]{:S(2)}, u32[]{:S(2)}) %collective-permute-start.1) | collective-permute-done | bytes 1835040 | tf_op jit(solution)/shard_map/ppermute | solution.py:38
  78.3 1.3 copy-done.8
  79.7 9.4 %weight_partials.1 = (bf16[16,112,896]{2,1,0:T(8,128)(2,1)}, f32[2,256,1]{2,1,0:T(8,128)}) custom-call(bf16[4,256,896]{2,1,0:T(8,128)(2,1)} %all-gather.4.cloned.1.call-done.own_hbm, bf16[4,256,896]{2,1,0:T(8,128)(2,1)} %copy-done.8, bf16[256,448]{1,0:T(8,128)(2,1)} %get-tuple-element.66.keep_ref, bf16[256,448]{1,0:T(8,128)(2,1)} %copy-done.12, ...), custom_call_target="tpu_custom_call" | custom-call | flops 1644167168 | bytes 8388608 | tf_op jit(solution)/shard_map/weight_partials/pallas_call | solution.py:195
  89.1 7.8 %all-to-all-start.2 = ((bf16[16,112,896]{2,1,0:T(8,128)(2,1)}), bf16[16,112,896]{2,1,0:T(8,128)(2,1)}, u32[]{:S(2)}, u32[]{:S(2)}) async-start(bf16[16,112,896]{2,1,0:T(8,128)(2,1)} %get-tuple-element.42), calls=%async_computation.2 | async-start | bytes 6422528 | tf_op jit(solution)/shard_map/all_to_all | solution.py:411
  97.5 0.7 pad.18.clone
  98.3 11.8 %collective-permute-start.5 = (f32[30,896]{1,0:T(8,128)S(1)}, f32[30,896]{1,0:T(8,128)S(1)}, u32[]{:S(2)}, u32[]{:S(2)}) collective-permute-start(f32[30,896]{1,0:T(8,128)S(1)} %get-tuple-element.70), channel_id=1, source_target_pairs={{0,3},{1,0},{2,1},{3,2},{4,7},{5,4},{6,5},{7,6},{8,11},{9,8},{10,9... | collective-permute-start | bytes 322568 | tf_op jit(solution)/shard_map/ppermute | solution.py:419
  110.2 0.7 pad_bitcast_fusion
  110.8 7.5 %collective-permute-start.4 = (f32[30,896]{1,0:T(8,128)S(1)}, f32[30,896]{1,0:T(8,128)S(1)}, u32[]{:S(2)}, u32[]{:S(2)}) collective-permute-start(f32[30,896]{1,0:T(8,128)S(1)} %get-tuple-element.69), channel_id=1, source_target_pairs={{0,2},{1,3},{2,0},{3,1},{4,6},{5,7},{6,4},{7,5},{8,10},{9,11},{10,... | collective-permute-start | bytes 322568 | tf_op jit(solution)/shard_map/ppermute | solution.py:419
  118.3 3.1 %collective-permute-start.3 = (f32[30,896]{1,0:T(8,128)S(1)}, f32[30,896]{1,0:T(8,128)S(1)}, u32[]{:S(2)}, u32[]{:S(2)}) collective-permute-start(f32[30,896]{1,0:T(8,128)S(1)} %get-tuple-element.68), channel_id=1, source_target_pairs={{0,1},{1,2},{2,3},{3,0},{4,5},{5,6},{6,7},{7,4},{8,9},{9,10},{10,1... | collective-permute-start | bytes 322568 | tf_op jit(solution)/shard_map/ppermute | solution.py:419
  121.4 0.8 collective-permute-done.5
  122.3 9.9 %collective-permute-done.4 = f32[30,896]{1,0:T(8,128)S(1)} collective-permute-done((f32[30,896]{1,0:T(8,128)S(1)}, f32[30,896]{1,0:T(8,128)S(1)}, u32[]{:S(2)}, u32[]{:S(2)}) %collective-permute-start.4) | collective-permute-done | bytes 107552 | tf_op jit(solution)/shard_map/ppermute | solution.py:419
  132.1 3.0 %collective-permute-done.3 = f32[30,896]{1,0:T(8,128)S(1)} collective-permute-done((f32[30,896]{1,0:T(8,128)S(1)}, f32[30,896]{1,0:T(8,128)S(1)}, u32[]{:S(2)}, u32[]{:S(2)}) %collective-permute-start.3) | collective-permute-done | bytes 107552 | tf_op jit(solution)/shard_map/ppermute | solution.py:419
  135.2 14.1 %all-to-all-done.2.spread_ref = bf16[16,112,896]{2,1,0:T(8,128)(2,1)} async-done(((bf16[16,112,896]{2,1,0:T(8,128)(2,1)}), bf16[16,112,896]{2,1,0:T(8,128)(2,1)}, u32[]{:S(2)}, u32[]{:S(2)}) %all-to-all-start.2) | async-done | bytes 3211296 | tf_op jit(solution)/shard_map/all_to_all | solution.py:411
  149.3 3.7 %sum_senders.1 = bf16[4,28,896]{2,1,0:T(8,128)(2,1)} custom-call(bf16[16,112,896]{2,1,0:T(8,128)(2,1)} %all-to-all-done.2.spread_ref), custom_call_target="tpu_custom_call" | custom-call | flops 1605632 | bytes 4194304 | tf_op jit(solution)/shard_map/sum_senders/pallas_call | solution.py:239
  153.0 4.6 %all-to-all-start.3 = ((bf16[4,28,896]{2,1,0:T(8,128)(2,1)}), bf16[4,28,896]{2,1,0:T(8,128)(2,1)S(1)}, u32[]{:S(2)}, u32[]{:S(2)}) async-start(bf16[4,28,896]{2,1,0:T(8,128)(2,1)} %sum_senders.1), calls=%async_computation.3 | async-start | bytes 458752 | tf_op jit(solution)/shard_map/all_to_all | solution.py:434
  157.6 8.6 %all-gather.6.cloned.1.call-done = bf16[1792,896]{1,0:T(8,128)(2,1)} async-done(((bf16[112,896]{1,0:T(8,128)(2,1)}), bf16[1792,896]{1,0:T(8,128)(2,1)}) %all-gather.6.cloned.1.call-update) | async-done | bytes 3211280 | tf_op jit(solution)/shard_map/all_gather | solution.py:406
  166.3 8.3 %attn_grads.1 = (bf16[256,448]{1,0:T(8,128)(2,1)}, bf16[256,448]{1,0:T(8,128)(2,1)}) custom-call(s32[1]{0:T(128)} %bitcast.26.shift_ref, bf16[4,256,896]{2,1,0:T(8,128)(2,1)} %all-gather.4.cloned.1.call-done.own_hbm, bf16[4,256,896]{2,1,0:T(8,128)(2,1)} %copy-done.8, bf16[2,4,16,896]{3,2,1,0:T(8,128)(2,1)} %copy-done.3, bf16[4,448,896]{2,1,0:T(8,128)(2,1)} %bitcast.68, ...), custom_call_target="tpu_custom_call" | custom-call | flops 1644167168 | bytes 8388608 | tf_op jit(solution)/shard_map/attn_grads/pallas_call | solution.py:323
  174.7 1.0 broadcast_in_dim.23
  175.7 12.1 %all-to-all-start.4 = ((bf16[16,28,896]{2,1,0:T(8,128)(2,1)}), bf16[16,28,896]{2,1,0:T(8,128)(2,1)S(1)}, u32[]{:S(2)}, u32[]{:S(2)}) async-start(bf16[16,28,896]{2,1,0:T(8,128)(2,1)} %broadcast_in_dim.23), calls=%async_computation.4 | async-start | bytes 1835008 | tf_op jit(solution)/shard_map/all_to_all | solution.py:449
  188.1 7.5 %collective-permute-start.6 = (bf16[256,448]{1,0:T(8,128)(2,1)}, bf16[256,448]{1,0:T(8,128)(2,1)S(1)}, u32[]{:S(2)}, u32[]{:S(2)}) collective-permute-start(bf16[256,448]{1,0:T(8,128)(2,1)} %get-tuple-element.55), channel_id=1, source_target_pairs={{0,16},{16,0},{1,17},{17,1},{2,18},{18,2},{3,19},{19,3},{4,20},{20... | collective-permute-start | bytes 688136 | tf_op jit(solution)/shard_map/ppermute | solution.py:38
  195.6 1.0 fusion.5
  196.9 2.1 maximum_select_fusion
  199.3 8.5 %collective-permute-start.7 = (bf16[16,28,896]{2,0,1:T(8,128)(2,1)S(1)}, bf16[16,28,896]{2,0,1:T(8,128)(2,1)S(1)}, u32[]{:S(2)}, u32[]{:S(2)}) collective-permute-start(bf16[16,28,896]{2,0,1:T(8,128)(2,1)S(1)} %copy.22), channel_id=1, source_target_pairs={{0,16},{16,0},{1,17},{17,1},{2,18},{18,2},{3,19},{19,3},{4,20},{20... | collective-permute-start | bytes 2408456 | tf_op jit(solution)/shard_map/ppermute | solution.py:38
  208.9 0.8 collective-permute-done.7
  209.8 1.4 join_halves.1
  (67 shorter events, 4.7 us)
Async XLA Ops:
  7.2 42.8 %copy-start = (bf16[896,896]{1,0:T(8,128)(2,1)S(1)}, bf16[896,896]{1,0:T(8,128)(2,1)}, u32[]{:S(2)}) copy-start(bf16[896,896]{1,0:T(8,128)(2,1)} %param.8) | copy-start | bytes 4816900
  7.2 64.5 %all-gather.4.cloned.1.call-start = ((), (), s32[]{:S(2)}) async-start(), calls=%async_computation.5 | async-start | bytes 2293760 | tf_op jit(solution)/shard_map/all_gather | solution.py:349
  25.1 7.8 %all-to-all-start = ((f32[4,3,896]{2,1,0:T(4,128)}), f32[4,3,896]{2,1,0:T(4,128)S(1)}, u32[]{:S(2)}, u32[]{:S(2)}) async-start(f32[4,3,896]{2,1,0:T(4,128)} %broadcast_in_dim.17), calls=%async_computation | async-start | bytes 114688 | tf_op jit(solution)/shard_map/all_to_all | solution.py:376
  33.0 0.6 copy-start.11
  33.6 13.3 %copy-start.7 = (bf16[1,2,128,896]{3,2,1,0:T(8,128)(2,1)S(1)}, bf16[1,2,128,896]{3,2,1,0:T(8,128)(2,1)}, u32[]{:S(2)}) copy-start(bf16[1,2,128,896]{3,2,1,0:T(8,128)(2,1)} %param.7) | copy-start | bytes 1376260
  35.9 28.9 %all-to-all-start.1 = ((f32[32,2,3840]{2,1,0:T(2,128)}), f32[32,2,3840]{2,1,0:T(2,128)S(1)}, u32[]{:S(2)}, u32[]{:S(2)}) async-start(f32[32,2,3840]{2,1,0:T(2,128)} %concatenate.50), calls=%async_computation.1 | async-start | bytes 1966080 | tf_op jit(solution)/shard_map/all_to_all | solution.py:395
  46.9 119.4 %all-gather.6.cloned.1.call-start = ((), (), s32[]{:S(2)}) async-start(), calls=%async_computation.6 | async-start | bytes 3411968 | tf_op jit(solution)/shard_map/all_gather | solution.py:406
  47.8 16.9 %collective-permute-start = (bf16[256,448]{1,0:T(8,128)(2,1)S(1)}, bf16[256,448]{1,0:T(8,128)(2,1)S(1)}, u32[]{:S(2)}, u32[]{:S(2)}) collective-permute-start(bf16[256,448]{1,0:T(8,128)(2,1)S(1)} %get-tuple-element.67), channel_id=1, source_target_pairs={{0,16},{16,0},{1,17},{17,1},{2,18},{18,2},{3,19},{19,3},{4,20},{20... | collective-permute-start | bytes 688136 | tf_op jit(solution)/shard_map/ppermute | solution.py:38
  50.7 21.1 %collective-permute-start.2 = (bf16[112,896]{1,0:T(8,128)(2,1)}, bf16[112,896]{1,0:T(8,128)(2,1)S(1)}, u32[]{:S(2)}, u32[]{:S(2)}) collective-permute-start(bf16[112,896]{1,0:T(8,128)(2,1)} %constant_dynamic-slice_fusion), channel_id=1, source_target_pairs={{0,0},{1,1},{2,2},{3,3},{18,16},{19,17},{16,18},{17,19},{129,128},... | collective-permute-start | bytes 602120 | tf_op jit(solution)/shard_map/ppermute | solution.py:352
  64.8 0.7 copy-start.12
  69.6 0.7 copy-start.1
  70.3 0.7 copy-start.3
  71.0 0.7 copy-start.5
  71.7 0.7 copy-start.10
  72.4 5.9 %collective-permute-start.1 = (bf16[4,256,896]{2,1,0:T(8,128)(2,1)}, bf16[4,256,896]{2,1,0:T(8,128)(2,1)S(1)}, u32[]{:S(2)}, u32[]{:S(2)}) collective-permute-start(bf16[4,256,896]{2,1,0:T(8,128)(2,1)} %all-gather.4.cloned.1.call-done.own_hbm), channel_id=1, source_target_pairs={{0,16},{16,0},{1,17},{17,1},{2,18},{18,2},{3,19},{19,3},{4,20},{20... | collective-permute-start | bytes 5505032 | tf_op jit(solution)/shard_map/ppermute | solution.py:38
  78.3 1.3 copy-start.8
  89.1 60.3 %all-to-all-start.2 = ((bf16[16,112,896]{2,1,0:T(8,128)(2,1)}), bf16[16,112,896]{2,1,0:T(8,128)(2,1)}, u32[]{:S(2)}, u32[]{:S(2)}) async-start(bf16[16,112,896]{2,1,0:T(8,128)(2,1)} %get-tuple-element.42), calls=%async_computation.2 | async-start | bytes 6422528 | tf_op jit(solution)/shard_map/all_to_all | solution.py:411
  98.3 23.9 %collective-permute-start.5 = (f32[30,896]{1,0:T(8,128)S(1)}, f32[30,896]{1,0:T(8,128)S(1)}, u32[]{:S(2)}, u32[]{:S(2)}) collective-permute-start(f32[30,896]{1,0:T(8,128)S(1)} %get-tuple-element.70), channel_id=1, source_target_pairs={{0,3},{1,0},{2,1},{3,2},{4,7},{5,4},{6,5},{7,6},{8,11},{9,8},{10,9... | collective-permute-start | bytes 322568 | tf_op jit(solution)/shard_map/ppermute | solution.py:419
  110.8 21.3 %collective-permute-start.4 = (f32[30,896]{1,0:T(8,128)S(1)}, f32[30,896]{1,0:T(8,128)S(1)}, u32[]{:S(2)}, u32[]{:S(2)}) collective-permute-start(f32[30,896]{1,0:T(8,128)S(1)} %get-tuple-element.69), channel_id=1, source_target_pairs={{0,2},{1,3},{2,0},{3,1},{4,6},{5,7},{6,4},{7,5},{8,10},{9,11},{10,... | collective-permute-start | bytes 322568 | tf_op jit(solution)/shard_map/ppermute | solution.py:419
  118.3 16.8 %collective-permute-start.3 = (f32[30,896]{1,0:T(8,128)S(1)}, f32[30,896]{1,0:T(8,128)S(1)}, u32[]{:S(2)}, u32[]{:S(2)}) collective-permute-start(f32[30,896]{1,0:T(8,128)S(1)} %get-tuple-element.68), channel_id=1, source_target_pairs={{0,1},{1,2},{2,3},{3,0},{4,5},{5,6},{6,7},{7,4},{8,9},{9,10},{10,1... | collective-permute-start | bytes 322568 | tf_op jit(solution)/shard_map/ppermute | solution.py:419
  135.2 22.4 %copy-start.4 = (bf16[2,4,16,896]{3,2,1,0:T(8,128)(2,1)S(1)}, bf16[2,4,16,896]{3,2,1,0:T(8,128)(2,1)}, u32[]{:S(2)}) copy-start(bf16[2,4,16,896]{3,2,1,0:T(8,128)(2,1)} %copy-done.3) | copy-start | bytes 688132
  153.0 21.6 %all-to-all-start.3 = ((bf16[4,28,896]{2,1,0:T(8,128)(2,1)}), bf16[4,28,896]{2,1,0:T(8,128)(2,1)S(1)}, u32[]{:S(2)}, u32[]{:S(2)}) async-start(bf16[4,28,896]{2,1,0:T(8,128)(2,1)} %sum_senders.1), calls=%async_computation.3 | async-start | bytes 458752 | tf_op jit(solution)/shard_map/all_to_all | solution.py:434
  174.6 13.3 %copy-start.2 = (f32[2,256,1]{2,1,0:T(8,128)S(1)}, f32[2,256,1]{2,1,0:T(8,128)}, u32[]{:S(2)}) copy-start(f32[2,256,1]{2,1,0:T(8,128)} %copy-done.1) | copy-start | bytes 6148
  174.6 13.4 %copy-start.9 = (f32[2,256,1]{2,1,0:T(8,128)S(1)}, f32[2,256,1]{2,1,0:T(8,128)}, u32[]{:S(2)}) copy-start(f32[2,256,1]{2,1,0:T(8,128)} %get-tuple-element.49.coef_ref) | copy-start | bytes 6148
  174.6 21.0 %copy-start.6 = (bf16[1,2,128,896]{3,2,1,0:T(8,128)(2,1)S(1)}, bf16[1,2,128,896]{3,2,1,0:T(8,128)(2,1)}, u32[]{:S(2)}) copy-start(bf16[1,2,128,896]{3,2,1,0:T(8,128)(2,1)} %param.6) | copy-start | bytes 1376260
  175.7 23.3 %all-to-all-start.4 = ((bf16[16,28,896]{2,1,0:T(8,128)(2,1)}), bf16[16,28,896]{2,1,0:T(8,128)(2,1)S(1)}, u32[]{:S(2)}, u32[]{:S(2)}) async-start(bf16[16,28,896]{2,1,0:T(8,128)(2,1)} %broadcast_in_dim.23), calls=%async_computation.4 | async-start | bytes 1835008 | tf_op jit(solution)/shard_map/all_to_all | solution.py:449
  188.1 8.8 %collective-permute-start.6 = (bf16[256,448]{1,0:T(8,128)(2,1)}, bf16[256,448]{1,0:T(8,128)(2,1)S(1)}, u32[]{:S(2)}, u32[]{:S(2)}) collective-permute-start(bf16[256,448]{1,0:T(8,128)(2,1)} %get-tuple-element.55), channel_id=1, source_target_pairs={{0,16},{16,0},{1,17},{17,1},{2,18},{18,2},{3,19},{19,3},{4,20},{20... | collective-permute-start | bytes 688136 | tf_op jit(solution)/shard_map/ppermute | solution.py:38
  199.3 10.4 %collective-permute-start.7 = (bf16[16,28,896]{2,0,1:T(8,128)(2,1)S(1)}, bf16[16,28,896]{2,0,1:T(8,128)(2,1)S(1)}, u32[]{:S(2)}, u32[]{:S(2)}) collective-permute-start(bf16[16,28,896]{2,0,1:T(8,128)(2,1)S(1)} %copy.22), channel_id=1, source_target_pairs={{0,16},{16,0},{1,17},{17,1},{2,18},{18,2},{3,19},{19,3},{4,20},{20... | collective-permute-start | bytes 2408456 | tf_op jit(solution)/shard_map/ppermute | solution.py:38
Sparse Core Ops, SparseCore 0:
  10.1 55.9 all-gather.3
  72.6 93.6 all-gather.5

commit v11 on v10

--- a/solution.py
+++ b/solution.py
@@ -23,7 +23,8 @@
 TOK = 2 * SEQ
 HALF = FEAT // NC
 SLICE = HALF // (NX * NY)
-W_ROWS = HALF // NY
+W_FIRST = 64
+W_REST = HALF // NY - W_FIRST
 PIECES = 16
 GROUP = NX * NY * NC
 
@@ -143,71 +144,48 @@
 
 
 def weight_kernel(
-    own_hbm, other_hbm, keep_ref, given_ref, pieces_ref, scale_ref, out_ref, coef_ref, acc_ref,
-    state_ref, stage_ref, in_sems, out_sems,
+    own_ref, other_ref, keep_ref, given_ref, pieces_ref, scale_ref, out_ref, coef_ref, acc_ref
 ):
-    loads = [
-        pltpu.make_async_copy(
-            source.at[block], state_ref.at[pair * NT + block], in_sems.at[pair * NT + block]
-        )
-        for pair, source in enumerate((own_hbm, other_hbm))
-        for block in range(NT)
-    ]
-    for load in loads:
-        load.start()
     token = lax.broadcasted_iota(jnp.int32, (TOK, PIECES), 0)
     part = lax.broadcasted_iota(jnp.int32, (TOK, PIECES), 1)
     part = part - jnp.where(token < SEQ, 0, 3)
     mask = (part >= 0) & (part < 3)
     scaled = []
-    for pair, attn_ref in enumerate((keep_ref, given_ref)):
+    for pair, (state_ref, attn_ref) in enumerate(
+        ((own_ref, keep_ref), (other_ref, given_ref))
+    ):
         inner = jnp.zeros((TOK, PIECES), f32)
         for block in range(NT):
-            loads[pair * NT + block].wait()
-            inner = inner + dot_last(state_ref[pair * NT + block], pieces_ref[pair, block])
+            inner = inner + dot_last(state_ref[block], pieces_ref[pair, block])
         inner = jnp.sum(jnp.where(mask, inner, 0.0), -1, keepdims=True)
         coef = scale_ref[pair] * inner
         coef_ref[pair] = coef
         scaled.append((attn_ref[...].astype(f32) * coef).astype(bf16))
     for block in range(NT):
         acc_ref[block] = lax.dot_general(
-            scaled[0], state_ref[block], contract_first, preferred_element_type=f32
+            scaled[0], own_ref[block], contract_first, preferred_element_type=f32
         ) + lax.dot_general(
-            scaled[1], state_ref[NT + block], contract_first, preferred_element_type=f32
+            scaled[1], other_ref[block], contract_first, preferred_element_type=f32
         )
-    stores = []
     for place in range(NX * NY):
         rows = [
             acc_ref[block, place * SLICE : (place + 1) * SLICE, :] for block in range(NR)
         ]
-        stage_ref[place] = jnp.concatenate(rows, 0).astype(bf16)
-        stores.append(
-            pltpu.make_async_copy(stage_ref.at[place], out_ref.at[place], out_sems.at[place])
-        )
-        stores[place].start()
-    for store in stores:
-        store.wait()
+        out_ref[place] = jnp.concatenate(rows, 0).astype(bf16)
 
 
 def weight_partials(own, other, keep, given, pieces, scale):
     spec = pl.BlockSpec(memory_space=pltpu.VMEM)
-    hbm = pl.BlockSpec(memory_space=pltpu.HBM)
     return pl.pallas_call(
         weight_kernel,
         out_shape=(
             jax.ShapeDtypeStruct((NX * NY, NR * SLICE, COLS), bf16),
             jax.ShapeDtypeStruct((NC, TOK, 1), f32),
         ),
-        in_specs=[hbm, hbm] + [spec] * 4,
-        out_specs=(hbm, spec),
-        scratch_shapes=[
-            pltpu.VMEM((NR, HALF, COLS), f32),
-            pltpu.VMEM((NC * NT, TOK, FEAT), bf16),
-            pltpu.VMEM((NX * NY, NR * SLICE, COLS), bf16),
-            pltpu.SemaphoreType.DMA((NC * NT,)),
-            pltpu.SemaphoreType.DMA((NX * NY,)),
-        ],
-        compiler_params=pltpu.CompilerParams(vmem_limit_bytes=58 * 1024 * 1024),
+        in_specs=[spec] * 6,
+        out_specs=(spec, spec),
+        scratch_shapes=[pltpu.VMEM((NR, HALF, COLS), f32)],
+        compiler_params=pltpu.CompilerParams(vmem_limit_bytes=24 * 1024 * 1024),
         cost_estimate=pl.CostEstimate(
             flops=4 * TOK * HALF * D, bytes_accessed=8 * 1024 * 1024, transcendentals=0
         ),
@@ -280,6 +258,7 @@
     state_ref, w_ref, state_sems, w_sems,
 ):
     shift = shift_ref[0]
+    columns = w_ref.shape[1]
     loads = []
     for block in range(NX):
         which = lax.rem(shift + block, NR)
@@ -296,8 +275,8 @@
         )
         for load in loads[block]:
             load.start()
-    tokens = [jnp.zeros((TOK, HALF), f32) for pair in range(NC)]
-    rows = [jnp.zeros((PIECES, HALF), f32) for pair in range(NC)]
+    tokens = [jnp.zeros((TOK, columns), f32) for pair in range(NC)]
+    rows = [jnp.zeros((PIECES, columns), f32) for pair in range(NC)]
     for block in range(NX):
         which = lax.rem(shift + block, NR)
         for load in loads[block]:
@@ -319,7 +298,8 @@
 def attn_grads(shift, own, other, pieces, w_all, coef, first):
     spec = pl.BlockSpec(memory_space=pltpu.VMEM)
     hbm = pl.BlockSpec(memory_space=pltpu.HBM)
-    out = jax.ShapeDtypeStruct((TOK, HALF), bf16)
+    columns = w_all.shape[1]
+    out = jax.ShapeDtypeStruct((TOK, columns), bf16)
     return pl.pallas_call(
         attn_kernel,
         out_shape=(out, out),
@@ -327,13 +307,13 @@
         out_specs=(spec, spec),
         scratch_shapes=[
             pltpu.VMEM((NC * NX, TOK, FEAT), bf16),
-            pltpu.VMEM((NX, HALF, COLS), bf16),
+            pltpu.VMEM((NX, columns, COLS), bf16),
             pltpu.SemaphoreType.DMA((NC * NX,)),
             pltpu.SemaphoreType.DMA((NX,)),
         ],
         compiler_params=pltpu.CompilerParams(vmem_limit_bytes=58 * 1024 * 1024),
         cost_estimate=pl.CostEstimate(
-            flops=4 * TOK * HALF * D, bytes_accessed=8 * 1024 * 1024, transcendentals=0
+            flops=4 * TOK * columns * D, bytes_accessed=8 * 1024 * 1024, transcendentals=0
         ),
         name="attn_grads",
     )(shift, own, other, pieces, w_all, coef, first)
@@ -347,17 +327,23 @@
     state = hidden_state.reshape(TOK, FEAT)
     attn = attn_out.reshape(TOK, FEAT)
     state_all = lax.all_gather(state, "t")
-    w_start = (ic * NY + iy) * W_ROWS
-    w_mine = lax.dynamic_slice(o_weight, (w_start, 0), (W_ROWS, COLS))
-    w_moved = lax.ppermute(
-        w_mine,
+    w_routes = [
+        ((i * NC + k) * NR + (j + i + 2 * k) % NR, (i * NC + k) * NR + j)
+        for i in range(NX)
+        for k in range(NC)
+        for j in range(NR)
+    ]
+    w_first = lax.ppermute(
+        lax.dynamic_slice(o_weight, (ic * HALF + iy * W_FIRST, 0), (W_FIRST, COLS)),
         ("x", "c", "r"),
-        [
-            ((i * NC + k) * NR + (j + i + 2 * k) % NR, (i * NC + k) * NR + j)
-            for i in range(NX)
-            for k in range(NC)
-            for j in range(NR)
-        ],
+        w_routes,
+    )
+    w_rest = lax.ppermute(
+        lax.dynamic_slice(
+            o_weight, (ic * HALF + NY * W_FIRST + iy * W_REST, 0), (W_REST, COLS)
+        ),
+        ("x", "c", "r"),
+        w_routes,
     )
     attn_keep = jnp.where(ic == 0, attn[:, :HALF], attn[:, HALF:])
     attn_give = jnp.where(ic == 0, attn[:, HALF:], attn[:, :HALF])
@@ -393,17 +379,16 @@
         -1,
     )
     got = lax.all_to_all(send, DP, 0, 0)
-    got, attn_other = lax.optimization_barrier((got, attn_other))
+    got, attn_other, w_first = lax.optimization_barrier((got, attn_other, w_first))
 
     other_index = dp_index + 1 - 2 * ic
+    got, state_all = lax.optimization_barrier((got, state_all))
+    state_other = swap_core(state_all)
+    w_first = lax.all_gather(w_first, PLANE).reshape(NX, NY * W_FIRST, COLS)
     first, gain_part, loss_part, pieces, scale, first_col = group_math(
         jnp.stack([dp_index, other_index]), got.transpose(1, 0, 2), gain
     )
 
-    scale, state_all = lax.optimization_barrier((scale, state_all))
-    state_other = swap_core(state_all)
-    scale, w_moved = lax.optimization_barrier((scale, w_moved))
-    w_all = lax.all_gather(w_moved, PLANE).reshape(NX, HALF, COLS)
     partial, coef = weight_partials(
         state_all, state_other, attn_keep, attn_other, pieces, scale
     )
@@ -430,31 +415,35 @@
             tails, (ir - source) % NR, 0, keepdims=False
         )
 
-    spread, first_sum, totals = lax.optimization_barrier((spread, first_sum, totals))
-    second = lax.all_to_all(sum_senders(spread), "r", 0, 0)
-
     row_here = lax.dynamic_index_in_dim(pieces[0], it, 0, keepdims=False)[:6]
     row_here = row_here.astype(f32).reshape(2, 3, FEAT)
     row_here = (row_here[:, :1] + row_here[:, 1:2]) + row_here[:, 2:]
     state_grad = first_col[0].reshape(2, SEQ, 1) * row_here - states * coef[0].reshape(2, SEQ, 1)
     grad_hidden = state_grad.astype(bf16).reshape(1, 2, SEQ, FEAT)
-    keep, give = attn_grads(
-        (ir + 2 * ic).reshape(1), state_all, state_other, pieces, w_all, coef, first_col
-    )
-
-    second, keep, give = lax.optimization_barrier((second, keep, give))
+    shift = (ir + 2 * ic).reshape(1)
+    keep, give = attn_grads(shift, state_all, state_other, pieces, w_first, coef, first_col)
+    arrived = swap_core(give)
+
+    spread, first_sum, totals, grad_hidden, arrived, w_rest = lax.optimization_barrier(
+        (spread, first_sum, totals, grad_hidden, arrived, w_rest)
+    )
+    w_rest = lax.all_gather(w_rest, PLANE).reshape(NX, NY * W_REST, COLS)
+    second = lax.all_to_all(sum_senders(spread), "r", 0, 0)
     second_sum = jnp.sum(second.astype(f32), 0)
     total = first_sum - second_sum
     done = jnp.broadcast_to(total.astype(bf16)[None], (NX * NY, SLICE, COLS))
     half = lax.all_to_all(done, PLANE, 0, 0)
-    arrived = swap_core(give)
+    keep_rest, give_rest = attn_grads(
+        shift, state_all, state_other, pieces, w_rest, coef, first_col
+    )
+    half, keep_rest, give_rest = lax.optimization_barrier((half, keep_rest, give_rest))
+    half_other = swap_core(half)
+    arrived_rest = swap_core(give_rest)
+    mine = [keep, keep_rest]
+    theirs = [arrived, arrived_rest]
     grad_attn = jnp.where(
-        ic == 0, jnp.concatenate([keep, arrived], 1), jnp.concatenate([arrived, keep], 1)
+        ic == 0, jnp.concatenate(mine + theirs, 1), jnp.concatenate(theirs + mine, 1)
     ).reshape(1, 2, SEQ, FEAT)
-    half, grad_attn, grad_hidden, totals = lax.optimization_barrier(
-        (half, grad_attn, grad_hidden, totals)
-    )
-    half_other = swap_core(half)
     grad_weight = join_halves(ic.reshape(1), half, half_other)
     return (grad_hidden, grad_attn, grad_weight, totals[0], totals[1, 0])
 

time: 219 us -> 253 us (1.16)
  blocking collectives: 11.8 us -> 38.5 us
  waiting for transfers between devices: 45.9 us -> 64.1 us
  starting transfers between devices: 94.4 us -> 82.6 us
    all_gather x1 -> x2, waiting for transfers between devices: 8.65 us -> 54.1 us  [the longest x1 30.4 us: body(): w_first = lax.all_gather(w_first, PLANE).reshape(NX, NY * W_FIRST, COLS)]
    all_to_all x0 -> x1, blocking collectives: none -> 26.7 us  [body(): second = lax.all_to_all(sum_senders(spread), 'r', 0, 0)]
    all_to_all x1, waiting for transfers between devices: 14.1 us -> 0.01 us  [body(): spread = lax.all_to_all(partial, PLANE, 0, 0)]
    ppermute x3, waiting for transfers between devices: 13.7 us -> 0.01 us  [body(): lax.ppermute(jnp.concatenate([outgoing, tail], 0), 'r', [(j, (j + step) %...]
    ppermute x1 -> x2, starting transfers between devices: 13.1 us -> 24.5 us  [the longest x1 13.2 us: body(): lax.ppermute(lax.dynamic_slice(o_weight, (ic * HALF + iy * W_FIRST, 0), (...]
    all_to_all x1, starting transfers between devices: 12.1 us -> 4.53 us  [body(): half = lax.all_to_all(done, PLANE, 0, 0)]
    ppermute x3, starting transfers between devices: 22.4 us -> 15.8 us  [body(): lax.ppermute(jnp.concatenate([outgoing, tail], 0), 'r', [(j, (j + step) %...]
    ppermute x4 -> x5, starting transfers between devices: 20 us -> 13.7 us  [swap_core(): return lax.ppermute(value, 'c', [(0, 1), (1, 0)])]
  transfers between devices with their start and end apart: 15 -> 17, of which waited for: 9 -> 5; matrix products, arithmetic and copies ran while one was open for 8% -> 8% of each run, Pallas kernels for 12% -> 10%
where the time goes in v11:
time: 253 us; the launch traced here: 250 us
  starting transfers between devices  82.6 us (33%)
  waiting for transfers between devices  64.1 us (25%)
  blocking collectives  38.5 us (15%)
  Pallas kernels  25.7 us (10%)
  local copies, waits for them, and re-layouts  15.4 us (6%)
  between operations  15.1 us (6%)
  other arithmetic  8.94 us (4%)
    all_gather x1, waiting for transfers between devices, body(): w_first = lax.all_gather(w_first, PLANE).reshape(NX, NY * W_FIRST, COLS)  30.4 us
    all_to_all x1, blocking collectives, body(): second = lax.all_to_all(sum_senders(spread), 'r', 0, 0)  26.7 us
    all_gather x1, waiting for transfers between devices, body(): w_rest = lax.all_gather(w_rest, PLANE).reshape(NX, NY * W_REST, COLS)  23.7 us
    ppermute x3, starting transfers between devices, body(): lax.ppermute(jnp.concatenate([outgoing, tail], 0), 'r', [(j, (j + step) %...  15.8 us
    ppermute x5, starting transfers between devices, swap_core(): return lax.ppermute(value, 'c', [(0, 1), (1, 0)])  13.7 us
    ppermute x1, starting transfers between devices, body(): lax.ppermute(lax.dynamic_slice(o_weight, (ic * HALF + iy * W_FIRST, 0), (...  13.2 us
    pallas_call x2, Pallas kernels, attn_grads(): pl.pallas_call(attn_kernel, out_shape=(out, out), in_specs=[pl.BlockSpec(...  12.1 us
    psum x1, blocking collectives, body(): square = lax.psum(jnp.sum(states * states, -1), 't') / D  11.8 us
  transfers between devices with their start and end apart: 17, of which 5 were waited for; matrix products, arithmetic and copies ran while one was open for 8% of the time, Pallas kernels for 10%

profile of v11, /device:TPU:1, one launch (start us, length us, event | category | flops | bytes accessed | tf_op | source)
XLA Modules:
  0.0 250.3 jit_solution(9246845601233458158)
XLA Ops:
  7.2 0.7 all-gather.6.cloned.1.call-update
  7.9 0.7 broadcast_in_dim.16
  8.6 1.2 fusion.2
  9.8 11.8 %psum.7 = f32[2,128]{1,0:T(2,128)S(1)} all-reduce(f32[2,128]{1,0:T(2,128)S(1)} %fusion.2), channel_id=1, replica_groups=mesh['x'=4,'y'=4,'c'=2,'t'=4,'r'=4] {'t'}, use_global_device_ids=true, to_apply=%region_1.2 | all-reduce | flops 256 | bytes 2048 | tf_op jit(solution)/shard_map/psum | solution.py:353
  21.6 0.7 convert_bitcast_fusion.1
  22.3 0.7 fusion.10
  23.1 1.4 fusion.6
  25.1 3.3 %all-to-all-start = ((f32[4,3,896]{2,1,0:T(4,128)}), f32[4,3,896]{2,1,0:T(4,128)S(1)}, u32[]{:S(2)}, u32[]{:S(2)}) async-start(f32[4,3,896]{2,1,0:T(4,128)} %broadcast_in_dim.17), calls=%async_computation | async-start | bytes 114688 | tf_op jit(solution)/shard_map/all_to_all | solution.py:362
  29.4 3.6 %all-to-all-done = f32[4,3,896]{2,1,0:T(4,128)S(1)} async-done(((f32[4,3,896]{2,1,0:T(4,128)}), f32[4,3,896]{2,1,0:T(4,128)S(1)}, u32[]{:S(2)}, u32[]{:S(2)}) %all-to-all-start) | async-done | bytes 43040 | tf_op jit(solution)/shard_map/all_to_all | solution.py:362
  33.3 2.2 concatenate.54
  35.5 11.1 %all-to-all-start.1 = ((f32[32,2,3840]{2,1,0:T(2,128)}), f32[32,2,3840]{2,1,0:T(2,128)}, u32[]{:S(2)}, u32[]{:S(2)}) async-start(f32[32,2,3840]{2,1,0:T(2,128)} %concatenate.54), calls=%async_computation.1 | async-start | bytes 1966080 | tf_op jit(solution)/shard_map/all_to_all | solution.py:381
  46.7 0.8 broadcast_select_fusion
  47.5 2.2 collective-permute-start
  49.8 13.2 %collective-permute-start.1 = (bf16[64,896]{1,0:T(8,128)(2,1)S(1)}, bf16[64,896]{1,0:T(8,128)(2,1)S(1)}, u32[]{:S(2)}, u32[]{:S(2)}) collective-permute-start(bf16[64,896]{1,0:T(8,128)(2,1)S(1)} %constant_dynamic-slice_fusion.1), channel_id=1, source_target_pairs={{0,0},{1,1},{2,2},{3,3},{18,16},{19,17},{16,18},{17,19},{129,128},... | collective-permute-start | bytes 344072 | tf_op jit(solution)/shard_map/ppermute | solution.py:336
  63.0 4.7 %collective-permute-done.1 = bf16[64,896]{1,0:T(8,128)(2,1)S(1)} collective-permute-done((bf16[64,896]{1,0:T(8,128)(2,1)S(1)}, bf16[64,896]{1,0:T(8,128)(2,1)S(1)}, u32[]{:S(2)}, u32[]{:S(2)}) %collective-permute-start.1) | collective-permute-done | bytes 114720 | tf_op jit(solution)/shard_map/ppermute | solution.py:336
  67.7 0.7 copy-done.12
  68.5 2.1 collective-permute-start.2
  70.7 1.3 copy.28
  72.0 4.1 %group_math.1 = (f32[4,28,896]{2,1,0:T(8,128)S(1)}, f32[4,1,896]{2,1,0:T(1,128)S(1)}, f32[8,128]{1,0:T(8,128)S(1)}, bf16[2,4,16,896]{3,2,1,0:T(8,128)(2,1)S(1)},...) custom-call(s32[2]{0:T(128)S(1)} %pad_add_fusion.index_ref, f32[2,32,3840]{2,1,0:T(8,128)S(1)} %bitcast.68, ...), custom_call_target="tpu_custom_call" | custom-call | flops 183500800 | bytes 3145728 | tf_op jit(solution)/shard_map/group_math/pallas_call | solution.py:125
  76.2 0.7 copy-done.3
  76.9 0.8 copy-done.9
  77.7 5.0 %weight_partials.1 = (bf16[16,112,896]{2,1,0:T(8,128)(2,1)S(1)}, f32[2,256,1]{2,1,0:T(8,128)S(1)}) custom-call(bf16[4,256,896]{2,1,0:T(8,128)(2,1)S(1)} %copy-done.1, bf16[4,256,896]{2,1,0:T(8,128)(2,1)} %collective-permute-done.2.other_ref.other_hbm, bf16[256,448]{1,0:T(8,128)(2,1)S(1)} %copy-done.11, bf16[256,448]{1,0:T(8,128)(2,1)S(1)} %copy-done.13, ...), custom_call_target="tpu_custom_call" | custom-call | flops 1644167168 | bytes 8388608 | tf_op jit(solution)/shard_map/weight_partials/pallas_call | solution.py:179
  82.7 1.7 copy-done.2
  84.4 0.7 copy-done.5
  85.2 9.6 %all-to-all-start.2 = ((bf16[16,112,896]{2,1,0:T(8,128)(2,1)}), bf16[16,112,896]{2,1,0:T(8,128)(2,1)}, u32[]{:S(2)}, u32[]{:S(2)}) async-start(bf16[16,112,896]{2,1,0:T(8,128)(2,1)} %copy-done.2), calls=%async_computation.2 | async-start | bytes 6422528 | tf_op jit(solution)/shard_map/all_to_all | solution.py:396
  94.8 0.6 constant_dynamic-slice_fusion
  95.4 11.4 %collective-permute-start.7 = (bf16[48,896]{1,0:T(8,128)(2,1)}, bf16[48,896]{1,0:T(8,128)(2,1)}, u32[]{:S(2)}, u32[]{:S(2)}) collective-permute-start(bf16[48,896]{1,0:T(8,128)(2,1)} %constant_dynamic-slice_fusion), channel_id=1, source_target_pairs={{0,0},{1,1},{2,2},{3,3},{18,16},{19,17},{16,18},{17,19},{129,128},... | collective-permute-start | bytes 258056 | tf_op jit(solution)/shard_map/ppermute | solution.py:341
  107.6 0.7 pad.22.clone
  108.3 0.7 pad_bitcast_fusion
  109.1 0.7 fusion.7
  109.8 4.4 %collective-permute-start.5 = (f32[30,896]{1,0:T(8,128)}, f32[30,896]{1,0:T(8,128)S(1)}, u32[]{:S(2)}, u32[]{:S(2)}) collective-permute-start(f32[30,896]{1,0:T(8,128)} %get-tuple-element.70), channel_id=1, source_target_pairs={{0,3},{1,0},{2,1},{3,2},{4,7},{5,4},{6,5},{7,6},{8,11},{9,8},{10,9... | collective-permute-start | bytes 322568 | tf_op jit(solution)/shard_map/ppermute | solution.py:404
  114.3 9.4 %collective-permute-start.4 = (f32[30,896]{1,0:T(8,128)S(1)}, f32[30,896]{1,0:T(8,128)S(1)}, u32[]{:S(2)}, u32[]{:S(2)}) collective-permute-start(f32[30,896]{1,0:T(8,128)S(1)} %get-tuple-element.69), channel_id=1, source_target_pairs={{0,2},{1,3},{2,0},{3,1},{4,6},{5,7},{6,4},{7,5},{8,10},{9,11},{10,... | collective-permute-start | bytes 322568 | tf_op jit(solution)/shard_map/ppermute | solution.py:404
  123.7 1.9 collective-permute-start.3
  125.6 30.4 %all-gather.8.cloned.1.call-done = bf16[1024,896]{1,0:T(8,128)(2,1)} async-done(((bf16[64,896]{1,0:T(8,128)(2,1)}), bf16[1024,896]{1,0:T(8,128)(2,1)}) %all-gather.8.cloned.1.call-update) | async-done | bytes 1835024 | tf_op jit(solution)/shard_map/all_gather | solution.py:387
  156.0 6.2 %attn_grads.2 = (bf16[256,256]{1,0:T(8,128)(2,1)}, bf16[256,256]{1,0:T(8,128)(2,1)}) custom-call(s32[1]{0:T(128)} %bitcast.26.shift_ref, bf16[4,256,896]{2,1,0:T(8,128)(2,1)} %all-gather.6.cloned.1.call-done.own_ref.own_hbm, bf16[4,256,896]{2,1,0:T(8,128)(2,1)} %collective-permute-done.2.other_ref.other_hbm, bf16[2,4,16,896]{3,2,1,0:T(8,128)(2,1)} %copy-done.7, ...), custom_call_target="tpu_custom_call" | custom-call | flops 939524096 | bytes 8388608 | tf_op jit(solution)/shard_map/attn_grads/pallas_call | solution.py:303
  162.2 3.7 %collective-permute-start.6 = (bf16[256,256]{1,0:T(8,128)(2,1)}, bf16[256,256]{1,0:T(8,128)(2,1)S(1)}, u32[]{:S(2)}, u32[]{:S(2)}) collective-permute-start(bf16[256,256]{1,0:T(8,128)(2,1)} %get-tuple-element.48), channel_id=1, source_target_pairs={{0,16},{16,0},{1,17},{17,1},{2,18},{18,2},{3,19},{19,3},{4,20},{20... | collective-permute-start | bytes 393224 | tf_op jit(solution)/shard_map/ppermute | solution.py:39
  166.1 1.0 fusion.5
  167.2 3.0 %sum_senders.1 = bf16[4,28,896]{2,1,0:T(8,128)(2,1)S(1)} custom-call(bf16[16,112,896]{2,1,0:T(8,128)(2,1)} %all-to-all-done.2.spread_ref), custom_call_target="tpu_custom_call" | custom-call | flops 1605632 | bytes 4194304 | tf_op jit(solution)/shard_map/sum_senders/pallas_call | solution.py:217
  170.3 26.7 %all_to_all.25 = bf16[4,28,896]{2,1,0:T(8,128)(2,1)S(1)} all-to-all(bf16[4,28,896]{2,1,0:T(8,128)(2,1)S(1)} %sum_senders.1), channel_id=1, replica_groups=mesh['x'=4,'y'=4,'c'=2,'t'=4,'r'=4] {'r'}, dimensions={0} | all-to-all | bytes 401408 | tf_op jit(solution)/shard_map/all_to_all | solution.py:431
  197.0 1.0 broadcast_in_dim.23
  198.0 4.5 %all-to-all-start.4 = ((bf16[16,28,896]{2,1,0:T(8,128)(2,1)}), bf16[16,28,896]{2,1,0:T(8,128)(2,1)S(1)}, u32[]{:S(2)}, u32[]{:S(2)}) async-start(bf16[16,28,896]{2,1,0:T(8,128)(2,1)} %broadcast_in_dim.23), calls=%async_computation.4 | async-start | bytes 1835008 | tf_op jit(solution)/shard_map/all_to_all | solution.py:435
  202.5 23.7 %all-gather.10.cloned.1.call-done = bf16[768,896]{1,0:T(8,128)(2,1)} async-done(((bf16[48,896]{1,0:T(8,128)(2,1)}), bf16[768,896]{1,0:T(8,128)(2,1)}) %all-gather.10.cloned.1.call-update) | async-done | bytes 1376272 | tf_op jit(solution)/shard_map/all_gather | solution.py:430
  226.2 5.9 %attn_grads.3 = (bf16[256,192]{1,0:T(8,128)(2,1)}, bf16[256,192]{1,0:T(8,128)(2,1)}) custom-call(s32[1]{0:T(128)} %bitcast.26.shift_ref, bf16[4,256,896]{2,1,0:T(8,128)(2,1)} %all-gather.6.cloned.1.call-done.own_ref.own_hbm, bf16[4,256,896]{2,1,0:T(8,128)(2,1)} %collective-permute-done.2.other_ref.other_hbm, bf16[2,4,16,896]{3,2,1,0:T(8,128)(2,1)} %copy-done.7, ...), custom_call_target="tpu_custom_call" | custom-call | flops 704643072 | bytes 8388608 | tf_op jit(solution)/shard_map/attn_grads/pallas_call | solution.py:303
  232.4 3.9 %collective-permute-start.9 = (bf16[16,28,896]{2,0,1:T(8,128)(2,1)S(1)}, bf16[16,28,896]{2,0,1:T(8,128)(2,1)S(1)}, u32[]{:S(2)}, u32[]{:S(2)}) collective-permute-start(bf16[16,28,896]{2,0,1:T(8,128)(2,1)S(1)} %copy.22), channel_id=1, source_target_pairs={{0,16},{16,0},{1,17},{17,1},{2,18},{18,2},{3,19},{19,3},{4,20},{20... | collective-permute-start | bytes 2408456 | tf_op jit(solution)/shard_map/ppermute | solution.py:39
  236.8 1.9 collective-permute-start.8
  239.3 0.9 collective-permute-done.8
  240.2 2.1 maximum_select_fusion
  242.4 1.4 join_halves.1
  (85 shorter events, 4.0 us)
Async XLA Ops:
  7.2 42.6 %copy-start = (bf16[896,896]{1,0:T(8,128)(2,1)S(1)}, bf16[896,896]{1,0:T(8,128)(2,1)}, u32[]{:S(2)}) copy-start(bf16[896,896]{1,0:T(8,128)(2,1)} %param.8) | copy-start | bytes 4816900
  7.2 61.3 %all-gather.6.cloned.1.call-start = ((), (), s32[]{:S(2)}) async-start(), calls=%async_computation.5 | async-start | bytes 2293760 | tf_op jit(solution)/shard_map/all_gather | solution.py:329
  25.1 7.8 %all-to-all-start = ((f32[4,3,896]{2,1,0:T(4,128)}), f32[4,3,896]{2,1,0:T(4,128)S(1)}, u32[]{:S(2)}, u32[]{:S(2)}) async-start(f32[4,3,896]{2,1,0:T(4,128)} %broadcast_in_dim.17), calls=%async_computation | async-start | bytes 114688 | tf_op jit(solution)/shard_map/all_to_all | solution.py:362
  33.3 13.4 %copy-start.15 = (bf16[1,2,128,896]{3,2,1,0:T(8,128)(2,1)S(1)}, bf16[1,2,128,896]{3,2,1,0:T(8,128)(2,1)}, u32[]{:S(2)}) copy-start(bf16[1,2,128,896]{3,2,1,0:T(8,128)(2,1)} %param.7) | copy-start | bytes 1376260
  35.5 32.9 %all-to-all-start.1 = ((f32[32,2,3840]{2,1,0:T(2,128)}), f32[32,2,3840]{2,1,0:T(2,128)}, u32[]{:S(2)}, u32[]{:S(2)}) async-start(f32[32,2,3840]{2,1,0:T(2,128)} %concatenate.54), calls=%async_computation.1 | async-start | bytes 1966080 | tf_op jit(solution)/shard_map/all_to_all | solution.py:381
  46.6 109.4 %all-gather.8.cloned.1.call-start = ((), (), s32[]{:S(2)}) async-start(), calls=%async_computation.6 | async-start | bytes 1949696 | tf_op jit(solution)/shard_map/all_gather | solution.py:387
  47.5 20.2 %collective-permute-start = (bf16[256,448]{1,0:T(8,128)(2,1)S(1)}, bf16[256,448]{1,0:T(8,128)(2,1)S(1)}, u32[]{:S(2)}, u32[]{:S(2)}) collective-permute-start(bf16[256,448]{1,0:T(8,128)(2,1)S(1)} %get-tuple-element.67), channel_id=1, source_target_pairs={{0,16},{16,0},{1,17},{17,1},{2,18},{18,2},{3,19},{19,3},{4,20},{20... | collective-permute-start | bytes 688136 | tf_op jit(solution)/shard_map/ppermute | solution.py:39
  49.8 17.9 %collective-permute-start.1 = (bf16[64,896]{1,0:T(8,128)(2,1)S(1)}, bf16[64,896]{1,0:T(8,128)(2,1)S(1)}, u32[]{:S(2)}, u32[]{:S(2)}) collective-permute-start(bf16[64,896]{1,0:T(8,128)(2,1)S(1)} %constant_dynamic-slice_fusion.1), channel_id=1, source_target_pairs={{0,0},{1,1},{2,2},{3,3},{18,16},{19,17},{16,18},{17,19},{129,128},... | collective-permute-start | bytes 344072 | tf_op jit(solution)/shard_map/ppermute | solution.py:336
  67.7 0.7 copy-start.17
  67.7 0.7 copy-start.12
  68.5 9.1 %copy-start.1 = (bf16[4,256,896]{2,1,0:T(8,128)(2,1)S(1)}, bf16[4,256,896]{2,1,0:T(8,128)(2,1)}, u32[]{:S(2)}) copy-start(bf16[4,256,896]{2,1,0:T(8,128)(2,1)} %all-gather.6.cloned.1.call-done.own_ref.own_hbm) | copy-start | bytes 5505028
  68.5 9.1 %collective-permute-start.2 = (bf16[4,256,896]{2,1,0:T(8,128)(2,1)}, bf16[4,256,896]{2,1,0:T(8,128)(2,1)}, u32[]{:S(2)}, u32[]{:S(2)}) collective-permute-start(bf16[4,256,896]{2,1,0:T(8,128)(2,1)} %all-gather.6.cloned.1.call-done.own_ref.own_hbm), channel_id=1, source_target_pairs={{0,16},{16,0},{1,17},{17,1},{2,18},{18,2},{3,19},{19,3},{4,20},{20... | collective-permute-start | bytes 5505032 | tf_op jit(solution)/shard_map/ppermute | solution.py:39
  70.6 7.1 %copy-start.11 = (bf16[256,448]{1,0:T(8,128)(2,1)S(1)}, bf16[256,448]{1,0:T(8,128)(2,1)}, u32[]{:S(2)}) copy-start(bf16[256,448]{1,0:T(8,128)(2,1)} %get-tuple-element.66.keep_ref) | copy-start | bytes 688132
  70.6 7.1 %copy-start.13 = (bf16[256,448]{1,0:T(8,128)(2,1)S(1)}, bf16[256,448]{1,0:T(8,128)(2,1)}, u32[]{:S(2)}) copy-start(bf16[256,448]{1,0:T(8,128)(2,1)} %copy-done.12) | copy-start | bytes 688132
  76.2 0.7 copy-start.3
  76.9 0.8 copy-start.9
  77.6 5.1 %copy-start.7 = (bf16[2,4,16,896]{3,2,1,0:T(8,128)(2,1)}, bf16[2,4,16,896]{3,2,1,0:T(8,128)(2,1)S(1)}, u32[]{:S(2)}) copy-start(bf16[2,4,16,896]{3,2,1,0:T(8,128)(2,1)S(1)} %get-tuple-element.37.pieces_ref) | copy-start | bytes 688132
  82.7 1.7 copy-start.2
  84.4 0.7 copy-start.5
  85.1 21.8 %copy-start.8 = (bf16[2,4,16,896]{3,2,1,0:T(8,128)(2,1)S(1)}, bf16[2,4,16,896]{3,2,1,0:T(8,128)(2,1)}, u32[]{:S(2)}) copy-start(bf16[2,4,16,896]{3,2,1,0:T(8,128)(2,1)} %copy-done.7) | copy-start | bytes 688132
  85.2 23.8 %copy-start.4 = (f32[2,256,1]{2,1,0:T(8,128)S(1)}, f32[2,256,1]{2,1,0:T(8,128)}, u32[]{:S(2)}) copy-start(f32[2,256,1]{2,1,0:T(8,128)} %copy-done.3) | copy-start | bytes 6148
  85.2 23.9 %copy-start.10 = (f32[4,28,896]{2,1,0:T(8,128)S(1)}, f32[4,28,896]{2,1,0:T(8,128)}, u32[]{:S(2)}) copy-start(f32[4,28,896]{2,1,0:T(8,128)} %copy-done.9) | copy-start | bytes 1204228
  85.2 82.1 %all-to-all-start.2 = ((bf16[16,112,896]{2,1,0:T(8,128)(2,1)}), bf16[16,112,896]{2,1,0:T(8,128)(2,1)}, u32[]{:S(2)}, u32[]{:S(2)}) async-start(bf16[16,112,896]{2,1,0:T(8,128)(2,1)} %copy-done.2), calls=%async_computation.2 | async-start | bytes 6422528 | tf_op jit(solution)/shard_map/all_to_all | solution.py:396
  94.7 131.5 %all-gather.10.cloned.1.call-start = ((), (), s32[]{:S(2)}) async-start(), calls=%async_computation.7 | async-start | bytes 1462272 | tf_op jit(solution)/shard_map/all_gather | solution.py:430
  95.4 71.8 %collective-permute-start.7 = (bf16[48,896]{1,0:T(8,128)(2,1)}, bf16[48,896]{1,0:T(8,128)(2,1)}, u32[]{:S(2)}, u32[]{:S(2)}) collective-permute-start(bf16[48,896]{1,0:T(8,128)(2,1)} %constant_dynamic-slice_fusion), channel_id=1, source_target_pairs={{0,0},{1,1},{2,2},{3,3},{18,16},{19,17},{16,18},{17,19},{129,128},... | collective-permute-start | bytes 258056 | tf_op jit(solution)/shard_map/ppermute | solution.py:341
  109.8 57.2 %collective-permute-start.5 = (f32[30,896]{1,0:T(8,128)}, f32[30,896]{1,0:T(8,128)S(1)}, u32[]{:S(2)}, u32[]{:S(2)}) collective-permute-start(f32[30,896]{1,0:T(8,128)} %get-tuple-element.70), channel_id=1, source_target_pairs={{0,3},{1,0},{2,1},{3,2},{4,7},{5,4},{6,5},{7,6},{8,11},{9,8},{10,9... | collective-permute-start | bytes 322568 | tf_op jit(solution)/shard_map/ppermute | solution.py:404
  114.3 52.8 %collective-permute-start.4 = (f32[30,896]{1,0:T(8,128)S(1)}, f32[30,896]{1,0:T(8,128)S(1)}, u32[]{:S(2)}, u32[]{:S(2)}) collective-permute-start(f32[30,896]{1,0:T(8,128)S(1)} %get-tuple-element.69), channel_id=1, source_target_pairs={{0,2},{1,3},{2,0},{3,1},{4,6},{5,7},{6,4},{7,5},{8,10},{9,11},{10,... | collective-permute-start | bytes 322568 | tf_op jit(solution)/shard_map/ppermute | solution.py:404
  123.7 43.4 %collective-permute-start.3 = (f32[30,896]{1,0:T(8,128)S(1)}, f32[30,896]{1,0:T(8,128)S(1)}, u32[]{:S(2)}, u32[]{:S(2)}) collective-permute-start(f32[30,896]{1,0:T(8,128)S(1)} %get-tuple-element.68), channel_id=1, source_target_pairs={{0,1},{1,2},{2,3},{3,0},{4,5},{5,6},{6,7},{7,4},{8,9},{9,10},{10,1... | collective-permute-start | bytes 322568 | tf_op jit(solution)/shard_map/ppermute | solution.py:404
  156.0 9.9 %copy-start.6 = (f32[2,256,1]{2,1,0:T(8,128)S(1)}, f32[2,256,1]{2,1,0:T(8,128)}, u32[]{:S(2)}) copy-start(f32[2,256,1]{2,1,0:T(8,128)} %copy-done.5) | copy-start | bytes 6148
  156.0 10.0 %copy-start.14 = (bf16[1,2,128,896]{3,2,1,0:T(8,128)(2,1)S(1)}, bf16[1,2,128,896]{3,2,1,0:T(8,128)(2,1)}, u32[]{:S(2)}) copy-start(bf16[1,2,128,896]{3,2,1,0:T(8,128)(2,1)} %param.6) | copy-start | bytes 1376260
  162.2 5.0 %collective-permute-start.6 = (bf16[256,256]{1,0:T(8,128)(2,1)}, bf16[256,256]{1,0:T(8,128)(2,1)S(1)}, u32[]{:S(2)}, u32[]{:S(2)}) collective-permute-start(bf16[256,256]{1,0:T(8,128)(2,1)} %get-tuple-element.48), channel_id=1, source_target_pairs={{0,16},{16,0},{1,17},{17,1},{2,18},{18,2},{3,19},{19,3},{4,20},{20... | collective-permute-start | bytes 393224 | tf_op jit(solution)/shard_map/ppermute | solution.py:39
  198.0 34.1 %all-to-all-start.4 = ((bf16[16,28,896]{2,1,0:T(8,128)(2,1)}), bf16[16,28,896]{2,1,0:T(8,128)(2,1)S(1)}, u32[]{:S(2)}, u32[]{:S(2)}) async-start(bf16[16,28,896]{2,1,0:T(8,128)(2,1)} %broadcast_in_dim.23), calls=%async_computation.4 | async-start | bytes 1835008 | tf_op jit(solution)/shard_map/all_to_all | solution.py:435
  226.2 14.0 %copy-start.16 = (bf16[256,256]{1,0:T(8,128)(2,1)S(1)}, bf16[256,256]{1,0:T(8,128)(2,1)}, u32[]{:S(2)}) copy-start(bf16[256,256]{1,0:T(8,128)(2,1)} %get-tuple-element.50) | copy-start | bytes 393220
  232.4 9.9 %collective-permute-start.9 = (bf16[16,28,896]{2,0,1:T(8,128)(2,1)S(1)}, bf16[16,28,896]{2,0,1:T(8,128)(2,1)S(1)}, u32[]{:S(2)}, u32[]{:S(2)}) collective-permute-start(bf16[16,28,896]{2,0,1:T(8,128)(2,1)S(1)} %copy.22), channel_id=1, source_target_pairs={{0,16},{16,0},{1,17},{17,1},{2,18},{18,2},{3,19},{19,3},{4,20},{20... | collective-permute-start | bytes 2408456 | tf_op jit(solution)/shard_map/ppermute | solution.py:39
  236.8 3.4 %collective-permute-start.8 = (bf16[256,192]{1,0:T(8,128)(2,1)}, bf16[256,192]{1,0:T(8,128)(2,1)S(1)}, u32[]{:S(2)}, u32[]{:S(2)}) collective-permute-start(bf16[256,192]{1,0:T(8,128)(2,1)} %get-tuple-element.58), channel_id=1, source_target_pairs={{0,16},{16,0},{1,17},{17,1},{2,18},{18,2},{3,19},{19,3},{4,20},{20... | collective-permute-start | bytes 294920 | tf_op jit(solution)/shard_map/ppermute | solution.py:39
Sparse Core Ops, SparseCore 0:
  10.1 56.8 all-gather.5
  70.0 85.9 all-gather.7
  167.4 58.8 all-gather.9

commit v12 on v11

--- a/solution.py
+++ b/solution.py
@@ -23,8 +23,7 @@
 TOK = 2 * SEQ
 HALF = FEAT // NC
 SLICE = HALF // (NX * NY)
-W_FIRST = 64
-W_REST = HALF // NY - W_FIRST
+W_ROWS = HALF // NY
 PIECES = 16
 GROUP = NX * NY * NC
 
@@ -333,15 +332,8 @@
         for k in range(NC)
         for j in range(NR)
     ]
-    w_first = lax.ppermute(
-        lax.dynamic_slice(o_weight, (ic * HALF + iy * W_FIRST, 0), (W_FIRST, COLS)),
-        ("x", "c", "r"),
-        w_routes,
-    )
-    w_rest = lax.ppermute(
-        lax.dynamic_slice(
-            o_weight, (ic * HALF + NY * W_FIRST + iy * W_REST, 0), (W_REST, COLS)
-        ),
+    w_moved = lax.ppermute(
+        lax.dynamic_slice(o_weight, (ic * HALF + iy * W_ROWS, 0), (W_ROWS, COLS)),
         ("x", "c", "r"),
         w_routes,
     )
@@ -379,12 +371,12 @@
         -1,
     )
     got = lax.all_to_all(send, DP, 0, 0)
-    got, attn_other, w_first = lax.optimization_barrier((got, attn_other, w_first))
+    got, attn_other, w_moved = lax.optimization_barrier((got, attn_other, w_moved))
 
     other_index = dp_index + 1 - 2 * ic
     got, state_all = lax.optimization_barrier((got, state_all))
     state_other = swap_core(state_all)
-    w_first = lax.all_gather(w_first, PLANE).reshape(NX, NY * W_FIRST, COLS)
+    w_all = lax.all_gather(w_moved, PLANE).reshape(NX, HALF, COLS)
     first, gain_part, loss_part, pieces, scale, first_col = group_math(
         jnp.stack([dp_index, other_index]), got.transpose(1, 0, 2), gain
     )
@@ -420,30 +412,24 @@
     row_here = (row_here[:, :1] + row_here[:, 1:2]) + row_here[:, 2:]
     state_grad = first_col[0].reshape(2, SEQ, 1) * row_here - states * coef[0].reshape(2, SEQ, 1)
     grad_hidden = state_grad.astype(bf16).reshape(1, 2, SEQ, FEAT)
-    shift = (ir + 2 * ic).reshape(1)
-    keep, give = attn_grads(shift, state_all, state_other, pieces, w_first, coef, first_col)
-    arrived = swap_core(give)
-
-    spread, first_sum, totals, grad_hidden, arrived, w_rest = lax.optimization_barrier(
-        (spread, first_sum, totals, grad_hidden, arrived, w_rest)
-    )
-    w_rest = lax.all_gather(w_rest, PLANE).reshape(NX, NY * W_REST, COLS)
+    spread, first_sum, totals, grad_hidden = lax.optimization_barrier(
+        (spread, first_sum, totals, grad_hidden)
+    )
     second = lax.all_to_all(sum_senders(spread), "r", 0, 0)
+    keep, give = attn_grads(
+        (ir + 2 * ic).reshape(1), state_all, state_other, pieces, w_all, coef, first_col
+    )
+    second, keep, give = lax.optimization_barrier((second, keep, give))
     second_sum = jnp.sum(second.astype(f32), 0)
     total = first_sum - second_sum
     done = jnp.broadcast_to(total.astype(bf16)[None], (NX * NY, SLICE, COLS))
     half = lax.all_to_all(done, PLANE, 0, 0)
-    keep_rest, give_rest = attn_grads(
-        shift, state_all, state_other, pieces, w_rest, coef, first_col
-    )
-    half, keep_rest, give_rest = lax.optimization_barrier((half, keep_rest, give_rest))
+    arrived = swap_core(give)
+    grad_attn = jnp.where(
+        ic == 0, jnp.concatenate([keep, arrived], 1), jnp.concatenate([arrived, keep], 1)
+    ).reshape(1, 2, SEQ, FEAT)
+    half, grad_attn = lax.optimization_barrier((half, grad_attn))
     half_other = swap_core(half)
-    arrived_rest = swap_core(give_rest)
-    mine = [keep, keep_rest]
-    theirs = [arrived, arrived_rest]
-    grad_attn = jnp.where(
-        ic == 0, jnp.concatenate(mine + theirs, 1), jnp.concatenate(theirs + mine, 1)
-    ).reshape(1, 2, SEQ, FEAT)
     grad_weight = join_halves(ic.reshape(1), half, half_other)
     return (grad_hidden, grad_attn, grad_weight, totals[0], totals[1, 0])
 

time: 253 us -> 219 us (0.87)
  the two profiles are of different devices: /device:TPU:1 before, /device:TPU:33 now
where the time goes in v12:
time: 219 us; the launch traced here: 218 us
  starting transfers between devices  86 us (39%)
  waiting for transfers between devices  64.8 us (30%)
  Pallas kernels  22.6 us (10%)
  between operations  15.4 us (7%)
  local copies, waits for them, and re-layouts  14.8 us (7%)
  blocking collectives  7.5 us (3%)
  other arithmetic  7.29 us (3%)
    ppermute x3, waiting for transfers between devices, body(): lax.ppermute(jnp.concatenate([outgoing, tail], 0), 'r', [(j, (j + step) %...  18.9 us
    ppermute x1, waiting for transfers between devices, body(): lax.ppermute(lax.dynamic_slice(o_weight, (ic * HALF + iy * W_ROWS, 0), (W...  15.8 us
    ppermute x3, starting transfers between devices, body(): lax.ppermute(jnp.concatenate([outgoing, tail], 0), 'r', [(j, (j + step) %...  14.5 us
    ppermute x4, starting transfers between devices, swap_core(): return lax.ppermute(value, 'c', [(0, 1), (1, 0)])  14.1 us
    all_to_all x1, starting transfers between devices, body(): half = lax.all_to_all(done, PLANE, 0, 0)  13.9 us
    ppermute x1, starting transfers between devices, body(): lax.ppermute(lax.dynamic_slice(o_weight, (ic * HALF + iy * W_ROWS, 0), (W...  13.5 us
    all_to_all x1, starting transfers between devices, body(): got = lax.all_to_all(send, DP, 0, 0)  11 us
    all_gather x1, waiting for transfers between devices, body(): w_all = lax.all_gather(w_moved, PLANE).reshape(NX, HALF, COLS)  9.45 us
  transfers between devices with their start and end apart: 15, of which 9 were waited for; matrix products, arithmetic and copies ran while one was open for 7% of the time, Pallas kernels for 10%

profile of v12, /device:TPU:33, one launch (start us, length us, event | category | flops | bytes accessed | tf_op | source)
XLA Modules:
  0.0 218.3 jit_solution(10835184212742972432)
XLA Ops:
  7.2 0.7 all-gather.4.cloned.1.call-update
  7.9 0.7 broadcast_in_dim.16
  8.6 1.2 fusion.2
  9.8 7.5 %psum.7 = f32[2,128]{1,0:T(2,128)S(1)} all-reduce(f32[2,128]{1,0:T(2,128)S(1)} %fusion.2), channel_id=1, replica_groups=mesh['x'=4,'y'=4,'c'=2,'t'=4,'r'=4] {'t'}, use_global_device_ids=true, to_apply=%region_1.2 | all-reduce | flops 256 | bytes 2048 | tf_op jit(solution)/shard_map/psum | solution.py:345
  17.3 0.7 convert_bitcast_fusion.1
  18.0 0.7 fusion.10
  18.8 1.4 fusion.6
  20.2 0.6 broadcast_in_dim.17
  20.8 6.5 %all-to-all-start = ((f32[4,3,896]{2,1,0:T(4,128)}), f32[4,3,896]{2,1,0:T(4,128)S(1)}, u32[]{:S(2)}, u32[]{:S(2)}) async-start(f32[4,3,896]{2,1,0:T(4,128)} %broadcast_in_dim.17), calls=%async_computation | async-start | bytes 114688 | tf_op jit(solution)/shard_map/all_to_all | solution.py:354
  28.3 2.8 %all-to-all-done = f32[4,3,896]{2,1,0:T(4,128)S(1)} async-done(((f32[4,3,896]{2,1,0:T(4,128)}), f32[4,3,896]{2,1,0:T(4,128)S(1)}, u32[]{:S(2)}, u32[]{:S(2)}) %all-to-all-start) | async-done | bytes 43040 | tf_op jit(solution)/shard_map/all_to_all | solution.py:354
  31.4 2.2 %concatenate.50 = f32[32,2,3840]{2,1,0:T(2,128)} concatenate(f32[32,2,3712]{2,1,0:T(2,128)S(1)} %broadcast_in_dim.18, f32[32,2,28]{2,1,0:T(2,128)S(1)} %copy.20, f32[32,2,2]{2,1,0:T(2,128)S(1)} %broadcast_in_dim.19, f32[32,2,98]{2,1,0:T(2,128)S(1)} %broadcast_in_dim.20), dimensions={2} | concatenate | bytes 1966080 | tf_op jit(solution)/shard_map/concatenate | solution.py:364
  33.7 11.0 %all-to-all-start.1 = ((f32[32,2,3840]{2,1,0:T(2,128)}), f32[32,2,3840]{2,1,0:T(2,128)}, u32[]{:S(2)}, u32[]{:S(2)}) async-start(f32[32,2,3840]{2,1,0:T(2,128)} %concatenate.50), calls=%async_computation.1 | async-start | bytes 1966080 | tf_op jit(solution)/shard_map/all_to_all | solution.py:373
  44.7 0.8 broadcast_select_fusion
  45.6 2.2 %collective-permute-start = (bf16[256,448]{1,0:T(8,128)(2,1)S(1)}, bf16[256,448]{1,0:T(8,128)(2,1)S(1)}, u32[]{:S(2)}, u32[]{:S(2)}) collective-permute-start(bf16[256,448]{1,0:T(8,128)(2,1)S(1)} %get-tuple-element.63), channel_id=1, source_target_pairs={{0,16},{16,0},{1,17},{17,1},{2,18},{18,2},{3,19},{19,3},{4,20},{20... | collective-permute-start | bytes 688136 | tf_op jit(solution)/shard_map/ppermute | solution.py:38
  47.8 13.5 %collective-permute-start.1 = (bf16[112,896]{1,0:T(8,128)(2,1)S(1)}, bf16[112,896]{1,0:T(8,128)(2,1)S(1)}, u32[]{:S(2)}, u32[]{:S(2)}) collective-permute-start(bf16[112,896]{1,0:T(8,128)(2,1)S(1)} %constant_dynamic-slice_fusion), channel_id=1, source_target_pairs={{0,0},{1,1},{2,2},{3,3},{18,16},{19,17},{16,18},{17,19},{129,128},... | collective-permute-start | bytes 602120 | tf_op jit(solution)/shard_map/ppermute | solution.py:335
  61.4 15.8 %collective-permute-done.1 = bf16[112,896]{1,0:T(8,128)(2,1)S(1)} collective-permute-done((bf16[112,896]{1,0:T(8,128)(2,1)S(1)}, bf16[112,896]{1,0:T(8,128)(2,1)S(1)}, u32[]{:S(2)}, u32[]{:S(2)}) %collective-permute-start.1) | collective-permute-done | bytes 200736 | tf_op jit(solution)/shard_map/ppermute | solution.py:335
  77.2 0.7 copy-done.12
  78.0 2.1 collective-permute-start.2
  80.2 1.3 copy.28
  81.5 4.1 %group_math.1 = (f32[4,28,896]{2,1,0:T(8,128)S(1)}, f32[4,1,896]{2,1,0:T(1,128)S(1)}, f32[8,128]{1,0:T(8,128)S(1)}, bf16[2,4,16,896]{3,2,1,0:T(8,128)(2,1)S(1)},...) custom-call(s32[2]{0:T(128)S(1)} %pad_add_fusion.index_ref, f32[2,32,3840]{2,1,0:T(8,128)S(1)} %bitcast.65, ...), custom_call_target="tpu_custom_call" | custom-call | flops 183500800 | bytes 3145728 | tf_op jit(solution)/shard_map/group_math/pallas_call | solution.py:124
  85.7 0.7 copy-done.3
  86.4 0.8 copy-done.9
  87.2 5.0 %weight_partials.1 = (bf16[16,112,896]{2,1,0:T(8,128)(2,1)S(1)}, f32[2,256,1]{2,1,0:T(8,128)S(1)}) custom-call(bf16[4,256,896]{2,1,0:T(8,128)(2,1)S(1)} %copy-done.2, bf16[4,256,896]{2,1,0:T(8,128)(2,1)} %collective-permute-done.2.other_ref.other_hbm, bf16[256,448]{1,0:T(8,128)(2,1)S(1)} %copy-done.11, bf16[256,448]{1,0:T(8,128)(2,1)S(1)} %copy-done.13, ...), custom_call_target="tpu_custom_call" | custom-call | flops 1644167168 | bytes 8388608 | tf_op jit(solution)/shard_map/weight_partials/pallas_call | solution.py:178
  92.2 1.7 copy-done.1
  93.9 0.7 copy-done.5
  94.7 8.7 %all-to-all-start.2 = ((bf16[16,112,896]{2,1,0:T(8,128)(2,1)}), bf16[16,112,896]{2,1,0:T(8,128)(2,1)}, u32[]{:S(2)}, u32[]{:S(2)}) async-start(bf16[16,112,896]{2,1,0:T(8,128)(2,1)} %copy-done.1), calls=%async_computation.2 | async-start | bytes 6422528 | tf_op jit(solution)/shard_map/all_to_all | solution.py:388
  104.1 0.7 pad.18.clone
  104.9 0.7 pad_bitcast_fusion
  105.8 5.5 %collective-permute-start.5 = (f32[30,896]{1,0:T(8,128)S(1)}, f32[30,896]{1,0:T(8,128)S(1)}, u32[]{:S(2)}, u32[]{:S(2)}) collective-permute-start(f32[30,896]{1,0:T(8,128)S(1)} %get-tuple-element.66), channel_id=1, source_target_pairs={{0,3},{1,0},{2,1},{3,2},{4,7},{5,4},{6,5},{7,6},{8,11},{9,8},{10,9... | collective-permute-start | bytes 322568 | tf_op jit(solution)/shard_map/ppermute | solution.py:396
  111.3 7.1 %collective-permute-start.4 = (f32[30,896]{1,0:T(8,128)S(1)}, f32[30,896]{1,0:T(8,128)S(1)}, u32[]{:S(2)}, u32[]{:S(2)}) collective-permute-start(f32[30,896]{1,0:T(8,128)S(1)} %get-tuple-element.65), channel_id=1, source_target_pairs={{0,2},{1,3},{2,0},{3,1},{4,6},{5,7},{6,4},{7,5},{8,10},{9,11},{10,... | collective-permute-start | bytes 322568 | tf_op jit(solution)/shard_map/ppermute | solution.py:396
  118.4 1.9 collective-permute-start.3
  120.5 1.0 fusion.5
  121.4 12.4 %collective-permute-done.4 = f32[30,896]{1,0:T(8,128)S(1)} collective-permute-done((f32[30,896]{1,0:T(8,128)S(1)}, f32[30,896]{1,0:T(8,128)S(1)}, u32[]{:S(2)}, u32[]{:S(2)}) %collective-permute-start.4) | collective-permute-done | bytes 107552 | tf_op jit(solution)/shard_map/ppermute | solution.py:396
  133.8 6.5 %collective-permute-done.3 = f32[30,896]{1,0:T(8,128)S(1)} collective-permute-done((f32[30,896]{1,0:T(8,128)S(1)}, f32[30,896]{1,0:T(8,128)S(1)}, u32[]{:S(2)}, u32[]{:S(2)}) %collective-permute-start.3) | collective-permute-done | bytes 107552 | tf_op jit(solution)/shard_map/ppermute | solution.py:396
  140.4 8.8 %all-to-all-done.2.spread_ref = bf16[16,112,896]{2,1,0:T(8,128)(2,1)} async-done(((bf16[16,112,896]{2,1,0:T(8,128)(2,1)}), bf16[16,112,896]{2,1,0:T(8,128)(2,1)}, u32[]{:S(2)}, u32[]{:S(2)}) %all-to-all-start.2) | async-done | bytes 3211296 | tf_op jit(solution)/shard_map/all_to_all | solution.py:388
  149.2 3.7 %sum_senders.1 = bf16[4,28,896]{2,1,0:T(8,128)(2,1)} custom-call(bf16[16,112,896]{2,1,0:T(8,128)(2,1)} %all-to-all-done.2.spread_ref), custom_call_target="tpu_custom_call" | custom-call | flops 1605632 | bytes 4194304 | tf_op jit(solution)/shard_map/sum_senders/pallas_call | solution.py:216
  152.9 3.6 %all-to-all-start.3 = ((bf16[4,28,896]{2,1,0:T(8,128)(2,1)}), bf16[4,28,896]{2,1,0:T(8,128)(2,1)S(1)}, u32[]{:S(2)}, u32[]{:S(2)}) async-start(bf16[4,28,896]{2,1,0:T(8,128)(2,1)} %sum_senders.1), calls=%async_computation.3 | async-start | bytes 458752 | tf_op jit(solution)/shard_map/all_to_all | solution.py:418
  156.5 9.4 %all-gather.6.cloned.1.call-done = bf16[1792,896]{1,0:T(8,128)(2,1)} async-done(((bf16[112,896]{1,0:T(8,128)(2,1)}), bf16[1792,896]{1,0:T(8,128)(2,1)}) %all-gather.6.cloned.1.call-update) | async-done | bytes 3211280 | tf_op jit(solution)/shard_map/all_gather | solution.py:379
  165.9 8.3 %attn_grads.1 = (bf16[256,448]{1,0:T(8,128)(2,1)}, bf16[256,448]{1,0:T(8,128)(2,1)}) custom-call(s32[1]{0:T(128)} %bitcast.26.shift_ref, bf16[4,256,896]{2,1,0:T(8,128)(2,1)} %all-gather.4.cloned.1.call-done.own_ref.own_hbm, bf16[4,256,896]{2,1,0:T(8,128)(2,1)} %collective-permute-done.2.other_ref.other_hbm, bf16[2,4,16,896]{3,2,1,0:T(8,128)(2,1)} %copy-done.7, ...), custom_call_target="tpu_custom_call" | custom-call | flops 1644167168 | bytes 8388608 | tf_op jit(solution)/shard_map/attn_grads/pallas_call | solution.py:302
  174.3 1.0 broadcast_in_dim.23
  175.3 13.9 %all-to-all-start.4 = ((bf16[16,28,896]{2,1,0:T(8,128)(2,1)}), bf16[16,28,896]{2,1,0:T(8,128)(2,1)S(1)}, u32[]{:S(2)}, u32[]{:S(2)}) async-start(bf16[16,28,896]{2,1,0:T(8,128)(2,1)} %broadcast_in_dim.23), calls=%async_computation.4 | async-start | bytes 1835008 | tf_op jit(solution)/shard_map/all_to_all | solution.py:426
  189.2 4.5 %collective-permute-start.6 = (bf16[256,448]{1,0:T(8,128)(2,1)S(1)}, bf16[256,448]{1,0:T(8,128)(2,1)S(1)}, u32[]{:S(2)}, u32[]{:S(2)}) collective-permute-start(bf16[256,448]{1,0:T(8,128)(2,1)S(1)} %copy-done.18), channel_id=1, source_target_pairs={{0,16},{16,0},{1,17},{17,1},{2,18},{18,2},{3,19},{19,3},{4,20},{20... | collective-permute-start | bytes 688136 | tf_op jit(solution)/shard_map/ppermute | solution.py:38
  193.7 1.1 collective-permute-done.6
  194.8 1.1 maximum_select_fusion
  195.9 6.5 %all-to-all-done.4.mine_ref = bf16[16,28,896]{2,1,0:T(8,128)(2,1)S(1)} async-done(((bf16[16,28,896]{2,1,0:T(8,128)(2,1)}), bf16[16,28,896]{2,1,0:T(8,128)(2,1)S(1)}, u32[]{:S(2)}, u32[]{:S(2)}) %all-to-all-start.4) | async-done | bytes 802848 | tf_op jit(solution)/shard_map/all_to_all | solution.py:426
  202.6 5.4 %collective-permute-start.7 = (bf16[16,28,896]{2,0,1:T(8,128)(2,1)S(1)}, bf16[16,28,896]{2,0,1:T(8,128)(2,1)S(1)}, u32[]{:S(2)}, u32[]{:S(2)}) collective-permute-start(bf16[16,28,896]{2,0,1:T(8,128)(2,1)S(1)} %copy.22), channel_id=1, source_target_pairs={{0,16},{16,0},{1,17},{17,1},{2,18},{18,2},{3,19},{19,3},{4,20},{20... | collective-permute-start | bytes 2408456 | tf_op jit(solution)/shard_map/ppermute | solution.py:38
  209.1 0.8 collective-permute-done.7
  210.1 1.4 join_halves.1
  (79 shorter events, 3.5 us)
Async XLA Ops:
  7.2 40.6 %copy-start = (bf16[896,896]{1,0:T(8,128)(2,1)S(1)}, bf16[896,896]{1,0:T(8,128)(2,1)}, u32[]{:S(2)}) copy-start(bf16[896,896]{1,0:T(8,128)(2,1)} %param.8) | copy-start | bytes 4816900
  7.2 70.8 %all-gather.4.cloned.1.call-start = ((), (), s32[]{:S(2)}) async-start(), calls=%async_computation.5 | async-start | bytes 2293760 | tf_op jit(solution)/shard_map/all_gather | solution.py:328
  20.8 10.2 %all-to-all-start = ((f32[4,3,896]{2,1,0:T(4,128)}), f32[4,3,896]{2,1,0:T(4,128)S(1)}, u32[]{:S(2)}, u32[]{:S(2)}) async-start(f32[4,3,896]{2,1,0:T(4,128)} %broadcast_in_dim.17), calls=%async_computation | async-start | bytes 114688 | tf_op jit(solution)/shard_map/all_to_all | solution.py:354
  31.4 13.3 %copy-start.15 = (bf16[1,2,128,896]{3,2,1,0:T(8,128)(2,1)S(1)}, bf16[1,2,128,896]{3,2,1,0:T(8,128)(2,1)}, u32[]{:S(2)}) copy-start(bf16[1,2,128,896]{3,2,1,0:T(8,128)(2,1)} %param.7) | copy-start | bytes 1376260
  33.7 44.3 %all-to-all-start.1 = ((f32[32,2,3840]{2,1,0:T(2,128)}), f32[32,2,3840]{2,1,0:T(2,128)}, u32[]{:S(2)}, u32[]{:S(2)}) async-start(f32[32,2,3840]{2,1,0:T(2,128)} %concatenate.50), calls=%async_computation.1 | async-start | bytes 1966080 | tf_op jit(solution)/shard_map/all_to_all | solution.py:373
  44.7 121.2 %all-gather.6.cloned.1.call-start = ((), (), s32[]{:S(2)}) async-start(), calls=%async_computation.6 | async-start | bytes 3411968 | tf_op jit(solution)/shard_map/all_gather | solution.py:379
  45.6 31.6 %collective-permute-start = (bf16[256,448]{1,0:T(8,128)(2,1)S(1)}, bf16[256,448]{1,0:T(8,128)(2,1)S(1)}, u32[]{:S(2)}, u32[]{:S(2)}) collective-permute-start(bf16[256,448]{1,0:T(8,128)(2,1)S(1)} %get-tuple-element.63), channel_id=1, source_target_pairs={{0,16},{16,0},{1,17},{17,1},{2,18},{18,2},{3,19},{19,3},{4,20},{20... | collective-permute-start | bytes 688136 | tf_op jit(solution)/shard_map/ppermute | solution.py:38
  47.8 29.4 %collective-permute-start.1 = (bf16[112,896]{1,0:T(8,128)(2,1)S(1)}, bf16[112,896]{1,0:T(8,128)(2,1)S(1)}, u32[]{:S(2)}, u32[]{:S(2)}) collective-permute-start(bf16[112,896]{1,0:T(8,128)(2,1)S(1)} %constant_dynamic-slice_fusion), channel_id=1, source_target_pairs={{0,0},{1,1},{2,2},{3,3},{18,16},{19,17},{16,18},{17,19},{129,128},... | collective-permute-start | bytes 602120 | tf_op jit(solution)/shard_map/ppermute | solution.py:335
  77.2 0.8 copy-start.17
  77.2 0.7 copy-start.12
  78.0 9.1 %copy-start.2 = (bf16[4,256,896]{2,1,0:T(8,128)(2,1)S(1)}, bf16[4,256,896]{2,1,0:T(8,128)(2,1)}, u32[]{:S(2)}) copy-start(bf16[4,256,896]{2,1,0:T(8,128)(2,1)} %all-gather.4.cloned.1.call-done.own_ref.own_hbm) | copy-start | bytes 5505028
  78.0 9.1 %collective-permute-start.2 = (bf16[4,256,896]{2,1,0:T(8,128)(2,1)}, bf16[4,256,896]{2,1,0:T(8,128)(2,1)}, u32[]{:S(2)}, u32[]{:S(2)}) collective-permute-start(bf16[4,256,896]{2,1,0:T(8,128)(2,1)} %all-gather.4.cloned.1.call-done.own_ref.own_hbm), channel_id=1, source_target_pairs={{0,16},{16,0},{1,17},{17,1},{2,18},{18,2},{3,19},{19,3},{4,20},{20... | collective-permute-start | bytes 5505032 | tf_op jit(solution)/shard_map/ppermute | solution.py:38
  80.1 7.1 %copy-start.11 = (bf16[256,448]{1,0:T(8,128)(2,1)S(1)}, bf16[256,448]{1,0:T(8,128)(2,1)}, u32[]{:S(2)}) copy-start(bf16[256,448]{1,0:T(8,128)(2,1)} %get-tuple-element.62.keep_ref) | copy-start | bytes 688132
  80.1 7.1 %copy-start.13 = (bf16[256,448]{1,0:T(8,128)(2,1)S(1)}, bf16[256,448]{1,0:T(8,128)(2,1)}, u32[]{:S(2)}) copy-start(bf16[256,448]{1,0:T(8,128)(2,1)} %copy-done.12) | copy-start | bytes 688132
  85.7 0.7 copy-start.3
  86.4 0.8 copy-start.9
  87.2 5.1 %copy-start.7 = (bf16[2,4,16,896]{3,2,1,0:T(8,128)(2,1)}, bf16[2,4,16,896]{3,2,1,0:T(8,128)(2,1)S(1)}, u32[]{:S(2)}) copy-start(bf16[2,4,16,896]{3,2,1,0:T(8,128)(2,1)S(1)} %get-tuple-element.35.pieces_ref) | copy-start | bytes 688132
  92.2 1.7 copy-start.1
  93.9 0.7 copy-start.5
  94.6 8.9 %copy-start.8 = (bf16[2,4,16,896]{3,2,1,0:T(8,128)(2,1)S(1)}, bf16[2,4,16,896]{3,2,1,0:T(8,128)(2,1)}, u32[]{:S(2)}) copy-start(bf16[2,4,16,896]{3,2,1,0:T(8,128)(2,1)} %copy-done.7) | copy-start | bytes 688132
  94.7 10.9 %copy-start.4 = (f32[2,256,1]{2,1,0:T(8,128)S(1)}, f32[2,256,1]{2,1,0:T(8,128)}, u32[]{:S(2)}) copy-start(f32[2,256,1]{2,1,0:T(8,128)} %copy-done.3) | copy-start | bytes 6148
  94.7 11.0 %copy-start.10 = (f32[4,28,896]{2,1,0:T(8,128)S(1)}, f32[4,28,896]{2,1,0:T(8,128)}, u32[]{:S(2)}) copy-start(f32[4,28,896]{2,1,0:T(8,128)} %copy-done.9) | copy-start | bytes 1204228
  94.7 54.5 %all-to-all-start.2 = ((bf16[16,112,896]{2,1,0:T(8,128)(2,1)}), bf16[16,112,896]{2,1,0:T(8,128)(2,1)}, u32[]{:S(2)}, u32[]{:S(2)}) async-start(bf16[16,112,896]{2,1,0:T(8,128)(2,1)} %copy-done.1), calls=%async_computation.2 | async-start | bytes 6422528 | tf_op jit(solution)/shard_map/all_to_all | solution.py:388
  103.4 16.9 %copy-start.6 = (f32[2,256,1]{2,1,0:T(8,128)S(1)}, f32[2,256,1]{2,1,0:T(8,128)}, u32[]{:S(2)}) copy-start(f32[2,256,1]{2,1,0:T(8,128)} %copy-done.5) | copy-start | bytes 6148
  103.4 17.0 %copy-start.14 = (bf16[1,2,128,896]{3,2,1,0:T(8,128)(2,1)S(1)}, bf16[1,2,128,896]{3,2,1,0:T(8,128)(2,1)}, u32[]{:S(2)}) copy-start(bf16[1,2,128,896]{3,2,1,0:T(8,128)(2,1)} %param.6) | copy-start | bytes 1376260
  105.8 15.6 %collective-permute-start.5 = (f32[30,896]{1,0:T(8,128)S(1)}, f32[30,896]{1,0:T(8,128)S(1)}, u32[]{:S(2)}, u32[]{:S(2)}) collective-permute-start(f32[30,896]{1,0:T(8,128)S(1)} %get-tuple-element.66), channel_id=1, source_target_pairs={{0,3},{1,0},{2,1},{3,2},{4,7},{5,4},{6,5},{7,6},{8,11},{9,8},{10,9... | collective-permute-start | bytes 322568 | tf_op jit(solution)/shard_map/ppermute | solution.py:396
  111.3 22.5 %collective-permute-start.4 = (f32[30,896]{1,0:T(8,128)S(1)}, f32[30,896]{1,0:T(8,128)S(1)}, u32[]{:S(2)}, u32[]{:S(2)}) collective-permute-start(f32[30,896]{1,0:T(8,128)S(1)} %get-tuple-element.65), channel_id=1, source_target_pairs={{0,2},{1,3},{2,0},{3,1},{4,6},{5,7},{6,4},{7,5},{8,10},{9,11},{10,... | collective-permute-start | bytes 322568 | tf_op jit(solution)/shard_map/ppermute | solution.py:396
  118.4 21.9 %collective-permute-start.3 = (f32[30,896]{1,0:T(8,128)S(1)}, f32[30,896]{1,0:T(8,128)S(1)}, u32[]{:S(2)}, u32[]{:S(2)}) collective-permute-start(f32[30,896]{1,0:T(8,128)S(1)} %get-tuple-element.64), channel_id=1, source_target_pairs={{0,1},{1,2},{2,3},{3,0},{4,5},{5,6},{6,7},{7,4},{8,9},{9,10},{10,1... | collective-permute-start | bytes 322568 | tf_op jit(solution)/shard_map/ppermute | solution.py:396
  152.9 21.4 %all-to-all-start.3 = ((bf16[4,28,896]{2,1,0:T(8,128)(2,1)}), bf16[4,28,896]{2,1,0:T(8,128)(2,1)S(1)}, u32[]{:S(2)}, u32[]{:S(2)}) async-start(bf16[4,28,896]{2,1,0:T(8,128)(2,1)} %sum_senders.1), calls=%async_computation.3 | async-start | bytes 458752 | tf_op jit(solution)/shard_map/all_to_all | solution.py:418
  174.2 15.0 %copy-start.18 = (bf16[256,448]{1,0:T(8,128)(2,1)S(1)}, bf16[256,448]{1,0:T(8,128)(2,1)}, u32[]{:S(2)}) copy-start(bf16[256,448]{1,0:T(8,128)(2,1)} %get-tuple-element.53) | copy-start | bytes 688132
  174.2 20.6 %copy-start.16 = (bf16[256,448]{1,0:T(8,128)(2,1)S(1)}, bf16[256,448]{1,0:T(8,128)(2,1)}, u32[]{:S(2)}) copy-start(bf16[256,448]{1,0:T(8,128)(2,1)} %get-tuple-element.52) | copy-start | bytes 688132
  175.3 27.1 %all-to-all-start.4 = ((bf16[16,28,896]{2,1,0:T(8,128)(2,1)}), bf16[16,28,896]{2,1,0:T(8,128)(2,1)S(1)}, u32[]{:S(2)}, u32[]{:S(2)}) async-start(bf16[16,28,896]{2,1,0:T(8,128)(2,1)} %broadcast_in_dim.23), calls=%async_computation.4 | async-start | bytes 1835008 | tf_op jit(solution)/shard_map/all_to_all | solution.py:426
  189.2 5.6 %collective-permute-start.6 = (bf16[256,448]{1,0:T(8,128)(2,1)S(1)}, bf16[256,448]{1,0:T(8,128)(2,1)S(1)}, u32[]{:S(2)}, u32[]{:S(2)}) collective-permute-start(bf16[256,448]{1,0:T(8,128)(2,1)S(1)} %copy-done.18), channel_id=1, source_target_pairs={{0,16},{16,0},{1,17},{17,1},{2,18},{18,2},{3,19},{19,3},{4,20},{20... | collective-permute-start | bytes 688136 | tf_op jit(solution)/shard_map/ppermute | solution.py:38
  202.6 7.3 %collective-permute-start.7 = (bf16[16,28,896]{2,0,1:T(8,128)(2,1)S(1)}, bf16[16,28,896]{2,0,1:T(8,128)(2,1)S(1)}, u32[]{:S(2)}, u32[]{:S(2)}) collective-permute-start(bf16[16,28,896]{2,0,1:T(8,128)(2,1)S(1)} %copy.22), channel_id=1, source_target_pairs={{0,16},{16,0},{1,17},{17,1},{2,18},{18,2},{3,19},{19,3},{4,20},{20... | collective-permute-start | bytes 2408456 | tf_op jit(solution)/shard_map/ppermute | solution.py:38
Sparse Core Ops, SparseCore 0:
  10.1 56.4 all-gather.3
  78.1 87.7 all-gather.5

commit v13 on v12

--- a/solution.py
+++ b/solution.py
@@ -143,8 +143,10 @@
 
 
 def weight_kernel(
-    own_ref, other_ref, keep_ref, given_ref, pieces_ref, scale_ref, out_ref, coef_ref, acc_ref
+    replica_ref, own_ref, other_ref, keep_ref, given_ref, pieces_ref, scale_ref,
+    far_ref, near_ref, coef_ref, acc_ref,
 ):
+    blocks = [lax.rem(replica_ref[0] + step, NR) for step in range(NR)]
     token = lax.broadcasted_iota(jnp.int32, (TOK, PIECES), 0)
     part = lax.broadcasted_iota(jnp.int32, (TOK, PIECES), 1)
     part = part - jnp.where(token < SEQ, 0, 3)
@@ -168,28 +170,30 @@
         )
     for place in range(NX * NY):
         rows = [
-            acc_ref[block, place * SLICE : (place + 1) * SLICE, :] for block in range(NR)
+            acc_ref[block, place * SLICE : (place + 1) * SLICE, :] for block in blocks
         ]
-        out_ref[place] = jnp.concatenate(rows, 0).astype(bf16)
-
-
-def weight_partials(own, other, keep, given, pieces, scale):
+        near_ref[place] = rows[0].astype(bf16)
+        far_ref[place] = jnp.concatenate(rows[1:], 0).astype(bf16)
+
+
+def weight_partials(replica, own, other, keep, given, pieces, scale):
     spec = pl.BlockSpec(memory_space=pltpu.VMEM)
     return pl.pallas_call(
         weight_kernel,
         out_shape=(
-            jax.ShapeDtypeStruct((NX * NY, NR * SLICE, COLS), bf16),
+            jax.ShapeDtypeStruct((NX * NY, (NR - 1) * SLICE, COLS), bf16),
+            jax.ShapeDtypeStruct((NX * NY, SLICE, COLS), bf16),
             jax.ShapeDtypeStruct((NC, TOK, 1), f32),
         ),
-        in_specs=[spec] * 6,
-        out_specs=(spec, spec),
+        in_specs=[pl.BlockSpec(memory_space=pltpu.SMEM)] + [spec] * 6,
+        out_specs=(spec,) * 3,
         scratch_shapes=[pltpu.VMEM((NR, HALF, COLS), f32)],
         compiler_params=pltpu.CompilerParams(vmem_limit_bytes=24 * 1024 * 1024),
         cost_estimate=pl.CostEstimate(
             flops=4 * TOK * HALF * D, bytes_accessed=8 * 1024 * 1024, transcendentals=0
         ),
         name="weight_partials",
-    )(own, other, keep, given, pieces, scale)
+    )(replica, own, other, keep, given, pieces, scale)
 
 
 def sum_kernel(spread_ref, out_ref, acc_ref):
@@ -208,7 +212,7 @@
 
     @pl.when(step == NX - 1)
     def _():
-        for block in range(NR):
+        for block in range(NR - 1):
             out_ref[block] = acc_ref[block * SLICE : (block + 1) * SLICE, :].astype(bf16)
 
 
@@ -216,10 +220,10 @@
     return pl.pallas_call(
         sum_kernel,
         grid=(NX,),
-        out_shape=jax.ShapeDtypeStruct((NR, SLICE, COLS), bf16),
-        in_specs=[pl.BlockSpec((NY, NR * SLICE, COLS), lambda step: (step, 0, 0))],
-        out_specs=pl.BlockSpec((NR, SLICE, COLS), lambda step: (0, 0, 0)),
-        scratch_shapes=[pltpu.VMEM((NR * SLICE, COLS), f32)],
+        out_shape=jax.ShapeDtypeStruct((NR - 1, SLICE, COLS), bf16),
+        in_specs=[pl.BlockSpec((NY, (NR - 1) * SLICE, COLS), lambda step: (step, 0, 0))],
+        out_specs=pl.BlockSpec((NR - 1, SLICE, COLS), lambda step: (0, 0, 0)),
+        scratch_shapes=[pltpu.VMEM(((NR - 1) * SLICE, COLS), f32)],
         compiler_params=pltpu.CompilerParams(vmem_limit_bytes=16 * 1024 * 1024),
         cost_estimate=pl.CostEstimate(
             flops=NX * NY * NR * SLICE * COLS, bytes_accessed=4 * 1024 * 1024, transcendentals=0
@@ -381,11 +385,11 @@
         jnp.stack([dp_index, other_index]), got.transpose(1, 0, 2), gain
     )
 
-    partial, coef = weight_partials(
-        state_all, state_other, attn_keep, attn_other, pieces, scale
-    )
-    partial, first = lax.optimization_barrier((partial, first))
-    spread = lax.all_to_all(partial, PLANE, 0, 0)
+    far, near_part, coef = weight_partials(
+        ir.reshape(1), state_all, state_other, attn_keep, attn_other, pieces, scale
+    )
+    far, first = lax.optimization_barrier((far, first))
+    far = lax.all_to_all(far, PLANE, 0, 0)
 
     gain_mine = lax.dynamic_index_in_dim(gain_part, it, 0, keepdims=False)
     tail = jnp.concatenate([gain_mine, jnp.broadcast_to(loss_part[:1, :1], (1, FEAT))], 0)
@@ -412,24 +416,28 @@
     row_here = (row_here[:, :1] + row_here[:, 1:2]) + row_here[:, 2:]
     state_grad = first_col[0].reshape(2, SEQ, 1) * row_here - states * coef[0].reshape(2, SEQ, 1)
     grad_hidden = state_grad.astype(bf16).reshape(1, 2, SEQ, FEAT)
-    spread, first_sum, totals, grad_hidden = lax.optimization_barrier(
-        (spread, first_sum, totals, grad_hidden)
-    )
-    second = lax.all_to_all(sum_senders(spread), "r", 0, 0)
-    keep, give = attn_grads(
-        (ir + 2 * ic).reshape(1), state_all, state_other, pieces, w_all, coef, first_col
-    )
-    second, keep, give = lax.optimization_barrier((second, keep, give))
-    second_sum = jnp.sum(second.astype(f32), 0)
+    far, near_part, first_sum, totals, grad_hidden = lax.optimization_barrier(
+        (far, near_part, first_sum, totals, grad_hidden)
+    )
+    near_part = lax.all_to_all(near_part, PLANE, 0, 0)
+    far = sum_senders(far)
+    second_sum = jnp.sum(near_part.astype(f32), 0)
+    for step in range(1, NR):
+        second_sum = second_sum + lax.ppermute(
+            far[step - 1], "r", [(j, (j + step) % NR) for j in range(NR)]
+        ).astype(f32)
     total = first_sum - second_sum
     done = jnp.broadcast_to(total.astype(bf16)[None], (NX * NY, SLICE, COLS))
     half = lax.all_to_all(done, PLANE, 0, 0)
+    keep, give = attn_grads(
+        (ir + 2 * ic).reshape(1), state_all, state_other, pieces, w_all, coef, first_col
+    )
+    half, keep, give = lax.optimization_barrier((half, keep, give))
+    half_other = swap_core(half)
     arrived = swap_core(give)
     grad_attn = jnp.where(
         ic == 0, jnp.concatenate([keep, arrived], 1), jnp.concatenate([arrived, keep], 1)
     ).reshape(1, 2, SEQ, FEAT)
-    half, grad_attn = lax.optimization_barrier((half, grad_attn))
-    half_other = swap_core(half)
     grad_weight = join_halves(ic.reshape(1), half, half_other)
     return (grad_hidden, grad_attn, grad_weight, totals[0], totals[1, 0])
 

time: 219 us -> 229 us (1.046)
  the two profiles are of different devices: /device:TPU:33 before, /device:TPU:1 now
where the time goes in v13:
time: 229 us; the launch traced here: 228 us
  starting transfers between devices  110 us (48%)
  waiting for transfers between devices  38.1 us (17%)
  Pallas kernels  23.2 us (10%)
  local copies, waits for them, and re-layouts  21.2 us (9%)
  between operations  16.8 us (7%)
  blocking collectives  11.8 us (5%)
  other arithmetic  7.43 us (3%)
    ppermute x3, starting transfers between devices, body(): lax.ppermute(jnp.concatenate([outgoing, tail], 0), 'r', [(j, (j + step) %...  22.2 us
    ppermute x3, starting transfers between devices, body(): lax.ppermute(far[step - 1], 'r', [(j, (j + step) % NR) for j in range(NR)])  19.9 us
    ppermute x4, starting transfers between devices, swap_core(): return lax.ppermute(value, 'c', [(0, 1), (1, 0)])  15.6 us
    ppermute x3, waiting for transfers between devices, body(): lax.ppermute(jnp.concatenate([outgoing, tail], 0), 'r', [(j, (j + step) %...  15 us
    ppermute x1, starting transfers between devices, body(): lax.ppermute(lax.dynamic_slice(o_weight, (ic * HALF + iy * W_ROWS, 0), (W...  13.2 us
    psum x1, blocking collectives, body(): square = lax.psum(jnp.sum(states * states, -1), 't') / D  11.8 us
    all_to_all x1, starting transfers between devices, body(): got = lax.all_to_all(send, DP, 0, 0)  11 us
    unnamed x46, local copies, waits for them, and re-layouts  10.3 us
  transfers between devices with their start and end apart: 18, of which 8 were waited for; matrix products, arithmetic and copies ran while one was open for 8% of the time, Pallas kernels for 10%

profile of v13, /device:TPU:1, one launch (start us, length us, event | category | flops | bytes accessed | tf_op | source)
XLA Modules:
  0.0 228.1 jit_solution(3855003278294421230)
XLA Ops:
  9.4 1.2 fusion.2
  10.6 11.8 %psum.7 = f32[2,128]{1,0:T(2,128)S(1)} all-reduce(f32[2,128]{1,0:T(2,128)S(1)} %fusion.2), channel_id=1, replica_groups=mesh['x'=4,'y'=4,'c'=2,'t'=4,'r'=4] {'t'}, use_global_device_ids=true, to_apply=%region_1.2 | all-reduce | flops 256 | bytes 2048 | tf_op jit(solution)/shard_map/psum | solution.py:349
  22.4 0.7 convert_bitcast_fusion.1
  23.2 0.7 fusion.10
  23.9 1.4 fusion.6
  26.0 3.3 %all-to-all-start = ((f32[4,3,896]{2,1,0:T(4,128)}), f32[4,3,896]{2,1,0:T(4,128)S(1)}, u32[]{:S(2)}, u32[]{:S(2)}) async-start(f32[4,3,896]{2,1,0:T(4,128)} %broadcast_in_dim.17), calls=%async_computation | async-start | bytes 114688 | tf_op jit(solution)/shard_map/all_to_all | solution.py:358
  30.2 3.6 %all-to-all-done = f32[4,3,896]{2,1,0:T(4,128)S(1)} async-done(((f32[4,3,896]{2,1,0:T(4,128)}), f32[4,3,896]{2,1,0:T(4,128)S(1)}, u32[]{:S(2)}, u32[]{:S(2)}) %all-to-all-start) | async-done | bytes 43040 | tf_op jit(solution)/shard_map/all_to_all | solution.py:358
  34.7 2.2 concatenate.50
  37.0 11.0 %all-to-all-start.1 = ((f32[32,2,3840]{2,1,0:T(2,128)}), f32[32,2,3840]{2,1,0:T(2,128)S(1)}, u32[]{:S(2)}, u32[]{:S(2)}) async-start(f32[32,2,3840]{2,1,0:T(2,128)} %concatenate.50), calls=%async_computation.1 | async-start | bytes 1966080 | tf_op jit(solution)/shard_map/all_to_all | solution.py:377
  48.1 0.8 broadcast_select_fusion
  48.9 2.1 collective-permute-start
  51.1 13.2 %collective-permute-start.1 = (bf16[112,896]{1,0:T(8,128)(2,1)S(1)}, bf16[112,896]{1,0:T(8,128)(2,1)S(1)}, u32[]{:S(2)}, u32[]{:S(2)}) collective-permute-start(bf16[112,896]{1,0:T(8,128)(2,1)S(1)} %constant_dynamic-slice_fusion), channel_id=1, source_target_pairs={{0,0},{1,1},{2,2},{3,3},{18,16},{19,17},{16,18},{17,19},{129,128},... | collective-permute-start | bytes 602120 | tf_op jit(solution)/shard_map/ppermute | solution.py:339
  64.3 7.8 %collective-permute-done.1 = bf16[112,896]{1,0:T(8,128)(2,1)S(1)} collective-permute-done((bf16[112,896]{1,0:T(8,128)(2,1)S(1)}, bf16[112,896]{1,0:T(8,128)(2,1)S(1)}, u32[]{:S(2)}, u32[]{:S(2)}) %collective-permute-start.1) | collective-permute-done | bytes 200736 | tf_op jit(solution)/shard_map/ppermute | solution.py:339
  72.1 0.7 copy-done.12
  72.9 1.9 collective-permute-start.2
  75.1 1.0 slice.98
  76.0 1.3 copy.28
  77.3 4.2 %group_math.1 = (f32[4,28,896]{2,1,0:T(8,128)S(1)}, f32[4,1,896]{2,1,0:T(1,128)S(1)}, f32[8,128]{1,0:T(8,128)S(1)}, bf16[2,4,16,896]{3,2,1,0:T(8,128)(2,1)S(1)},...) custom-call(s32[2]{0:T(128)S(1)} %pad_add_fusion.index_ref, f32[2,32,3840]{2,1,0:T(8,128)S(1)} %bitcast.72, ...), custom_call_target="tpu_custom_call" | custom-call | flops 183500800 | bytes 3145728 | tf_op jit(solution)/shard_map/group_math/pallas_call | solution.py:124
  82.2 0.8 copy-done.9
  84.4 0.9 copy-done.8
  85.3 0.9 copy-done.11
  86.3 0.9 copy-done.13
  87.2 0.9 copy-done.15
  88.2 6.6 %weight_partials.1 = (bf16[16,84,896]{2,1,0:T(8,128)(2,1)S(1)}, bf16[16,28,896]{2,1,0:T(8,128)(2,1)}, f32[2,256,1]{2,1,0:T(8,128)S(1)}) custom-call(s32[1]{0:T(128)} %bitcast.replica_ref, bf16[4,256,896]{2,1,0:T(8,128)(2,1)S(1)} %copy-done.2, bf16[4,256,896]{2,1,0:T(8,128)(2,1)} %collective-permute-done.2.other_ref.other_hbm, ...), custom_call_target="tpu_custom_call" | custom-call | flops 1644167168 | bytes 8388608 | tf_op jit(solution)/shard_map/weight_partials/pallas_call | solution.py:181
  94.8 1.4 copy-done.1
  96.9 8.1 %all-to-all-start.2 = ((bf16[16,84,896]{2,1,0:T(8,128)(2,1)}), bf16[16,84,896]{2,1,0:T(8,128)(2,1)}, u32[]{:S(2)}, u32[]{:S(2)}) async-start(bf16[16,84,896]{2,1,0:T(8,128)(2,1)} %copy-done.1), calls=%async_computation.2 | async-start | bytes 5046272 | tf_op jit(solution)/shard_map/all_to_all | solution.py:392
  105.6 0.7 pad.18.clone
  107.2 12.6 %collective-permute-start.5 = (f32[30,896]{1,0:T(8,128)S(1)}, f32[30,896]{1,0:T(8,128)S(1)}, u32[]{:S(2)}, u32[]{:S(2)}) collective-permute-start(f32[30,896]{1,0:T(8,128)S(1)} %get-tuple-element.69), channel_id=1, source_target_pairs={{0,3},{1,0},{2,1},{3,2},{4,7},{5,4},{6,5},{7,6},{8,11},{9,8},{10,9... | collective-permute-start | bytes 322568 | tf_op jit(solution)/shard_map/ppermute | solution.py:400
  119.9 6.6 %collective-permute-start.4 = (f32[30,896]{1,0:T(8,128)S(1)}, f32[30,896]{1,0:T(8,128)S(1)}, u32[]{:S(2)}, u32[]{:S(2)}) collective-permute-start(f32[30,896]{1,0:T(8,128)S(1)} %get-tuple-element.68), channel_id=1, source_target_pairs={{0,2},{1,3},{2,0},{3,1},{4,6},{5,7},{6,4},{7,5},{8,10},{9,11},{10,... | collective-permute-start | bytes 322568 | tf_op jit(solution)/shard_map/ppermute | solution.py:400
  126.5 3.0 %collective-permute-start.3 = (f32[30,896]{1,0:T(8,128)S(1)}, f32[30,896]{1,0:T(8,128)S(1)}, u32[]{:S(2)}, u32[]{:S(2)}) collective-permute-start(f32[30,896]{1,0:T(8,128)S(1)} %get-tuple-element.67), channel_id=1, source_target_pairs={{0,1},{1,2},{2,3},{3,0},{4,5},{5,6},{6,7},{7,4},{8,9},{9,10},{10,1... | collective-permute-start | bytes 322568 | tf_op jit(solution)/shard_map/ppermute | solution.py:400
  129.6 1.0 fusion.5
  130.6 2.7 %collective-permute-done.5 = f32[30,896]{1,0:T(8,128)S(1)} collective-permute-done((f32[30,896]{1,0:T(8,128)S(1)}, f32[30,896]{1,0:T(8,128)S(1)}, u32[]{:S(2)}, u32[]{:S(2)}) %collective-permute-start.5) | collective-permute-done | bytes 107552 | tf_op jit(solution)/shard_map/ppermute | solution.py:400
  133.3 12.3 %collective-permute-done.4 = f32[30,896]{1,0:T(8,128)S(1)} collective-permute-done((f32[30,896]{1,0:T(8,128)S(1)}, f32[30,896]{1,0:T(8,128)S(1)}, u32[]{:S(2)}, u32[]{:S(2)}) %collective-permute-start.4) | collective-permute-done | bytes 107552 | tf_op jit(solution)/shard_map/ppermute | solution.py:400
  145.7 9.1 %all-to-all-start.3 = ((bf16[16,28,896]{2,1,0:T(8,128)(2,1)}), bf16[16,28,896]{2,1,0:T(8,128)(2,1)S(1)}, u32[]{:S(2)}, u32[]{:S(2)}) async-start(bf16[16,28,896]{2,1,0:T(8,128)(2,1)} %get-tuple-element.48), calls=%async_computation.3 | async-start | bytes 1835008 | tf_op jit(solution)/shard_map/all_to_all | solution.py:422
  154.8 2.7 %sum_senders.1 = bf16[3,28,896]{2,1,0:T(8,128)(2,1)S(1)} custom-call(bf16[16,84,896]{2,1,0:T(8,128)(2,1)} %all-to-all-done.2.spread_ref), custom_call_target="tpu_custom_call" | custom-call | flops 1605632 | bytes 4194304 | tf_op jit(solution)/shard_map/sum_senders/pallas_call | solution.py:220
  157.6 11.0 %collective-permute-start.8 = (bf16[28,896]{1,0:T(8,128)(2,1)S(1)}, bf16[28,896]{1,0:T(8,128)(2,1)S(1)}, u32[]{:S(2)}, u32[]{:S(2)}) collective-permute-start(bf16[28,896]{1,0:T(8,128)(2,1)S(1)} %get-tuple-element.65), channel_id=1, source_target_pairs={{0,3},{1,0},{2,1},{3,2},{4,7},{5,4},{6,5},{7,6},{8,11},{9,8},{10,9... | collective-permute-start | bytes 150536 | tf_op jit(solution)/shard_map/ppermute | solution.py:426
  168.6 6.8 %collective-permute-start.7 = (bf16[28,896]{1,0:T(8,128)(2,1)S(1)}, bf16[28,896]{1,0:T(8,128)(2,1)S(1)}, u32[]{:S(2)}, u32[]{:S(2)}) collective-permute-start(bf16[28,896]{1,0:T(8,128)(2,1)S(1)} %get-tuple-element.66), channel_id=1, source_target_pairs={{0,2},{1,3},{2,0},{3,1},{4,6},{5,7},{6,4},{7,5},{8,10},{9,11},{10,... | collective-permute-start | bytes 150536 | tf_op jit(solution)/shard_map/ppermute | solution.py:426
  175.4 2.2 collective-permute-start.6
  177.7 5.0 %collective-permute-done.7 = bf16[28,896]{1,0:T(8,128)(2,1)S(1)} collective-permute-done((bf16[28,896]{1,0:T(8,128)(2,1)S(1)}, bf16[28,896]{1,0:T(8,128)(2,1)S(1)}, u32[]{:S(2)}, u32[]{:S(2)}) %collective-permute-start.7) | collective-permute-done | bytes 50208 | tf_op jit(solution)/shard_map/ppermute | solution.py:426
  182.7 2.6 %collective-permute-done.6 = bf16[28,896]{1,0:T(8,128)(2,1)S(1)} collective-permute-done((bf16[28,896]{1,0:T(8,128)(2,1)S(1)}, bf16[28,896]{1,0:T(8,128)(2,1)S(1)}, u32[]{:S(2)}, u32[]{:S(2)}) %collective-permute-start.6) | collective-permute-done | bytes 50208 | tf_op jit(solution)/shard_map/ppermute | solution.py:426
  185.3 1.0 broadcast_in_dim.23
  186.3 7.1 %all-to-all-start.4 = ((bf16[16,28,896]{2,1,0:T(8,128)(2,1)}), bf16[16,28,896]{2,1,0:T(8,128)(2,1)S(1)}, u32[]{:S(2)}, u32[]{:S(2)}) async-start(bf16[16,28,896]{2,1,0:T(8,128)(2,1)} %broadcast_in_dim.23), calls=%async_computation.4 | async-start | bytes 1835008 | tf_op jit(solution)/shard_map/all_to_all | solution.py:431
  193.4 8.3 %attn_grads.1 = (bf16[256,448]{1,0:T(8,128)(2,1)}, bf16[256,448]{1,0:T(8,128)(2,1)}) custom-call(s32[1]{0:T(128)} %bitcast.30.shift_ref, bf16[4,256,896]{2,1,0:T(8,128)(2,1)} %all-gather.4.cloned.1.call-done.own_ref.own_hbm, bf16[4,256,896]{2,1,0:T(8,128)(2,1)} %collective-permute-done.2.other_ref.other_hbm, bf16[2,4,16,896]{3,2,1,0:T(8,128)(2,1)} %copy-done.7, ...), custom_call_target="tpu_custom_call" | custom-call | flops 1644167168 | bytes 8388608 | tf_op jit(solution)/shard_map/attn_grads/pallas_call | solution.py:306
  201.7 2.8 %all-to-all-done.4.mine_ref = bf16[16,28,896]{2,1,0:T(8,128)(2,1)S(1)} async-done(((bf16[16,28,896]{2,1,0:T(8,128)(2,1)}), bf16[16,28,896]{2,1,0:T(8,128)(2,1)S(1)}, u32[]{:S(2)}, u32[]{:S(2)}) %all-to-all-start.4) | async-done | bytes 802848 | tf_op jit(solution)/shard_map/all_to_all | solution.py:431
  204.8 9.6 %collective-permute-start.10 = (bf16[16,28,896]{2,0,1:T(8,128)(2,1)S(1)}, bf16[16,28,896]{2,0,1:T(8,128)(2,1)S(1)}, u32[]{:S(2)}, u32[]{:S(2)}) collective-permute-start(bf16[16,28,896]{2,0,1:T(8,128)(2,1)S(1)} %copy.22), channel_id=1, source_target_pairs={{0,16},{16,0},{1,17},{17,1},{2,18},{18,2},{3,19},{19,3},{4,20},{20... | collective-permute-start | bytes 2408456 | tf_op jit(solution)/shard_map/ppermute | solution.py:38
  214.4 1.9 collective-permute-start.9
  218.1 1.1 maximum_select_fusion
  219.3 1.4 join_halves.1
  (92 shorter events, 10.2 us)
Async XLA Ops:
  8.0 43.1 %copy-start = (bf16[896,896]{1,0:T(8,128)(2,1)S(1)}, bf16[896,896]{1,0:T(8,128)(2,1)}, u32[]{:S(2)}) copy-start(bf16[896,896]{1,0:T(8,128)(2,1)} %param.8) | copy-start | bytes 4816900
  8.0 64.9 %all-gather.4.cloned.1.call-start = ((), (), s32[]{:S(2)}) async-start(), calls=%async_computation.5 | async-start | bytes 2293760 | tf_op jit(solution)/shard_map/all_gather | solution.py:332
  26.0 7.8 %all-to-all-start = ((f32[4,3,896]{2,1,0:T(4,128)}), f32[4,3,896]{2,1,0:T(4,128)S(1)}, u32[]{:S(2)}, u32[]{:S(2)}) async-start(f32[4,3,896]{2,1,0:T(4,128)} %broadcast_in_dim.17), calls=%async_computation | async-start | bytes 114688 | tf_op jit(solution)/shard_map/all_to_all | solution.py:358
  33.8 0.6 copy-start.21
  34.7 13.3 %copy-start.18 = (bf16[1,2,128,896]{3,2,1,0:T(8,128)(2,1)S(1)}, bf16[1,2,128,896]{3,2,1,0:T(8,128)(2,1)}, u32[]{:S(2)}) copy-start(bf16[1,2,128,896]{3,2,1,0:T(8,128)(2,1)} %param.7) | copy-start | bytes 1376260
  37.0 35.9 %all-to-all-start.1 = ((f32[32,2,3840]{2,1,0:T(2,128)}), f32[32,2,3840]{2,1,0:T(2,128)S(1)}, u32[]{:S(2)}, u32[]{:S(2)}) async-start(f32[32,2,3840]{2,1,0:T(2,128)} %concatenate.50), calls=%async_computation.1 | async-start | bytes 1966080 | tf_op jit(solution)/shard_map/all_to_all | solution.py:377
  48.0 145.4 %all-gather.6.cloned.1.call-start = ((), (), s32[]{:S(2)}) async-start(), calls=%async_computation.6 | async-start | bytes 3411968 | tf_op jit(solution)/shard_map/all_gather | solution.py:383
  48.9 23.2 %collective-permute-start = (bf16[256,448]{1,0:T(8,128)(2,1)S(1)}, bf16[256,448]{1,0:T(8,128)(2,1)S(1)}, u32[]{:S(2)}, u32[]{:S(2)}) collective-permute-start(bf16[256,448]{1,0:T(8,128)(2,1)S(1)} %get-tuple-element.63), channel_id=1, source_target_pairs={{0,16},{16,0},{1,17},{17,1},{2,18},{18,2},{3,19},{19,3},{4,20},{20... | collective-permute-start | bytes 688136 | tf_op jit(solution)/shard_map/ppermute | solution.py:38
  51.1 21.0 %collective-permute-start.1 = (bf16[112,896]{1,0:T(8,128)(2,1)S(1)}, bf16[112,896]{1,0:T(8,128)(2,1)S(1)}, u32[]{:S(2)}, u32[]{:S(2)}) collective-permute-start(bf16[112,896]{1,0:T(8,128)(2,1)S(1)} %constant_dynamic-slice_fusion), channel_id=1, source_target_pairs={{0,0},{1,1},{2,2},{3,3},{18,16},{19,17},{16,18},{17,19},{129,128},... | collective-permute-start | bytes 602120 | tf_op jit(solution)/shard_map/ppermute | solution.py:339
  72.1 2.7 %copy-start.20 = (bf16[112,896]{1,0:T(8,128)(2,1)}, bf16[112,896]{1,0:T(8,128)(2,1)S(1)}, u32[]{:S(2)}) copy-start(bf16[112,896]{1,0:T(8,128)(2,1)S(1)} %collective-permute-done.1) | copy-start | bytes 602116
  72.1 0.7 copy-start.12
  72.9 1.9 copy-start.17
  72.9 11.5 %collective-permute-start.2 = (bf16[4,256,896]{2,1,0:T(8,128)(2,1)}, bf16[4,256,896]{2,1,0:T(8,128)(2,1)}, u32[]{:S(2)}, u32[]{:S(2)}) collective-permute-start(bf16[4,256,896]{2,1,0:T(8,128)(2,1)} %all-gather.4.cloned.1.call-done.own_ref.own_hbm), channel_id=1, source_target_pairs={{0,16},{16,0},{1,17},{17,1},{2,18},{18,2},{3,19},{19,3},{4,20},{20... | collective-permute-start | bytes 5505032 | tf_op jit(solution)/shard_map/ppermute | solution.py:38
  74.8 9.6 %copy-start.2 = (bf16[4,256,896]{2,1,0:T(8,128)(2,1)S(1)}, bf16[4,256,896]{2,1,0:T(8,128)(2,1)}, u32[]{:S(2)}) copy-start(bf16[4,256,896]{2,1,0:T(8,128)(2,1)} %all-gather.4.cloned.1.call-done.own_ref.own_hbm) | copy-start | bytes 5505028
  81.5 0.7 copy-start.3
  82.2 0.8 copy-start.9
  82.9 0.7 copy-start.14
  83.7 0.7 copy-start.7
  84.4 0.9 copy-start.8
  85.3 0.9 copy-start.11
  86.3 0.9 copy-start.13
  87.2 0.9 copy-start.15
  94.8 1.4 copy-start.1
  96.2 0.7 copy-start.5
  96.9 10.0 %copy-start.4 = (f32[2,256,1]{2,1,0:T(8,128)S(1)}, f32[2,256,1]{2,1,0:T(8,128)}, u32[]{:S(2)}) copy-start(f32[2,256,1]{2,1,0:T(8,128)} %copy-done.3) | copy-start | bytes 6148
  96.9 10.2 %copy-start.10 = (f32[4,28,896]{2,1,0:T(8,128)S(1)}, f32[4,28,896]{2,1,0:T(8,128)}, u32[]{:S(2)}) copy-start(f32[4,28,896]{2,1,0:T(8,128)} %copy-done.9) | copy-start | bytes 1204228
  96.9 32.6 %copy-start.6 = (f32[2,256,1]{2,1,0:T(8,128)S(1)}, f32[2,256,1]{2,1,0:T(8,128)}, u32[]{:S(2)}) copy-start(f32[2,256,1]{2,1,0:T(8,128)} %copy-done.5) | copy-start | bytes 6148
  96.9 48.8 %all-to-all-start.2 = ((bf16[16,84,896]{2,1,0:T(8,128)(2,1)}), bf16[16,84,896]{2,1,0:T(8,128)(2,1)}, u32[]{:S(2)}, u32[]{:S(2)}) async-start(bf16[16,84,896]{2,1,0:T(8,128)(2,1)} %copy-done.1), calls=%async_computation.2 | async-start | bytes 5046272 | tf_op jit(solution)/shard_map/all_to_all | solution.py:392
  105.0 24.6 %copy-start.16 = (bf16[1,2,128,896]{3,2,1,0:T(8,128)(2,1)S(1)}, bf16[1,2,128,896]{3,2,1,0:T(8,128)(2,1)}, u32[]{:S(2)}) copy-start(bf16[1,2,128,896]{3,2,1,0:T(8,128)(2,1)} %param.6) | copy-start | bytes 1376260
  107.2 26.1 %collective-permute-start.5 = (f32[30,896]{1,0:T(8,128)S(1)}, f32[30,896]{1,0:T(8,128)S(1)}, u32[]{:S(2)}, u32[]{:S(2)}) collective-permute-start(f32[30,896]{1,0:T(8,128)S(1)} %get-tuple-element.69), channel_id=1, source_target_pairs={{0,3},{1,0},{2,1},{3,2},{4,7},{5,4},{6,5},{7,6},{8,11},{9,8},{10,9... | collective-permute-start | bytes 322568 | tf_op jit(solution)/shard_map/ppermute | solution.py:400
  119.9 25.7 %collective-permute-start.4 = (f32[30,896]{1,0:T(8,128)S(1)}, f32[30,896]{1,0:T(8,128)S(1)}, u32[]{:S(2)}, u32[]{:S(2)}) collective-permute-start(f32[30,896]{1,0:T(8,128)S(1)} %get-tuple-element.68), channel_id=1, source_target_pairs={{0,2},{1,3},{2,0},{3,1},{4,6},{5,7},{6,4},{7,5},{8,10},{9,11},{10,... | collective-permute-start | bytes 322568 | tf_op jit(solution)/shard_map/ppermute | solution.py:400
  126.5 19.2 %collective-permute-start.3 = (f32[30,896]{1,0:T(8,128)S(1)}, f32[30,896]{1,0:T(8,128)S(1)}, u32[]{:S(2)}, u32[]{:S(2)}) collective-permute-start(f32[30,896]{1,0:T(8,128)S(1)} %get-tuple-element.67), channel_id=1, source_target_pairs={{0,1},{1,2},{2,3},{3,0},{4,5},{5,6},{6,7},{7,4},{8,9},{9,10},{10,1... | collective-permute-start | bytes 322568 | tf_op jit(solution)/shard_map/ppermute | solution.py:400
  145.7 31.8 %all-to-all-start.3 = ((bf16[16,28,896]{2,1,0:T(8,128)(2,1)}), bf16[16,28,896]{2,1,0:T(8,128)(2,1)S(1)}, u32[]{:S(2)}, u32[]{:S(2)}) async-start(bf16[16,28,896]{2,1,0:T(8,128)(2,1)} %get-tuple-element.48), calls=%async_computation.3 | async-start | bytes 1835008 | tf_op jit(solution)/shard_map/all_to_all | solution.py:422
  157.6 20.1 %collective-permute-start.8 = (bf16[28,896]{1,0:T(8,128)(2,1)S(1)}, bf16[28,896]{1,0:T(8,128)(2,1)S(1)}, u32[]{:S(2)}, u32[]{:S(2)}) collective-permute-start(bf16[28,896]{1,0:T(8,128)(2,1)S(1)} %get-tuple-element.65), channel_id=1, source_target_pairs={{0,3},{1,0},{2,1},{3,2},{4,7},{5,4},{6,5},{7,6},{8,11},{9,8},{10,9... | collective-permute-start | bytes 150536 | tf_op jit(solution)/shard_map/ppermute | solution.py:426
  168.6 14.1 %collective-permute-start.7 = (bf16[28,896]{1,0:T(8,128)(2,1)S(1)}, bf16[28,896]{1,0:T(8,128)(2,1)S(1)}, u32[]{:S(2)}, u32[]{:S(2)}) collective-permute-start(bf16[28,896]{1,0:T(8,128)(2,1)S(1)} %get-tuple-element.66), channel_id=1, source_target_pairs={{0,2},{1,3},{2,0},{3,1},{4,6},{5,7},{6,4},{7,5},{8,10},{9,11},{10,... | collective-permute-start | bytes 150536 | tf_op jit(solution)/shard_map/ppermute | solution.py:426
  175.4 9.9 %collective-permute-start.6 = (bf16[28,896]{1,0:T(8,128)(2,1)S(1)}, bf16[28,896]{1,0:T(8,128)(2,1)S(1)}, u32[]{:S(2)}, u32[]{:S(2)}) collective-permute-start(bf16[28,896]{1,0:T(8,128)(2,1)S(1)} %get-tuple-element.64), channel_id=1, source_target_pairs={{0,1},{1,2},{2,3},{3,0},{4,5},{5,6},{6,7},{7,4},{8,9},{9,10},{10,1... | collective-permute-start | bytes 150536 | tf_op jit(solution)/shard_map/ppermute | solution.py:426
  186.3 18.2 %all-to-all-start.4 = ((bf16[16,28,896]{2,1,0:T(8,128)(2,1)}), bf16[16,28,896]{2,1,0:T(8,128)(2,1)S(1)}, u32[]{:S(2)}, u32[]{:S(2)}) async-start(bf16[16,28,896]{2,1,0:T(8,128)(2,1)} %broadcast_in_dim.23), calls=%async_computation.4 | async-start | bytes 1835008 | tf_op jit(solution)/shard_map/all_to_all | solution.py:431
  201.7 16.3 %copy-start.19 = (bf16[256,448]{1,0:T(8,128)(2,1)S(1)}, bf16[256,448]{1,0:T(8,128)(2,1)}, u32[]{:S(2)}) copy-start(bf16[256,448]{1,0:T(8,128)(2,1)} %get-tuple-element.53) | copy-start | bytes 688132
  204.8 14.3 %collective-permute-start.10 = (bf16[16,28,896]{2,0,1:T(8,128)(2,1)S(1)}, bf16[16,28,896]{2,0,1:T(8,128)(2,1)S(1)}, u32[]{:S(2)}, u32[]{:S(2)}) collective-permute-start(bf16[16,28,896]{2,0,1:T(8,128)(2,1)S(1)} %copy.22), channel_id=1, source_target_pairs={{0,16},{16,0},{1,17},{17,1},{2,18},{18,2},{3,19},{19,3},{4,20},{20... | collective-permute-start | bytes 2408456 | tf_op jit(solution)/shard_map/ppermute | solution.py:38
  214.4 3.6 %collective-permute-start.9 = (bf16[256,448]{1,0:T(8,128)(2,1)}, bf16[256,448]{1,0:T(8,128)(2,1)S(1)}, u32[]{:S(2)}, u32[]{:S(2)}) collective-permute-start(bf16[256,448]{1,0:T(8,128)(2,1)} %get-tuple-element.54), channel_id=1, source_target_pairs={{0,16},{16,0},{1,17},{17,1},{2,18},{18,2},{3,19},{19,3},{4,20},{20... | collective-permute-start | bytes 688136 | tf_op jit(solution)/shard_map/ppermute | solution.py:38
Sparse Core Ops, SparseCore 0:
  10.9 56.4 all-gather.3
Sparse Core Ops, SparseCore 1:
  74.9 80.1 all-gather.5

commit v14 on v12

--- a/solution.py
+++ b/solution.py
@@ -371,12 +371,11 @@
         -1,
     )
     got = lax.all_to_all(send, DP, 0, 0)
-    got, attn_other, w_moved = lax.optimization_barrier((got, attn_other, w_moved))
+    got, attn_other = lax.optimization_barrier((got, attn_other))
 
     other_index = dp_index + 1 - 2 * ic
     got, state_all = lax.optimization_barrier((got, state_all))
     state_other = swap_core(state_all)
-    w_all = lax.all_gather(w_moved, PLANE).reshape(NX, HALF, COLS)
     first, gain_part, loss_part, pieces, scale, first_col = group_math(
         jnp.stack([dp_index, other_index]), got.transpose(1, 0, 2), gain
     )
@@ -384,7 +383,8 @@
     partial, coef = weight_partials(
         state_all, state_other, attn_keep, attn_other, pieces, scale
     )
-    partial, first = lax.optimization_barrier((partial, first))
+    partial, first, w_moved = lax.optimization_barrier((partial, first, w_moved))
+    w_all = lax.all_gather(w_moved, PLANE).reshape(NX, HALF, COLS)
     spread = lax.all_to_all(partial, PLANE, 0, 0)
 
     gain_mine = lax.dynamic_index_in_dim(gain_part, it, 0, keepdims=False)
@@ -416,20 +416,19 @@
         (spread, first_sum, totals, grad_hidden)
     )
     second = lax.all_to_all(sum_senders(spread), "r", 0, 0)
-    keep, give = attn_grads(
-        (ir + 2 * ic).reshape(1), state_all, state_other, pieces, w_all, coef, first_col
-    )
-    second, keep, give = lax.optimization_barrier((second, keep, give))
     second_sum = jnp.sum(second.astype(f32), 0)
     total = first_sum - second_sum
     done = jnp.broadcast_to(total.astype(bf16)[None], (NX * NY, SLICE, COLS))
     half = lax.all_to_all(done, PLANE, 0, 0)
+    keep, give = attn_grads(
+        (ir + 2 * ic).reshape(1), state_all, state_other, pieces, w_all, coef, first_col
+    )
+    half, keep, give = lax.optimization_barrier((half, keep, give))
+    half_other = swap_core(half)
     arrived = swap_core(give)
     grad_attn = jnp.where(
         ic == 0, jnp.concatenate([keep, arrived], 1), jnp.concatenate([arrived, keep], 1)
     ).reshape(1, 2, SEQ, FEAT)
-    half, grad_attn = lax.optimization_barrier((half, grad_attn))
-    half_other = swap_core(half)
     grad_weight = join_halves(ic.reshape(1), half, half_other)
     return (grad_hidden, grad_attn, grad_weight, totals[0], totals[1, 0])
 

time: 219 us -> 214 us (0.977)
  the two profiles are of different devices: /device:TPU:33 before, /device:TPU:1 now
where the time goes in v14:
time: 214 us; the launch traced here: 213 us
  starting transfers between devices  69.8 us (33%)
  waiting for transfers between devices  44.7 us (21%)
  blocking collectives  38.1 us (18%)
  Pallas kernels  21.9 us (10%)
  local copies, waits for them, and re-layouts  15.4 us (7%)
  between operations  15.3 us (7%)
  other arithmetic  7.29 us (3%)
    all_to_all x1, blocking collectives, body(): second = lax.all_to_all(sum_senders(spread), 'r', 0, 0)  26.3 us
    ppermute x3, starting transfers between devices, body(): lax.ppermute(jnp.concatenate([outgoing, tail], 0), 'r', [(j, (j + step) %...  15 us
    ppermute x4, starting transfers between devices, swap_core(): return lax.ppermute(value, 'c', [(0, 1), (1, 0)])  14.3 us
    psum x1, blocking collectives, body(): square = lax.psum(jnp.sum(states * states, -1), 't') / D  11.8 us
    all_to_all x1, waiting for transfers between devices, body(): spread = lax.all_to_all(partial, PLANE, 0, 0)  11.7 us
    all_to_all x1, waiting for transfers between devices, body(): got = lax.all_to_all(send, DP, 0, 0)  11.2 us
    ppermute x1, starting transfers between devices, body(): lax.ppermute(lax.dynamic_slice(o_weight, (ic * HALF + iy * W_ROWS, 0), (W...  11.1 us
    all_to_all x1, starting transfers between devices, body(): got = lax.all_to_all(send, DP, 0, 0)  11.1 us
  transfers between devices with their start and end apart: 14, of which 9 were waited for; matrix products, arithmetic and copies ran while one was open for 8% of the time, Pallas kernels for 10%

profile of v14, /device:TPU:1, one launch (start us, length us, event | category | flops | bytes accessed | tf_op | source)
XLA Modules:
  0.0 212.6 jit_solution(954217252396949832)
XLA Ops:
  7.2 0.7 all-gather.4.cloned.1.call-update
  7.9 0.7 broadcast_in_dim.16
  8.6 1.2 fusion.2
  9.8 11.8 %psum.7 = f32[2,128]{1,0:T(2,128)S(1)} all-reduce(f32[2,128]{1,0:T(2,128)S(1)} %fusion.2), channel_id=1, replica_groups=mesh['x'=4,'y'=4,'c'=2,'t'=4,'r'=4] {'t'}, use_global_device_ids=true, to_apply=%region_1.2 | all-reduce | flops 256 | bytes 2048 | tf_op jit(solution)/shard_map/psum | solution.py:345
  21.6 0.7 convert_bitcast_fusion.1
  22.3 0.7 fusion.10
  23.1 1.4 fusion.6
  24.5 0.6 broadcast_in_dim.17
  25.1 3.3 %all-to-all-start = ((f32[4,3,896]{2,1,0:T(4,128)}), f32[4,3,896]{2,1,0:T(4,128)S(1)}, u32[]{:S(2)}, u32[]{:S(2)}) async-start(f32[4,3,896]{2,1,0:T(4,128)} %broadcast_in_dim.17), calls=%async_computation | async-start | bytes 114688 | tf_op jit(solution)/shard_map/all_to_all | solution.py:354
  29.4 3.6 %all-to-all-done = f32[4,3,896]{2,1,0:T(4,128)S(1)} async-done(((f32[4,3,896]{2,1,0:T(4,128)}), f32[4,3,896]{2,1,0:T(4,128)S(1)}, u32[]{:S(2)}, u32[]{:S(2)}) %all-to-all-start) | async-done | bytes 43040 | tf_op jit(solution)/shard_map/all_to_all | solution.py:354
  33.3 2.2 %concatenate.50 = f32[32,2,3840]{2,1,0:T(2,128)} concatenate(f32[32,2,3712]{2,1,0:T(2,128)S(1)} %broadcast_in_dim.18, f32[32,2,28]{2,1,0:T(2,128)S(1)} %copy.20, f32[32,2,2]{2,1,0:T(2,128)S(1)} %broadcast_in_dim.19, f32[32,2,98]{2,1,0:T(2,128)S(1)} %broadcast_in_dim.20), dimensions={2} | concatenate | bytes 1966080 | tf_op jit(solution)/shard_map/concatenate | solution.py:364
  35.5 11.1 %all-to-all-start.1 = ((f32[32,2,3840]{2,1,0:T(2,128)}), f32[32,2,3840]{2,1,0:T(2,128)}, u32[]{:S(2)}, u32[]{:S(2)}) async-start(f32[32,2,3840]{2,1,0:T(2,128)} %concatenate.50), calls=%async_computation.1 | async-start | bytes 1966080 | tf_op jit(solution)/shard_map/all_to_all | solution.py:373
  46.7 0.8 broadcast_select_fusion
  47.5 2.2 %collective-permute-start = (bf16[256,448]{1,0:T(8,128)(2,1)S(1)}, bf16[256,448]{1,0:T(8,128)(2,1)S(1)}, u32[]{:S(2)}, u32[]{:S(2)}) collective-permute-start(bf16[256,448]{1,0:T(8,128)(2,1)S(1)} %get-tuple-element.59), channel_id=1, source_target_pairs={{0,16},{16,0},{1,17},{17,1},{2,18},{18,2},{3,19},{19,3},{4,20},{20... | collective-permute-start | bytes 688136 | tf_op jit(solution)/shard_map/ppermute | solution.py:38
  49.8 1.2 collective-permute-done.given_ref
  51.0 0.7 copy-done.12
  51.7 11.2 %all-to-all-done.1 = f32[32,2,3840]{2,1,0:T(2,128)} async-done(((f32[32,2,3840]{2,1,0:T(2,128)}), f32[32,2,3840]{2,1,0:T(2,128)}, u32[]{:S(2)}, u32[]{:S(2)}) %all-to-all-start.1) | async-done | bytes 983072 | tf_op jit(solution)/shard_map/all_to_all | solution.py:373
  62.9 3.2 %all-gather.4.cloned.1.call-done.own_ref.own_hbm = bf16[4,256,896]{2,1,0:T(8,128)(2,1)} async-done(((bf16[1,256,896]{2,1,0:T(8,128)(2,1)}), bf16[4,256,896]{2,1,0:T(8,128)(2,1)}) %all-gather.4.cloned.1.call-update) | async-done | bytes 1835024 | tf_op jit(solution)/shard_map/all_gather | solution.py:328
  66.1 3.0 %collective-permute-start.1 = (bf16[4,256,896]{2,1,0:T(8,128)(2,1)}, bf16[4,256,896]{2,1,0:T(8,128)(2,1)}, u32[]{:S(2)}, u32[]{:S(2)}) collective-permute-start(bf16[4,256,896]{2,1,0:T(8,128)(2,1)} %all-gather.4.cloned.1.call-done.own_ref.own_hbm), channel_id=1, source_target_pairs={{0,16},{16,0},{1,17},{17,1},{2,18},{18,2},{3,19},{19,3},{4,20},{20... | collective-permute-start | bytes 5505032 | tf_op jit(solution)/shard_map/ppermute | solution.py:38
  69.1 0.7 constant_dynamic-slice_fusion
  69.8 11.1 %collective-permute-start.2 = (bf16[112,896]{1,0:T(8,128)(2,1)}, bf16[112,896]{1,0:T(8,128)(2,1)}, u32[]{:S(2)}, u32[]{:S(2)}) collective-permute-start(bf16[112,896]{1,0:T(8,128)(2,1)} %constant_dynamic-slice_fusion), channel_id=1, source_target_pairs={{0,0},{1,1},{2,2},{3,3},{18,16},{19,17},{16,18},{17,19},{129,128},... | collective-permute-start | bytes 602120 | tf_op jit(solution)/shard_map/ppermute | solution.py:335
  81.1 1.3 copy.28
  82.4 4.1 %group_math.1 = (f32[4,28,896]{2,1,0:T(8,128)S(1)}, f32[4,1,896]{2,1,0:T(1,128)S(1)}, f32[8,128]{1,0:T(8,128)S(1)}, bf16[2,4,16,896]{3,2,1,0:T(8,128)(2,1)S(1)},...) custom-call(s32[2]{0:T(128)S(1)} %pad_add_fusion.index_ref, f32[2,32,3840]{2,1,0:T(8,128)S(1)} %bitcast.65, ...), custom_call_target="tpu_custom_call" | custom-call | flops 183500800 | bytes 3145728 | tf_op jit(solution)/shard_map/group_math/pallas_call | solution.py:124
  86.5 0.7 copy-done.3
  87.2 0.8 copy-done.9
  88.0 5.0 %weight_partials.1 = (bf16[16,112,896]{2,1,0:T(8,128)(2,1)S(1)}, f32[2,256,1]{2,1,0:T(8,128)S(1)}) custom-call(bf16[4,256,896]{2,1,0:T(8,128)(2,1)S(1)} %copy-done.2, bf16[4,256,896]{2,1,0:T(8,128)(2,1)} %collective-permute-done.1.other_ref.other_hbm, bf16[256,448]{1,0:T(8,128)(2,1)S(1)} %copy-done.11, bf16[256,448]{1,0:T(8,128)(2,1)S(1)} %copy-done.13, ...), custom_call_target="tpu_custom_call" | custom-call | flops 1644167168 | bytes 8388608 | tf_op jit(solution)/shard_map/weight_partials/pallas_call | solution.py:178
  93.1 1.7 copy-done.1
  94.8 0.7 copy-done.5
  95.5 4.6 %all-to-all-start.2 = ((bf16[16,112,896]{2,1,0:T(8,128)(2,1)}), bf16[16,112,896]{2,1,0:T(8,128)(2,1)}, u32[]{:S(2)}, u32[]{:S(2)}) async-start(bf16[16,112,896]{2,1,0:T(8,128)(2,1)} %copy-done.1), calls=%async_computation.2 | async-start | bytes 6422528 | tf_op jit(solution)/shard_map/all_to_all | solution.py:388
  100.9 0.7 pad.18.clone
  101.6 0.7 pad_bitcast_fusion
  102.6 4.0 %collective-permute-start.5 = (f32[30,896]{1,0:T(8,128)S(1)}, f32[30,896]{1,0:T(8,128)S(1)}, u32[]{:S(2)}, u32[]{:S(2)}) collective-permute-start(f32[30,896]{1,0:T(8,128)S(1)} %get-tuple-element.62), channel_id=1, source_target_pairs={{0,3},{1,0},{2,1},{3,2},{4,7},{5,4},{6,5},{7,6},{8,11},{9,8},{10,9... | collective-permute-start | bytes 322568 | tf_op jit(solution)/shard_map/ppermute | solution.py:396
  106.6 5.9 %collective-permute-start.4 = (f32[30,896]{1,0:T(8,128)S(1)}, f32[30,896]{1,0:T(8,128)S(1)}, u32[]{:S(2)}, u32[]{:S(2)}) collective-permute-start(f32[30,896]{1,0:T(8,128)S(1)} %get-tuple-element.61), channel_id=1, source_target_pairs={{0,2},{1,3},{2,0},{3,1},{4,6},{5,7},{6,4},{7,5},{8,10},{9,11},{10,... | collective-permute-start | bytes 322568 | tf_op jit(solution)/shard_map/ppermute | solution.py:396
  112.4 5.1 %collective-permute-start.3 = (f32[30,896]{1,0:T(8,128)S(1)}, f32[30,896]{1,0:T(8,128)S(1)}, u32[]{:S(2)}, u32[]{:S(2)}) collective-permute-start(f32[30,896]{1,0:T(8,128)S(1)} %get-tuple-element.60), channel_id=1, source_target_pairs={{0,1},{1,2},{2,3},{3,0},{4,5},{5,6},{6,7},{7,4},{8,9},{9,10},{10,1... | collective-permute-start | bytes 322568 | tf_op jit(solution)/shard_map/ppermute | solution.py:396
  117.7 1.0 fusion.5
  118.7 2.5 %collective-permute-done.4 = f32[30,896]{1,0:T(8,128)S(1)} collective-permute-done((f32[30,896]{1,0:T(8,128)S(1)}, f32[30,896]{1,0:T(8,128)S(1)}, u32[]{:S(2)}, u32[]{:S(2)}) %collective-permute-start.4) | collective-permute-done | bytes 107552 | tf_op jit(solution)/shard_map/ppermute | solution.py:396
  121.2 7.0 %collective-permute-done.3 = f32[30,896]{1,0:T(8,128)S(1)} collective-permute-done((f32[30,896]{1,0:T(8,128)S(1)}, f32[30,896]{1,0:T(8,128)S(1)}, u32[]{:S(2)}, u32[]{:S(2)}) %collective-permute-start.3) | collective-permute-done | bytes 107552 | tf_op jit(solution)/shard_map/ppermute | solution.py:396
  128.3 11.7 %all-to-all-done.2.spread_ref = bf16[16,112,896]{2,1,0:T(8,128)(2,1)} async-done(((bf16[16,112,896]{2,1,0:T(8,128)(2,1)}), bf16[16,112,896]{2,1,0:T(8,128)(2,1)}, u32[]{:S(2)}, u32[]{:S(2)}) %all-to-all-start.2) | async-done | bytes 3211296 | tf_op jit(solution)/shard_map/all_to_all | solution.py:388
  139.9 3.0 %sum_senders.1 = bf16[4,28,896]{2,1,0:T(8,128)(2,1)S(1)} custom-call(bf16[16,112,896]{2,1,0:T(8,128)(2,1)} %all-to-all-done.2.spread_ref), custom_call_target="tpu_custom_call" | custom-call | flops 1605632 | bytes 4194304 | tf_op jit(solution)/shard_map/sum_senders/pallas_call | solution.py:216
  143.0 26.3 %all_to_all.25 = bf16[4,28,896]{2,1,0:T(8,128)(2,1)S(1)} all-to-all(bf16[4,28,896]{2,1,0:T(8,128)(2,1)S(1)} %sum_senders.1), channel_id=1, replica_groups=mesh['x'=4,'y'=4,'c'=2,'t'=4,'r'=4] {'r'}, dimensions={0} | all-to-all | bytes 401408 | tf_op jit(solution)/shard_map/all_to_all | solution.py:418
  169.3 1.0 broadcast_in_dim.23
  170.3 10.4 %all-to-all-start.4 = ((bf16[16,28,896]{2,1,0:T(8,128)(2,1)}), bf16[16,28,896]{2,1,0:T(8,128)(2,1)S(1)}, u32[]{:S(2)}, u32[]{:S(2)}) async-start(bf16[16,28,896]{2,1,0:T(8,128)(2,1)} %broadcast_in_dim.23), calls=%async_computation.4 | async-start | bytes 1835008 | tf_op jit(solution)/shard_map/all_to_all | solution.py:422
  180.7 8.3 %attn_grads.1 = (bf16[256,448]{1,0:T(8,128)(2,1)}, bf16[256,448]{1,0:T(8,128)(2,1)}) custom-call(s32[1]{0:T(128)} %bitcast.26.shift_ref, bf16[4,256,896]{2,1,0:T(8,128)(2,1)} %all-gather.4.cloned.1.call-done.own_ref.own_hbm, bf16[4,256,896]{2,1,0:T(8,128)(2,1)} %collective-permute-done.1.other_ref.other_hbm, bf16[2,4,16,896]{3,2,1,0:T(8,128)(2,1)} %copy-done.7, ...), custom_call_target="tpu_custom_call" | custom-call | flops 1644167168 | bytes 8388608 | tf_op jit(solution)/shard_map/attn_grads/pallas_call | solution.py:302
  189.0 3.0 %all-to-all-done.4.mine_ref = bf16[16,28,896]{2,1,0:T(8,128)(2,1)S(1)} async-done(((bf16[16,28,896]{2,1,0:T(8,128)(2,1)}), bf16[16,28,896]{2,1,0:T(8,128)(2,1)S(1)}, u32[]{:S(2)}, u32[]{:S(2)}) %all-to-all-start.4) | async-done | bytes 802848 | tf_op jit(solution)/shard_map/all_to_all | solution.py:422
  192.3 7.2 %collective-permute-start.7 = (bf16[16,28,896]{2,0,1:T(8,128)(2,1)S(1)}, bf16[16,28,896]{2,0,1:T(8,128)(2,1)S(1)}, u32[]{:S(2)}, u32[]{:S(2)}) collective-permute-start(bf16[16,28,896]{2,0,1:T(8,128)(2,1)S(1)} %copy.22), channel_id=1, source_target_pairs={{0,16},{16,0},{1,17},{17,1},{2,18},{18,2},{3,19},{19,3},{4,20},{20... | collective-permute-start | bytes 2408456 | tf_op jit(solution)/shard_map/ppermute | solution.py:38
  199.5 1.9 collective-permute-start.6
  203.1 1.1 maximum_select_fusion
  204.3 1.4 join_halves.1
  (74 shorter events, 4.0 us)
Async XLA Ops:
  7.2 61.9 %copy-start = (bf16[896,896]{1,0:T(8,128)(2,1)S(1)}, bf16[896,896]{1,0:T(8,128)(2,1)}, u32[]{:S(2)}) copy-start(bf16[896,896]{1,0:T(8,128)(2,1)} %param.8) | copy-start | bytes 4816900
  7.2 58.9 %all-gather.4.cloned.1.call-start = ((), (), s32[]{:S(2)}) async-start(), calls=%async_computation.5 | async-start | bytes 2293760 | tf_op jit(solution)/shard_map/all_gather | solution.py:328
  25.1 7.8 %all-to-all-start = ((f32[4,3,896]{2,1,0:T(4,128)}), f32[4,3,896]{2,1,0:T(4,128)S(1)}, u32[]{:S(2)}, u32[]{:S(2)}) async-start(f32[4,3,896]{2,1,0:T(4,128)} %broadcast_in_dim.17), calls=%async_computation | async-start | bytes 114688 | tf_op jit(solution)/shard_map/all_to_all | solution.py:354
  33.3 13.4 %copy-start.15 = (bf16[1,2,128,896]{3,2,1,0:T(8,128)(2,1)S(1)}, bf16[1,2,128,896]{3,2,1,0:T(8,128)(2,1)}, u32[]{:S(2)}) copy-start(bf16[1,2,128,896]{3,2,1,0:T(8,128)(2,1)} %param.7) | copy-start | bytes 1376260
  35.5 27.3 %all-to-all-start.1 = ((f32[32,2,3840]{2,1,0:T(2,128)}), f32[32,2,3840]{2,1,0:T(2,128)}, u32[]{:S(2)}, u32[]{:S(2)}) async-start(f32[32,2,3840]{2,1,0:T(2,128)} %concatenate.50), calls=%async_computation.1 | async-start | bytes 1966080 | tf_op jit(solution)/shard_map/all_to_all | solution.py:373
  46.6 134.0 %all-gather.6.cloned.1.call-start = ((), (), s32[]{:S(2)}) async-start(), calls=%async_computation.6 | async-start | bytes 3411968 | tf_op jit(solution)/shard_map/all_gather | solution.py:387
  47.5 3.4 %collective-permute-start = (bf16[256,448]{1,0:T(8,128)(2,1)S(1)}, bf16[256,448]{1,0:T(8,128)(2,1)S(1)}, u32[]{:S(2)}, u32[]{:S(2)}) collective-permute-start(bf16[256,448]{1,0:T(8,128)(2,1)S(1)} %get-tuple-element.59), channel_id=1, source_target_pairs={{0,16},{16,0},{1,17},{17,1},{2,18},{18,2},{3,19},{19,3},{4,20},{20... | collective-permute-start | bytes 688136 | tf_op jit(solution)/shard_map/ppermute | solution.py:38
  51.0 0.7 copy-start.12
  66.1 21.9 %copy-start.2 = (bf16[4,256,896]{2,1,0:T(8,128)(2,1)S(1)}, bf16[4,256,896]{2,1,0:T(8,128)(2,1)}, u32[]{:S(2)}) copy-start(bf16[4,256,896]{2,1,0:T(8,128)(2,1)} %all-gather.4.cloned.1.call-done.own_ref.own_hbm) | copy-start | bytes 5505028
  66.1 21.9 %collective-permute-start.1 = (bf16[4,256,896]{2,1,0:T(8,128)(2,1)}, bf16[4,256,896]{2,1,0:T(8,128)(2,1)}, u32[]{:S(2)}, u32[]{:S(2)}) collective-permute-start(bf16[4,256,896]{2,1,0:T(8,128)(2,1)} %all-gather.4.cloned.1.call-done.own_ref.own_hbm), channel_id=1, source_target_pairs={{0,16},{16,0},{1,17},{17,1},{2,18},{18,2},{3,19},{19,3},{4,20},{20... | collective-permute-start | bytes 5505032 | tf_op jit(solution)/shard_map/ppermute | solution.py:38
  69.8 25.7 %collective-permute-start.2 = (bf16[112,896]{1,0:T(8,128)(2,1)}, bf16[112,896]{1,0:T(8,128)(2,1)}, u32[]{:S(2)}, u32[]{:S(2)}) collective-permute-start(bf16[112,896]{1,0:T(8,128)(2,1)} %constant_dynamic-slice_fusion), channel_id=1, source_target_pairs={{0,0},{1,1},{2,2},{3,3},{18,16},{19,17},{16,18},{17,19},{129,128},... | collective-permute-start | bytes 602120 | tf_op jit(solution)/shard_map/ppermute | solution.py:335
  81.0 7.1 %copy-start.11 = (bf16[256,448]{1,0:T(8,128)(2,1)S(1)}, bf16[256,448]{1,0:T(8,128)(2,1)}, u32[]{:S(2)}) copy-start(bf16[256,448]{1,0:T(8,128)(2,1)} %get-tuple-element.58.keep_ref) | copy-start | bytes 688132
  81.0 7.0 %copy-start.13 = (bf16[256,448]{1,0:T(8,128)(2,1)S(1)}, bf16[256,448]{1,0:T(8,128)(2,1)}, u32[]{:S(2)}) copy-start(bf16[256,448]{1,0:T(8,128)(2,1)} %copy-done.12) | copy-start | bytes 688132
  86.5 0.7 copy-start.3
  87.2 0.8 copy-start.9
  88.0 5.1 %copy-start.7 = (bf16[2,4,16,896]{3,2,1,0:T(8,128)(2,1)}, bf16[2,4,16,896]{3,2,1,0:T(8,128)(2,1)S(1)}, u32[]{:S(2)}) copy-start(bf16[2,4,16,896]{3,2,1,0:T(8,128)(2,1)S(1)} %get-tuple-element.33.pieces_ref) | copy-start | bytes 688132
  93.1 1.7 copy-start.1
  94.8 0.7 copy-start.5
  95.5 4.8 %copy-start.8 = (bf16[2,4,16,896]{3,2,1,0:T(8,128)(2,1)S(1)}, bf16[2,4,16,896]{3,2,1,0:T(8,128)(2,1)}, u32[]{:S(2)}) copy-start(bf16[2,4,16,896]{3,2,1,0:T(8,128)(2,1)} %copy-done.7) | copy-start | bytes 688132
  95.5 6.8 %copy-start.4 = (f32[2,256,1]{2,1,0:T(8,128)S(1)}, f32[2,256,1]{2,1,0:T(8,128)}, u32[]{:S(2)}) copy-start(f32[2,256,1]{2,1,0:T(8,128)} %copy-done.3) | copy-start | bytes 6148
  95.5 6.9 %copy-start.10 = (f32[4,28,896]{2,1,0:T(8,128)S(1)}, f32[4,28,896]{2,1,0:T(8,128)}, u32[]{:S(2)}) copy-start(f32[4,28,896]{2,1,0:T(8,128)} %copy-done.9) | copy-start | bytes 1204228
  95.5 44.4 %all-to-all-start.2 = ((bf16[16,112,896]{2,1,0:T(8,128)(2,1)}), bf16[16,112,896]{2,1,0:T(8,128)(2,1)}, u32[]{:S(2)}, u32[]{:S(2)}) async-start(bf16[16,112,896]{2,1,0:T(8,128)(2,1)} %copy-done.1), calls=%async_computation.2 | async-start | bytes 6422528 | tf_op jit(solution)/shard_map/all_to_all | solution.py:388
  100.2 17.4 %copy-start.6 = (f32[2,256,1]{2,1,0:T(8,128)S(1)}, f32[2,256,1]{2,1,0:T(8,128)}, u32[]{:S(2)}) copy-start(f32[2,256,1]{2,1,0:T(8,128)} %copy-done.5) | copy-start | bytes 6148
  100.2 17.5 %copy-start.14 = (bf16[1,2,128,896]{3,2,1,0:T(8,128)(2,1)S(1)}, bf16[1,2,128,896]{3,2,1,0:T(8,128)(2,1)}, u32[]{:S(2)}) copy-start(bf16[1,2,128,896]{3,2,1,0:T(8,128)(2,1)} %param.6) | copy-start | bytes 1376260
  102.6 16.1 %collective-permute-start.5 = (f32[30,896]{1,0:T(8,128)S(1)}, f32[30,896]{1,0:T(8,128)S(1)}, u32[]{:S(2)}, u32[]{:S(2)}) collective-permute-start(f32[30,896]{1,0:T(8,128)S(1)} %get-tuple-element.62), channel_id=1, source_target_pairs={{0,3},{1,0},{2,1},{3,2},{4,7},{5,4},{6,5},{7,6},{8,11},{9,8},{10,9... | collective-permute-start | bytes 322568 | tf_op jit(solution)/shard_map/ppermute | solution.py:396
  106.6 14.6 %collective-permute-start.4 = (f32[30,896]{1,0:T(8,128)S(1)}, f32[30,896]{1,0:T(8,128)S(1)}, u32[]{:S(2)}, u32[]{:S(2)}) collective-permute-start(f32[30,896]{1,0:T(8,128)S(1)} %get-tuple-element.61), channel_id=1, source_target_pairs={{0,2},{1,3},{2,0},{3,1},{4,6},{5,7},{6,4},{7,5},{8,10},{9,11},{10,... | collective-permute-start | bytes 322568 | tf_op jit(solution)/shard_map/ppermute | solution.py:396
  112.4 15.8 %collective-permute-start.3 = (f32[30,896]{1,0:T(8,128)S(1)}, f32[30,896]{1,0:T(8,128)S(1)}, u32[]{:S(2)}, u32[]{:S(2)}) collective-permute-start(f32[30,896]{1,0:T(8,128)S(1)} %get-tuple-element.60), channel_id=1, source_target_pairs={{0,1},{1,2},{2,3},{3,0},{4,5},{5,6},{6,7},{7,4},{8,9},{9,10},{10,1... | collective-permute-start | bytes 322568 | tf_op jit(solution)/shard_map/ppermute | solution.py:396
  170.3 21.8 %all-to-all-start.4 = ((bf16[16,28,896]{2,1,0:T(8,128)(2,1)}), bf16[16,28,896]{2,1,0:T(8,128)(2,1)S(1)}, u32[]{:S(2)}, u32[]{:S(2)}) async-start(bf16[16,28,896]{2,1,0:T(8,128)(2,1)} %broadcast_in_dim.23), calls=%async_computation.4 | async-start | bytes 1835008 | tf_op jit(solution)/shard_map/all_to_all | solution.py:422
  189.0 14.1 %copy-start.16 = (bf16[256,448]{1,0:T(8,128)(2,1)S(1)}, bf16[256,448]{1,0:T(8,128)(2,1)}, u32[]{:S(2)}) copy-start(bf16[256,448]{1,0:T(8,128)(2,1)} %get-tuple-element.49) | copy-start | bytes 688132
  192.3 11.9 %collective-permute-start.7 = (bf16[16,28,896]{2,0,1:T(8,128)(2,1)S(1)}, bf16[16,28,896]{2,0,1:T(8,128)(2,1)S(1)}, u32[]{:S(2)}, u32[]{:S(2)}) collective-permute-start(bf16[16,28,896]{2,0,1:T(8,128)(2,1)S(1)} %copy.22), channel_id=1, source_target_pairs={{0,16},{16,0},{1,17},{17,1},{2,18},{18,2},{3,19},{19,3},{4,20},{20... | collective-permute-start | bytes 2408456 | tf_op jit(solution)/shard_map/ppermute | solution.py:38
  199.5 3.6 %collective-permute-start.6 = (bf16[256,448]{1,0:T(8,128)(2,1)}, bf16[256,448]{1,0:T(8,128)(2,1)S(1)}, u32[]{:S(2)}, u32[]{:S(2)}) collective-permute-start(bf16[256,448]{1,0:T(8,128)(2,1)} %get-tuple-element.50), channel_id=1, source_target_pairs={{0,16},{16,0},{1,17},{17,1},{2,18},{18,2},{3,19},{19,3},{4,20},{20... | collective-permute-start | bytes 688136 | tf_op jit(solution)/shard_map/ppermute | solution.py:38
Sparse Core Ops, SparseCore 0:
  10.1 55.9 all-gather.3
  95.6 82.0 all-gather.5

commit v15 on v14

--- a/solution.py
+++ b/solution.py
@@ -228,28 +228,25 @@
     )(spread)
 
 
-def join_kernel(core_ref, mine_ref, other_ref, out_ref):
-    core = core_ref[0]
-    for which, ref in ((core, mine_ref), (1 - core, other_ref)):
-        rows = [ref[place].astype(f32) for place in range(NX * NY)]
-        out_ref[pl.ds(pl.multiple_of(which * HALF, HALF), HALF), :] = jnp.concatenate(
-            rows, 0
-        ).astype(bf16)
-
-
-def join_halves(core, mine, other):
+def join_kernel(whole_ref, out_ref):
+    for core in range(NC):
+        rows = [whole_ref[place * NC + core].astype(f32) for place in range(NX * NY)]
+        out_ref[core * HALF : (core + 1) * HALF, :] = jnp.concatenate(rows, 0).astype(bf16)
+
+
+def join_slices(whole):
     spec = pl.BlockSpec(memory_space=pltpu.VMEM)
     return pl.pallas_call(
         join_kernel,
         out_shape=jax.ShapeDtypeStruct((FEAT, COLS), bf16),
-        in_specs=[pl.BlockSpec(memory_space=pltpu.SMEM), spec, spec],
+        in_specs=[spec],
         out_specs=spec,
         compiler_params=pltpu.CompilerParams(vmem_limit_bytes=16 * 1024 * 1024),
         cost_estimate=pl.CostEstimate(
             flops=0, bytes_accessed=4 * 1024 * 1024, transcendentals=0
         ),
-        name="join_halves",
-    )(core, mine, other)
+        name="join_slices",
+    )(whole)
 
 
 def attn_kernel(
@@ -418,18 +415,17 @@
     second = lax.all_to_all(sum_senders(spread), "r", 0, 0)
     second_sum = jnp.sum(second.astype(f32), 0)
     total = first_sum - second_sum
-    done = jnp.broadcast_to(total.astype(bf16)[None], (NX * NY, SLICE, COLS))
-    half = lax.all_to_all(done, PLANE, 0, 0)
+    done = jnp.broadcast_to(total.astype(bf16)[None], (GROUP, SLICE, COLS))
+    whole = lax.all_to_all(done, DP, 0, 0)
     keep, give = attn_grads(
         (ir + 2 * ic).reshape(1), state_all, state_other, pieces, w_all, coef, first_col
     )
-    half, keep, give = lax.optimization_barrier((half, keep, give))
-    half_other = swap_core(half)
     arrived = swap_core(give)
     grad_attn = jnp.where(
         ic == 0, jnp.concatenate([keep, arrived], 1), jnp.concatenate([arrived, keep], 1)
     ).reshape(1, 2, SEQ, FEAT)
-    grad_weight = join_halves(ic.reshape(1), half, half_other)
+    whole, grad_attn = lax.optimization_barrier((whole, grad_attn))
+    grad_weight = join_slices(whole)
     return (grad_hidden, grad_attn, grad_weight, totals[0], totals[1, 0])
 
 

time: 214 us -> 219 us (1.023)
  waiting for transfers between devices: 44.7 us -> 52.7 us
  starting transfers between devices: 69.8 us -> 66.4 us
    all_to_all x1, waiting for transfers between devices: 3.01 us -> 11.4 us  [body(): whole = lax.all_to_all(done, DP, 0, 0)]
    ppermute x4 -> x3, starting transfers between devices: 14.3 us -> 7.47 us  [swap_core(): return lax.ppermute(value, 'c', [(0, 1), (1, 0)])]
    all_to_all x1, starting transfers between devices: 10.4 us -> 13.7 us  [body(): whole = lax.all_to_all(done, DP, 0, 0)]
    unnamed x36 -> x34, local copies, waits for them, and re-layouts: 4.73 us -> 4.72 us
  transfers between devices with their start and end apart: 14 -> 13, of which waited for: 9 -> 9; matrix products, arithmetic and copies ran while one was open for 8% -> 9% of each run, Pallas kernels for 10% -> 9%
where the time goes in v15:
time: 219 us; the launch traced here: 218 us
  starting transfers between devices  66.4 us (30%)
  waiting for transfers between devices  52.7 us (24%)
  blocking collectives  38 us (17%)
  Pallas kernels  21.9 us (10%)
  local copies, waits for them, and re-layouts  15.4 us (7%)
  between operations  15.3 us (7%)
  other arithmetic  8.32 us (4%)
    all_to_all x1, blocking collectives, body(): second = lax.all_to_all(sum_senders(spread), 'r', 0, 0)  26.2 us
    ppermute x3, starting transfers between devices, body(): lax.ppermute(jnp.concatenate([outgoing, tail], 0), 'r', [(j, (j + step) %...  15 us
    all_to_all x1, starting transfers between devices, body(): whole = lax.all_to_all(done, DP, 0, 0)  13.7 us
    psum x1, blocking collectives, body(): square = lax.psum(jnp.sum(states * states, -1), 't') / D  11.8 us
    all_to_all x1, waiting for transfers between devices, body(): spread = lax.all_to_all(partial, PLANE, 0, 0)  11.6 us
    all_to_all x1, waiting for transfers between devices, body(): whole = lax.all_to_all(done, DP, 0, 0)  11.4 us
    all_to_all x1, waiting for transfers between devices, body(): got = lax.all_to_all(send, DP, 0, 0)  11.2 us
    ppermute x1, starting transfers between devices, body(): lax.ppermute(lax.dynamic_slice(o_weight, (ic * HALF + iy * W_ROWS, 0), (W...  11.1 us
  transfers between devices with their start and end apart: 13, of which 9 were waited for; matrix products, arithmetic and copies ran while one was open for 9% of the time, Pallas kernels for 9%

profile of v15, /device:TPU:1, one launch (start us, length us, event | category | flops | bytes accessed | tf_op | source)
XLA Modules:
  0.0 218.1 jit_solution(9470849708507355181)
XLA Ops:
  7.2 0.7 all-gather.4.cloned.1.call-update
  7.9 0.7 broadcast_in_dim.16
  8.6 1.2 fusion.2
  9.8 11.8 %psum.7 = f32[2,128]{1,0:T(2,128)S(1)} all-reduce(f32[2,128]{1,0:T(2,128)S(1)} %fusion.2), channel_id=1, replica_groups=mesh['x'=4,'y'=4,'c'=2,'t'=4,'r'=4] {'t'}, use_global_device_ids=true, to_apply=%region_1.2 | all-reduce | flops 256 | bytes 2048 | tf_op jit(solution)/shard_map/psum | solution.py:342
  21.6 0.7 convert_bitcast_fusion.1
  22.3 0.7 fusion.10
  23.1 1.4 fusion.6
  24.5 0.6 broadcast_in_dim.17
  25.1 3.3 %all-to-all-start = ((f32[4,3,896]{2,1,0:T(4,128)}), f32[4,3,896]{2,1,0:T(4,128)S(1)}, u32[]{:S(2)}, u32[]{:S(2)}) async-start(f32[4,3,896]{2,1,0:T(4,128)} %broadcast_in_dim.17), calls=%async_computation | async-start | bytes 114688 | tf_op jit(solution)/shard_map/all_to_all | solution.py:351
  29.4 3.6 %all-to-all-done = f32[4,3,896]{2,1,0:T(4,128)S(1)} async-done(((f32[4,3,896]{2,1,0:T(4,128)}), f32[4,3,896]{2,1,0:T(4,128)S(1)}, u32[]{:S(2)}, u32[]{:S(2)}) %all-to-all-start) | async-done | bytes 43040 | tf_op jit(solution)/shard_map/all_to_all | solution.py:351
  33.3 2.2 %concatenate.50 = f32[32,2,3840]{2,1,0:T(2,128)} concatenate(f32[32,2,3712]{2,1,0:T(2,128)S(1)} %broadcast_in_dim.18, f32[32,2,28]{2,1,0:T(2,128)S(1)} %copy.18, f32[32,2,2]{2,1,0:T(2,128)S(1)} %broadcast_in_dim.19, f32[32,2,98]{2,1,0:T(2,128)S(1)} %broadcast_in_dim.20), dimensions={2} | concatenate | bytes 1966080 | tf_op jit(solution)/shard_map/concatenate | solution.py:361
  35.5 11.1 %all-to-all-start.1 = ((f32[32,2,3840]{2,1,0:T(2,128)}), f32[32,2,3840]{2,1,0:T(2,128)}, u32[]{:S(2)}, u32[]{:S(2)}) async-start(f32[32,2,3840]{2,1,0:T(2,128)} %concatenate.50), calls=%async_computation.1 | async-start | bytes 1966080 | tf_op jit(solution)/shard_map/all_to_all | solution.py:370
  46.7 0.8 broadcast_select_fusion
  47.5 2.2 %collective-permute-start = (bf16[256,448]{1,0:T(8,128)(2,1)S(1)}, bf16[256,448]{1,0:T(8,128)(2,1)S(1)}, u32[]{:S(2)}, u32[]{:S(2)}) collective-permute-start(bf16[256,448]{1,0:T(8,128)(2,1)S(1)} %get-tuple-element.57), channel_id=1, source_target_pairs={{0,16},{16,0},{1,17},{17,1},{2,18},{18,2},{3,19},{19,3},{4,20},{20... | collective-permute-start | bytes 688136 | tf_op jit(solution)/shard_map/ppermute | solution.py:38
  49.8 1.2 collective-permute-done.given_ref
  51.0 0.7 copy-done.12
  51.7 11.2 %all-to-all-done.1 = f32[32,2,3840]{2,1,0:T(2,128)} async-done(((f32[32,2,3840]{2,1,0:T(2,128)}), f32[32,2,3840]{2,1,0:T(2,128)}, u32[]{:S(2)}, u32[]{:S(2)}) %all-to-all-start.1) | async-done | bytes 983072 | tf_op jit(solution)/shard_map/all_to_all | solution.py:370
  62.9 3.2 %all-gather.4.cloned.1.call-done.own_ref.own_hbm = bf16[4,256,896]{2,1,0:T(8,128)(2,1)} async-done(((bf16[1,256,896]{2,1,0:T(8,128)(2,1)}), bf16[4,256,896]{2,1,0:T(8,128)(2,1)}) %all-gather.4.cloned.1.call-update) | async-done | bytes 1835024 | tf_op jit(solution)/shard_map/all_gather | solution.py:325
  66.1 3.0 %collective-permute-start.1 = (bf16[4,256,896]{2,1,0:T(8,128)(2,1)}, bf16[4,256,896]{2,1,0:T(8,128)(2,1)}, u32[]{:S(2)}, u32[]{:S(2)}) collective-permute-start(bf16[4,256,896]{2,1,0:T(8,128)(2,1)} %all-gather.4.cloned.1.call-done.own_ref.own_hbm), channel_id=1, source_target_pairs={{0,16},{16,0},{1,17},{17,1},{2,18},{18,2},{3,19},{19,3},{4,20},{20... | collective-permute-start | bytes 5505032 | tf_op jit(solution)/shard_map/ppermute | solution.py:38
  69.1 0.7 constant_dynamic-slice_fusion
  69.8 11.1 %collective-permute-start.2 = (bf16[112,896]{1,0:T(8,128)(2,1)}, bf16[112,896]{1,0:T(8,128)(2,1)}, u32[]{:S(2)}, u32[]{:S(2)}) collective-permute-start(bf16[112,896]{1,0:T(8,128)(2,1)} %constant_dynamic-slice_fusion), channel_id=1, source_target_pairs={{0,0},{1,1},{2,2},{3,3},{18,16},{19,17},{16,18},{17,19},{129,128},... | collective-permute-start | bytes 602120 | tf_op jit(solution)/shard_map/ppermute | solution.py:332
  81.1 1.3 copy.24
  82.4 4.1 %group_math.1 = (f32[4,28,896]{2,1,0:T(8,128)S(1)}, f32[4,1,896]{2,1,0:T(1,128)S(1)}, f32[8,128]{1,0:T(8,128)S(1)}, bf16[2,4,16,896]{3,2,1,0:T(8,128)(2,1)S(1)},...) custom-call(s32[2]{0:T(128)S(1)} %pad_add_fusion.index_ref, f32[2,32,3840]{2,1,0:T(8,128)S(1)} %bitcast.64, ...), custom_call_target="tpu_custom_call" | custom-call | flops 183500800 | bytes 3145728 | tf_op jit(solution)/shard_map/group_math/pallas_call | solution.py:124
  86.5 0.7 copy-done.3
  87.2 0.8 copy-done.9
  88.0 5.0 %weight_partials.1 = (bf16[16,112,896]{2,1,0:T(8,128)(2,1)S(1)}, f32[2,256,1]{2,1,0:T(8,128)S(1)}) custom-call(bf16[4,256,896]{2,1,0:T(8,128)(2,1)S(1)} %copy-done.2, bf16[4,256,896]{2,1,0:T(8,128)(2,1)} %collective-permute-done.1.other_ref.other_hbm, bf16[256,448]{1,0:T(8,128)(2,1)S(1)} %copy-done.11, bf16[256,448]{1,0:T(8,128)(2,1)S(1)} %copy-done.13, ...), custom_call_target="tpu_custom_call" | custom-call | flops 1644167168 | bytes 8388608 | tf_op jit(solution)/shard_map/weight_partials/pallas_call | solution.py:178
  93.1 1.7 copy-done.1
  94.8 0.7 copy-done.5
  95.5 4.6 %all-to-all-start.2 = ((bf16[16,112,896]{2,1,0:T(8,128)(2,1)}), bf16[16,112,896]{2,1,0:T(8,128)(2,1)}, u32[]{:S(2)}, u32[]{:S(2)}) async-start(bf16[16,112,896]{2,1,0:T(8,128)(2,1)} %copy-done.1), calls=%async_computation.2 | async-start | bytes 6422528 | tf_op jit(solution)/shard_map/all_to_all | solution.py:385
  100.9 0.7 pad.18.clone
  101.7 0.7 pad_bitcast_fusion
  102.6 4.0 %collective-permute-start.5 = (f32[30,896]{1,0:T(8,128)S(1)}, f32[30,896]{1,0:T(8,128)S(1)}, u32[]{:S(2)}, u32[]{:S(2)}) collective-permute-start(f32[30,896]{1,0:T(8,128)S(1)} %get-tuple-element.60), channel_id=1, source_target_pairs={{0,3},{1,0},{2,1},{3,2},{4,7},{5,4},{6,5},{7,6},{8,11},{9,8},{10,9... | collective-permute-start | bytes 322568 | tf_op jit(solution)/shard_map/ppermute | solution.py:393
  106.6 5.9 %collective-permute-start.4 = (f32[30,896]{1,0:T(8,128)S(1)}, f32[30,896]{1,0:T(8,128)S(1)}, u32[]{:S(2)}, u32[]{:S(2)}) collective-permute-start(f32[30,896]{1,0:T(8,128)S(1)} %get-tuple-element.59), channel_id=1, source_target_pairs={{0,2},{1,3},{2,0},{3,1},{4,6},{5,7},{6,4},{7,5},{8,10},{9,11},{10,... | collective-permute-start | bytes 322568 | tf_op jit(solution)/shard_map/ppermute | solution.py:393
  112.5 5.1 %collective-permute-start.3 = (f32[30,896]{1,0:T(8,128)S(1)}, f32[30,896]{1,0:T(8,128)S(1)}, u32[]{:S(2)}, u32[]{:S(2)}) collective-permute-start(f32[30,896]{1,0:T(8,128)S(1)} %get-tuple-element.58), channel_id=1, source_target_pairs={{0,1},{1,2},{2,3},{3,0},{4,5},{5,6},{6,7},{7,4},{8,9},{9,10},{10,1... | collective-permute-start | bytes 322568 | tf_op jit(solution)/shard_map/ppermute | solution.py:393
  117.7 1.0 fusion.5
  118.7 2.5 %collective-permute-done.4 = f32[30,896]{1,0:T(8,128)S(1)} collective-permute-done((f32[30,896]{1,0:T(8,128)S(1)}, f32[30,896]{1,0:T(8,128)S(1)}, u32[]{:S(2)}, u32[]{:S(2)}) %collective-permute-start.4) | collective-permute-done | bytes 107552 | tf_op jit(solution)/shard_map/ppermute | solution.py:393
  121.2 7.0 %collective-permute-done.3 = f32[30,896]{1,0:T(8,128)S(1)} collective-permute-done((f32[30,896]{1,0:T(8,128)S(1)}, f32[30,896]{1,0:T(8,128)S(1)}, u32[]{:S(2)}, u32[]{:S(2)}) %collective-permute-start.3) | collective-permute-done | bytes 107552 | tf_op jit(solution)/shard_map/ppermute | solution.py:393
  128.3 11.6 %all-to-all-done.2.spread_ref = bf16[16,112,896]{2,1,0:T(8,128)(2,1)} async-done(((bf16[16,112,896]{2,1,0:T(8,128)(2,1)}), bf16[16,112,896]{2,1,0:T(8,128)(2,1)}, u32[]{:S(2)}, u32[]{:S(2)}) %all-to-all-start.2) | async-done | bytes 3211296 | tf_op jit(solution)/shard_map/all_to_all | solution.py:385
  140.0 3.0 %sum_senders.1 = bf16[4,28,896]{2,1,0:T(8,128)(2,1)S(1)} custom-call(bf16[16,112,896]{2,1,0:T(8,128)(2,1)} %all-to-all-done.2.spread_ref), custom_call_target="tpu_custom_call" | custom-call | flops 1605632 | bytes 4194304 | tf_op jit(solution)/shard_map/sum_senders/pallas_call | solution.py:216
  143.0 26.2 %all_to_all.25 = bf16[4,28,896]{2,1,0:T(8,128)(2,1)S(1)} all-to-all(bf16[4,28,896]{2,1,0:T(8,128)(2,1)S(1)} %sum_senders.1), channel_id=1, replica_groups=mesh['x'=4,'y'=4,'c'=2,'t'=4,'r'=4] {'r'}, dimensions={0} | all-to-all | bytes 401408 | tf_op jit(solution)/shard_map/all_to_all | solution.py:415
  169.3 1.4 broadcast_in_dim.23
  170.6 13.7 %all-to-all-start.4 = ((bf16[32,28,896]{2,1,0:T(8,128)(2,1)}), bf16[32,28,896]{2,1,0:T(8,128)(2,1)S(1)}, u32[]{:S(2)}, u32[]{:S(2)}) async-start(bf16[32,28,896]{2,1,0:T(8,128)(2,1)} %broadcast_in_dim.23), calls=%async_computation.4 | async-start | bytes 3670016 | tf_op jit(solution)/shard_map/all_to_all | solution.py:419
  184.4 8.3 %attn_grads.1 = (bf16[256,448]{1,0:T(8,128)(2,1)}, bf16[256,448]{1,0:T(8,128)(2,1)}) custom-call(s32[1]{0:T(128)} %bitcast.26.shift_ref, bf16[4,256,896]{2,1,0:T(8,128)(2,1)} %all-gather.4.cloned.1.call-done.own_ref.own_hbm, bf16[4,256,896]{2,1,0:T(8,128)(2,1)} %collective-permute-done.1.other_ref.other_hbm, bf16[2,4,16,896]{3,2,1,0:T(8,128)(2,1)} %copy-done.7, ...), custom_call_target="tpu_custom_call" | custom-call | flops 1644167168 | bytes 8388608 | tf_op jit(solution)/shard_map/attn_grads/pallas_call | solution.py:299
  192.7 2.3 %collective-permute-start.6 = (bf16[256,448]{1,0:T(8,128)(2,1)}, bf16[256,448]{1,0:T(8,128)(2,1)S(1)}, u32[]{:S(2)}, u32[]{:S(2)}) collective-permute-start(bf16[256,448]{1,0:T(8,128)(2,1)} %get-tuple-element.47), channel_id=1, source_target_pairs={{0,16},{16,0},{1,17},{17,1},{2,18},{18,2},{3,19},{19,3},{4,20},{20... | collective-permute-start | bytes 688136 | tf_op jit(solution)/shard_map/ppermute | solution.py:38
  195.5 0.6 slice_reduce_fusion.2
  196.4 2.1 maximum_select_fusion
  198.5 11.4 %all-to-all-done.4.whole_ref = bf16[32,28,896]{2,1,0:T(8,128)(2,1)S(1)} async-done(((bf16[32,28,896]{2,1,0:T(8,128)(2,1)}), bf16[32,28,896]{2,1,0:T(8,128)(2,1)S(1)}, u32[]{:S(2)}, u32[]{:S(2)}) %all-to-all-start.4) | async-done | bytes 1605664 | tf_op jit(solution)/shard_map/all_to_all | solution.py:419
  209.8 1.4 join_slices.1
  (68 shorter events, 2.6 us)
Async XLA Ops:
  7.2 61.9 %copy-start = (bf16[896,896]{1,0:T(8,128)(2,1)S(1)}, bf16[896,896]{1,0:T(8,128)(2,1)}, u32[]{:S(2)}) copy-start(bf16[896,896]{1,0:T(8,128)(2,1)} %param.8) | copy-start | bytes 4816900
  7.2 58.9 %all-gather.4.cloned.1.call-start = ((), (), s32[]{:S(2)}) async-start(), calls=%async_computation.5 | async-start | bytes 2293760 | tf_op jit(solution)/shard_map/all_gather | solution.py:325
  25.1 7.8 %all-to-all-start = ((f32[4,3,896]{2,1,0:T(4,128)}), f32[4,3,896]{2,1,0:T(4,128)S(1)}, u32[]{:S(2)}, u32[]{:S(2)}) async-start(f32[4,3,896]{2,1,0:T(4,128)} %broadcast_in_dim.17), calls=%async_computation | async-start | bytes 114688 | tf_op jit(solution)/shard_map/all_to_all | solution.py:351
  33.3 13.4 %copy-start.15 = (bf16[1,2,128,896]{3,2,1,0:T(8,128)(2,1)S(1)}, bf16[1,2,128,896]{3,2,1,0:T(8,128)(2,1)}, u32[]{:S(2)}) copy-start(bf16[1,2,128,896]{3,2,1,0:T(8,128)(2,1)} %param.7) | copy-start | bytes 1376260
  35.5 27.3 %all-to-all-start.1 = ((f32[32,2,3840]{2,1,0:T(2,128)}), f32[32,2,3840]{2,1,0:T(2,128)}, u32[]{:S(2)}, u32[]{:S(2)}) async-start(f32[32,2,3840]{2,1,0:T(2,128)} %concatenate.50), calls=%async_computation.1 | async-start | bytes 1966080 | tf_op jit(solution)/shard_map/all_to_all | solution.py:370
  46.6 137.7 %all-gather.6.cloned.1.call-start = ((), (), s32[]{:S(2)}) async-start(), calls=%async_computation.6 | async-start | bytes 3411968 | tf_op jit(solution)/shard_map/all_gather | solution.py:384
  47.5 3.4 %collective-permute-start = (bf16[256,448]{1,0:T(8,128)(2,1)S(1)}, bf16[256,448]{1,0:T(8,128)(2,1)S(1)}, u32[]{:S(2)}, u32[]{:S(2)}) collective-permute-start(bf16[256,448]{1,0:T(8,128)(2,1)S(1)} %get-tuple-element.57), channel_id=1, source_target_pairs={{0,16},{16,0},{1,17},{17,1},{2,18},{18,2},{3,19},{19,3},{4,20},{20... | collective-permute-start | bytes 688136 | tf_op jit(solution)/shard_map/ppermute | solution.py:38
  51.0 0.7 copy-start.12
  66.1 21.9 %copy-start.2 = (bf16[4,256,896]{2,1,0:T(8,128)(2,1)S(1)}, bf16[4,256,896]{2,1,0:T(8,128)(2,1)}, u32[]{:S(2)}) copy-start(bf16[4,256,896]{2,1,0:T(8,128)(2,1)} %all-gather.4.cloned.1.call-done.own_ref.own_hbm) | copy-start | bytes 5505028
  66.1 21.9 %collective-permute-start.1 = (bf16[4,256,896]{2,1,0:T(8,128)(2,1)}, bf16[4,256,896]{2,1,0:T(8,128)(2,1)}, u32[]{:S(2)}, u32[]{:S(2)}) collective-permute-start(bf16[4,256,896]{2,1,0:T(8,128)(2,1)} %all-gather.4.cloned.1.call-done.own_ref.own_hbm), channel_id=1, source_target_pairs={{0,16},{16,0},{1,17},{17,1},{2,18},{18,2},{3,19},{19,3},{4,20},{20... | collective-permute-start | bytes 5505032 | tf_op jit(solution)/shard_map/ppermute | solution.py:38
  69.8 25.7 %collective-permute-start.2 = (bf16[112,896]{1,0:T(8,128)(2,1)}, bf16[112,896]{1,0:T(8,128)(2,1)}, u32[]{:S(2)}, u32[]{:S(2)}) collective-permute-start(bf16[112,896]{1,0:T(8,128)(2,1)} %constant_dynamic-slice_fusion), channel_id=1, source_target_pairs={{0,0},{1,1},{2,2},{3,3},{18,16},{19,17},{16,18},{17,19},{129,128},... | collective-permute-start | bytes 602120 | tf_op jit(solution)/shard_map/ppermute | solution.py:332
  81.0 7.1 %copy-start.11 = (bf16[256,448]{1,0:T(8,128)(2,1)S(1)}, bf16[256,448]{1,0:T(8,128)(2,1)}, u32[]{:S(2)}) copy-start(bf16[256,448]{1,0:T(8,128)(2,1)} %get-tuple-element.56.keep_ref) | copy-start | bytes 688132
  81.0 7.1 %copy-start.13 = (bf16[256,448]{1,0:T(8,128)(2,1)S(1)}, bf16[256,448]{1,0:T(8,128)(2,1)}, u32[]{:S(2)}) copy-start(bf16[256,448]{1,0:T(8,128)(2,1)} %copy-done.12) | copy-start | bytes 688132
  86.5 0.7 copy-start.3
  87.2 0.8 copy-start.9
  88.0 5.1 %copy-start.7 = (bf16[2,4,16,896]{3,2,1,0:T(8,128)(2,1)}, bf16[2,4,16,896]{3,2,1,0:T(8,128)(2,1)S(1)}, u32[]{:S(2)}) copy-start(bf16[2,4,16,896]{3,2,1,0:T(8,128)(2,1)S(1)} %get-tuple-element.32.pieces_ref) | copy-start | bytes 688132
  93.1 1.7 copy-start.1
  94.8 0.7 copy-start.5
  95.5 4.8 %copy-start.8 = (bf16[2,4,16,896]{3,2,1,0:T(8,128)(2,1)S(1)}, bf16[2,4,16,896]{3,2,1,0:T(8,128)(2,1)}, u32[]{:S(2)}) copy-start(bf16[2,4,16,896]{3,2,1,0:T(8,128)(2,1)} %copy-done.7) | copy-start | bytes 688132
  95.5 6.8 %copy-start.4 = (f32[2,256,1]{2,1,0:T(8,128)S(1)}, f32[2,256,1]{2,1,0:T(8,128)}, u32[]{:S(2)}) copy-start(f32[2,256,1]{2,1,0:T(8,128)} %copy-done.3) | copy-start | bytes 6148
  95.5 6.9 %copy-start.10 = (f32[4,28,896]{2,1,0:T(8,128)S(1)}, f32[4,28,896]{2,1,0:T(8,128)}, u32[]{:S(2)}) copy-start(f32[4,28,896]{2,1,0:T(8,128)} %copy-done.9) | copy-start | bytes 1204228
  95.5 44.4 %all-to-all-start.2 = ((bf16[16,112,896]{2,1,0:T(8,128)(2,1)}), bf16[16,112,896]{2,1,0:T(8,128)(2,1)}, u32[]{:S(2)}, u32[]{:S(2)}) async-start(bf16[16,112,896]{2,1,0:T(8,128)(2,1)} %copy-done.1), calls=%async_computation.2 | async-start | bytes 6422528 | tf_op jit(solution)/shard_map/all_to_all | solution.py:385
  100.2 17.4 %copy-start.6 = (f32[2,256,1]{2,1,0:T(8,128)S(1)}, f32[2,256,1]{2,1,0:T(8,128)}, u32[]{:S(2)}) copy-start(f32[2,256,1]{2,1,0:T(8,128)} %copy-done.5) | copy-start | bytes 6148
  100.2 17.5 %copy-start.14 = (bf16[1,2,128,896]{3,2,1,0:T(8,128)(2,1)S(1)}, bf16[1,2,128,896]{3,2,1,0:T(8,128)(2,1)}, u32[]{:S(2)}) copy-start(bf16[1,2,128,896]{3,2,1,0:T(8,128)(2,1)} %param.6) | copy-start | bytes 1376260
  102.6 16.1 %collective-permute-start.5 = (f32[30,896]{1,0:T(8,128)S(1)}, f32[30,896]{1,0:T(8,128)S(1)}, u32[]{:S(2)}, u32[]{:S(2)}) collective-permute-start(f32[30,896]{1,0:T(8,128)S(1)} %get-tuple-element.60), channel_id=1, source_target_pairs={{0,3},{1,0},{2,1},{3,2},{4,7},{5,4},{6,5},{7,6},{8,11},{9,8},{10,9... | collective-permute-start | bytes 322568 | tf_op jit(solution)/shard_map/ppermute | solution.py:393
  106.6 14.6 %collective-permute-start.4 = (f32[30,896]{1,0:T(8,128)S(1)}, f32[30,896]{1,0:T(8,128)S(1)}, u32[]{:S(2)}, u32[]{:S(2)}) collective-permute-start(f32[30,896]{1,0:T(8,128)S(1)} %get-tuple-element.59), channel_id=1, source_target_pairs={{0,2},{1,3},{2,0},{3,1},{4,6},{5,7},{6,4},{7,5},{8,10},{9,11},{10,... | collective-permute-start | bytes 322568 | tf_op jit(solution)/shard_map/ppermute | solution.py:393
  112.5 15.8 %collective-permute-start.3 = (f32[30,896]{1,0:T(8,128)S(1)}, f32[30,896]{1,0:T(8,128)S(1)}, u32[]{:S(2)}, u32[]{:S(2)}) collective-permute-start(f32[30,896]{1,0:T(8,128)S(1)} %get-tuple-element.58), channel_id=1, source_target_pairs={{0,1},{1,2},{2,3},{3,0},{4,5},{5,6},{6,7},{7,4},{8,9},{9,10},{10,1... | collective-permute-start | bytes 322568 | tf_op jit(solution)/shard_map/ppermute | solution.py:393
  170.6 39.2 %all-to-all-start.4 = ((bf16[32,28,896]{2,1,0:T(8,128)(2,1)}), bf16[32,28,896]{2,1,0:T(8,128)(2,1)S(1)}, u32[]{:S(2)}, u32[]{:S(2)}) async-start(bf16[32,28,896]{2,1,0:T(8,128)(2,1)} %broadcast_in_dim.23), calls=%async_computation.4 | async-start | bytes 3670016 | tf_op jit(solution)/shard_map/all_to_all | solution.py:419
  192.7 3.7 %collective-permute-start.6 = (bf16[256,448]{1,0:T(8,128)(2,1)}, bf16[256,448]{1,0:T(8,128)(2,1)S(1)}, u32[]{:S(2)}, u32[]{:S(2)}) collective-permute-start(bf16[256,448]{1,0:T(8,128)(2,1)} %get-tuple-element.47), channel_id=1, source_target_pairs={{0,16},{16,0},{1,17},{17,1},{2,18},{18,2},{3,19},{19,3},{4,20},{20... | collective-permute-start | bytes 688136 | tf_op jit(solution)/shard_map/ppermute | solution.py:38
Sparse Core Ops, SparseCore 0:
  10.1 55.9 all-gather.3
  95.6 82.0 all-gather.5
